TPU v7x, 32 devices: a whole 2x2x4 slice. The times are simulated.
32 devices in a mesh: section: 4 (over z), dp: 2 (over y), tensor: 4 (over x, core).
Axes of the slice: x: 2, y: 2, z: 4, core: 2. Of those that a mesh axis runs over, the one named last changes fastest.
Arguments:
- images: float32 [4, 732, 1152], P('dp', 'tensor'), may hold values from -6 to 6
- valid_len: int32 [4], P('dp'), may hold values from 366 to 732
- query_weight: bfloat16 [4, 1152, 1152], P('section', 'dp', 'tensor'), may hold values from -0.1875 to 0.1875
- key_weight: bfloat16 [4, 1152, 1152], P('section', 'dp', 'tensor'), may hold values from -0.1875 to 0.1875
- value_weight: bfloat16 [4, 1152, 1152], P('section', 'dp', 'tensor'), may hold values from -0.1875 to 0.1875
- output_weight: bfloat16 [4, 1152, 1152], P('section', 'tensor', 'dp'), may hold values from -1 to 1
- up_weight: bfloat16 [4, 1152, 4304], P('section', 'dp', 'tensor'), may hold values from -0.1875 to 0.1875
- down_weight: bfloat16 [4, 4304, 1152], P('section', 'tensor', 'dp'), may hold values from -0.09375 to 0.09375
- norm_gains: float32 [4, 2, 1152], P('section', None, ('dp', 'tensor')), may hold values from 0.5 to 1.5
- cotangent: float32 [4, 732, 1152], P('dp', 'tensor'), may hold values from -6 to 6
Outputs:
- activations: float32 [4, 4, 732, 1152], P('section', 'dp', 'tensor')
- input_grads: float32 [4, 4, 732, 1152], P('section', 'dp', 'tensor')
- grad_query: float32 [4, 1152, 1152], P('section', 'dp', 'tensor')
- grad_key: float32 [4, 1152, 1152], P('section', 'dp', 'tensor')
- grad_value: float32 [4, 1152, 1152], P('section', 'dp', 'tensor')
- grad_output: float32 [4, 1152, 1152], P('section', 'tensor', 'dp')
- grad_up: float32 [4, 1152, 4304], P('section', 'dp', 'tensor')
- grad_down: float32 [4, 4304, 1152], P('section', 'tensor', 'dp')
- grad_gains: float32 [4, 2, 1152], P('section', None, ('dp', 'tensor'))
Inputs may be any that keep to these rules, and one draw needn't show every extreme that they name: `valid_len`: number of valid tokens of each image; the keys of later slots are masked.
All inputs are finite; a program needn't handle non-finite values.
Results may differ from a plain program's by a relative error of at most 0.025.
Values may be sent and summed in bfloat16 or wider, within the bound.
No kernel may reach another device: no remote copies, remote signals or barrier semaphores. Data moves between devices by JAX's collectives and lax.ppermute only.
A program may use at most 320 MiB of HBM per device.

v0:
```python
import jax
import jax.numpy as jnp
from jax import lax
from jax.sharding import PartitionSpec as P

HD = 72
IMG_MB = 1


EPS = 1e-06


def shifted_2(shard, axis, by):
    peers = lax.axis_size(axis)
    pairs = [(i, i + by) for i in range(peers) if 0 <= i + by < peers]
    return lax.ppermute(shard, axis, pairs)


def layer_norm(values, gain):
    centre = jnp.mean(values, axis=-1, keepdims=True)
    centred = values - centre
    spread = jnp.mean(centred * centred, axis=-1, keepdims=True)
    return centred * lax.rsqrt(spread + EPS) * gain


def gelu_tanh(values):
    return jax.nn.gelu(values, approximate=True)


def widen(token_rows):
    return lax.all_gather(token_rows, "tensor", axis=1, tiled=True)


def attention_scores(queries, keys_all, valid_rows):
    seq_len = queries.shape[1]
    scores = jnp.einsum(
        "bqhd,bkhd->bhqk", queries, keys_all, preferred_element_type=jnp.float32
    ) * HD ** (-0.5)
    live = jnp.arange(seq_len)[None, :] < valid_rows[:, None]
    return jnp.where(live[:, None, None, :], scores, -1e30)


def forward_pass(start, valid_rows, packed, gains_full):
    w_qkv, w_output, w_upper, w_lower = packed
    batch_size = start.shape[0]
    head_count = w_output.shape[0] // HD
    head_span = head_count * HD
    normed_a = layer_norm(start, gains_full[0]).astype(jnp.bfloat16)
    wide_a = widen(normed_a)
    seq_len = wide_a.shape[1]
    proj_qkv = jnp.einsum("bsd,dc->bsc", wide_a, w_qkv, preferred_element_type=jnp.float32).astype(
        jnp.bfloat16
    )
    queries = proj_qkv[:, :, :head_span].reshape(batch_size, seq_len, head_count, HD)
    keys_all = proj_qkv[:, :, head_span : 2 * head_span].reshape(
        batch_size, seq_len, head_count, HD
    )
    values_all = proj_qkv[:, :, 2 * head_span :].reshape(batch_size, seq_len, head_count, HD)
    scores = attention_scores(queries, keys_all, valid_rows)
    row_max = jnp.max(scores, axis=-1, keepdims=True)
    shifted = jnp.exp(scores - row_max)
    row_total = jnp.sum(shifted, axis=-1, keepdims=True)
    log_total = (row_max + jnp.log(row_total))[..., 0]
    soft_low = (shifted / row_total).astype(jnp.bfloat16)
    head_mix = jnp.einsum(
        "bhqk,bkhd->bqhd", soft_low, values_all, preferred_element_type=jnp.float32
    )
    head_mix = head_mix.astype(jnp.bfloat16).reshape(batch_size, seq_len, head_span)
    attn_terms = jnp.einsum("bsc,cd->bsd", head_mix, w_output, preferred_element_type=jnp.float32)
    hidden = start + lax.psum_scatter(
        attn_terms.astype(jnp.bfloat16), "tensor", scatter_dimension=1, tiled=True
    ).astype(jnp.float32)
    normed_b = layer_norm(hidden, gains_full[1]).astype(jnp.bfloat16)
    inner_pre = jnp.einsum("bsd,df->bsf", normed_b, w_upper, preferred_element_type=jnp.float32)
    activated = gelu_tanh(inner_pre).astype(jnp.bfloat16)
    block_out = hidden + jnp.einsum(
        "bsf,fd->bsd", activated, w_lower, preferred_element_type=jnp.float32
    )
    saved = (
        queries,
        keys_all,
        values_all,
        log_total,
        head_mix,
        hidden,
        inner_pre,
        activated,
        normed_b,
        normed_a,
    )
    return (block_out, saved)


def backward_pass(out_grad, start, valid_rows, saved, packed, gains_full):
    w_qkv, w_output, w_upper, w_lower = packed
    (
        queries,
        keys_all,
        values_all,
        log_total,
        head_mix,
        hidden,
        inner_pre,
        activated,
        normed_b,
        first_rows,
    ) = saved
    batch_size, seq_len, head_count = (queries.shape[0], queries.shape[1], queries.shape[2])
    head_span = head_count * HD
    down_low = out_grad.astype(jnp.bfloat16)
    act_grad = jnp.einsum("bsd,fd->bsf", down_low, w_lower, preferred_element_type=jnp.float32)
    _, gelu_pull = jax.vjp(gelu_tanh, inner_pre)
    inner_grad = gelu_pull(act_grad)[0].astype(jnp.bfloat16)
    normb_grad = jnp.einsum("bsf,df->bsd", inner_grad, w_upper, preferred_element_type=jnp.float32)
    _, norm_pull = jax.vjp(layer_norm, hidden, gains_full[1])
    hidden_part, gain_second = norm_pull(normb_grad)
    hidden_grad = out_grad + hidden_part
    mix_wide = lax.all_gather(hidden_grad.astype(jnp.bfloat16), "tensor", axis=1, tiled=True)
    headmix_grad = jnp.einsum("bsd,cd->bsc", mix_wide, w_output, preferred_element_type=jnp.float32)
    headmix_grad = headmix_grad.astype(jnp.bfloat16).reshape(batch_size, seq_len, head_count, HD)
    scores = attention_scores(queries, keys_all, valid_rows)
    soft = jnp.exp(scores - log_total[..., None])
    soft_low = soft.astype(jnp.bfloat16)
    soft_grad = jnp.einsum(
        "bqhd,bkhd->bhqk", headmix_grad, values_all, preferred_element_type=jnp.float32
    )
    row_dot = jnp.sum(soft * soft_grad, axis=-1, keepdims=True)
    score_grad = (soft * (soft_grad - row_dot)).astype(jnp.bfloat16)
    scale = HD ** (-0.5)
    query_grad = (
        jnp.einsum("bhqk,bkhd->bqhd", score_grad, keys_all, preferred_element_type=jnp.float32)
        * scale
    ).astype(jnp.bfloat16)
    key_grad = (
        jnp.einsum("bhqk,bqhd->bkhd", score_grad, queries, preferred_element_type=jnp.float32)
        * scale
    ).astype(jnp.bfloat16)
    value_grad = jnp.einsum(
        "bhqk,bqhd->bkhd", soft_low, headmix_grad, preferred_element_type=jnp.float32
    ).astype(jnp.bfloat16)
    qkv_grad = jnp.concatenate(
        (
            query_grad.reshape(batch_size, seq_len, head_span),
            key_grad.reshape(batch_size, seq_len, head_span),
            value_grad.reshape(batch_size, seq_len, head_span),
        ),
        axis=2,
    )
    norma_terms = jnp.einsum("bsc,dc->bsd", qkv_grad, w_qkv, preferred_element_type=jnp.float32)
    norma_grad = lax.psum_scatter(
        norma_terms.astype(jnp.bfloat16), "tensor", scatter_dimension=1, tiled=True
    ).astype(jnp.float32)
    _, first_pull = jax.vjp(layer_norm, start, gains_full[0])
    start_part, gain_first = first_pull(norma_grad)
    start_grad = hidden_grad + start_part
    return (
        start_grad,
        jnp.stack((gain_first, gain_second)),
        (qkv_grad, mix_wide, inner_grad, down_low),
    )


def flat_rows(buffer, micro_count):
    used = buffer[:micro_count]
    return used.reshape(-1, used.shape[-1])


def local(
    images,
    valid_len,
    query_weight,
    key_weight,
    value_weight,
    output_weight,
    up_weight,
    down_weight,
    norm_gains,
    cotangent,
):
    section_idx = lax.axis_index("section")
    section_count = lax.axis_size("section")
    micro_count = images.shape[0] // IMG_MB
    tick_count = micro_count + section_count - 1
    gains_full = lax.all_gather(norm_gains[0], ("dp", "tensor"), axis=1, tiled=True)
    gathered = (
        lax.all_gather(query_weight[0], "dp", axis=0, tiled=True),
        lax.all_gather(key_weight[0], "dp", axis=0, tiled=True),
        lax.all_gather(value_weight[0], "dp", axis=0, tiled=True),
        lax.all_gather(output_weight[0], "dp", axis=1, tiled=True),
        lax.all_gather(up_weight[0], "dp", axis=0, tiled=True),
        lax.all_gather(down_weight[0], "dp", axis=1, tiled=True),
    )
    w_query, w_key, w_value, w_output, w_upper, w_lower = gathered
    w_upper, w_lower = (
        lax.all_gather(w_upper, "tensor", axis=1, tiled=True),
        lax.all_gather(w_lower, "tensor", axis=0, tiled=True),
    )
    head_span = w_query.shape[1]
    w_qkv = jnp.concatenate((w_query, w_key, w_value), axis=1)
    packed = (w_qkv, w_output, w_upper, w_lower)
    slot_shape = (micro_count + 1, IMG_MB) + images.shape[1:]
    acts_slots = jnp.zeros(slot_shape, jnp.float32)
    inflow = jnp.zeros((IMG_MB,) + images.shape[1:], jnp.float32)
    buffers = ()
    for step_tick in range(tick_count):
        micro_index = step_tick - section_idx
        active = (micro_index >= 0) & (micro_index < micro_count)
        read_index = jnp.clip(micro_index, 0, micro_count - 1)
        write_index = jnp.where(active, read_index, micro_count)
        row_start = read_index * IMG_MB
        start = jnp.where(
            section_idx == 0, lax.dynamic_slice_in_dim(images, row_start, IMG_MB, 0), inflow
        )
        valid_rows = lax.dynamic_slice_in_dim(valid_len, row_start, IMG_MB, 0)
        block_out, saved = forward_pass(start, valid_rows, packed, gains_full)
        saved = (start,) + saved
        if step_tick == 0:
            buffers = tuple(
                (jnp.zeros((micro_count + 1,) + piece.shape, piece.dtype) for piece in saved)
            )
        buffers = tuple(
            (
                lax.dynamic_update_index_in_dim(buffer, piece, write_index, 0)
                for buffer, piece in zip(buffers, saved)
            )
        )
        acts_slots = lax.dynamic_update_index_in_dim(acts_slots, block_out, write_index, 0)
        if step_tick + 1 < tick_count:
            inflow = shifted_2(block_out.astype(jnp.bfloat16), "section", 1).astype(block_out.dtype)
    grads_slots = jnp.zeros(slot_shape, jnp.float32)
    gain_sums = jnp.zeros(gains_full.shape, jnp.float32)
    back_inflow = jnp.zeros((IMG_MB,) + images.shape[1:], jnp.float32)
    grad_buffers = ()
    for step_tick in range(tick_count):
        micro_index = step_tick - (section_count - 1 - section_idx)
        active = (micro_index >= 0) & (micro_index < micro_count)
        read_index = jnp.clip(micro_index, 0, micro_count - 1)
        write_index = jnp.where(active, read_index, micro_count)
        row_start = read_index * IMG_MB
        out_grad = jnp.where(
            section_idx == section_count - 1,
            lax.dynamic_slice_in_dim(cotangent, row_start, IMG_MB, 0),
            back_inflow,
        )
        valid_rows = lax.dynamic_slice_in_dim(valid_len, row_start, IMG_MB, 0)
        stored = tuple(
            (lax.dynamic_index_in_dim(buffer, read_index, 0, keepdims=False) for buffer in buffers)
        )
        start_grad, gain_terms, grad_rows = backward_pass(
            out_grad, stored[0], valid_rows, stored[1:], packed, gains_full
        )
        if step_tick == 0:
            grad_buffers = tuple(
                (jnp.zeros((micro_count + 1,) + piece.shape, piece.dtype) for piece in grad_rows)
            )
        grad_buffers = tuple(
            (
                lax.dynamic_update_index_in_dim(buffer, piece, write_index, 0)
                for buffer, piece in zip(grad_buffers, grad_rows)
            )
        )
        gain_sums = gain_sums + jnp.where(active, gain_terms, 0.0)
        grads_slots = lax.dynamic_update_index_in_dim(grads_slots, start_grad, write_index, 0)
        if step_tick + 1 < tick_count:
            back_inflow = shifted_2(start_grad.astype(jnp.bfloat16), "section", -1).astype(
                start_grad.dtype
            )
    first_slots = buffers[10][:micro_count]
    first_slots = first_slots.reshape((micro_count * IMG_MB,) + first_slots.shape[2:])
    wide_all = widen(first_slots)
    wide_rows = wide_all.reshape(-1, wide_all.shape[-1])
    qkv_rows = flat_rows(grad_buffers[0], micro_count)
    mix_rows = flat_rows(grad_buffers[1], micro_count)
    inner_rows = flat_rows(grad_buffers[2], micro_count)
    down_rows = flat_rows(grad_buffers[3], micro_count)
    grad_qkv = jnp.einsum("rd,rc->dc", wide_rows, qkv_rows, preferred_element_type=jnp.float32)
    grad_out_local = jnp.einsum(
        "rc,rd->cd",
        flat_rows(buffers[5], micro_count),
        mix_rows,
        preferred_element_type=jnp.float32,
    )
    grad_upper = jnp.einsum(
        "rd,rf->df",
        flat_rows(buffers[9], micro_count),
        inner_rows,
        preferred_element_type=jnp.float32,
    )
    grad_lower = jnp.einsum(
        "rf,rd->fd",
        flat_rows(buffers[8], micro_count),
        down_rows,
        preferred_element_type=jnp.float32,
    )
    query_part = grad_qkv[:, :head_span]
    key_part = grad_qkv[:, head_span : 2 * head_span]
    value_part = grad_qkv[:, 2 * head_span :]
    reduced = (
        lax.psum_scatter(
            query_part.astype(jnp.bfloat16), "dp", scatter_dimension=0, tiled=True
        ).astype(jnp.float32),
        lax.psum_scatter(
            key_part.astype(jnp.bfloat16), "dp", scatter_dimension=0, tiled=True
        ).astype(jnp.float32),
        lax.psum_scatter(
            value_part.astype(jnp.bfloat16), "dp", scatter_dimension=0, tiled=True
        ).astype(jnp.float32),
        lax.psum_scatter(
            grad_out_local.astype(jnp.bfloat16), "dp", scatter_dimension=1, tiled=True
        ).astype(jnp.float32),
        lax.psum_scatter(
            grad_upper.astype(jnp.bfloat16), "dp", scatter_dimension=0, tiled=True
        ).astype(jnp.float32),
        lax.psum_scatter(
            grad_lower.astype(jnp.bfloat16), "dp", scatter_dimension=1, tiled=True
        ).astype(jnp.float32),
    )
    upper_part, lower_part = (
        lax.psum_scatter(
            reduced[4].astype(jnp.bfloat16), "tensor", scatter_dimension=1, tiled=True
        ).astype(jnp.float32),
        lax.psum_scatter(
            reduced[5].astype(jnp.bfloat16), "tensor", scatter_dimension=0, tiled=True
        ).astype(jnp.float32),
    )
    gain_shard = lax.psum_scatter(gain_sums, ("dp", "tensor"), scatter_dimension=1, tiled=True)
    attn_parts = reduced[:4]
    acts_out = acts_slots[:micro_count].reshape(images.shape)
    grads_out = grads_slots[:micro_count].reshape(images.shape)
    return (
        acts_out[None],
        grads_out[None],
        attn_parts[0][None],
        attn_parts[1][None],
        attn_parts[2][None],
        attn_parts[3][None],
        upper_part[None],
        lower_part[None],
        gain_shard[None],
    )


def solution(mesh):
    return jax.shard_map(
        local,
        mesh=mesh,
        in_specs=(
            P("dp", "tensor", None),
            P("dp"),
            P("section", "dp", "tensor"),
            P("section", "dp", "tensor"),
            P("section", "dp", "tensor"),
            P("section", "tensor", "dp"),
            P("section", "dp", "tensor"),
            P("section", "tensor", "dp"),
            P("section", None, ("dp", "tensor")),
            P("dp", "tensor", None),
        ),
        out_specs=(
            P("section", "dp", "tensor", None),
            P("section", "dp", "tensor", None),
            P("section", "dp", "tensor"),
            P("section", "dp", "tensor"),
            P("section", "dp", "tensor"),
            P("section", "tensor", "dp"),
            P("section", "dp", "tensor"),
            P("section", "tensor", "dp"),
            P("section", None, ("dp", "tensor")),
        ),
        check_vma=False,
    )
```

profile of v0, /device:TPU:0, one launch (start us, length us, event | category | flops | bytes accessed | tf_op | source)
XLA Modules:
  0.0 1986.0 jit_solution(7939150724147806573)
XLA Ops:
  9.5 11.4 all-gather
  30.6 18.9 slice_reduce_fusion
  53.4 12.6 copy.522
  66.1 26.6 %all-gather.50.cloned.1.call-done = bf16[1,1076,1152]{1,2,0:T(8,128)(2,1)} async-done(((bf16[1,1076,576]{1,2,0:T(8,128)(2,1)}), bf16[1,1076,1152]{1,2,0:T(8,128)(2,1)}) %all-gather.50.cloned.1.call-update) | async-done | bytes 2479120 | tf_op jit(solution)/shard_map/all_gather | solution.py:191
  92.7 12.5 copy.523
  108.1 28.7 %all-gather.3 = bf16[1,1152,288]{2,0,1:T(2,128)(2,1)} all-gather(bf16[1,576,288]{2,0,1:T(2,128)(2,1)} %copy.514), channel_id=5, replica_groups=mesh['section'=4,'dp'=2,'tensor'=4] {'dp'}, dimensions={1}, use_global_device_ids=true | all-gather | bytes 995328 | tf_op jit(solution)/shard_map/all_gather | solution.py:188
  143.3 29.3 %all-gather.2 = bf16[1,1152,288]{2,0,1:T(2,128)(2,1)} all-gather(bf16[1,576,288]{2,0,1:T(2,128)(2,1)} %copy.512), channel_id=4, replica_groups=mesh['section'=4,'dp'=2,'tensor'=4] {'dp'}, dimensions={1}, use_global_device_ids=true | all-gather | bytes 995328 | tf_op jit(solution)/shard_map/all_gather | solution.py:187
  180.2 27.9 %all-gather.1 = bf16[1,1152,288]{2,0,1:T(2,128)(2,1)} all-gather(bf16[1,576,288]{2,0,1:T(2,128)(2,1)} %copy.510), channel_id=3, replica_groups=mesh['section'=4,'dp'=2,'tensor'=4] {'dp'}, dimensions={1}, use_global_device_ids=true | all-gather | bytes 995328 | tf_op jit(solution)/shard_map/all_gather | solution.py:186
  215.7 27.7 %all-gather.4 = bf16[1,288,1152]{1,0,2:T(2,128)(2,1)} all-gather(bf16[1,288,576]{1,0,2:T(2,128)(2,1)} %copy.520), channel_id=6, replica_groups=mesh['section'=4,'dp'=2,'tensor'=4] {'dp'}, dimensions={2}, use_global_device_ids=true | all-gather | bytes 995328 | tf_op jit(solution)/shard_map/all_gather | solution.py:189
  268.0 38.8 %fusion = bf16[192,1152]{1,0:T(8,128)(2,1)S(1)} fusion(bf16[1,732,1152]{2,1,0:T(8,128)(2,1)} %fusion.188), kind=kCustom, calls=%all-reduce-scatter | all-reduce-scatter fusion | flops 884737 | bytes 2129408
  313.6 10.6 copy.697
  337.2 55.3 %all-gather.52.cloned.1.call-done = bf16[1,4304,1152]{2,0,1:T(2,128)(2,1)} async-done(((bf16[1,1076,1152]{2,0,1:T(2,128)(2,1)}), bf16[1,4304,1152]{2,0,1:T(2,128)(2,1)}) %all-gather.52.cloned.1.call-update) | async-done | bytes 9916432 | tf_op jit(solution)/shard_map/all_gather | solution.py:196
  392.4 10.8 copy.698
  425.2 30.9 %all-gather.28.cloned.1.call-done = bf16[1,732,1152]{2,0,1:T(2,128)(2,1)} async-done(((bf16[1,183,1152]{2,0,1:T(2,128)(2,1)}), bf16[1,732,1152]{2,0,1:T(2,128)(2,1)}) %all-gather.28.cloned.1.call-update) | async-done | bytes 1686544 | tf_op jit(solution)/shard_map/all_gather | solution.py:31
  470.7 19.4 fusion.1
  539.2 32.4 %all-gather.30.cloned.1.call-done = bf16[1,732,1152]{2,0,1:T(2,128)(2,1)} async-done(((bf16[1,183,1152]{2,0,1:T(2,128)(2,1)}), bf16[1,732,1152]{2,0,1:T(2,128)(2,1)}) %all-gather.30.cloned.1.call-update) | async-done | bytes 1686544 | tf_op jit(solution)/shard_map/all_gather | solution.py:31
  590.7 20.0 %fusion.2 = bf16[192,1152]{1,0:T(8,128)(2,1)S(1)} fusion(bf16[1,732,1152]{2,1,0:T(8,128)(2,1)} %fusion.190), kind=kCustom, calls=%all-reduce-scatter.2 | all-reduce-scatter fusion | flops 884737 | bytes 2129408
  658.4 32.4 %all-gather.32.cloned.1.call-done = bf16[1,732,1152]{2,0,1:T(2,128)(2,1)} async-done(((bf16[1,183,1152]{2,0,1:T(2,128)(2,1)}), bf16[1,732,1152]{2,0,1:T(2,128)(2,1)}) %all-gather.32.cloned.1.call-update) | async-done | bytes 1686544 | tf_op jit(solution)/shard_map/all_gather | solution.py:31
  709.7 20.0 %fusion.3 = bf16[192,1152]{1,0:T(8,128)(2,1)S(1)} fusion(bf16[1,732,1152]{2,1,0:T(8,128)(2,1)} %fusion.191), kind=kCustom, calls=%all-reduce-scatter.3 | all-reduce-scatter fusion | flops 884737 | bytes 2129408
  797.0 12.8 all-gather.34.cloned.1.call-done
  829.8 20.0 %fusion.4 = bf16[192,1152]{1,0:T(8,128)(2,1)S(1)} fusion(bf16[1,732,1152]{2,1,0:T(8,128)(2,1)} %fusion.192), kind=kCustom, calls=%all-reduce-scatter.4 | all-reduce-scatter fusion | flops 884737 | bytes 2129408
  867.8 10.3 bitcast_dynamic-update-slice_fusion
  880.6 10.0 bitcast_dynamic-update-slice_fusion.19
  916.2 17.1 all-gather.36.cloned.1.call-done
  967.7 20.7 %fusion.5 = bf16[192,1152]{1,0:T(8,128)(2,1)} fusion(bf16[1,732,1152]{2,1,0:T(8,128)(2,1)} %fusion.183), kind=kCustom, calls=%all-reduce-scatter.5 | all-reduce-scatter fusion | flops 884737 | bytes 2129408
  1002.4 11.3 collective-permute-done.4
  1013.7 10.3 bitcast_dynamic-update-slice_fusion.18
  1038.8 25.0 %all-gather.38.cloned.1.call-done = bf16[1,732,1152]{2,0,1:T(2,128)(2,1)} async-done(((bf16[1,183,1152]{2,0,1:T(2,128)(2,1)}), bf16[1,732,1152]{2,0,1:T(2,128)(2,1)}) %all-gather.38.cloned.1.call-update) | async-done | bytes 1686544 | tf_op jit(solution)/shard_map/all_gather | solution.py:118
  1090.9 20.0 %fusion.6 = bf16[192,1152]{1,0:T(8,128)(2,1)S(1)} fusion(bf16[1,732,1152]{2,1,0:T(8,128)(2,1)} %fusion.184), kind=kCustom, calls=%all-reduce-scatter.6 | all-reduce-scatter fusion | flops 884737 | bytes 2129408
  1124.0 11.2 collective-permute-done.5
  1135.2 10.1 bitcast_dynamic-update-slice_fusion.17
  1160.4 24.6 %all-gather.40.cloned.1.call-done = bf16[1,732,1152]{2,0,1:T(2,128)(2,1)} async-done(((bf16[1,183,1152]{2,0,1:T(2,128)(2,1)}), bf16[1,732,1152]{2,0,1:T(2,128)(2,1)}) %all-gather.40.cloned.1.call-update) | async-done | bytes 1686544 | tf_op jit(solution)/shard_map/all_gather | solution.py:118
  1212.0 20.0 %fusion.7 = bf16[192,1152]{1,0:T(8,128)(2,1)S(1)} fusion(bf16[1,732,1152]{2,1,0:T(8,128)(2,1)} %fusion.185), kind=kCustom, calls=%all-reduce-scatter.7 | all-reduce-scatter fusion | flops 884737 | bytes 2129408
  1244.3 11.3 collective-permute-done.6
  1255.6 10.2 bitcast_dynamic-update-slice_fusion.16
  1285.5 20.8 %all-gather.42.cloned.1.call-done = bf16[1,732,1152]{2,0,1:T(2,128)(2,1)} async-done(((bf16[1,183,1152]{2,0,1:T(2,128)(2,1)}), bf16[1,732,1152]{2,0,1:T(2,128)(2,1)}) %all-gather.42.cloned.1.call-update) | async-done | bytes 1686544 | tf_op jit(solution)/shard_map/all_gather | solution.py:118
  1334.5 20.2 %fusion.8 = bf16[192,1152]{1,0:T(8,128)(2,1)S(1)} fusion(bf16[1,732,1152]{2,1,0:T(8,128)(2,1)} %fusion.186), kind=kCustom, calls=%all-reduce-scatter.8 | all-reduce-scatter fusion | flops 884737 | bytes 2129408
  1367.0 10.3 collective-permute-done.7
  1377.3 11.8 bitcast_dynamic-update-slice_fusion.15
  1402.7 9.8 fusion.10
  1521.5 23.0 %fusion.9 = bf16[192,1152]{1,0:T(8,128)(2,1)} fusion(bf16[1,732,1152]{2,1,0:T(8,128)(2,1)} %fusion.187), kind=kCustom, calls=%all-reduce-scatter.9 | all-reduce-scatter fusion | flops 884737 | bytes 2129408
  1601.7 65.9 %reduce-scatter.52.cloned.1.call-done = bf16[4304,576]{0,1:T(8,128)(2,1)} async-done(((bf16[4304,1152]{0,1:T(8,128)(2,1)}), bf16[4304,576]{0,1:T(8,128)(2,1)}) %reduce-scatter.52.cloned.1.call-update) | async-done | bytes 4958224 | tf_op jit(solution)/shard_map/reduce_scatter | solution.py:314
  1677.6 27.8 %reduce-scatter.62.cloned.1.call-done = f32[144,2]{1,0:T(8,128)} async-done(((f32[1152,2]{1,0:T(8,128)}), f32[144,2]{1,0:T(8,128)}) %reduce-scatter.62.cloned.1.call-update) | async-done | bytes 1168
  1707.0 19.3 reduce-scatter.60.cloned.1.call-done
  1727.5 20.0 %reduce-scatter.54.cloned.1.call-done = bf16[576,288]{1,0:T(8,128)(2,1)} async-done(((bf16[1152,288]{1,0:T(8,128)(2,1)}), bf16[576,288]{1,0:T(8,128)(2,1)}) %reduce-scatter.54.cloned.1.call-update) | async-done | bytes 331792
  1748.7 20.2 %reduce-scatter.56.cloned.1.call-done = bf16[576,288]{1,0:T(8,128)(2,1)} async-done(((bf16[1152,288]{1,0:T(8,128)(2,1)}), bf16[576,288]{1,0:T(8,128)(2,1)}) %reduce-scatter.56.cloned.1.call-update) | async-done | bytes 331792
  1770.1 19.6 reduce-scatter.58.cloned.1.call-done
  1794.6 177.5 %all-reduce.25.cloned.1.call-done = (bf16[576,4304]{1,0:T(8,128)(2,1)}, bf16[4304,576]{0,1:T(8,128)(2,1)}) async-done(((bf16[576,4304]{1,0:T(8,128)(2,1)}, bf16[4304,576]{0,1:T(8,128)(2,1)}), (bf16[576,4304]{1,0:T(8,128)(2,1)}, bf16[4304,576]{0,1:T(8,128)(2,1)})) %all-reduce.25.cloned.1.call-update) | async-done | bytes 9916432
  (948 shorter events, 809.8 us)
Async XLA Ops:
  7.2 46.2 %all-gather.46.cloned.1.call-start = ((), (), s32[]{:S(2)}) async-start(), calls=%async_computation.19 | async-start | bytes 3981312 | tf_op jit(solution)/shard_map/all_gather | solution.py:190
  7.9 84.7 %all-gather.50.cloned.1.call-start = ((), (), s32[]{:S(2)}) async-start(), calls=%async_computation.21 | async-start | bytes 3981312 | tf_op jit(solution)/shard_map/all_gather | solution.py:191
  8.7 240.9 %all-gather.26.cloned.1.call-start = ((), (), s32[]{:S(2)}) async-start(), calls=%async_computation.7 | async-start | bytes 4216320 | tf_op jit(solution)/shard_map/all_gather | solution.py:31
  30.2 391.6 %copy-start.16 = (f32[1,183,1152]{2,0,1:T(1,128)}, f32[1,183,1152]{2,0,1:T(1,128)S(1)}, u32[]{:S(2)}) copy-start(f32[1,183,1152]{2,0,1:T(1,128)S(1)} %get-tuple-element.144) | copy-start | bytes 2529796
  53.1 260.4 %all-gather.48.cloned.1.call-start = ((), (), s32[]{:S(2)}) async-start(), calls=%async_computation.20 | async-start | bytes 24791040 | tf_op jit(solution)/shard_map/all_gather | solution.py:195
  66.0 326.4 %all-gather.52.cloned.1.call-start = ((), (), s32[]{:S(2)}) async-start(), calls=%async_computation.22 | async-start | bytes 24791040 | tf_op jit(solution)/shard_map/all_gather | solution.py:196
  105.2 350.8 %all-gather.28.cloned.1.call-start = ((), (), s32[]{:S(2)}) async-start(), calls=%async_computation.8 | async-start | bytes 4216320 | tf_op jit(solution)/shard_map/all_gather | solution.py:31
  141.3 108.2 %copy-start.126 = (bf16[1,1152,288]{1,2,0:T(8,128)(2,1)}, bf16[1,1152,288]{1,2,0:T(8,128)(2,1)S(1)}, u32[]{:S(2)}) copy-start(bf16[1,1152,288]{1,2,0:T(8,128)(2,1)S(1)} %copy.515) | copy-start | bytes 1990660
  306.8 3.0 collective-permute-start.8
  313.1 90.2 %copy-start.14 = (f32[1,183,1152]{2,1,0:T(8,128)}, f32[1,183,1152]{2,1,0:T(8,128)S(1)}, u32[]{:S(2)}) copy-start(f32[1,183,1152]{2,1,0:T(8,128)S(1)} %get-tuple-element.132) | copy-start | bytes 2529796
  408.5 12.8 collective-permute-start
  424.3 147.3 %all-gather.30.cloned.1.call-start = ((), (), s32[]{:S(2)}) async-start(), calls=%async_computation.9 | async-start | bytes 4216320 | tf_op jit(solution)/shard_map/all_gather | solution.py:31
  490.9 2.4 collective-permute-start.9
  519.3 12.3 collective-permute-start.1
  538.3 152.5 %all-gather.32.cloned.1.call-start = ((), (), s32[]{:S(2)}) async-start(), calls=%async_computation.10 | async-start | bytes 4216320 | tf_op jit(solution)/shard_map/all_gather | solution.py:31
  610.7 2.4 collective-permute-start.10
  638.5 12.5 collective-permute-start.2
  657.5 152.3 %all-gather.34.cloned.1.call-start = ((), (), s32[]{:S(2)}) async-start(), calls=%async_computation.11 | async-start | bytes 4216320 | tf_op jit(solution)/shard_map/all_gather | solution.py:31
  729.8 2.3 collective-permute-start.11
  757.5 12.4 collective-permute-start.3
  776.5 156.9 %all-gather.36.cloned.1.call-start = ((), (), s32[]{:S(2)}) async-start(), calls=%async_computation.12 | async-start | bytes 4216320 | tf_op jit(solution)/shard_map/all_gather | solution.py:118
  849.9 2.7 collective-permute-start.12
  859.6 136.1 %copy-start.1 = (f32[3,1,183,1152]{3,2,1,0:T(8,128)}, f32[3,1,183,1152]{3,2,1,0:T(8,128)S(1)}, u32[]{:S(2)}) copy-start(f32[3,1,183,1152]{3,2,1,0:T(8,128)S(1)} %get-tuple-element.161) | copy-start | bytes 7589380
  896.4 103.4 %copy-start.159 = (f32[183]{0:T(256)}, f32[183]{0:T(256)S(1)}, u32[]{:S(2)}) copy-start(f32[183]{0:T(256)S(1)} %negate_multiply_fusion.9) | copy-start | bytes 2200
  899.1 164.7 %all-gather.38.cloned.1.call-start = ((), (), s32[]{:S(2)}) async-start(), calls=%async_computation.13 | async-start | bytes 4216320 | tf_op jit(solution)/shard_map/all_gather | solution.py:118
  989.3 2.2 collective-permute-start.13
  1000.9 12.8 collective-permute-start.4
  1030.1 91.1 %copy-start.35 = (f32[1,183,1152]{2,1,0:T(8,128)}, f32[1,183,1152]{2,1,0:T(8,128)S(1)}, u32[]{:S(2)}) copy-start(f32[1,183,1152]{2,1,0:T(8,128)S(1)} %get-tuple-element.116) | copy-start | bytes 2529796
  1031.7 153.2 %all-gather.40.cloned.1.call-start = ((), (), s32[]{:S(2)}) async-start(), calls=%async_computation.14 | async-start | bytes 4216320 | tf_op jit(solution)/shard_map/all_gather | solution.py:118
  1110.9 2.2 collective-permute-start.14
  1122.4 12.8 collective-permute-start.5
  1151.3 90.4 %copy-start.39 = (f32[1,183,1152]{2,1,0:T(8,128)}, f32[1,183,1152]{2,1,0:T(8,128)S(1)}, u32[]{:S(2)}) copy-start(f32[1,183,1152]{2,1,0:T(8,128)S(1)} %get-tuple-element.110) | copy-start | bytes 2529796
  1152.9 153.3 %all-gather.42.cloned.1.call-start = ((), (), s32[]{:S(2)}) async-start(), calls=%async_computation.15 | async-start | bytes 4216320 | tf_op jit(solution)/shard_map/all_gather | solution.py:118
  1232.0 2.2 collective-permute-start.15
  1242.8 12.8 collective-permute-start.6
  1274.2 173.9 %all-gather.54.cloned.1.call-start = ((), (), s32[]{:S(2)}) async-start(), calls=%async_computation.23 | async-start | bytes 4216320 | tf_op jit(solution)/shard_map/all_gather | solution.py:31
  1278.5 200.3 %all-gather.44.cloned.1.call-start = ((), (), s32[]{:S(2)}) async-start(), calls=%async_computation.16 | async-start | bytes 4216320 | tf_op jit(solution)/shard_map/all_gather | solution.py:118
  1354.8 2.2 collective-permute-start.16
  1364.7 12.6 collective-permute-start.7
  1397.4 204.3 %reduce-scatter.50.cloned.1.call-start = ((), (), s32[]{:S(2)}) async-start(), calls=%async_computation.17 | async-start | bytes 15040512 | tf_op jit(solution)/shard_map/reduce_scatter | solution.py:311
  1412.6 255.0 %reduce-scatter.52.cloned.1.call-start = ((), (), s32[]{:S(2)}) async-start(), calls=%async_computation.18 | async-start | bytes 15040512 | tf_op jit(solution)/shard_map/reduce_scatter | solution.py:314
  1433.7 271.7 %reduce-scatter.62.cloned.1.call-start = ((), (), s32[]{:S(2)}) async-start(), calls=%async_computation.28 | async-start | bytes 663552
  1545.4 9.2 collective-permute-start.17
  1563.9 162.4 %reduce-scatter.60.cloned.1.call-start = ((), (), s32[]{:S(2)}) async-start(), calls=%async_computation.27 | async-start | bytes 1327104
  1577.3 170.2 %reduce-scatter.54.cloned.1.call-start = ((), (), s32[]{:S(2)}) async-start(), calls=%async_computation.24 | async-start | bytes 1327104
  1587.6 181.3 %reduce-scatter.56.cloned.1.call-start = ((), (), s32[]{:S(2)}) async-start(), calls=%async_computation.25 | async-start | bytes 1327104
  1590.0 199.7 %reduce-scatter.58.cloned.1.call-start = ((), (), s32[]{:S(2)}) async-start(), calls=%async_computation.26 | async-start | bytes 1327104
  1592.4 379.7 %all-reduce.25.cloned.1.call-start = ((), (), s32[]{:S(2)}) async-start(), calls=%async_computation.29 | async-start | bytes 20054016
  (224 other events, 1832.5 us)
Sparse Core Ops, SparseCore 0:
  9.6 42.0 all-gather.45
  53.2 39.3 all-gather.49
  94.8 29.8 all-gather.25
  126.1 125.3 all-gather.47
  252.9 139.5 all-gather.51
  424.4 31.6 all-gather.27
  538.4 33.2 all-gather.29
  657.6 33.0 all-gather.31
  776.6 33.2 all-gather.33
  899.2 34.0 all-gather.35
  1031.9 31.9 all-gather.37
  1153.1 31.8 all-gather.39
  1274.4 31.8 all-gather.41
  1307.7 29.8 all-gather.53
  1397.5 31.7 all-gather.43
  1431.5 116.9 reduce-scatter.49
  1550.6 116.8 reduce-scatter.51
  1671.1 34.3 reduce-scatter.61
  1707.7 18.5 reduce-scatter.59
  1729.0 18.4 reduce-scatter.53
  1750.3 18.5 reduce-scatter.55
  1771.2 18.5 reduce-scatter.57
  1792.3 179.7 all-reduce.24
where the time goes:
time: 2010 us; the launch traced here: 1990 us
  waiting for transfers between devices  714 us (36%)
  matrix products  391 us (19%)
  blocking collectives  347 us (17%)
  local copies, waits for them, and re-layouts  331 us (16%)
  other arithmetic  143 us (7%)
  starting transfers between devices  40.7 us (2%)
    unnamed x39, waiting for transfers between devices  290 us
    unnamed x10, blocking collectives  222 us
    unnamed x502, local copies, waits for them, and re-layouts  120 us
    all_gather x6, waiting for transfers between devices, widen(): return lax.all_gather(token_rows, 'tensor', axis=1, tiled=True)  109 us
    all_gather x5, waiting for transfers between devices, backward_pass(): lax.all_gather(hidden_grad.astype(jnp.bfloat16), 'tensor', axis=1, tiled=...  87.5 us
    ppermute x8, waiting for transfers between devices, shifted_2(): return lax.ppermute(shard, axis, pairs)  79.9 us
    reduce_scatter x1, waiting for transfers between devices, local(): lax.psum_scatter(grad_lower.astype(jnp.bfloat16), 'dp', scatter_dimension...  65.9 us
    all_gather x1, waiting for transfers between devices, local(): lax.all_gather(w_lower, 'tensor', axis=0, tiled=True)  55.3 us
  transfers between devices with their start and end apart: 41, of which 30 were waited for; matrix products, arithmetic and copies ran while one was open for 26% of the time, Pallas kernels for 0%

commit v1 on v0

v1 whole, which is shorter than its diff:
```python
import jax
import jax.numpy as jnp
from jax import lax
from jax.experimental import pallas as pl
from jax.experimental.pallas import tpu as pltpu
from jax.sharding import PartitionSpec as P

HD = 72
EPS = 1e-06
SCALE = HD ** (-0.5)
LOG2E = 1.4426950408889634
BF = jnp.bfloat16
F32 = jnp.float32
WIN = 256
LANES = 128
K0 = 0.7978845608028654
K1 = 0.044715
VMEM = pl.BlockSpec(memory_space=pltpu.VMEM)
SMEM = pl.BlockSpec(memory_space=pltpu.SMEM)
ANY = pl.BlockSpec(memory_space=pl.ANY)


def swap_core(a):
    n = lax.axis_size("tensor")
    return lax.ppermute(a, "tensor", [(i, i ^ 1) for i in range(n)])


def swap_x(a):
    n = lax.axis_size("tensor")
    return lax.ppermute(a, "tensor", [(i, i ^ 2) for i in range(n)])


def swap_y(a):
    return lax.ppermute(a, "dp", [(0, 1), (1, 0)])


def shift(a, by):
    n = lax.axis_size("section")
    pairs = [(i, i + by) for i in range(n) if 0 <= i + by < n]
    return lax.ppermute(a, "section", pairs)


def two_rows():
    return lax.axis_size("dp") == 2


def half_cut(rows):
    return (rows // 2 + 15) // 16 * 16


def row_gather(rows):
    if not two_rows():
        return lax.all_gather(rows, ("dp", "tensor"), axis=0, tiled=True)
    cut = half_cut(rows.shape[0])
    from_x = swap_x(rows)
    from_y = swap_y(rows)
    four = jnp.concatenate((rows, from_x, from_y, swap_x(from_y[:cut]), swap_y(from_x[cut:])), axis=0)
    return jnp.concatenate((four, swap_core(four)), axis=0)


def up32(a):
    return a.astype(F32)


def low16(a):
    return a.astype(BF)


def dot(a, b):
    return jnp.dot(a, b, preferred_element_type=F32)


def dot_t(a, b):
    return lax.dot_general(a, b, (((1,), (1,)), ((), ())), preferred_element_type=F32)


def t_dot(a, b):
    return lax.dot_general(a, b, (((0,), (0,)), ((), ())), preferred_element_type=F32)


def spans(total, size):
    return [(at, min(size, total - at)) for at in range(0, total, size)]


def norm_parts(values):
    centre = jnp.mean(values, axis=-1, keepdims=True)
    centred = values - centre
    spread = jnp.mean(centred * centred, axis=-1, keepdims=True)
    inverse = lax.rsqrt(spread + EPS)
    return centred * inverse, inverse


def norm_back(grad, unit, inverse, gain):
    e = grad * gain
    return inverse * (e - jnp.mean(e, axis=-1, keepdims=True) - unit * jnp.mean(e * unit, axis=-1, keepdims=True))


def gelu_one(u):
    return u * (0.5 + 0.5 * jnp.tanh(u * (K0 + (K0 * K1) * (u * u))))


def gelu_both(u):
    sq = u * u
    th = jnp.tanh(u * (K0 + (K0 * K1) * sq))
    half = 0.5 + 0.5 * th
    return u * half, half + (0.5 * u) * (1.0 - th * th) * (K0 + (3.0 * K1 * K0) * sq)


def head_window(h, width):
    tile = min(h * HD // LANES, width // LANES - WIN // LANES)
    off = h * HD - tile * LANES
    lane = lax.broadcasted_iota(jnp.int32, (1, WIN), 1)
    return slice(tile * LANES, tile * LANES + WIN), (lane >= off) & (lane < off + HD)


def shape(dims, dtype):
    return jax.ShapeDtypeStruct(dims, dtype)


def call(kernel, name, outs, ins, scratch, args, flops, limit=60):
    moved = sum(a.size * a.dtype.itemsize for a in args) + sum(o.size * o.dtype.itemsize for o in outs)
    return pl.pallas_call(
        kernel,
        out_shape=tuple(outs),
        in_specs=ins,
        out_specs=tuple([VMEM] * len(outs)),
        scratch_shapes=scratch,
        compiler_params=pltpu.CompilerParams(vmem_limit_bytes=limit * 2**20),
        cost_estimate=pl.CostEstimate(flops=int(flops * 1.4), bytes_accessed=moved, transcendentals=0),
        name=name,
    )(*args)


def assemble(name, pieces, flags, place, out_dims, extra=()):
    flat = [a for by_x in pieces for by_core in by_x for a in by_core]
    count = len(pieces[0][0])

    def kernel(flag_ref, *refs):
        out = refs[-1]
        grid = [[[refs[(xr * 2 + cr) * count + i] for i in range(count)] for cr in (0, 1)] for xr in (0, 1)]
        first_row = flag_ref[0] == 0
        first_core = flag_ref[1] == 0

        def row(xr, cr, i):
            cell = grid[xr][cr]
            if count != 2:
                return cell[i][...]
            return jnp.where(first_row, cell[i][...], cell[1 - i][...])

        def by_core(xr, c, i):
            return jnp.where(first_core, row(xr, c, i), row(xr, 1 - c, i))

        place(out, row, by_core, count)

    outs = [shape(out_dims, BF)]
    return call(kernel, name, outs, [SMEM] + [VMEM] * len(flat), [], [flags] + flat, 0)[0]


def kv_kernel(*refs):
    held = len(refs) == 11
    if held:
        sel, got, old, gain, w_hbm, x_out, normed_out, kv_out, w, sem, _ = refs
        x = jnp.where(sel[0] == 1, up32(got[...]), old[...])
    else:
        old, gain, w_hbm, normed_out, kv_out, w, sem = refs
    width = w.shape[0]
    parts = spans(2 * width, 512)
    copies = [
        pltpu.make_async_copy(w_hbm.at[:, width + at : width + at + n], w.at[:, at : at + n], sem.at[i])
        for i, (at, n) in enumerate(parts)
    ]
    for copy in copies:
        copy.start()
    if held:
        x_out[...] = x
    else:
        x = old[...]
    normed = low16(norm_parts(x)[0] * gain[...])
    normed_out[...] = normed
    for copy, (at, n) in zip(copies, parts):
        copy.wait()
        kv_out[:, at : at + n] = low16(dot(normed, w[:, at : at + n]))


def project_kv(sel, got, old, gain, w_qkv):
    rows, width = old.shape
    scratch = [pltpu.VMEM((width, 2 * width), BF), pltpu.SemaphoreType.DMA((len(spans(2 * width, 512)),))]
    outs = [shape((rows, width), BF), shape((rows, 2 * width), BF)]
    flops = 4 * rows * width * width
    if got is None:
        return (old, *call(kv_kernel, "keys_values", outs, [VMEM, VMEM, ANY], scratch, [old, gain, w_qkv], flops))
    scratch.append(pltpu.SemaphoreType.DMA((1,)))
    outs = [shape((rows, width), F32)] + outs
    ins = [SMEM, VMEM, VMEM, VMEM, ANY]
    return call(kv_kernel, "keys_values", outs, ins, scratch, [sel, got, old, gain, w_qkv], flops)


def q_kernel(normed, w_hbm, q_out, w, sem):
    width = w.shape[0]
    parts = spans(width, 512)
    copies = [
        pltpu.make_async_copy(w_hbm.at[:, at : at + n], w.at[:, at : at + n], sem.at[i]) for i, (at, n) in enumerate(parts)
    ]
    for copy in copies:
        copy.start()
    for copy, (at, n) in zip(copies, parts):
        copy.wait()
        q_out[:, at : at + n] = low16(dot(normed[...], w[:, at : at + n]))


def project_q(normed, w_qkv):
    rows, width = normed.shape
    scratch = [pltpu.VMEM((width, width), BF), pltpu.SemaphoreType.DMA((len(spans(width, 512)),))]
    return call(
        q_kernel, "queries", [shape((rows, width), BF)], [VMEM, ANY], scratch, [normed, w_qkv], 2 * rows * width * width
    )[0]


def attend(q_ref, kv, bias, mix, lse_ref):
    rows, width = q_ref.shape
    lane = lax.broadcasted_iota(jnp.int32, (1, LANES), 1)
    for h in range(width // HD):
        win, live = head_window(h, width)
        keys = jnp.where(live, kv[:, win], jnp.zeros((), BF))
        vals = kv[:, width + win.start : width + win.stop]
        s = dot_t(q_ref[:, win], keys) * (SCALE * LOG2E) + bias
        top = jnp.max(s, axis=-1, keepdims=True)
        p = jnp.exp2(s - top)
        total = jnp.sum(p, axis=-1, keepdims=True)
        o = dot(low16(p), vals) * (1.0 / total)
        mix[:, win] = jnp.where(live, low16(o), mix[:, win])
        if lse_ref is not None:
            lse_ref[...] = jnp.where(lane == h, top + jnp.log2(total), lse_ref[...])


def feed(normed, hidden, w_up, w_down, act, ups, downs, slope_out, outs):
    units = w_up.shape[1]
    for copy, (at, n) in zip(ups, spans(units, 512)):
        copy.wait()
        u = dot(normed, w_up[:, at : at + n])
        if slope_out is None:
            act[:, at : at + n] = low16(gelu_one(u))
        else:
            a, slope = gelu_both(u)
            act[:, at : at + n] = low16(a)
            slope_out[:, at : at + n] = low16(slope)
    for copy in downs:
        copy.wait()
    for at, n in spans(w_down.shape[1], 256):
        total = hidden[:, at : at + n] + dot(act[...], w_down[:, at : at + n])
        for out in outs:
            out[:, at : at + n] = total.astype(out.dtype)


def layer_attention(q, own, far, bias, x, gain, w_o):
    rows, width = q.shape

    def kernel(q_ref, own_ref, far_ref, bias_ref, x_ref, gain_ref, wo_hbm, hid_ref, nb_ref, kv, wo, mix, sem):
        copies = [
            pltpu.make_async_copy(own_ref, kv.at[:rows], sem.at[0]),
            pltpu.make_async_copy(far_ref, kv.at[rows:], sem.at[1]),
            pltpu.make_async_copy(wo_hbm, wo, sem.at[2]),
        ]
        for copy in copies:
            copy.start()
        copies[0].wait()
        copies[1].wait()
        mix[...] = jnp.zeros_like(mix)
        attend(q_ref, kv, bias_ref[0:1, :], mix, None)
        copies[2].wait()
        hidden = x_ref[...] + dot(mix[...], wo[...])
        hid_ref[...] = hidden
        nb_ref[...] = low16(norm_parts(hidden)[0] * gain_ref[...])

    scratch = [
        pltpu.VMEM((2 * rows, 2 * width), BF),
        pltpu.VMEM((width, width), BF),
        pltpu.VMEM((rows, width), BF),
        pltpu.SemaphoreType.DMA((3,)),
    ]
    outs = [shape((rows, width), F32), shape((rows, width), BF)]
    ins = [VMEM, ANY, ANY, VMEM, VMEM, VMEM, ANY]
    flops = 16 * rows * 2 * rows * WIN * 4 + 2 * rows * width * width
    return call(kernel, "attention_part", outs, ins, scratch, [q, own, far, bias, x, gain, w_o], flops)


def layer_feed(hidden, normed, w_up, w_down):
    rows, width = hidden.shape
    units = w_up.shape[1]
    parts = spans(units, 512)

    def kernel(hid_ref, nb_ref, wu_hbm, wd_hbm, low_ref, wu, wd, act, sem):
        n = len(parts)
        ups = [pltpu.make_async_copy(wu_hbm.at[:, a : a + k], wu.at[:, a : a + k], sem.at[i]) for i, (a, k) in enumerate(parts)]
        downs = [pltpu.make_async_copy(wd_hbm.at[a : a + k], wd.at[a : a + k], sem.at[n + i]) for i, (a, k) in enumerate(parts)]
        for copy in ups + downs:
            copy.start()
        feed(nb_ref[...], hid_ref, wu, wd, act, ups, downs, None, [low_ref])

    scratch = [
        pltpu.VMEM((width, units), BF),
        pltpu.VMEM((units, width), BF),
        pltpu.VMEM((rows, units), BF),
        pltpu.SemaphoreType.DMA((2 * len(parts),)),
    ]
    return call(
        kernel, "feed_part", [shape((rows, width), BF)], [VMEM, VMEM, ANY, ANY], scratch, [hidden, normed, w_up, w_down],
        4 * rows * width * units,
    )[0]


def layer_whole(full, q, own, far, bias, x, gain, w_o, w_up, w_down):
    rows, width = q.shape
    units = w_up.shape[1]
    parts = spans(units, 512)

    def kernel(q_ref, own_ref, far_ref, bias_ref, x_ref, gain_ref, wo_hbm, wu_hbm, wd_hbm, *rest):
        if full:
            low_ref, out_ref, hid_ref, nb_ref, slope_ref, mix, lse_ref, kv, wo, wu, wd, act, sem = rest
        else:
            low_ref, kv, wo, wu, wd, act, sem, mix, hid_ref = rest
            slope_ref = lse_ref = None
        n = len(parts)
        first = [
            pltpu.make_async_copy(own_ref, kv.at[:rows], sem.at[0]),
            pltpu.make_async_copy(far_ref, kv.at[rows:], sem.at[1]),
            pltpu.make_async_copy(wo_hbm, wo, sem.at[2]),
        ]
        ups = [
            pltpu.make_async_copy(wu_hbm.at[:, a : a + k], wu.at[:, a : a + k], sem.at[3 + i]) for i, (a, k) in enumerate(parts)
        ]
        downs = [
            pltpu.make_async_copy(wd_hbm.at[a : a + k], wd.at[a : a + k], sem.at[3 + n + i]) for i, (a, k) in enumerate(parts)
        ]
        for copy in first + ups + downs:
            copy.start()
        first[0].wait()
        first[1].wait()
        mix[...] = jnp.zeros_like(mix)
        if full:
            lse_ref[...] = jnp.zeros_like(lse_ref)
        attend(q_ref, kv, bias_ref[0:1, :], mix, lse_ref)
        first[2].wait()
        hidden = x_ref[...] + dot(mix[...], wo[...])
        hid_ref[...] = hidden
        normed = low16(norm_parts(hidden)[0] * gain_ref[...])
        if full:
            nb_ref[...] = normed
        feed(normed, hid_ref, wu, wd, act, ups, downs, slope_ref, [low_ref, out_ref] if full else [low_ref])

    outs = [shape((rows, width), BF)]
    scratch = [
        pltpu.VMEM((2 * rows, 2 * width), BF),
        pltpu.VMEM((width, width), BF),
        pltpu.VMEM((width, units), BF),
        pltpu.VMEM((units, width), BF),
        pltpu.VMEM((rows, units), BF),
        pltpu.SemaphoreType.DMA((3 + 2 * len(parts),)),
    ]
    if full:
        outs += [shape((rows, width), F32), shape((rows, width), F32), shape((rows, width), BF)]
        outs += [shape((rows, units), BF), shape((rows, width), BF), shape((rows, LANES), F32)]
    else:
        scratch += [pltpu.VMEM((rows, width), BF), pltpu.VMEM((rows, width), F32)]
    ins = [VMEM, ANY, ANY, VMEM, VMEM, VMEM, ANY, ANY, ANY]
    flops = 16 * rows * 2 * rows * WIN * 4 + 2 * rows * width * width + 4 * rows * width * units
    return call(kernel, "layer", outs, ins, scratch, [q, own, far, bias, x, gain, w_o, w_up, w_down], flops)


def feed_back(full, sel, got, old, slope, hidden, gain, w_up, w_down, w_o):
    rows, width = old.shape
    units = w_up.shape[1]
    parts = spans(units, 512)
    bands = spans(width, 256)
    held = got is not None

    def kernel(*refs):
        if held:
            sel_ref, got_ref, refs = refs[0], refs[1], refs[2:]
        old_ref, slope_hbm, hid_ref, gain_ref, wu_hbm, wd_hbm, wo_hbm = refs[:7]
        refs = refs[7:]
        if held:
            dy_ref, refs = refs[0], refs[1:]
        hg_ref, do_ref, refs = refs[0], refs[1], refs[2:]
        if full:
            dyl_ref, ml_ref, gs_ref, refs = refs[0], refs[1], refs[2], refs[3:]
        wu, wd, wo, slope_s, ig, nbg, sem = refs
        n = len(parts)
        m = len(bands)
        downs = [pltpu.make_async_copy(wd_hbm.at[a : a + k], wd.at[a : a + k], sem.at[i]) for i, (a, k) in enumerate(parts)]
        slopes = [
            pltpu.make_async_copy(slope_hbm.at[:, a : a + k], slope_s.at[:, a : a + k], sem.at[n + i])
            for i, (a, k) in enumerate(parts)
        ]
        ups = [
            pltpu.make_async_copy(wu_hbm.at[a : a + k], wu.at[a : a + k], sem.at[2 * n + i]) for i, (a, k) in enumerate(bands)
        ]
        last = pltpu.make_async_copy(wo_hbm, wo, sem.at[2 * n + m])
        for a, b in zip(downs, slopes):
            a.start()
            b.start()
        for copy in ups + [last]:
            copy.start()
        dy = old_ref[...]
        if held:
            dy = jnp.where(sel_ref[0] == 1, up32(got_ref[...]), dy)
            dy_ref[...] = dy
        down_low = low16(dy)
        if full:
            dyl_ref[...] = down_low
        for i, (at, k) in enumerate(parts):
            downs[i].wait()
            slopes[i].wait()
            ig[:, at : at + k] = low16(dot_t(down_low, wd[at : at + k, :]) * up32(slope_s[:, at : at + k]))
        for i, (at, k) in enumerate(bands):
            ups[i].wait()
            nbg[:, at : at + k] = dot_t(ig[...], wu[at : at + k, :])
        unit, inverse = norm_parts(hid_ref[...])
        grad = nbg[...]
        if full:
            gs_ref[...] = jnp.sum(grad * unit, axis=0, keepdims=True)
        hidden_grad = dy + norm_back(grad, unit, inverse, gain_ref[...])
        hg_ref[...] = hidden_grad
        mix_low = low16(hidden_grad)
        if full:
            ml_ref[...] = mix_low
        last.wait()
        do_ref[...] = low16(dot_t(mix_low, wo[...]))

    ins = [VMEM, ANY, VMEM, VMEM, ANY, ANY, ANY]
    args = [old, slope, hidden, gain, w_up, w_down, w_o]
    outs = [shape((rows, width), F32), shape((rows, width), BF)]
    if held:
        ins = [SMEM, VMEM] + ins
        args = [sel, got] + args
        outs = [shape((rows, width), F32)] + outs
    if full:
        outs += [shape((rows, width), BF), shape((rows, width), BF), shape((1, width), F32)]
    scratch = [
        pltpu.VMEM((width, units), BF),
        pltpu.VMEM((units, width), BF),
        pltpu.VMEM((width, width), BF),
        pltpu.VMEM((rows, units), BF),
        pltpu.VMEM((rows, units), BF),
        pltpu.VMEM((rows, width), F32),
        pltpu.SemaphoreType.DMA((2 * len(parts) + len(bands) + 1,)),
    ]
    flops = 4 * rows * width * units + 2 * rows * width * width
    return call(kernel, "feed_back", outs, ins, scratch, args, flops)


def attention_back(q, own, far, do, mix, lse, bias):
    rows, width = q.shape
    keys_n = 2 * rows

    def kernel(q_ref, own_ref, far_ref, do_ref, o_ref, lse_ref, bias_ref, dq_ref, dkv_own, dkv_far, kv, qt, dt, dkt, dvt, sem):
        copies = [
            pltpu.make_async_copy(own_ref, kv.at[:rows], sem.at[0]),
            pltpu.make_async_copy(far_ref, kv.at[rows:], sem.at[1]),
        ]
        for copy in copies:
            copy.start()
        bias_row = bias_ref[0:1, :]
        qt[...] = up32(q_ref[...]).T
        dt[...] = up32(do_ref[...]).T
        dq_ref[...] = jnp.zeros_like(dq_ref)
        for copy in copies:
            copy.wait()
        zero = jnp.zeros((), BF)
        for h in range(width // HD):
            win, live = head_window(h, width)
            here = slice(h * HD, (h + 1) * HD)
            keys = jnp.where(live, kv[:, win], zero)
            vals = jnp.where(live, kv[:, width + win.start : width + win.stop], zero)
            d_out = do_ref[:, win]
            row_dot = jnp.sum(jnp.where(live, up32(d_out) * up32(o_ref[:, win]), 0.0), axis=-1, keepdims=True)
            s = dot_t(q_ref[:, win], keys) * (SCALE * LOG2E) + bias_row
            p = jnp.exp2(s - lse_ref[:, h : h + 1])
            ds = low16(p * (dot_t(d_out, vals) - row_dot))
            dq = dot(ds, keys) * SCALE
            dq_ref[:, win] = jnp.where(live, low16(dq), dq_ref[:, win])
            dkt[here, :] = dot(low16(qt[here, :]), ds) * SCALE
            dvt[here, :] = dot(low16(dt[here, :]), low16(p))
        dk = low16(dkt[...].T)
        dv = low16(dvt[...].T)
        dkv_own[:, :width] = dk[:rows]
        dkv_own[:, width:] = dv[:rows]
        dkv_far[:, :width] = dk[rows:]
        dkv_far[:, width:] = dv[rows:]

    outs = [shape((rows, width), BF), shape((rows, 2 * width), BF), shape((rows, 2 * width), BF)]
    scratch = [
        pltpu.VMEM((keys_n, 2 * width), BF),
        pltpu.VMEM((width, rows), F32),
        pltpu.VMEM((width, rows), F32),
        pltpu.VMEM((width, keys_n), F32),
        pltpu.VMEM((width, keys_n), F32),
        pltpu.SemaphoreType.DMA((2,)),
    ]
    ins = [VMEM, ANY, ANY, VMEM, VMEM, VMEM, VMEM]
    flops = 16 * rows * keys_n * WIN * 10
    return call(kernel, "attention_back", outs, ins, scratch, [q, own, far, do, mix, lse, bias], flops)


def qkv_back(full, dq, own, got, x, hidden_grad, gain, w_qkv, core):
    rows, width = dq.shape
    span = width // 4
    bands = spans(width, 256)

    def kernel(dq_ref, own_ref, got_ref, x_ref, hg_ref, gain_ref, w_hbm, *rest):
        if full:
            core_ref, rest = rest[0], rest[1:]
            dx_ref, low_ref, keep_ref, give_ref, gs_ref, w, grads, nag, sem = rest
        else:
            low_ref, w, grads, nag, sem = rest
        copies = [pltpu.make_async_copy(w_hbm.at[a : a + k], w.at[a : a + k], sem.at[i]) for i, (a, k) in enumerate(bands)]
        for copy in copies:
            copy.start()
        grads[:, :width] = dq_ref[...]
        grads[:, width:] = low16(up32(own_ref[...]) + up32(got_ref[...]))
        if full:
            mine = core_ref[0] == 0
            for i in range(3):
                for xr in (0, 1):
                    at = i * width + 2 * xr * span
                    lo = grads[:, at : at + span]
                    hi = grads[:, at + span : at + 2 * span]
                    to = xr * 3 * span + i * span
                    keep_ref[:, to : to + span] = jnp.where(mine, lo, hi)
                    give_ref[:, to : to + span] = jnp.where(mine, hi, lo)
        for copy, (at, k) in zip(copies, bands):
            copy.wait()
            nag[:, at : at + k] = dot_t(grads[...], w[at : at + k, :])
        unit, inverse = norm_parts(x_ref[...])
        grad = nag[...]
        if full:
            gs_ref[...] = jnp.sum(grad * unit, axis=0, keepdims=True)
        dx = hg_ref[...] + norm_back(grad, unit, inverse, gain_ref[...])
        low_ref[...] = low16(dx)
        if full:
            dx_ref[...] = dx

    outs = [shape((rows, width), BF)]
    ins = [VMEM, VMEM, VMEM, VMEM, VMEM, VMEM, ANY]
    args = [dq, own, got, x, hidden_grad, gain, w_qkv]
    if full:
        outs = [shape((rows, width), F32)] + outs
        outs += [shape((rows, 6 * span), BF), shape((rows, 6 * span), BF), shape((1, width), F32)]
        ins.append(SMEM)
        args.append(core)
    scratch = [
        pltpu.VMEM((width, 3 * width), BF),
        pltpu.VMEM((rows, 3 * width), BF),
        pltpu.VMEM((rows, width), F32),
        pltpu.SemaphoreType.DMA((len(bands),)),
    ]
    return call(kernel, "qkv_back", outs, ins, scratch, args, 6 * rows * width * width)


def unit_grads(normed_all, dy_all, w_up, w_down, flags, units, part):
    total, width = normed_all.shape
    n = w_up.shape[1]
    block = total // max(1, total // 736)
    if total % block:
        block = total
    steps = total // block
    dp = width // part

    def kernel(flag_ref, nb_ref, dy_ref, wu_ref, wd_ref, gu_ref, gd_ref, gdt):
        step = pl.program_id(0)
        nb = nb_ref[...]
        dy = dy_ref[...]

        def cols(a):
            picked = a[:, :part]
            for i in range(1, dp):
                picked = jnp.where(flag_ref[0] == i, a[:, i * part : (i + 1) * part], picked)
            return picked

        nb_cols, dy_cols = cols(nb), cols(dy)

        @pl.when(step == 0)
        def _():
            gu_ref[...] = jnp.zeros_like(gu_ref)
            gdt[...] = jnp.zeros_like(gdt)

        for at, k in spans(n, 512):
            act, slope = gelu_both(dot(nb, wu_ref[:, at : at + k]))
            inner = low16(dot_t(dy, wd_ref[at : at + k, :]) * slope)
            real = min(k, units - at)
            gu_ref[:, at : at + real] += t_dot(nb_cols, inner)[:, :real]
            gdt[:, at : at + k] += t_dot(dy_cols, low16(act))

        @pl.when(step == steps - 1)
        def _():
            gd_ref[...] = gdt[...].T[:units, :]

    args = [flags, normed_all, dy_all, w_up, w_down]
    return pl.pallas_call(
        kernel,
        grid=(steps,),
        in_specs=[
            SMEM,
            pl.BlockSpec((block, width), lambda i: (i, 0)),
            pl.BlockSpec((block, width), lambda i: (i, 0)),
            VMEM,
            VMEM,
        ],
        out_specs=(VMEM, VMEM),
        out_shape=(shape((part, units), F32), shape((units, part), F32)),
        scratch_shapes=[pltpu.VMEM((part, n), F32)],
        compiler_params=pltpu.CompilerParams(vmem_limit_bytes=60 * 2**20),
        cost_estimate=pl.CostEstimate(flops=int(6 * 1.4 * total * width * n), bytes_accessed=4 * total * width, transcendentals=0),
        name="unit_grads",
    )(*args)


def head_grads(flags, na_own, na_far, keep, got, mix_own, mix_far, ml_own, ml_far):
    rows, width = na_own.shape
    span3 = keep.shape[1] // 2
    span = span3 // 3
    part = width // 2

    def kernel(flag_ref, na0, na1, k0, k1, m0, m1, l0, l1, *rest):
        qkv_out, o_out, na, kk, mm, ml = rest[:4], rest[4:8], rest[8], rest[9], rest[10], rest[11]
        for a, b, c in ((na0, na1, na), (k0, k1, kk), (m0, m1, mm), (l0, l1, ml)):
            c[:rows] = a[...]
            c[rows:] = b[...]
        first = flag_ref[0] == 0
        lo, hi = na[:, :part], na[:, part:]
        by_row = (jnp.where(first, lo, hi), jnp.where(first, hi, lo))
        lo, hi = ml[:, :part], ml[:, part:]
        by_col = (jnp.where(first, lo, hi), jnp.where(first, hi, lo))
        for yr in (0, 1):
            for xr in (0, 1):
                out = qkv_out[yr * 2 + xr]
                out[...] = t_dot(by_row[yr], kk[:, xr * span3 : (xr + 1) * span3]).astype(out.dtype)
                out = o_out[yr * 2 + xr]
                out[...] = t_dot(mm[:, xr * span : (xr + 1) * span], by_col[yr]).astype(out.dtype)

    types = (F32, BF, BF, BF)
    outs = [shape((part, span3), t) for t in types] + [shape((span, part), t) for t in types]
    scratch = [
        pltpu.VMEM((2 * rows, width), BF),
        pltpu.VMEM((2 * rows, 2 * span3), BF),
        pltpu.VMEM((2 * rows, 2 * span), BF),
        pltpu.VMEM((2 * rows, width), BF),
    ]
    args = [flags, na_own, na_far, keep, got, mix_own, mix_far, ml_own, ml_far]
    flops = 8 * 2 * rows * width * width
    got = call(kernel, "head_grads", outs, [SMEM] + [VMEM] * 8, scratch, args, flops)
    return got[:4], got[4:]


def plane_scatter(own, beside, above, across):
    cut = half_cut(own.shape[0])
    rest = own.shape[0] - cut
    via_x = swap_x(jnp.concatenate((beside[:cut], across[:cut]), axis=0))
    via_y = swap_y(jnp.concatenate((above[cut:], across[cut:]), axis=0))
    up_top = swap_y(low16(up32(above[:cut]) + up32(via_x[cut:])))
    x_bottom = swap_x(low16(up32(beside[cut:]) + up32(via_y[rest:])))
    top = own[:cut] + up32(via_x[:cut]) + up32(up_top)
    bottom = own[cut:] + up32(via_y[:rest]) + up32(x_bottom)
    return jnp.concatenate((top, bottom), axis=0)


def gather_gains(shard, dp_idx, x_idx, core):
    if not two_rows():
        return lax.all_gather(shard, ("dp", "tensor"), axis=1, tiled=True)
    for index, swap in ((core, swap_core), (x_idx, swap_x), (dp_idx, swap_y)):
        other = swap(shard)
        shard = jnp.where(index == 0, jnp.concatenate((shard, other), axis=1), jnp.concatenate((other, shard), axis=1))
    return shard


def scatter_gains(sums, dp_idx, tensor_idx):
    if not two_rows():
        return lax.psum_scatter(sums, ("dp", "tensor"), scatter_dimension=1, tiled=True)
    for swap in (swap_core, swap_x, swap_y):
        sums = sums + swap(sums)
    part = sums.shape[1] // 8
    return lax.dynamic_slice_in_dim(sums, (dp_idx * 4 + tensor_idx) * part, part, 1)


def local(images, valid_len, query_weight, key_weight, value_weight, output_weight, up_weight, down_weight, norm_gains, cotangent):
    section = lax.axis_index("section")
    sections = lax.axis_size("section")
    dp_idx = lax.axis_index("dp")
    dp = lax.axis_size("dp")
    tensor_idx = lax.axis_index("tensor")
    x_idx, core = tensor_idx // 2, tensor_idx % 2
    per_dp, quarter, width = images.shape
    assert per_dp == 2 and lax.axis_size("tensor") == 4
    padded_quarter = (quarter + 7) // 8 * 8
    flags = jnp.stack((dp_idx, core)).astype(jnp.int32)
    core_flag = flags[1:]

    def pad_rows(a):
        return jnp.pad(a, ((0, padded_quarter - quarter), (0, 0)))

    def pick(a):
        own = lax.dynamic_index_in_dim(a, x_idx, 0, keepdims=False)
        give = lax.dynamic_index_in_dim(a, 1 - x_idx, 0, keepdims=False)
        got = up32(swap_x(pad_rows(low16(give))))
        return jnp.concatenate((pad_rows(own), got), axis=0)

    def unpick(rows):
        own, give = rows[:quarter], rows[padded_quarter:]
        got = up32(swap_x(low16(give))[:quarter])
        return jnp.where(x_idx == 0, jnp.stack((own, got)), jnp.stack((got, own)))

    first_rows = pick(images)
    rows = 2 * padded_quarter
    valid = lax.dynamic_index_in_dim(valid_len, x_idx, 0, keepdims=False)
    spot = jnp.arange(padded_quarter)
    live = [
        (spot < quarter) & ((2 * xx + cc) * quarter + spot < valid) for cc in (core, 1 - core) for xx in (x_idx, 1 - x_idx)
    ]
    bias = jnp.where(jnp.concatenate(live), 0.0, -1e30).astype(F32)[None, :]
    bias = jnp.broadcast_to(bias, (8, bias.shape[1]))
    gains = gather_gains(norm_gains[0], dp_idx, x_idx, core)
    gain_a, gain_b = gains[0:1], gains[1:2]

    def plane_pieces(w, after):
        if not two_rows():
            mine = lax.all_gather(w, "dp")
            other = swap_x(mine)
            mine_far, other_far = swap_core(mine), swap_core(other)
            split = lambda a: [a[i] for i in range(dp)]
            return [[split(mine), split(mine_far)], [split(other), split(other_far)]], other
        w = lax.optimization_barrier((w, after))[0] if after is not None else w
        cut = half_cut(w.shape[0])
        from_x = swap_x(w)
        from_y = swap_y(w)
        far = jnp.concatenate((swap_x(from_y[:cut]), swap_y(from_x[cut:])), axis=0)
        mine, other = [w, from_y], [from_x, far]
        pieces = [[mine, [swap_core(a) for a in mine]], [other, [swap_core(a) for a in other]]]
        return pieces, (from_x, from_y)

    span = query_weight.shape[2]
    units = up_weight.shape[2]
    wide = (units + 15) // 16 * 16

    def place_qkv(out, row, by_core, count):
        part = width // count
        for xr in (0, 1):
            for c in (0, 1):
                for i in range(count):
                    block = by_core(xr, c, i)
                    for k in range(3):
                        to = k * width + (2 * xr + c) * span
                        out[i * part : (i + 1) * part, to : to + span] = block[:, k * span : (k + 1) * span]

    def place_o(out, row, by_core, count):
        part = width // count
        for xr in (0, 1):
            for c in (0, 1):
                at = (2 * xr + c) * span
                for i in range(count):
                    out[at : at + span, i * part : (i + 1) * part] = by_core(xr, c, i)

    def place_up(out, row, by_core, count):
        part = width // count
        out[...] = jnp.zeros_like(out)
        for cr in (0, 1):
            for xr in (0, 1):
                at = (2 * cr + xr) * wide
                for i in range(count):
                    out[i * part : (i + 1) * part, at : at + units] = row(xr, cr, i)

    def place_down(out, row, by_core, count):
        part = width // count
        out[...] = jnp.zeros_like(out)
        for cr in (0, 1):
            for xr in (0, 1):
                at = (2 * cr + xr) * wide
                for i in range(count):
                    out[at : at + units, i * part : (i + 1) * part] = row(xr, cr, i)

    qkv_shard = jnp.concatenate((query_weight[0], key_weight[0], value_weight[0]), axis=1)
    qkv_pieces, token = plane_pieces(qkv_shard, first_rows)
    o_pieces, token = plane_pieces(output_weight[0], token)
    up_pieces, token = plane_pieces(up_weight[0], token)
    down_pieces, token = plane_pieces(down_weight[0], token)
    w_qkv = assemble("assemble_qkv", qkv_pieces, flags, place_qkv, (width, 3 * width))
    w_o = assemble("assemble_output", o_pieces, flags, place_o, (width, width))
    w_up = assemble("assemble_up", up_pieces, flags, place_up, (width, 4 * wide))
    w_down = assemble("assemble_down", down_pieces, flags, place_down, (4 * wide, width))

    x, got = first_rows, None
    for tick in range(sections):
        sel = (section == tick).astype(jnp.int32)[None]
        x, normed_a, kv = project_kv(sel, got, x, gain_a, w_qkv)
        kv_far = swap_core(kv)
        q = project_q(normed_a, w_qkv)
        if tick == 0:
            hidden, normed_b = layer_attention(q, kv, kv_far, bias, x, gain_b, w_o)
            out = layer_feed(hidden, normed_b, w_up, w_down)
        else:
            last = tick + 1 == sections
            got = layer_whole(last, q, kv, kv_far, bias, x, gain_b, w_o, w_up, w_down)
            out = got[0]
        if tick + 1 < sections:
            got = shift(out, 1)
    _, out, hidden, normed_b, slope, mix, lse = got
    acts = unpick(out)
    normed_b_all = row_gather(normed_b)

    dy, got = pick(cotangent), None
    for tick in range(sections):
        last = tick + 1 == sections
        sel = (section == sections - 1 - tick).astype(jnp.int32)[None]
        results = feed_back(last, sel, got, dy, slope, hidden, gain_b, w_up, w_down, w_o)
        if got is not None:
            dy, results = results[0], results[1:]
        hidden_grad, do = results[:2]
        dq, dkv, dkv_far = attention_back(q, kv, kv_far, do, mix, lse, bias)
        dkv_got = swap_core(dkv_far)
        back = qkv_back(last, dq, dkv, dkv_got, x, hidden_grad, gain_a, w_qkv, core_flag)
        if not last:
            got = shift(back[0], -1)
    dy_low, mix_low, gain_sum_b = results[2:]
    dx, _, keep, give, gain_sum_a = back
    grads = unpick(dx)

    dy_all = row_gather(dy_low)
    part = width // dp
    grad_up, grad_down = unit_grads(normed_b_all, dy_all, w_up[:, :wide], w_down[:wide], flags, units, part)

    def core_halves(a):
        lo = jnp.concatenate((a[:, :span], a[:, 2 * span : 3 * span]), axis=1)
        hi = jnp.concatenate((a[:, span : 2 * span], a[:, 3 * span :]), axis=1)
        return jnp.where(core == 0, lo, hi), jnp.where(core == 0, hi, lo)

    mix_keep, mix_give = core_halves(mix)
    na_far, ml_far = swap_core(normed_a), swap_core(mix_low)
    mix_got, got = swap_core(mix_give), swap_core(give)
    if two_rows():
        qkv_parts, o_parts = head_grads(flags, normed_a, na_far, keep, got, mix_keep, mix_got, mix_low, ml_far)
        grad_o = plane_scatter(*o_parts)
        grad_qkv = plane_scatter(*qkv_parts)
    else:
        both = lambda a, b: jnp.concatenate((a, b), axis=0)
        g = t_dot(both(normed_a, na_far), both(keep, got))
        g = g[:, : 3 * span] + up32(swap_x(low16(g[:, 3 * span :])))
        grad_qkv = up32(lax.psum_scatter(low16(g), "dp", scatter_dimension=0, tiled=True))
        g = t_dot(both(mix_keep, mix_got), both(mix_low, ml_far))
        g = g[:span] + up32(swap_x(low16(g[span:])))
        grad_o = up32(lax.psum_scatter(low16(g), "dp", scatter_dimension=1, tiled=True))
    gain_shard = scatter_gains(jnp.concatenate((gain_sum_a, gain_sum_b), axis=0), dp_idx, tensor_idx)

    return (
        acts[None],
        grads[None],
        grad_qkv[None, :, :span],
        grad_qkv[None, :, span : 2 * span],
        grad_qkv[None, :, 2 * span :],
        grad_o[None],
        grad_up[None],
        grad_down[None],
        gain_shard[None],
    )


def solution(mesh):
    return jax.shard_map(
        local,
        mesh=mesh,
        in_specs=(
            P("dp", "tensor", None),
            P("dp"),
            P("section", "dp", "tensor"),
            P("section", "dp", "tensor"),
            P("section", "dp", "tensor"),
            P("section", "tensor", "dp"),
            P("section", "dp", "tensor"),
            P("section", "tensor", "dp"),
            P("section", None, ("dp", "tensor")),
            P("dp", "tensor", None),
        ),
        out_specs=(
            P("section", "dp", "tensor", None),
            P("section", "dp", "tensor", None),
            P("section", "dp", "tensor"),
            P("section", "dp", "tensor"),
            P("section", "dp", "tensor"),
            P("section", "tensor", "dp"),
            P("section", "dp", "tensor"),
            P("section", "tensor", "dp"),
            P("section", None, ("dp", "tensor")),
        ),
        check_vma=False,
    )
```

time: 2010 us -> 986 us (0.49)
  Pallas kernels: 0 us -> 463 us
  waiting for transfers between devices: 714 us -> 319 us
  matrix products: 391 us -> 0 us
  blocking collectives: 347 us -> 0 us
  local copies, waits for them, and re-layouts: 331 us -> 111 us
  other arithmetic: 143 us -> 18.9 us
  starting transfers between devices: 40.7 us -> 66.1 us
    pallas_call x0 -> x31, Pallas kernels: none -> 463 us  [the longest x30 422 us: call(): pl.pallas_call(kernel, out_shape=tuple(outs), in_specs=ins, out_specs=tup...]
    dot_general x79 -> x0, matrix products: 391 us -> none  [the longest x5 52.4 us: backward_pass(): jnp.einsum('bsd,fd->bsf', down_low, w_lower, preferred_element_type=jnp.f...]
    unnamed x39 -> x0, waiting for transfers between devices: 290 us -> none
    all_gather x15 -> x0, waiting for transfers between devices: 278 us -> none  [the longest x6 109 us: widen(): return lax.all_gather(token_rows, 'tensor', axis=1, tiled=True)]
    ppermute x8 -> x78, waiting for transfers between devices: 79.9 us -> 319 us  [the longest x22 144 us: swap_x(): return lax.ppermute(a, 'tensor', [(i, i ^ 2) for i in range(n)])]
    unnamed x10 -> x0, blocking collectives: 222 us -> none
    all_gather x5 -> x0, blocking collectives: 125 us -> none  [the longest x1 29.3 us: local(): lax.all_gather(key_weight[0], 'dp', axis=0, tiled=True)]
    unnamed x502 -> x124, local copies, waits for them, and re-layouts: 120 us -> 46.1 us
  transfers between devices with their start and end apart: 41 -> 78, of which waited for: 30 -> 28; matrix products, arithmetic and copies ran while one was open for 26% -> 9% of each run, Pallas kernels for 0% -> 19%
where the time goes in v1:
time: 986 us; the launch traced here: 980 us
  Pallas kernels  463 us (47%)
  waiting for transfers between devices  319 us (32%)
  local copies, waits for them, and re-layouts  111 us (11%)
  starting transfers between devices  66.1 us (7%)
  other arithmetic  18.9 us (2%)
    pallas_call x30, Pallas kernels, call(): pl.pallas_call(kernel, out_shape=tuple(outs), in_specs=ins, out_specs=tup...  422 us
    ppermute x22, waiting for transfers between devices, swap_x(): return lax.ppermute(a, 'tensor', [(i, i ^ 2) for i in range(n)])  144 us
    ppermute x6, waiting for transfers between devices, shift(): return lax.ppermute(a, 'section', pairs)  106 us
    ppermute x18, waiting for transfers between devices, swap_y(): return lax.ppermute(a, 'dp', [(0, 1), (1, 0)])  59.6 us
    unnamed x124, local copies, waits for them, and re-layouts  46.1 us
    pallas_call x1, Pallas kernels, unit_grads(): pl.pallas_call(kernel, grid=(steps,), in_specs=[SMEM, pl.BlockSpec((block...  41.2 us
    ppermute x22, starting transfers between devices, swap_x(): return lax.ppermute(a, 'tensor', [(i, i ^ 2) for i in range(n)])  23.8 us
    ppermute x18, starting transfers between devices, swap_y(): return lax.ppermute(a, 'dp', [(0, 1), (1, 0)])  20.8 us
  transfers between devices with their start and end apart: 78, of which 28 were waited for; matrix products, arithmetic and copies ran while one was open for 9% of the time, Pallas kernels for 19%

profile of v1, /device:TPU:0, one launch (start us, length us, event | category | flops | bytes accessed | tf_op | source)
XLA Modules:
  0.0 979.7 jit_solution(5527414027897386619)
XLA Ops:
  23.7 20.7 %collective-permute-done.4.refs_1_ = bf16[576,864]{1,0:T(8,128)(2,1)S(1)} collective-permute-done((bf16[576,864]{1,0:T(8,128)(2,1)S(1)}, bf16[576,864]{1,0:T(8,128)(2,1)S(1)}, u32[]{:S(2)}, u32[]{:S(2)}) %collective-permute-start.4) | collective-permute-done | bytes 995360 | tf_op jit(solution)/shard_map/ppermute | solution.py:34
  48.7 6.5 collective-permute-done.13.refs_1_
  63.8 31.8 %collective-permute-done.2 = f32[2,288]{1,0:T(2,128)S(1)} collective-permute-done((f32[2,288]{1,0:T(2,128)S(1)}, f32[2,288]{1,0:T(2,128)S(1)}, u32[]{:S(2)}, u32[]{:S(2)}) %collective-permute-start.2) | collective-permute-done | bytes 2336 | tf_op jit(solution)/shard_map/ppermute | solution.py:30
  116.5 17.7 %collective-permute-done.32 = bf16[1076,576]{0,1:T(8,128)(2,1)} collective-permute-done((bf16[1076,576]{0,1:T(8,128)(2,1)}, bf16[1076,576]{0,1:T(8,128)(2,1)}, u32[]{:S(2)}, u32[]{:S(2)}) %collective-permute-start.32) | collective-permute-done | bytes 1239584 | tf_op jit(solution)/shard_map/ppermute | solution.py:30
  134.8 9.6 assemble_qkv.1.refs_2_.w_hbm.refs_4_
  155.0 7.5 keys_values.4
  162.5 6.9 collective-permute-done.25
  174.0 10.9 %collective-permute-done.34 = bf16[532,576]{1,0:T(8,128)(2,1)S(1)} collective-permute-done((bf16[532,576]{1,0:T(8,128)(2,1)}, bf16[532,576]{1,0:T(8,128)(2,1)S(1)}, u32[]{:S(2)}, u32[]{:S(2)}) %collective-permute-start.34) | collective-permute-done | bytes 612896 | tf_op jit(solution)/shard_map/ppermute | solution.py:34
  188.0 14.6 %collective-permute-done.33 = bf16[544,576]{1,0:T(8,128)(2,1)S(1)} collective-permute-done((bf16[544,576]{1,0:T(8,128)(2,1)S(1)}, bf16[544,576]{1,0:T(8,128)(2,1)S(1)}, u32[]{:S(2)}, u32[]{:S(2)}) %collective-permute-start.33) | collective-permute-done | bytes 626720 | tf_op jit(solution)/shard_map/ppermute | solution.py:30
  214.9 5.6 queries.4.q_ref
  223.9 13.4 %attention_part.1 = (f32[368,1152]{1,0:T(8,128)}, bf16[368,1152]{1,0:T(8,128)(2,1)}) custom-call(bf16[368,1152]{1,0:T(8,128)(2,1)} %queries.4.q_ref, bf16[368,2304]{1,0:T(8,128)(2,1)} %get-tuple-element.73.own_ref, bf16[368,2304]{1,0:T(8,128)(2,1)} %collective-permute-done.12.far_ref, f32[8,736]{1,0:T(8,128)} %broadcast_in_dim.67.bias_ref, ...), custom_call_target="tpu_custom_call" | custom-call | flops 7580050944 | bytes 11161088 | tf_op jit(solution)/shard_map/attention_part/pallas_call | solution.py:122
  237.3 10.0 %assemble_up.1.wu_hbm.refs_4_.refs_6_ = bf16[1152,4352]{1,0:T(8,128)(2,1)} custom-call(s32[2]{0:T(128)} %pad_add_fusion.flag_ref, bf16[576,1076]{1,0:T(8,128)(2,1)} %bitcast.13.refs_0_, bf16[576,1076]{1,0:T(8,128)(2,1)} %collective-permute-done.21.refs_1_, bf16[576,1076]{1,0:T(8,128)(2,1)} %collective-permute-done.22.refs_2_, ...), custom_call_target="tpu_custom_call" | custom-call | bytes 19943432 | tf_op jit(solution)/shard_map/assemble_up/pallas_call | solution.py:122
  255.4 10.4 %assemble_down.1.wd_hbm.refs_5_.refs_7_ = bf16[4352,1152]{1,0:T(8,128)(2,1)} custom-call(s32[2]{0:T(128)} %pad_add_fusion.flag_ref, bf16[1076,576]{1,0:T(8,128)(2,1)} %bitcast.53, bf16[1076,576]{1,0:T(8,128)(2,1)} %copy-done.1, bf16[1076,576]{1,0:T(8,128)(2,1)} %copy.58.refs_2_, bf16[1076,576]{1,0:T(8,128)(2,1)} %copy.59.refs_3_, ...), custom_call_target="tpu_custom_call" | custom-call | bytes 19943432 | tf_op jit(solution)/shard_map/assemble_down/pallas_call | solution.py:122
  265.8 15.3 %feed_part.1 = bf16[368,1152]{1,0:T(8,128)(2,1)} custom-call(f32[368,1152]{1,0:T(8,128)} %get-tuple-element.75.hid_ref, bf16[368,1152]{1,0:T(8,128)(2,1)} %get-tuple-element.76.nb_ref, bf16[1152,4352]{1,0:T(8,128)(2,1)} %assemble_up.1.wu_hbm.refs_4_.refs_6_, bf16[4352,1152]{1,0:T(8,128)(2,1)} %assemble_down.1.wd_hbm.refs_5_.refs_7_), custom_call_target="tpu_custom_call" | custom-call | flops 10331829248 | bytes 23445504 | tf_op jit(solution)/shard_map/feed_part/pallas_call | solution.py:122
  284.8 18.4 %collective-permute-done.37.refs_1_ = bf16[368,1152]{1,0:T(8,128)(2,1)S(1)} collective-permute-done((bf16[368,1152]{1,0:T(8,128)(2,1)}, bf16[368,1152]{1,0:T(8,128)(2,1)S(1)}, u32[]{:S(2)}, u32[]{:S(2)}) %collective-permute-start.37) | collective-permute-done | bytes 847904 | tf_op jit(solution)/shard_map/ppermute | solution.py:40
  304.2 7.9 keys_values.5
  312.1 5.5 queries.5.q_ref
  318.9 25.0 %layer.3 = bf16[368,1152]{1,0:T(8,128)(2,1)} custom-call(bf16[368,1152]{1,0:T(8,128)(2,1)} %queries.5.q_ref, bf16[368,2304]{1,0:T(8,128)(2,1)} %get-tuple-element.80.own_ref, bf16[368,2304]{1,0:T(8,128)(2,1)} %copy-done.42, f32[8,736]{1,0:T(8,128)} %broadcast_in_dim.67.bias_ref, f32[368,1152]{1,0:T(8,128)} %get-tuple-element.81.x_ref.refs_2_, ...), custom_call_target="tpu_custom_call" | custom-call | flops 17911879680 | bytes 29519360 | tf_op jit(solution)/shard_map/layer/pallas_call | solution.py:122
  348.6 18.6 %collective-permute-done.39.refs_1_ = bf16[368,1152]{1,0:T(8,128)(2,1)S(1)} collective-permute-done((bf16[368,1152]{1,0:T(8,128)(2,1)}, bf16[368,1152]{1,0:T(8,128)(2,1)S(1)}, u32[]{:S(2)}, u32[]{:S(2)}) %collective-permute-start.39) | collective-permute-done | bytes 847904 | tf_op jit(solution)/shard_map/ppermute | solution.py:40
  368.1 7.9 keys_values.6
  376.1 5.5 queries.6.q_ref
  382.9 25.0 %layer.4 = bf16[368,1152]{1,0:T(8,128)(2,1)} custom-call(bf16[368,1152]{1,0:T(8,128)(2,1)} %queries.6.q_ref, bf16[368,2304]{1,0:T(8,128)(2,1)} %get-tuple-element.83.own_ref, bf16[368,2304]{1,0:T(8,128)(2,1)} %copy-done.43, f32[8,736]{1,0:T(8,128)} %broadcast_in_dim.67.bias_ref, f32[368,1152]{1,0:T(8,128)} %get-tuple-element.84.x_ref.refs_2_, ...), custom_call_target="tpu_custom_call" | custom-call | flops 17911879680 | bytes 29519360 | tf_op jit(solution)/shard_map/layer/pallas_call | solution.py:122
  412.4 18.8 %collective-permute-done.41.refs_1_ = bf16[368,1152]{1,0:T(8,128)(2,1)S(1)} collective-permute-done((bf16[368,1152]{1,0:T(8,128)(2,1)}, bf16[368,1152]{1,0:T(8,128)(2,1)S(1)}, u32[]{:S(2)}, u32[]{:S(2)}) %collective-permute-start.41) | collective-permute-done | bytes 847904 | tf_op jit(solution)/shard_map/ppermute | solution.py:40
  432.1 7.8 keys_values.7
  442.2 10.2 %collective-permute-done.44 = bf16[184,1152]{1,0:T(8,128)(2,1)S(1)} collective-permute-done((bf16[184,1152]{1,0:T(8,128)(2,1)S(1)}, bf16[184,1152]{1,0:T(8,128)(2,1)S(1)}, u32[]{:S(2)}, u32[]{:S(2)}) %collective-permute-start.44) | collective-permute-done | bytes 423968 | tf_op jit(solution)/shard_map/ppermute | solution.py:30
  453.7 5.5 queries.7.q_ref
  460.4 28.3 %layer.5 = (bf16[368,1152]{1,0:T(8,128)(2,1)}, f32[368,1152]{1,0:T(8,128)}, f32[368,1152]{1,0:T(8,128)}, bf16[368,1152]{1,0:T(8,128)(2,1)}, bf16[368,4352]{1,0:T...) custom-call(bf16[368,1152]{1,0:T(8,128)(2,1)} %queries.7.q_ref, ...), custom_call_target="tpu_custom_call" | custom-call | flops 17911879680 | bytes 37998080 | tf_op jit(solution)/shard_map/layer/pallas_call | solution.py:122
  488.8 22.6 %feed_back.4 = (f32[368,1152]{1,0:T(8,128)}, bf16[368,1152]{1,0:T(8,128)(2,1)}) custom-call(f32[368,1152]{1,0:T(8,128)} %select_maximum_fusion.refs_0_.refs_2_, bf16[368,4352]{1,0:T(8,128)(2,1)} %get-tuple-element.89.refs_1_.refs_3_, f32[368,1152]{1,0:T(8,128)} %get-tuple-element.90.refs_2_.refs_4_, f32[1,1152]{1,0:T(1,128)} %get-tuple-element.197.gain_ref.refs_3_.refs_5_, ...), custom_call_target="tpu_custom_call" | custom-call | flops 11699276800 | bytes 31851008 | tf_op jit(solution)/shard_map/feed_back/pallas_call | solution.py:122
  511.4 17.8 %attention_back.4 = (bf16[368,1152]{1,0:T(8,128)(2,1)}, bf16[368,2304]{1,0:T(8,128)(2,1)}, bf16[368,2304]{1,0:T(8,128)(2,1)}) custom-call(bf16[368,1152]{1,0:T(8,128)(2,1)} %queries.7.q_ref, bf16[368,2304]{1,0:T(8,128)(2,1)} %get-tuple-element.86.own_ref, bf16[368,2304]{1,0:T(8,128)(2,1)} %copy-done.41, bf16[368,1152]{1,0:T(8,128)(2,1)} %get-tuple-element.91.do_ref, ...), custom_call_target="tpu_custom_call" | custom-call | flops 15531507712 | bytes 10386432 | tf_op jit(solution)/shard_map/attention_back/pallas_call | solution.py:122
  534.3 13.4 %qkv_back.4 = bf16[368,1152]{1,0:T(8,128)(2,1)} custom-call(bf16[368,1152]{1,0:T(8,128)(2,1)} %get-tuple-element.94.dq_ref, bf16[368,2304]{1,0:T(8,128)(2,1)} %get-tuple-element.95.own_ref, bf16[368,2304]{1,0:T(8,128)(2,1)} %copy-done.10, f32[368,1152]{1,0:T(8,128)} %get-tuple-element.87.x_ref, f32[368,1152]{1,0:T(8,128)} %get-tuple-element.97.hg_ref, ...), custom_call_target="tpu_custom_call" | custom-call | flops 4102343936 | bytes 16445952 | tf_op jit(solution)/shard_map/qkv_back/pallas_call | solution.py:122
  549.0 22.3 %collective-permute-done.46.refs_1_ = bf16[368,1152]{1,0:T(8,128)(2,1)S(1)} collective-permute-done((bf16[368,1152]{1,0:T(8,128)(2,1)}, bf16[368,1152]{1,0:T(8,128)(2,1)S(1)}, u32[]{:S(2)}, u32[]{:S(2)}) %collective-permute-start.46) | collective-permute-done | bytes 847904 | tf_op jit(solution)/shard_map/ppermute | solution.py:40
  572.2 22.7 %feed_back.5 = (f32[368,1152]{1,0:T(8,128)}, f32[368,1152]{1,0:T(8,128)}, bf16[368,1152]{1,0:T(8,128)(2,1)}) custom-call(s32[1]{0:T(128)} %bitcast.1.refs_0_, bf16[368,1152]{1,0:T(8,128)(2,1)} %copy-done.47, f32[368,1152]{1,0:T(8,128)} %select_maximum_fusion.refs_0_.refs_2_, bf16[368,4352]{1,0:T(8,128)(2,1)} %get-tuple-element.89.refs_1_.refs_3_, ...), custom_call_target="tpu_custom_call" | custom-call | flops 11699276800 | bytes 34394628 | tf_op jit(solution)/shard_map/feed_back/pallas_call | solution.py:122
  594.9 17.8 %attention_back.5 = (bf16[368,1152]{1,0:T(8,128)(2,1)}, bf16[368,2304]{1,0:T(8,128)(2,1)}, bf16[368,2304]{1,0:T(8,128)(2,1)}) custom-call(bf16[368,1152]{1,0:T(8,128)(2,1)} %queries.7.q_ref, bf16[368,2304]{1,0:T(8,128)(2,1)} %get-tuple-element.86.own_ref, bf16[368,2304]{1,0:T(8,128)(2,1)} %copy-done.41, bf16[368,1152]{1,0:T(8,128)(2,1)} %get-tuple-element.98.do_ref, ...), custom_call_target="tpu_custom_call" | custom-call | flops 15531507712 | bytes 10386432 | tf_op jit(solution)/shard_map/attention_back/pallas_call | solution.py:122
  617.8 13.4 %qkv_back.5 = bf16[368,1152]{1,0:T(8,128)(2,1)} custom-call(bf16[368,1152]{1,0:T(8,128)(2,1)} %get-tuple-element.99.dq_ref, bf16[368,2304]{1,0:T(8,128)(2,1)} %get-tuple-element.100.own_ref, bf16[368,2304]{1,0:T(8,128)(2,1)} %copy-done.11, f32[368,1152]{1,0:T(8,128)} %get-tuple-element.87.x_ref, f32[368,1152]{1,0:T(8,128)} %get-tuple-element.102.hg_ref, ...), custom_call_target="tpu_custom_call" | custom-call | flops 4102343936 | bytes 16445952 | tf_op jit(solution)/shard_map/qkv_back/pallas_call | solution.py:122
  641.2 13.0 %collective-permute-done.48.refs_1_ = bf16[368,1152]{1,0:T(8,128)(2,1)S(1)} collective-permute-done((bf16[368,1152]{1,0:T(8,128)(2,1)}, bf16[368,1152]{1,0:T(8,128)(2,1)S(1)}, u32[]{:S(2)}, u32[]{:S(2)}) %collective-permute-start.48) | collective-permute-done | bytes 847904 | tf_op jit(solution)/shard_map/ppermute | solution.py:40
  655.1 22.8 %feed_back.6 = (f32[368,1152]{1,0:T(8,128)}, f32[368,1152]{1,0:T(8,128)}, bf16[368,1152]{1,0:T(8,128)(2,1)}) custom-call(s32[1]{0:T(128)} %bitcast.2.refs_0_, bf16[368,1152]{1,0:T(8,128)(2,1)} %copy-done.46, f32[368,1152]{1,0:T(8,128)} %get-tuple-element.103.refs_2_, bf16[368,4352]{1,0:T(8,128)(2,1)} %get-tuple-element.89.refs_1_.refs_3_, ...), custom_call_target="tpu_custom_call" | custom-call | flops 11699276800 | bytes 34394628 | tf_op jit(solution)/shard_map/feed_back/pallas_call | solution.py:122
  677.9 17.9 %attention_back.6 = (bf16[368,1152]{1,0:T(8,128)(2,1)}, bf16[368,2304]{1,0:T(8,128)(2,1)}, bf16[368,2304]{1,0:T(8,128)(2,1)}) custom-call(bf16[368,1152]{1,0:T(8,128)(2,1)} %queries.7.q_ref, bf16[368,2304]{1,0:T(8,128)(2,1)} %get-tuple-element.86.own_ref, bf16[368,2304]{1,0:T(8,128)(2,1)} %copy-done.41, bf16[368,1152]{1,0:T(8,128)(2,1)} %get-tuple-element.104.do_ref, ...), custom_call_target="tpu_custom_call" | custom-call | flops 15531507712 | bytes 10386432 | tf_op jit(solution)/shard_map/attention_back/pallas_call | solution.py:122
  706.1 14.9 %collective-permute-done.67 = bf16[192,1152]{1,0:T(8,128)(2,1)S(1)} collective-permute-done((bf16[192,1152]{1,0:T(8,128)(2,1)S(1)}, bf16[192,1152]{1,0:T(8,128)(2,1)S(1)}, u32[]{:S(2)}, u32[]{:S(2)}) %collective-permute-start.67) | collective-permute-done | bytes 442400 | tf_op jit(solution)/shard_map/ppermute | solution.py:30
  725.6 13.2 %qkv_back.6 = bf16[368,1152]{1,0:T(8,128)(2,1)} custom-call(bf16[368,1152]{1,0:T(8,128)(2,1)} %get-tuple-element.105.dq_ref, bf16[368,2304]{1,0:T(8,128)(2,1)} %get-tuple-element.106.own_ref, bf16[368,2304]{1,0:T(8,128)(2,1)} %copy-done.9, f32[368,1152]{1,0:T(8,128)} %get-tuple-element.87.x_ref, f32[368,1152]{1,0:T(8,128)} %get-tuple-element.108.hg_ref, ...), custom_call_target="tpu_custom_call" | custom-call | flops 4102343936 | bytes 16445952 | tf_op jit(solution)/shard_map/qkv_back/pallas_call | solution.py:122
  746.9 14.4 %collective-permute-done.50.refs_1_ = bf16[368,1152]{1,0:T(8,128)(2,1)} collective-permute-done((bf16[368,1152]{1,0:T(8,128)(2,1)}, bf16[368,1152]{1,0:T(8,128)(2,1)}, u32[]{:S(2)}, u32[]{:S(2)}) %collective-permute-start.50) | collective-permute-done | bytes 847904 | tf_op jit(solution)/shard_map/ppermute | solution.py:40
  761.3 22.9 %feed_back.7 = (f32[368,1152]{1,0:T(8,128)}, f32[368,1152]{1,0:T(8,128)}, bf16[368,1152]{1,0:T(8,128)(2,1)}, bf16[368,1152]{1,0:T(8,128)(2,1)}, bf16[368,1152]{1,0:T(8,128)(2,1)}, /*index=5*/f32[1,1152]{1,0:T(1,128)}) custom-call(s32[1]{0:T(128)} %bitcast.18.refs_0_, bf16[368,1152]{1,0:T(8,128)(2,1)} %collective-permute-done.50.refs_1_, ...), custom_call_target="tpu_custom_call" | custom-call | flops 11699276800 | bytes 36094980 | tf_op jit(solution)/shard_map/feed_back/pallas_call | solution.py:122
  784.2 17.8 %attention_back.7 = (bf16[368,1152]{1,0:T(8,128)(2,1)}, bf16[368,2304]{1,0:T(8,128)(2,1)}, bf16[368,2304]{1,0:T(8,128)(2,1)}) custom-call(bf16[368,1152]{1,0:T(8,128)(2,1)} %queries.7.q_ref, bf16[368,2304]{1,0:T(8,128)(2,1)} %get-tuple-element.86.own_ref, bf16[368,2304]{1,0:T(8,128)(2,1)} %copy-done.41, bf16[368,1152]{1,0:T(8,128)(2,1)} %get-tuple-element.110.do_ref, ...), custom_call_target="tpu_custom_call" | custom-call | flops 15531507712 | bytes 10386432 | tf_op jit(solution)/shard_map/attention_back/pallas_call | solution.py:122
  810.5 17.6 %collective-permute-done.71 = bf16[368,1152]{1,0:T(8,128)(2,1)S(1)} collective-permute-done((bf16[368,1152]{1,0:T(8,128)(2,1)S(1)}, bf16[368,1152]{1,0:T(8,128)(2,1)S(1)}, u32[]{:S(2)}, u32[]{:S(2)}) %collective-permute-start.71) | collective-permute-done | bytes 847904 | tf_op jit(solution)/shard_map/ppermute | solution.py:34
  834.1 15.0 %qkv_back.7 = (f32[368,1152]{1,0:T(8,128)}, bf16[368,1152]{1,0:T(8,128)(2,1)}, bf16[368,1728]{1,0:T(8,128)(2,1)}, bf16[368,1728]{1,0:T(8,128)(2,1)}, f32[1,1152]{1,0:T(1,128)}) custom-call(bf16[368,1152]{1,0:T(8,128)(2,1)} %get-tuple-element.111.dq_ref, bf16[368,2304]{1,0:T(8,128)(2,1)} %get-tuple-element.112.own_ref, ...), custom_call_target="tpu_custom_call" | custom-call | flops 4102343936 | bytes 20689924 | tf_op jit(solution)/shard_map/qkv_back/pallas_call | solution.py:122
  861.9 10.7 %head_grads.1 = (f32[576,864]{1,0:T(8,128)}, bf16[576,864]{1,0:T(8,128)(2,1)}, bf16[576,864]{1,0:T(8,128)(2,1)}, bf16[576,864]{1,0:T(8,128)(2,1)}, f32[288,576]{...) custom-call(s32[2]{0:T(128)} %pad_add_fusion.flag_ref, ...), custom_call_target="tpu_custom_call" | custom-call | flops 10939583488 | bytes 13418504 | tf_op jit(solution)/shard_map/head_grads/pallas_call | solution.py:122
  879.3 29.1 %collective-permute-done.61 = bf16[288,576]{1,0:T(8,128)(2,1)S(1)} collective-permute-done((bf16[288,576]{1,0:T(8,128)(2,1)S(1)}, bf16[288,576]{1,0:T(8,128)(2,1)S(1)}, u32[]{:S(2)}, u32[]{:S(2)}) %collective-permute-start.61) | collective-permute-done | bytes 331808 | tf_op jit(solution)/shard_map/ppermute | solution.py:30
  918.4 8.1 collective-permute-done.60
  934.9 41.2 %unit_grads.1 = (f32[576,1076]{1,0:T(8,128)}, f32[1076,576]{1,0:T(8,128)}) custom-call(s32[2]{0:T(128)} %pad_add_fusion.flag_ref, bf16[2944,1152]{1,0:T(8,128)(2,1)} %constant_dynamic-update-slice_fusion.13.nb_ref, bf16[2944,1152]{1,0:T(8,128)(2,1)} %constant_dynamic-update-slice_fusion.24.dy_ref, bf16[1152,1088]{1,0:T(8,128)(2,1)} %slice.244.wu_ref, ...), custom_call_target="tpu_custom_call" | custom-call | flops 30995486720 | bytes 13565952 | tf_op jit(solution)/shard_map/unit_grads/pallas_call | solution.py:599
  (345 shorter events, 223.8 us)
Async XLA Ops:
  20.4 24.0 %collective-permute-start.4 = (bf16[576,864]{1,0:T(8,128)(2,1)S(1)}, bf16[576,864]{1,0:T(8,128)(2,1)S(1)}, u32[]{:S(2)}, u32[]{:S(2)}) collective-permute-start(bf16[576,864]{1,0:T(8,128)(2,1)S(1)} %pad_maximum_fusion.refs_0_), channel_id=1, source_target_pairs={{0,4},{4,0},{1,5},{5,1},{2,6},{6,2},{3,7},{7,3},{8,12},{12,8},{9,1... | collective-permute-start | bytes 2985992 | tf_op jit(solution)/shard_map/ppermute | solution.py:34
  22.2 23.4 %collective-permute-start.7 = (bf16[576,864]{1,0:T(8,128)(2,1)S(1)}, bf16[576,864]{1,0:T(8,128)(2,1)S(1)}, u32[]{:S(2)}, u32[]{:S(2)}) collective-permute-start(bf16[576,864]{1,0:T(8,128)(2,1)S(1)} %pad_maximum_fusion.refs_0_), channel_id=1, source_target_pairs={{0,2},{1,3},{2,0},{3,1},{4,6},{5,7},{6,4},{7,5},{8,10},{9,11},{10,... | collective-permute-start | bytes 2985992 | tf_op jit(solution)/shard_map/ppermute | solution.py:30
  55.8 42.6 %collective-permute-start.21 = (bf16[576,1076]{1,0:T(8,128)(2,1)}, bf16[576,1076]{1,0:T(8,128)(2,1)}, u32[]{:S(2)}, u32[]{:S(2)}) collective-permute-start(bf16[576,1076]{1,0:T(8,128)(2,1)} %bitcast.13.refs_0_), channel_id=1, source_target_pairs={{0,4},{4,0},{1,5},{5,1},{2,6},{6,2},{3,7},{7,3},{8,12},{12,8},{9,1... | collective-permute-start | bytes 3718664 | tf_op jit(solution)/shard_map/ppermute | solution.py:34
  56.9 42.7 %collective-permute-start.24 = (bf16[576,1076]{1,0:T(8,128)(2,1)}, bf16[576,1076]{1,0:T(8,128)(2,1)}, u32[]{:S(2)}, u32[]{:S(2)}) collective-permute-start(bf16[576,1076]{1,0:T(8,128)(2,1)} %bitcast.13.refs_0_), channel_id=1, source_target_pairs={{0,2},{1,3},{2,0},{3,1},{4,6},{5,7},{6,4},{7,5},{8,10},{9,11},{10,... | collective-permute-start | bytes 3718664 | tf_op jit(solution)/shard_map/ppermute | solution.py:30
  59.3 42.5 %collective-permute-start.8 = (bf16[288,864]{1,0:T(8,128)(2,1)}, bf16[288,864]{1,0:T(8,128)(2,1)}, u32[]{:S(2)}, u32[]{:S(2)}) collective-permute-start(bf16[288,864]{1,0:T(8,128)(2,1)} %slice.215), channel_id=1, source_target_pairs={{0,2},{1,3},{2,0},{3,1},{4,6},{5,7},{6,4},{7,5},{8,10},{9,11},{10,... | collective-permute-start | bytes 1493000 | tf_op jit(solution)/shard_map/ppermute | solution.py:30
  61.6 43.3 %collective-permute-start.9 = (bf16[288,864]{1,0:T(8,128)(2,1)}, bf16[288,864]{1,0:T(8,128)(2,1)}, u32[]{:S(2)}, u32[]{:S(2)}) collective-permute-start(bf16[288,864]{1,0:T(8,128)(2,1)} %slice.216), channel_id=1, source_target_pairs={{0,4},{4,0},{1,5},{5,1},{2,6},{6,2},{3,7},{7,3},{8,12},{12,8},{9,1... | collective-permute-start | bytes 1493000 | tf_op jit(solution)/shard_map/ppermute | solution.py:34
  62.6 33.0 %collective-permute-start.2 = (f32[2,288]{1,0:T(2,128)S(1)}, f32[2,288]{1,0:T(2,128)S(1)}, u32[]{:S(2)}, u32[]{:S(2)}) collective-permute-start(f32[2,288]{1,0:T(2,128)S(1)} %maximum_select_fusion.4), channel_id=1, source_target_pairs={{0,2},{1,3},{2,0},{3,1},{4,6},{5,7},{6,4},{7,5},{8,10},{9,11},{10,... | collective-permute-start | bytes 6920 | tf_op jit(solution)/shard_map/ppermute | solution.py:30
  101.9 32.3 %collective-permute-start.32 = (bf16[1076,576]{0,1:T(8,128)(2,1)}, bf16[1076,576]{0,1:T(8,128)(2,1)}, u32[]{:S(2)}, u32[]{:S(2)}) collective-permute-start(bf16[1076,576]{0,1:T(8,128)(2,1)} %copy.51), channel_id=1, source_target_pairs={{0,2},{1,3},{2,0},{3,1},{4,6},{5,7},{6,4},{7,5},{8,10},{9,11},{10,... | collective-permute-start | bytes 3718664 | tf_op jit(solution)/shard_map/ppermute | solution.py:30
  110.2 60.8 %collective-permute-start.29 = (bf16[1076,576]{0,1:T(8,128)(2,1)}, bf16[1076,576]{0,1:T(8,128)(2,1)}, u32[]{:S(2)}, u32[]{:S(2)}) collective-permute-start(bf16[1076,576]{0,1:T(8,128)(2,1)} %copy.51), channel_id=1, source_target_pairs={{0,4},{4,0},{1,5},{5,1},{2,6},{6,2},{3,7},{7,3},{8,12},{12,8},{9,1... | collective-permute-start | bytes 3718664 | tf_op jit(solution)/shard_map/ppermute | solution.py:34
  114.7 37.1 %collective-permute-start.17 = (bf16[144,576]{1,0:T(8,128)(2,1)}, bf16[144,576]{1,0:T(8,128)(2,1)S(1)}, u32[]{:S(2)}, u32[]{:S(2)}) collective-permute-start(bf16[144,576]{1,0:T(8,128)(2,1)} %slice.218), channel_id=1, source_target_pairs={{0,2},{1,3},{2,0},{3,1},{4,6},{5,7},{6,4},{7,5},{8,10},{9,11},{10,... | collective-permute-start | bytes 497672 | tf_op jit(solution)/shard_map/ppermute | solution.py:30
  115.3 37.7 %collective-permute-start.18 = (bf16[144,576]{1,0:T(8,128)(2,1)}, bf16[144,576]{1,0:T(8,128)(2,1)S(1)}, u32[]{:S(2)}, u32[]{:S(2)}) collective-permute-start(bf16[144,576]{1,0:T(8,128)(2,1)} %slice.219), channel_id=1, source_target_pairs={{0,4},{4,0},{1,5},{5,1},{2,6},{6,2},{3,7},{7,3},{8,12},{12,8},{9,1... | collective-permute-start | bytes 497672 | tf_op jit(solution)/shard_map/ppermute | solution.py:34
  116.5 37.7 %collective-permute-start.15 = (bf16[288,576]{1,0:T(8,128)(2,1)}, bf16[288,576]{1,0:T(8,128)(2,1)}, u32[]{:S(2)}, u32[]{:S(2)}) collective-permute-start(bf16[288,576]{1,0:T(8,128)(2,1)} %collective-permute-done.13.refs_1_), channel_id=1, source_target_pairs={{0,1},{1,0},{2,3},{3,2},{4,5},{5,4},{6,7},{7,6},{8,9},{9,8},{10,11... | collective-permute-start | bytes 995336 | tf_op jit(solution)/shard_map/ppermute | solution.py:25
  134.1 28.3 %collective-permute-start.19 = (bf16[288,576]{1,0:T(8,128)(2,1)}, bf16[288,576]{1,0:T(8,128)(2,1)}, u32[]{:S(2)}, u32[]{:S(2)}) collective-permute-start(bf16[288,576]{1,0:T(8,128)(2,1)} %collective-permute-done.16.refs_4_), channel_id=1, source_target_pairs={{0,1},{1,0},{2,3},{3,2},{4,5},{5,4},{6,7},{7,6},{8,9},{9,8},{10,11... | collective-permute-start | bytes 995336 | tf_op jit(solution)/shard_map/ppermute | solution.py:25
  154.1 30.7 %collective-permute-start.34 = (bf16[532,576]{1,0:T(8,128)(2,1)}, bf16[532,576]{1,0:T(8,128)(2,1)S(1)}, u32[]{:S(2)}, u32[]{:S(2)}) collective-permute-start(bf16[532,576]{1,0:T(8,128)(2,1)} %slice.223), channel_id=1, source_target_pairs={{0,4},{4,0},{1,5},{5,1},{2,6},{6,2},{3,7},{7,3},{8,12},{12,8},{9,1... | collective-permute-start | bytes 1838600 | tf_op jit(solution)/shard_map/ppermute | solution.py:34
  162.4 46.0 %collective-permute-start.12 = (bf16[368,2304]{1,0:T(8,128)(2,1)}, bf16[368,2304]{1,0:T(8,128)(2,1)}, u32[]{:S(2)}, u32[]{:S(2)}) collective-permute-start(bf16[368,2304]{1,0:T(8,128)(2,1)} %get-tuple-element.73.own_ref), channel_id=1, source_target_pairs={{0,1},{1,0},{2,3},{3,2},{4,5},{5,4},{6,7},{7,6},{8,9},{9,8},{10,11... | collective-permute-start | bytes 5087240 | tf_op jit(solution)/shard_map/ppermute | solution.py:25
  169.4 38.4 %collective-permute-start.22 = (bf16[576,1076]{1,0:T(8,128)(2,1)}, bf16[576,1076]{1,0:T(8,128)(2,1)}, u32[]{:S(2)}, u32[]{:S(2)}) collective-permute-start(bf16[576,1076]{1,0:T(8,128)(2,1)} %bitcast.13.refs_0_), channel_id=1, source_target_pairs={{0,1},{1,0},{2,3},{3,2},{4,5},{5,4},{6,7},{7,6},{8,9},{9,8},{10,11... | collective-permute-start | bytes 3718664 | tf_op jit(solution)/shard_map/ppermute | solution.py:25
  171.0 37.0 %collective-permute-start.23 = (bf16[576,1076]{1,0:T(8,128)(2,1)}, bf16[576,1076]{1,0:T(8,128)(2,1)}, u32[]{:S(2)}, u32[]{:S(2)}) collective-permute-start(bf16[576,1076]{1,0:T(8,128)(2,1)} %collective-permute-done.21.refs_1_), channel_id=1, source_target_pairs={{0,1},{1,0},{2,3},{3,2},{4,5},{5,4},{6,7},{7,6},{8,9},{9,8},{10,11... | collective-permute-start | bytes 3718664 | tf_op jit(solution)/shard_map/ppermute | solution.py:25
  171.0 37.4 %collective-permute-start.30 = (bf16[1076,576]{0,1:T(8,128)(2,1)}, bf16[1076,576]{0,1:T(8,128)(2,1)}, u32[]{:S(2)}, u32[]{:S(2)}) collective-permute-start(bf16[1076,576]{0,1:T(8,128)(2,1)} %copy.51), channel_id=1, source_target_pairs={{0,1},{1,0},{2,3},{3,2},{4,5},{5,4},{6,7},{7,6},{8,9},{9,8},{10,11... | collective-permute-start | bytes 3718664 | tf_op jit(solution)/shard_map/ppermute | solution.py:25
  207.4 29.9 %collective-permute-start.27 = (bf16[576,1076]{1,0:T(8,128)(2,1)}, bf16[576,1076]{1,0:T(8,128)(2,1)}, u32[]{:S(2)}, u32[]{:S(2)}) collective-permute-start(bf16[576,1076]{1,0:T(8,128)(2,1)} %collective-permute-done.24.refs_4_), channel_id=1, source_target_pairs={{0,1},{1,0},{2,3},{3,2},{4,5},{5,4},{6,7},{7,6},{8,9},{9,8},{10,11... | collective-permute-start | bytes 3718664 | tf_op jit(solution)/shard_map/ppermute | solution.py:25
  207.9 29.4 %collective-permute-start.28 = (bf16[576,1076]{1,0:T(8,128)(2,1)}, bf16[576,1076]{1,0:T(8,128)(2,1)}, u32[]{:S(2)}, u32[]{:S(2)}) collective-permute-start(bf16[576,1076]{1,0:T(8,128)(2,1)} %copy-done.5), channel_id=1, source_target_pairs={{0,1},{1,0},{2,3},{3,2},{4,5},{5,4},{6,7},{7,6},{8,9},{9,8},{10,11... | collective-permute-start | bytes 3718664 | tf_op jit(solution)/shard_map/ppermute | solution.py:25
  207.9 39.4 %collective-permute-start.31 = (bf16[1076,576]{0,1:T(8,128)(2,1)}, bf16[1076,576]{0,1:T(8,128)(2,1)}, u32[]{:S(2)}, u32[]{:S(2)}) collective-permute-start(bf16[1076,576]{0,1:T(8,128)(2,1)} %collective-permute-done.29), channel_id=1, source_target_pairs={{0,1},{1,0},{2,3},{3,2},{4,5},{5,4},{6,7},{7,6},{8,9},{9,8},{10,11... | collective-permute-start | bytes 3718664 | tf_op jit(solution)/shard_map/ppermute | solution.py:25
  208.4 41.5 %collective-permute-start.35 = (bf16[1076,576]{0,1:T(8,128)(2,1)}, bf16[1076,576]{0,1:T(8,128)(2,1)}, u32[]{:S(2)}, u32[]{:S(2)}) collective-permute-start(bf16[1076,576]{0,1:T(8,128)(2,1)} %collective-permute-done.32), channel_id=1, source_target_pairs={{0,1},{1,0},{2,3},{3,2},{4,5},{5,4},{6,7},{7,6},{8,9},{9,8},{10,11... | collective-permute-start | bytes 3718664 | tf_op jit(solution)/shard_map/ppermute | solution.py:25
  208.5 44.0 %collective-permute-start.36 = (bf16[1076,576]{0,1:T(8,128)(2,1)}, bf16[1076,576]{0,1:T(8,128)(2,1)}, u32[]{:S(2)}, u32[]{:S(2)}) collective-permute-start(bf16[1076,576]{0,1:T(8,128)(2,1)} %copy.56), channel_id=1, source_target_pairs={{0,1},{1,0},{2,3},{3,2},{4,5},{5,4},{6,7},{7,6},{8,9},{9,8},{10,11... | collective-permute-start | bytes 3718664 | tf_op jit(solution)/shard_map/ppermute | solution.py:25
  281.1 22.1 %collective-permute-start.37 = (bf16[368,1152]{1,0:T(8,128)(2,1)}, bf16[368,1152]{1,0:T(8,128)(2,1)S(1)}, u32[]{:S(2)}, u32[]{:S(2)}) collective-permute-start(bf16[368,1152]{1,0:T(8,128)(2,1)} %feed_part.1), channel_id=1, source_target_pairs={{0,8},{8,16},{16,24},{1,9},{9,17},{17,25},{2,10},{10,18},{18,26},{... | collective-permute-start | bytes 2543624 | tf_op jit(solution)/shard_map/ppermute | solution.py:40
  343.9 23.4 %collective-permute-start.39 = (bf16[368,1152]{1,0:T(8,128)(2,1)}, bf16[368,1152]{1,0:T(8,128)(2,1)S(1)}, u32[]{:S(2)}, u32[]{:S(2)}) collective-permute-start(bf16[368,1152]{1,0:T(8,128)(2,1)} %layer.3), channel_id=1, source_target_pairs={{0,8},{8,16},{16,24},{1,9},{9,17},{17,25},{2,10},{10,18},{18,26},{... | collective-permute-start | bytes 2543624 | tf_op jit(solution)/shard_map/ppermute | solution.py:40
  407.8 23.4 %collective-permute-start.41 = (bf16[368,1152]{1,0:T(8,128)(2,1)}, bf16[368,1152]{1,0:T(8,128)(2,1)S(1)}, u32[]{:S(2)}, u32[]{:S(2)}) collective-permute-start(bf16[368,1152]{1,0:T(8,128)(2,1)} %layer.4), channel_id=1, source_target_pairs={{0,8},{8,16},{16,24},{1,9},{9,17},{17,25},{2,10},{10,18},{18,26},{... | collective-permute-start | bytes 2543624 | tf_op jit(solution)/shard_map/ppermute | solution.py:40
  547.7 23.6 %collective-permute-start.46 = (bf16[368,1152]{1,0:T(8,128)(2,1)}, bf16[368,1152]{1,0:T(8,128)(2,1)S(1)}, u32[]{:S(2)}, u32[]{:S(2)}) collective-permute-start(bf16[368,1152]{1,0:T(8,128)(2,1)} %qkv_back.4), channel_id=1, source_target_pairs={{8,0},{16,8},{24,16},{9,1},{17,9},{25,17},{10,2},{18,10},{26,18},{... | collective-permute-start | bytes 2543624 | tf_op jit(solution)/shard_map/ppermute | solution.py:40
  631.2 23.0 %collective-permute-start.48 = (bf16[368,1152]{1,0:T(8,128)(2,1)}, bf16[368,1152]{1,0:T(8,128)(2,1)S(1)}, u32[]{:S(2)}, u32[]{:S(2)}) collective-permute-start(bf16[368,1152]{1,0:T(8,128)(2,1)} %qkv_back.5), channel_id=1, source_target_pairs={{8,0},{16,8},{24,16},{9,1},{17,9},{25,17},{10,2},{18,10},{26,18},{... | collective-permute-start | bytes 2543624 | tf_op jit(solution)/shard_map/ppermute | solution.py:40
  639.3 221.0 %collective-permute-start.53 = (bf16[368,1152]{1,0:T(8,128)(2,1)}, bf16[368,1152]{1,0:T(8,128)(2,1)}, u32[]{:S(2)}, u32[]{:S(2)}) collective-permute-start(bf16[368,1152]{1,0:T(8,128)(2,1)} %get-tuple-element.85.normed.na0), channel_id=1, source_target_pairs={{0,1},{1,0},{2,3},{3,2},{4,5},{5,4},{6,7},{7,6},{8,9},{9,8},{10,11... | collective-permute-start | bytes 2543624 | tf_op jit(solution)/shard_map/ppermute | solution.py:25
  639.4 64.2 %collective-permute-start.65 = (bf16[368,1152]{1,0:T(8,128)(2,1)}, bf16[368,1152]{1,0:T(8,128)(2,1)S(1)}, u32[]{:S(2)}, u32[]{:S(2)}) collective-permute-start(bf16[368,1152]{1,0:T(8,128)(2,1)} %get-tuple-element.127), channel_id=1, source_target_pairs={{0,2},{1,3},{2,0},{3,1},{4,6},{5,7},{6,4},{7,5},{8,10},{9,11},{10,... | collective-permute-start | bytes 2543624 | tf_op jit(solution)/shard_map/ppermute | solution.py:30
  640.0 62.0 %collective-permute-start.66 = (bf16[368,1152]{1,0:T(8,128)(2,1)}, bf16[368,1152]{1,0:T(8,128)(2,1)S(1)}, u32[]{:S(2)}, u32[]{:S(2)}) collective-permute-start(bf16[368,1152]{1,0:T(8,128)(2,1)} %get-tuple-element.127), channel_id=1, source_target_pairs={{0,4},{4,0},{1,5},{5,1},{2,6},{6,2},{3,7},{7,3},{8,12},{12,8},{9,1... | collective-permute-start | bytes 2543624 | tf_op jit(solution)/shard_map/ppermute | solution.py:34
  695.7 25.5 %collective-permute-start.49 = (bf16[368,2304]{1,0:T(8,128)(2,1)}, bf16[368,2304]{1,0:T(8,128)(2,1)S(1)}, u32[]{:S(2)}, u32[]{:S(2)}) collective-permute-start(bf16[368,2304]{1,0:T(8,128)(2,1)} %get-tuple-element.107), channel_id=1, source_target_pairs={{0,1},{1,0},{2,3},{3,2},{4,5},{5,4},{6,7},{7,6},{8,9},{9,8},{10,11... | collective-permute-start | bytes 5087240 | tf_op jit(solution)/shard_map/ppermute | solution.py:25
  699.2 45.7 %collective-permute-start.43 = (bf16[184,1152]{1,0:T(8,128)(2,1)}, bf16[184,1152]{1,0:T(8,128)(2,1)}, u32[]{:S(2)}, u32[]{:S(2)}) collective-permute-start(bf16[184,1152]{1,0:T(8,128)(2,1)} %slice.289), channel_id=1, source_target_pairs={{0,2},{1,3},{2,0},{3,1},{4,6},{5,7},{6,4},{7,5},{8,10},{9,11},{10,... | collective-permute-start | bytes 1271816 | tf_op jit(solution)/shard_map/ppermute | solution.py:30
  704.4 35.7 %collective-permute-start.68 = (bf16[176,1152]{1,0:T(8,128)(2,1)}, bf16[176,1152]{1,0:T(8,128)(2,1)}, u32[]{:S(2)}, u32[]{:S(2)}) collective-permute-start(bf16[176,1152]{1,0:T(8,128)(2,1)} %slice.241), channel_id=1, source_target_pairs={{0,4},{4,0},{1,5},{5,1},{2,6},{6,2},{3,7},{7,3},{8,12},{12,8},{9,1... | collective-permute-start | bytes 1216520 | tf_op jit(solution)/shard_map/ppermute | solution.py:34
  738.8 22.5 %collective-permute-start.50 = (bf16[368,1152]{1,0:T(8,128)(2,1)}, bf16[368,1152]{1,0:T(8,128)(2,1)}, u32[]{:S(2)}, u32[]{:S(2)}) collective-permute-start(bf16[368,1152]{1,0:T(8,128)(2,1)} %qkv_back.6), channel_id=1, source_target_pairs={{8,0},{16,8},{24,16},{9,1},{17,9},{25,17},{10,2},{18,10},{26,18},{... | collective-permute-start | bytes 2543624 | tf_op jit(solution)/shard_map/ppermute | solution.py:40
  742.1 64.9 %collective-permute-start.69 = (bf16[1472,1152]{1,0:T(8,128)(2,1)}, bf16[1472,1152]{1,0:T(8,128)(2,1)S(1)}, u32[]{:S(2)}, u32[]{:S(2)}) collective-permute-start(bf16[1472,1152]{1,0:T(8,128)(2,1)} %get-tuple-element.193), channel_id=1, source_target_pairs={{0,1},{1,0},{2,3},{3,2},{4,5},{5,4},{6,7},{7,6},{8,9},{9,8},{10,11... | collective-permute-start | bytes 10174472 | tf_op jit(solution)/shard_map/ppermute | solution.py:25
  744.4 116.5 %collective-permute-start.55 = (bf16[368,576]{1,0:T(8,128)(2,1)}, bf16[368,576]{1,0:T(8,128)(2,1)}, u32[]{:S(2)}, u32[]{:S(2)}) collective-permute-start(bf16[368,576]{1,0:T(8,128)(2,1)} %get-tuple-element.165), channel_id=1, source_target_pairs={{0,1},{1,0},{2,3},{3,2},{4,5},{5,4},{6,7},{7,6},{8,9},{9,8},{10,11... | collective-permute-start | bytes 1271816 | tf_op jit(solution)/shard_map/ppermute | solution.py:25
  802.0 28.2 %collective-permute-start.51 = (bf16[368,2304]{1,0:T(8,128)(2,1)}, bf16[368,2304]{1,0:T(8,128)(2,1)}, u32[]{:S(2)}, u32[]{:S(2)}) collective-permute-start(bf16[368,2304]{1,0:T(8,128)(2,1)} %get-tuple-element.113), channel_id=1, source_target_pairs={{0,1},{1,0},{2,3},{3,2},{4,5},{5,4},{6,7},{7,6},{8,9},{9,8},{10,11... | collective-permute-start | bytes 5087240 | tf_op jit(solution)/shard_map/ppermute | solution.py:25
  806.4 21.7 %collective-permute-start.70 = (bf16[368,1152]{1,0:T(8,128)(2,1)S(1)}, bf16[368,1152]{1,0:T(8,128)(2,1)S(1)}, u32[]{:S(2)}, u32[]{:S(2)}) collective-permute-start(bf16[368,1152]{1,0:T(8,128)(2,1)S(1)} %copy-done.22), channel_id=1, source_target_pairs={{0,2},{1,3},{2,0},{3,1},{4,6},{5,7},{6,4},{7,5},{8,10},{9,11},{10,... | collective-permute-start | bytes 2543624 | tf_op jit(solution)/shard_map/ppermute | solution.py:30
  806.9 21.2 %collective-permute-start.71 = (bf16[368,1152]{1,0:T(8,128)(2,1)S(1)}, bf16[368,1152]{1,0:T(8,128)(2,1)S(1)}, u32[]{:S(2)}, u32[]{:S(2)}) collective-permute-start(bf16[368,1152]{1,0:T(8,128)(2,1)S(1)} %copy-done.22), channel_id=1, source_target_pairs={{0,4},{4,0},{1,5},{5,1},{2,6},{6,2},{3,7},{7,3},{8,12},{12,8},{9,1... | collective-permute-start | bytes 2543624 | tf_op jit(solution)/shard_map/ppermute | solution.py:34
  828.1 32.8 %collective-permute-start.56 = (bf16[368,1152]{1,0:T(8,128)(2,1)S(1)}, bf16[368,1152]{1,0:T(8,128)(2,1)}, u32[]{:S(2)}, u32[]{:S(2)}) collective-permute-start(bf16[368,1152]{1,0:T(8,128)(2,1)S(1)} %copy-done.45), channel_id=1, source_target_pairs={{0,1},{1,0},{2,3},{3,2},{4,5},{5,4},{6,7},{7,6},{8,9},{9,8},{10,11... | collective-permute-start | bytes 2543624 | tf_op jit(solution)/shard_map/ppermute | solution.py:25
  828.1 21.8 %collective-permute-start.72 = (bf16[192,1152]{1,0:T(8,128)(2,1)S(1)}, bf16[192,1152]{1,0:T(8,128)(2,1)S(1)}, u32[]{:S(2)}, u32[]{:S(2)}) collective-permute-start(bf16[192,1152]{1,0:T(8,128)(2,1)S(1)} %slice.242), channel_id=1, source_target_pairs={{0,2},{1,3},{2,0},{3,1},{4,6},{5,7},{6,4},{7,5},{8,10},{9,11},{10,... | collective-permute-start | bytes 1327112 | tf_op jit(solution)/shard_map/ppermute | solution.py:30
  830.3 21.9 %collective-permute-start.73 = (bf16[176,1152]{1,0:T(8,128)(2,1)S(1)}, bf16[176,1152]{1,0:T(8,128)(2,1)S(1)}, u32[]{:S(2)}, u32[]{:S(2)}) collective-permute-start(bf16[176,1152]{1,0:T(8,128)(2,1)S(1)} %slice.243), channel_id=1, source_target_pairs={{0,4},{4,0},{1,5},{5,1},{2,6},{6,2},{3,7},{7,3},{8,12},{12,8},{9,1... | collective-permute-start | bytes 1216520 | tf_op jit(solution)/shard_map/ppermute | solution.py:34
  859.7 71.2 %collective-permute-start.74 = (bf16[1472,1152]{1,0:T(8,128)(2,1)}, bf16[1472,1152]{1,0:T(8,128)(2,1)}, u32[]{:S(2)}, u32[]{:S(2)}) collective-permute-start(bf16[1472,1152]{1,0:T(8,128)(2,1)} %get-tuple-element.191), channel_id=1, source_target_pairs={{0,1},{1,0},{2,3},{3,2},{4,5},{5,4},{6,7},{7,6},{8,9},{9,8},{10,11... | collective-permute-start | bytes 10174472 | tf_op jit(solution)/shard_map/ppermute | solution.py:25
  874.3 36.9 %collective-permute-start.59 = (bf16[576,864]{1,0:T(8,128)(2,1)S(1)}, bf16[576,864]{1,0:T(8,128)(2,1)S(1)}, u32[]{:S(2)}, u32[]{:S(2)}) collective-permute-start(bf16[576,864]{1,0:T(8,128)(2,1)S(1)} %pad_maximum_fusion.2), channel_id=1, source_target_pairs={{0,4},{4,0},{1,5},{5,1},{2,6},{6,2},{3,7},{7,3},{8,12},{12,8},{9,1... | collective-permute-start | bytes 2985992 | tf_op jit(solution)/shard_map/ppermute | solution.py:34
  875.7 36.3 %collective-permute-start.57 = (bf16[576,864]{1,0:T(8,128)(2,1)S(1)}, bf16[576,864]{1,0:T(8,128)(2,1)S(1)}, u32[]{:S(2)}, u32[]{:S(2)}) collective-permute-start(bf16[576,864]{1,0:T(8,128)(2,1)S(1)} %pad_maximum_fusion.1), channel_id=1, source_target_pairs={{0,2},{1,3},{2,0},{3,1},{4,6},{5,7},{6,4},{7,5},{8,10},{9,11},{10,... | collective-permute-start | bytes 2985992 | tf_op jit(solution)/shard_map/ppermute | solution.py:30
  877.4 31.0 %collective-permute-start.61 = (bf16[288,576]{1,0:T(8,128)(2,1)S(1)}, bf16[288,576]{1,0:T(8,128)(2,1)S(1)}, u32[]{:S(2)}, u32[]{:S(2)}) collective-permute-start(bf16[288,576]{1,0:T(8,128)(2,1)S(1)} %pad_maximum_fusion.6), channel_id=1, source_target_pairs={{0,2},{1,3},{2,0},{3,1},{4,6},{5,7},{6,4},{7,5},{8,10},{9,11},{10,... | collective-permute-start | bytes 995336 | tf_op jit(solution)/shard_map/ppermute | solution.py:30
  878.3 31.4 %collective-permute-start.63 = (bf16[288,576]{1,0:T(8,128)(2,1)S(1)}, bf16[288,576]{1,0:T(8,128)(2,1)S(1)}, u32[]{:S(2)}, u32[]{:S(2)}) collective-permute-start(bf16[288,576]{1,0:T(8,128)(2,1)S(1)} %pad_maximum_fusion.7), channel_id=1, source_target_pairs={{0,4},{4,0},{1,5},{5,1},{2,6},{6,2},{3,7},{7,3},{8,12},{12,8},{9,1... | collective-permute-start | bytes 995336 | tf_op jit(solution)/shard_map/ppermute | solution.py:34
  (79 other events, 725.1 us)

commit v2 on v0

v2 whole, which is shorter than its diff:
```python
import jax
import jax.numpy as jnp
from jax import lax
from jax.experimental import pallas as pl
from jax.experimental.pallas import tpu as pltpu
from jax.sharding import PartitionSpec as P

HD = 72
EPS = 1e-06
SCALE = HD ** (-0.5)
LOG2E = 1.4426950408889634
BF = jnp.bfloat16
F32 = jnp.float32
WIN = 256
LANES = 128
COST = 0.1
ROOM = 28
K0 = 0.7978845608028654
K1 = 0.044715
VMEM = pl.BlockSpec(memory_space=pltpu.VMEM)
SMEM = pl.BlockSpec(memory_space=pltpu.SMEM)
ANY = pl.BlockSpec(memory_space=pl.ANY)


def swap_core(a):
    n = lax.axis_size("tensor")
    return lax.ppermute(a, "tensor", [(i, i ^ 1) for i in range(n)])


def swap_x(a):
    n = lax.axis_size("tensor")
    return lax.ppermute(a, "tensor", [(i, i ^ 2) for i in range(n)])


def swap_y(a):
    return lax.ppermute(a, "dp", [(0, 1), (1, 0)])


def swap_both(a):
    n = lax.axis_size("tensor")
    pairs = [(y * n + i, (1 - y) * n + (i ^ 2)) for y in (0, 1) for i in range(n)]
    return lax.ppermute(a, ("dp", "tensor"), pairs)


def shift(a, by):
    n = lax.axis_size("section")
    pairs = [(i, i + by) for i in range(n) if 0 <= i + by < n]
    return lax.ppermute(a, "section", pairs)


def two_rows():
    return lax.axis_size("dp") == 2


def half_cut(rows):
    return (rows // 2 + 15) // 16 * 16


def up32(a):
    return a.astype(F32)


def low16(a):
    return a.astype(BF)


def dot(a, b):
    return jnp.dot(a, b, preferred_element_type=F32)


def dot_t(a, b):
    return lax.dot_general(a, b, (((1,), (1,)), ((), ())), preferred_element_type=F32)


def t_dot(a, b):
    return lax.dot_general(a, b, (((0,), (0,)), ((), ())), preferred_element_type=F32)


def in_hbm(a):
    return pltpu.with_memory_space_constraint(a, pltpu.HBM)


def spans(total, size):
    return [(at, min(size, total - at)) for at in range(0, total, size)]


def norm_parts(values):
    centre = jnp.mean(values, axis=-1, keepdims=True)
    centred = values - centre
    spread = jnp.mean(centred * centred, axis=-1, keepdims=True)
    inverse = lax.rsqrt(spread + EPS)
    return centred * inverse, inverse


def norm_back(grad, unit, inverse, gain):
    e = grad * gain
    return inverse * (e - jnp.mean(e, axis=-1, keepdims=True) - unit * jnp.mean(e * unit, axis=-1, keepdims=True))


def span_copies(pieces, whole, sems, base):
    rows = pieces[0].shape[0]
    return [
        (pltpu.make_async_copy(piece, whole.at[i * rows : (i + 1) * rows], sems.at[base + i]), (i + 1) * rows)
        for i, piece in enumerate(pieces)
    ]


class Arrivals:
    def __init__(self, copies):
        self.left = list(copies)
        self.have = 0

    def start(self):
        for copy, _ in self.left:
            copy.start()

    def need(self, row):
        while self.left and self.have < row:
            copy, self.have = self.left.pop(0)
            copy.wait()

    def rest(self):
        self.need(1 << 30)


def gelu_one(u):
    return u * (0.5 + 0.5 * jnp.tanh(u * (K0 + (K0 * K1) * (u * u))))


def gelu_both(u):
    sq = u * u
    th = jnp.tanh(u * (K0 + (K0 * K1) * sq))
    half = 0.5 + 0.5 * th
    return u * half, half + (0.5 * u) * (1.0 - th * th) * (K0 + (3.0 * K1 * K0) * sq)


def head_window(h, width):
    tile = min(h * HD // LANES, width // LANES - WIN // LANES)
    off = h * HD - tile * LANES
    lane = lax.broadcasted_iota(jnp.int32, (1, WIN), 1)
    return slice(tile * LANES, tile * LANES + WIN), (lane >= off) & (lane < off + HD)


def shape(dims, dtype):
    return jax.ShapeDtypeStruct(dims, dtype)


def past(kernel, inputs, after):
    return lambda *refs: kernel(*refs[:inputs], *refs[inputs + len(after) :])


def call(kernel, name, outs, ins, scratch, args, flops, limit=60, after=()):
    moved = sum(a.size * a.dtype.itemsize for a in args) + sum(o.size * o.dtype.itemsize for o in outs)
    return pl.pallas_call(
        past(kernel, len(args), after),
        out_shape=tuple(outs),
        in_specs=[*ins, *[ANY] * len(after)],
        out_specs=tuple([VMEM] * len(outs)),
        scratch_shapes=scratch,
        compiler_params=pltpu.CompilerParams(vmem_limit_bytes=limit * 2**20),
        cost_estimate=pl.CostEstimate(flops=int(flops * COST), bytes_accessed=int(moved * COST), transcendentals=0),
        name=name,
    )(*args, *after)


def pack(flags, heads, up, down, pair, quarter):
    span, part = heads[0].shape
    units = up.shape[1]
    h = span // 2
    hu = (units + 31) // 32 * 16

    def kernel(flag_ref, *refs):
        pair_ref, out, out_x, mine_ref = refs[6:]
        got = pair_ref.shape[0]
        first = flag_ref[3] == 0
        one, two = pair_ref[:, 0, :], pair_ref[:, 1, :]
        mine_ref[...] = jnp.zeros_like(mine_ref)
        mine_ref[:got] = jnp.where(first, one, two)
        for i, ref in enumerate(refs[:4]):
            out[i * h : (i + 1) * h, :part] = ref[:h, :]
            out[i * h : (i + 1) * h, part:] = ref[h:, :]
        for i, ref in enumerate(refs[4:6]):
            base = 4 * h + i * hu
            rows = low16(up32(ref[...]).T)
            out[base : base + hu, :part] = rows[:hu]
            out[base : base + units - hu, part:] = rows[hu:]
            out[base + units - hu : base + hu, part:] = jnp.zeros((2 * hu - units, part), BF)
        if ride:
            out_x[:total] = out[...]
            out_x[total : total + quarter] = low16(jnp.concatenate((jnp.where(first, two, one), jnp.zeros((spare, width), F32)), axis=0))

    total = 4 * h + 2 * hu
    spare = quarter - pair.shape[0]
    width = pair.shape[2]
    ride = 2 * part == width
    outs = [shape((total, 2 * part), BF), shape((total + quarter if ride else 16, 2 * part), BF), shape((quarter, width), F32)]
    got = call(kernel, "pack", outs, [SMEM] + [VMEM] * 7, [], [flags, *heads, up, down, pair], 0, 30)
    return *got, (0, 4 * h, 4 * h + hu), hu


def put_together(name, pieces, flags, groups, h, after=()):
    count = len(pieces)
    parts = [(i, *p) for i, piece in enumerate(pieces) for p in piece]
    part = parts[0][1].shape[1] // 2
    width = part * count

    def kernel(flag_ref, *refs):
        out, held, sem = refs[len(parts) :]
        copies, at = [], [0] * count
        for j, (ref, (i, _, row, rows)) in enumerate(zip(refs, parts)):
            copies.append(pltpu.make_async_copy(ref.at[row : row + rows], held.at[i, at[i] : at[i] + rows], sem.at[j]))
            at[i] += rows
        for copy in copies:
            copy.start()
        wait_all(copies)
        first = flag_ref[0] == 0
        for i in range(count):
            for g in range(groups):
                rows = slice(g * h, (g + 1) * h)
                piece = jnp.where(first, held[i, rows], held[1 - i, rows]) if count == 2 else held[i, rows]
                out[g, :h, i * part : (i + 1) * part] = piece[:, :part]
                out[g, h:, i * part : (i + 1) * part] = piece[:, part:]

    scratch = [pltpu.VMEM((count, groups * h, 2 * part), BF), pltpu.SemaphoreType.DMA((len(parts),))]
    outs = [shape((groups, 2 * h, width), BF)]
    args = [flags, *[in_hbm(p[1]) for p in parts]]
    return call(kernel, name, outs, [SMEM] + [ANY] * len(parts), scratch, args, 0, 24, after)[0]


def head_copies(pieces, core, kinds, whole, sems, base):
    span, width = pieces[0].shape[1], pieces[0].shape[2]
    out = []
    for n, kind in enumerate(kinds):
        group = []
        for i, piece in enumerate(pieces):
            c = core if i < 2 else 1 - core
            at = pl.multiple_of(n * width + (2 * (i % 2) + c) * span, span)
            sem = sems.at[base + 4 * n + i]
            group.append(pltpu.make_async_copy(piece.at[kind], whole.at[pl.ds(at, span)], sem))
        out.append(group)
    return out


def wait_all(copies):
    for copy in copies:
        copy.wait()


def attend(q, kv, bias, mix, rest, lse_ref):
    rows, width = q.shape
    lane = lax.broadcasted_iota(jnp.int32, (1, LANES), 1)
    for h in range(width // HD):
        win, live = head_window(h, width)
        keys = jnp.where(live, kv[:, win], jnp.zeros((), BF))
        vals = kv[:, width + win.start : width + win.stop]
        s = dot_t(q[:, win], keys) * (SCALE * LOG2E) + bias
        top = jnp.max(s, axis=-1, keepdims=True)
        p = jnp.exp2(s - top)
        total = jnp.sum(p, axis=-1, keepdims=True)
        o = dot(low16(p), vals) * (1.0 / total)
        o_low = low16(o)
        mix[:, win] = jnp.where(live, o_low, mix[:, win])
        if rest is not None:
            rest[:, win] = jnp.where(live, low16(o - up32(o_low)), rest[:, win])
            lse_ref[...] = jnp.where(lane == h, top + jnp.log2(total), lse_ref[...])


def feed_up(normed, pieces, after=()):
    rows, width = normed.shape
    units = sum(piece.shape[0] for piece in pieces)
    n = len(pieces)

    def kernel(nb_ref, *refs):
        act, w, sem = refs[n:]
        arrivals = Arrivals(span_copies(refs[:n], w, sem, 0))
        arrivals.start()
        for at, k in spans(units, 512):
            arrivals.need(at + k)
            act[:, at : at + k] = low16(gelu_one(dot_t(nb_ref[...], w[at : at + k, :])))

    scratch = [pltpu.VMEM((units, width), BF), pltpu.SemaphoreType.DMA((n,))]
    outs = [shape((rows, units), BF)]
    return call(kernel, "feed_up", outs, [VMEM] + [ANY] * n, scratch, [normed, *pieces], 2 * rows * width * units, 30, after)[0]


def feed_down(base, act, pieces, out_type, after=()):
    rows, width = base.shape
    units = act.shape[1]
    n = len(pieces)

    def kernel(base_ref, act_ref, *refs):
        out, w, sem = refs[n:]
        arrivals = Arrivals(span_copies(refs[:n], w, sem, 0))
        arrivals.start()
        arrivals.rest()
        for at, k in spans(width, 256):
            out[:, at : at + k] = (base_ref[:, at : at + k] + dot(act_ref[...], w[:, at : at + k])).astype(out.dtype)

    scratch = [pltpu.VMEM((units, width), BF), pltpu.SemaphoreType.DMA((n,))]
    outs = [shape((rows, width), out_type)]
    args = [base, act, *pieces]
    return call(kernel, "feed_down", outs, [VMEM, VMEM] + [ANY] * n, scratch, args, 2 * rows * width * units, 30, after)[0]


def project(nall, w, q, kv):
    rows, width = q.shape
    for at, n in spans(width, 512):
        q[:, at : at + n] = low16(dot_t(nall[:rows], w[width + at : width + at + n, :]))
    for at, n in spans(2 * width, 512):
        kv[:, at : at + n] = low16(dot_t(nall[...], w[2 * width + at : 2 * width + at + n, :]))


def layer_first(flags, rows32, far, bias, gains, heads):
    rows, width = rows32.shape

    def kernel(flag_ref, bias_ref, gain_ref, x_ref, far_ref, *refs):
        heads_r, hid_ref, nb_ref, w, nall, q, kv, mix, sem = refs[:4], *refs[4:]
        groups = head_copies(heads_r, flag_ref[1], (3, 0, 1, 2), w, sem, 0)
        for group in groups:
            for copy in group:
                copy.start()
        gain_a, gain_b = gain_ref[0:1, :], gain_ref[1:2, :]
        nall[:rows] = low16(norm_parts(x_ref[...])[0] * gain_a)
        nall[rows:] = low16(norm_parts(up32(far_ref[...]))[0] * gain_a)
        for group in groups:
            wait_all(group)
        project(nall, w, q, kv)
        mix[...] = jnp.zeros_like(mix)
        attend(q, kv, bias_ref[0:1, :], mix, None, None)
        hidden = x_ref[...] + dot(mix[...], w[:width, :])
        hid_ref[...] = hidden
        nb_ref[...] = low16(norm_parts(hidden)[0] * gain_b)

    scratch = [
        pltpu.VMEM((4 * width, width), BF),
        pltpu.VMEM((2 * rows, width), BF),
        pltpu.VMEM((rows, width), BF),
        pltpu.VMEM((2 * rows, 2 * width), BF),
        pltpu.VMEM((rows, width), BF),
        pltpu.SemaphoreType.DMA((16,)),
    ]
    outs = [shape((rows, width), F32), shape((rows, width), BF)]
    ins = [SMEM] + [VMEM] * 4 + [ANY] * 4
    flops = 16 * rows * 2 * rows * WIN * 4 + 12 * rows * width * width
    return call(kernel, "layer_first", outs, ins, scratch, [flags, bias, gains, rows32, far, *heads], flops, 44)


def settle(flags, after, heads, ups, downs):
    kinds, span, width = heads[0].shape
    units = 4 * ups[0].shape[0]

    def kernel(flag_ref, *refs):
        wh, wu, wd, token, sem = refs[13:]
        copies = sum(head_copies(refs[:4], flag_ref[1], (3, 0, 1, 2), wh, sem, 0), [])
        copies += [copy for copy, _ in span_copies(refs[4:8], wu, sem, 16) + span_copies(refs[8:12], wd, sem, 20)]
        for copy in copies:
            copy.start()
        token[...] = jnp.zeros_like(token)
        wait_all(copies)

    pieces = [pltpu.with_memory_space_constraint(a, pltpu.HBM) for a in (*heads, *ups, *downs)]
    wh, wu, wd, token = pl.pallas_call(
        kernel,
        out_shape=(
            pltpu.VMEM((kinds * 4 * span, width), BF),
            pltpu.VMEM((units, width), BF),
            pltpu.VMEM((units, width), BF),
            shape((8, LANES), F32),
        ),
        in_specs=[SMEM] + [ANY] * 13,
        out_specs=(ANY, ANY, ANY, VMEM),
        scratch_shapes=[pltpu.SemaphoreType.DMA((24,))],
        compiler_params=pltpu.CompilerParams(vmem_limit_bytes=ROOM * 2**20),
        cost_estimate=pl.CostEstimate(flops=0, bytes_accessed=int(60 * COST * 2**20), transcendentals=0),
        name="settle",
    )(flags, *pieces, after)
    return [pltpu.with_memory_space_constraint(a, pltpu.VMEM) for a in (wh, wu, wd)], token


def feed(normed, hidden, w_up, w_down, act, slope_out, out):
    for at, n in spans(w_up.shape[0], 512):
        u = dot_t(normed, w_up[at : at + n, :])
        if slope_out is None:
            act[:, at : at + n] = low16(gelu_one(u))
        else:
            a, slope = gelu_both(u)
            act[:, at : at + n] = low16(a)
            slope_out[:, at : at + n] = low16(slope)
    for at, n in spans(w_down.shape[1], 256):
        out[:, at : at + n] = (hidden[:, at : at + n] + dot(act[...], w_down[:, at : at + n])).astype(out.dtype)


def layer_mid(flags, own, far, bias, gains, w_heads, w_up, w_down, after=()):
    rows, width = own.shape
    units = w_up.shape[0]

    def kernel(bias_ref, gain_ref, wh, wu, wd, own_ref, far_ref, out_ref, x_ref, q, kv, mix, hid_ref, nall, act):
        gain_a, gain_b = gain_ref[0:1, :], gain_ref[1:2, :]
        x_ref[...] = up32(own_ref[...])
        nall[:rows] = low16(norm_parts(x_ref[...])[0] * gain_a)
        nall[rows:] = low16(norm_parts(up32(far_ref[...]))[0] * gain_a)
        project(nall, wh, q, kv)
        mix[...] = jnp.zeros_like(mix)
        attend(q, kv, bias_ref[0:1, :], mix, None, None)
        hidden = x_ref[...] + dot(mix[...], wh[:width, :])
        hid_ref[...] = hidden
        feed(low16(norm_parts(hidden)[0] * gain_b), hid_ref, wu, wd, act, None, out_ref)

    scratch = [
        pltpu.VMEM((rows, width), F32),
        pltpu.VMEM((rows, width), BF),
        pltpu.VMEM((2 * rows, 2 * width), BF),
        pltpu.VMEM((rows, width), BF),
        pltpu.VMEM((rows, width), F32),
        pltpu.VMEM((2 * rows, width), BF),
        pltpu.VMEM((rows, units), BF),
    ]
    flops = 16 * rows * 2 * rows * WIN * 4 + 12 * rows * width * width + 4 * rows * width * units
    args = [bias, gains, w_heads, w_up, w_down, own, far]
    return call(kernel, "layer_mid", [shape((rows, width), BF)], [VMEM] * 7, scratch, args, flops, ROOM, after)[0]


def last_project(flags, sources, gains, w_heads):
    rows, width = sources[0].shape
    sections = len(sources) // 2

    def kernel(flag_ref, gain_ref, wh, *refs):
        src, refs = refs[: len(sources)], refs[len(sources) :]
        x_ref, na_ref, q, kv, nall, sem = refs

        def load(i, go):
            own, far = src[2 * i], src[2 * i + 1]
            near = pltpu.make_async_copy(own, x_ref if own.dtype == F32 else na_ref, sem.at[0])
            other = pltpu.make_async_copy(far, nall.at[rows:], sem.at[1])
            for copy in (near, other):
                if go:
                    copy.start()
                else:
                    copy.wait()
            if not go and own.dtype != F32:
                x_ref[...] = up32(na_ref[...])

        for go in (True, False):
            for i in range(sections):
                pl.when(flag_ref[2] == i)(lambda i=i, go=go: load(i, go))
        gain_a = gain_ref[0:1, :]
        normed = low16(norm_parts(x_ref[...])[0] * gain_a)
        na_ref[...] = normed
        nall[:rows] = normed
        nall[rows:] = low16(norm_parts(up32(nall[rows:]))[0] * gain_a)
        project(nall, wh, q, kv)

    row32, row16 = shape((rows, width), F32), shape((rows, width), BF)
    outs = [row32, row16, row16, shape((2 * rows, 2 * width), BF)]
    scratch = [pltpu.VMEM((2 * rows, width), BF), pltpu.SemaphoreType.DMA((2,))]
    ins = [SMEM, VMEM, VMEM] + [ANY] * len(sources)
    args = [flags, gains, w_heads, *[in_hbm(a) for a in sources]]
    return call(kernel, "last_project", outs, ins, scratch, args, 10 * rows * width * width, 12)


def last_attention(q, kv, bias, x, gains, w_heads, after=()):
    rows, width = q.shape

    def kernel(q_ref, kv_ref, bias_ref, x_ref, gain_ref, wh, mix, rest_ref, lse_ref, hid_ref, nb_ref):
        mix[...] = jnp.zeros_like(mix)
        lse_ref[...] = jnp.zeros_like(lse_ref)
        rest_ref[...] = jnp.zeros_like(rest_ref)
        attend(q_ref, kv_ref, bias_ref[0:1, :], mix, rest_ref, lse_ref)
        hidden = x_ref[...] + dot(mix[...], wh[:width, :])
        hid_ref[...] = hidden
        nb_ref[...] = low16(norm_parts(hidden)[0] * gain_ref[1:2, :])

    row32, row16 = shape((rows, width), F32), shape((rows, width), BF)
    outs = [row16, row16, shape((rows, LANES), F32), row32, row16]
    flops = 16 * rows * 2 * rows * WIN * 4 + 2 * rows * width * width
    return call(kernel, "last_attention", outs, [VMEM] * 6, [], [q, kv, bias, x, gains, w_heads], flops, 18, after)


def feed_turn(hidden, normed, dy_own, dy_got, gains, w_heads, w_up, w_down):
    rows, width = hidden.shape
    units = w_up.shape[0]

    half = dy_own.shape[0]

    def kernel(hid_ref, nb_ref, own_ref, got_ref, gain_ref, wh, wu, wd, out_ref, slope_ref, hg_ref, do_ref, dy_ref, act, nbg):
        dy_ref[:half] = own_ref[...]
        dy_ref[half:] = up32(got_ref[...])
        feed(nb_ref[...], hid_ref, wu, wd, act, slope_ref, out_ref)
        feed_grads(low16(dy_ref[...]), slope_ref, wu, wd, act, nbg)
        unit, inverse = norm_parts(hid_ref[...])
        hidden_grad = dy_ref[...] + norm_back(nbg[...], unit, inverse, gain_ref[1:2, :])
        hg_ref[...] = hidden_grad
        do_ref[...] = low16(dot_t(low16(hidden_grad), wh[:width, :]))

    row32 = shape((rows, width), F32)
    outs = [row32, shape((rows, units), BF), row32, shape((rows, width), BF), row32]
    scratch = [pltpu.VMEM((rows, units), BF), pltpu.VMEM((rows, width), F32)]
    flops = 8 * rows * width * units
    args = [hidden, normed, dy_own, dy_got, gains, w_heads, w_up, w_down]
    return call(kernel, "feed_turn", outs, [VMEM] * 8, scratch, args, flops, 22)


def feed_grads(low, slope_ref, w_up, w_down, inner, out):
    for at, n in spans(w_up.shape[0], 512):
        inner[:, at : at + n] = low16(dot_t(low, w_down[at : at + n, :]) * up32(slope_ref[:, at : at + n]))
    for at, n in spans(w_up.shape[1], 256):
        out[:, at : at + n] = dot(inner[...], w_up[:, at : at + n])


def feed_back(mode, flags, sources, slope, hidden, gains, w_heads, w_up, w_down, after=()):
    last = mode == "last"
    rows, width = hidden.shape
    units = w_up.shape[0]

    def kernel(flag_ref, gain_ref, hid_ref, slope_ref, wh, wu, wd, *refs):
        src, refs = refs[: len(sources)], refs[len(sources) :]
        hg_ref, do_ref, refs = refs[0], refs[1], refs[2:]
        if last:
            ml_ref, gs_ref, ig, nbg, dy_ref, low, sem = refs

            def load(a, go):
                copy = pltpu.make_async_copy(a, dy_ref if a.dtype == F32 else low, sem.at[0])
                if go:
                    copy.start()
                    return
                copy.wait()
                if a.dtype == F32:
                    low[...] = low16(dy_ref[...])
                else:
                    dy_ref[...] = up32(low[...])

            for go in (True, False):
                for i, a in enumerate(src):
                    pl.when(flag_ref[2] == len(src) - 1 - i)(lambda a=a, go=go: load(a, go))
        else:
            ig, nbg, dy_ref, low = refs
            dy_ref[...] = src[0][...].astype(F32)
            low[...] = low16(src[0][...])
        feed_grads(low[...], slope_ref, wu, wd, ig, nbg)
        unit, inverse = norm_parts(hid_ref[...])
        grad = nbg[...]
        if last:
            gs_ref[...] = jnp.sum(grad * unit, axis=0, keepdims=True)
        hidden_grad = dy_ref[...] + norm_back(grad, unit, inverse, gain_ref[1:2, :])
        hg_ref[...] = hidden_grad
        mix_low = low16(hidden_grad)
        if last:
            ml_ref[...] = mix_low
        do_ref[...] = low16(dot_t(mix_low, wh[:width, :]))

    sources = [in_hbm(a) if last else a for a in sources]
    args = [flags, gains, hidden, slope, w_heads, w_up, w_down, *sources]
    outs = [shape((rows, width), F32), shape((rows, width), BF)]
    if last:
        outs += [shape((rows, width), BF), shape((1, width), F32)]
    scratch = [
        pltpu.VMEM((rows, units), BF),
        pltpu.VMEM((rows, width), F32),
        pltpu.VMEM((rows, width), F32),
        pltpu.VMEM((rows, width), BF),
    ]
    if last:
        scratch.append(pltpu.SemaphoreType.DMA((1,)))
    ins = [SMEM] + [VMEM] * 6 + [ANY if last else VMEM] * len(sources)
    flops = 4 * rows * width * units + 2 * rows * width * width
    return call(kernel, "feed_back_" + mode, outs, ins, scratch, args, flops, 13, after)


def attention_back(q, kv_all, do, mix, mix_rest, lse, bias, after=()):
    rows, width = q.shape
    keys_n = 2 * rows

    def kernel(q_ref, kv, do_ref, o_ref, rest_ref, lse_ref, bias_ref, dq_ref, dkv_own, dkv_far, qt, dt, dkt, dvt):
        bias_row = bias_ref[0:1, :]
        qt[...] = q_ref[...].T
        dt[...] = do_ref[...].T
        dq_ref[...] = jnp.zeros_like(dq_ref)
        zero = jnp.zeros((), BF)
        parts = ([], [])
        for h in range(width // HD):
            win, live = head_window(h, width)
            keys = jnp.where(live, kv[:, win], zero)
            vals = jnp.where(live, kv[:, width + win.start : width + win.stop], zero)
            d_out = do_ref[:, win]
            whole = up32(o_ref[:, win]) + up32(rest_ref[:, win])
            row_dot = jnp.sum(jnp.where(live, up32(d_out) * whole, 0.0), axis=-1, keepdims=True)
            s = dot_t(q_ref[:, win], keys) * (SCALE * LOG2E) + bias_row
            p = jnp.exp2(s - lse_ref[:, h : h + 1])
            ds = low16(p * (dot_t(d_out, vals) - row_dot))
            dq = dot(ds, keys) * SCALE
            dq_ref[:, win] = jnp.where(live, low16(dq), dq_ref[:, win])
            row = h % 2 * HD
            pair = slice((h - h % 2) * HD, (h - h % 2 + 2) * HD)
            parts[0].append(low16(dot(qt[pair, :][row : row + HD], ds) * SCALE))
            parts[1].append(low16(dot(dt[pair, :][row : row + HD], low16(p))))
            if h % 2:
                dkt[pair, :] = jnp.concatenate(parts[0], axis=0)
                dvt[pair, :] = jnp.concatenate(parts[1], axis=0)
                parts = ([], [])
        dk = dkt[...].T
        dv = dvt[...].T
        dkv_own[:, :width] = dk[:rows]
        dkv_own[:, width:] = dv[:rows]
        dkv_far[:, :width] = dk[rows:]
        dkv_far[:, width:] = dv[rows:]

    outs = [shape((rows, width), BF), shape((rows, 2 * width), BF), shape((rows, 2 * width), BF)]
    scratch = [
        pltpu.VMEM((width, rows), BF),
        pltpu.VMEM((width, rows), BF),
        pltpu.VMEM((width, keys_n), BF),
        pltpu.VMEM((width, keys_n), BF),
    ]
    flops = 16 * rows * keys_n * WIN * 10
    return call(kernel, "attention_back", outs, [VMEM] * 7, scratch, [q, kv_all, do, mix, mix_rest, lse, bias], flops, 17, after)


def qkv_back(full, flags, dq, own, got, x, hidden_grad, gains, w_heads, after=()):
    rows, width = dq.shape
    span = width // 4

    def kernel(flag_ref, gain_ref, dq_ref, own_ref, got_ref, x_ref, hg_ref, w, *refs):
        if full:
            dx_ref, low_ref, keep_ref, give_ref, gs_ref, grads, nag = refs
        else:
            low_ref, grads, nag = refs
        grads[:, :width] = dq_ref[...]
        grads[:, width:] = low16(up32(own_ref[...]) + up32(got_ref[...]))
        if full:
            mine = flag_ref[1] == 0
            for i in range(3):
                for xr in (0, 1):
                    at = i * width + 2 * xr * span
                    lo = grads[:, at : at + span]
                    hi = grads[:, at + span : at + 2 * span]
                    to = xr * 3 * span + i * span
                    keep_ref[:, to : to + span] = jnp.where(mine, lo, hi)
                    give_ref[:, to : to + span] = jnp.where(mine, hi, lo)
        for at, n in spans(width, 256):
            nag[:, at : at + n] = dot(grads[...], w[width:, at : at + n])
        unit, inverse = norm_parts(x_ref[...])
        grad = nag[...]
        if full:
            gs_ref[...] = jnp.sum(grad * unit, axis=0, keepdims=True)
        dx = hg_ref[...] + norm_back(grad, unit, inverse, gain_ref[0:1, :])
        low_ref[...] = low16(dx)
        if full:
            dx_ref[...] = dx

    outs = [shape((rows, width), BF)]
    if full:
        outs = [shape((rows, width), F32)] + outs
        outs += [shape((rows, 6 * span), BF), shape((rows, 6 * span), BF), shape((1, width), F32)]
    scratch = [pltpu.VMEM((rows, 3 * width), BF), pltpu.VMEM((rows, width), F32)]
    args = [flags, gains, dq, own, got, x, hidden_grad, w_heads]
    return call(kernel, "qkv_back", outs, [SMEM] + [VMEM] * 7, scratch, args, 6 * rows * width * width, 11, after)


def halves_of(total):
    steps = max(1, total // 736)
    return steps, total // steps


def halves_specs(steps, block, cols):
    return [
        pl.BlockSpec((block, cols), lambda i: (jnp.minimum(i, steps - 1), 0)),
        pl.BlockSpec((block, cols), lambda i: (jnp.maximum(i, steps) - steps, 0)),
    ]


def unit_forward(normed_four, normed_far, w_up, after=()):
    total, width = normed_four.shape
    n = w_up.shape[0]
    half, block = halves_of(total)

    def kernel(a_ref, b_ref, wu_ref, act_ref, slope_ref):
        nb = jnp.where(pl.program_id(0) < half, a_ref[...], b_ref[...])
        for at, k in spans(n, 512):
            act, slope = gelu_both(dot_t(nb, wu_ref[at : at + k, :]))
            act_ref[:, at : at + k] = low16(act)
            slope_ref[:, at : at + k] = low16(slope)

    by_rows = pl.BlockSpec((block, n), lambda i: (i, 0))
    return pl.pallas_call(
        past(kernel, 3, after),
        grid=(2 * half,),
        in_specs=[*halves_specs(half, block, width), VMEM, *[ANY] * len(after)],
        out_specs=(by_rows, by_rows),
        out_shape=(shape((2 * total, n), BF), shape((2 * total, n), BF)),
        compiler_params=pltpu.CompilerParams(vmem_limit_bytes=26 * 2**20),
        cost_estimate=pl.CostEstimate(flops=int(5.6 * COST * total * width * n), bytes_accessed=int(12 * COST * total * width), transcendentals=0),
        name="unit_forward",
    )(normed_four, normed_far, w_up, *after)


def pick_cols(a, which, part):
    picked = a[:, :part]
    for i in range(1, a.shape[1] // part):
        picked = jnp.where(which == i, a[:, i * part : (i + 1) * part], picked)
    return picked


def up_grads(normed_four, normed_far, dy_four, dy_far, slope_all, w_down, flags, units, part, after=()):
    total, width = normed_four.shape
    n = w_down.shape[0]
    half, block = halves_of(total)

    def kernel(flag_ref, na_ref, nb_ref, da_ref, db_ref, slope_ref, wd_ref, gu_ref):
        step = pl.program_id(0)
        dy = jnp.where(step < half, da_ref[...], db_ref[...])
        turned = pick_cols(jnp.where(step < half, na_ref[...], nb_ref[...]), flag_ref[0], part).T

        @pl.when(step == 0)
        def _():
            gu_ref[...] = jnp.zeros_like(gu_ref)

        for at, k in spans(n, 512):
            inner = low16(dot_t(dy, wd_ref[at : at + k, :]) * up32(slope_ref[:, at : at + k]))
            real = min(k, units - at)
            gu_ref[:, at : at + real] += dot(turned, inner)[:, :real]

    by_rows = pl.BlockSpec((block, n), lambda i: (i, 0))
    return pl.pallas_call(
        past(kernel, 7, after),
        grid=(2 * half,),
        in_specs=[
            SMEM, *halves_specs(half, block, width), *halves_specs(half, block, width), by_rows, VMEM, *[ANY] * len(after)
        ],
        out_specs=VMEM,
        out_shape=shape((part, units), F32),
        compiler_params=pltpu.CompilerParams(vmem_limit_bytes=48 * 2**20),
        cost_estimate=pl.CostEstimate(flops=int(8.4 * COST * total * width * n), bytes_accessed=int(12 * COST * total * width), transcendentals=0),
        name="up_grads",
    )(flags, normed_four, normed_far, dy_four, dy_far, slope_all, w_down, *after)


def down_grads(dy_four, dy_far, act_all, flags, units, part, after=()):
    total, width = dy_four.shape
    n = act_all.shape[1]
    half, block = halves_of(total)

    def kernel(flag_ref, da_ref, db_ref, act_ref, gdt):
        step = pl.program_id(0)
        turned = pick_cols(jnp.where(step < half, da_ref[...], db_ref[...]), flag_ref[0], part).T

        @pl.when(step == 0)
        def _():
            gdt[...] = jnp.zeros_like(gdt)

        for at, k in spans(n, 512):
            real = min(k, units - at)
            gdt[:, at : at + real] += dot(turned, act_ref[:, at : at + k])[:, :real]

    return pl.pallas_call(
        past(kernel, 4, after),
        grid=(2 * half,),
        in_specs=[
            SMEM, *halves_specs(half, block, width), pl.BlockSpec((block, n), lambda i: (i, 0)), *[ANY] * len(after)
        ],
        out_specs=VMEM,
        out_shape=shape((part, units), F32),
        compiler_params=pltpu.CompilerParams(vmem_limit_bytes=44 * 2**20),
        cost_estimate=pl.CostEstimate(flops=int(4.2 * COST * total * width * n), bytes_accessed=int(8 * COST * total * width), transcendentals=0),
        name="down_grads",
    )(flags, dy_four, dy_far, act_all, *after)


def join(name, pieces, after=()):
    n = len(pieces)

    def kernel(*refs):
        out, at = refs[n], 0
        for ref in refs[:n]:
            out[at : at + ref.shape[0]] = ref[...]
            at += ref.shape[0]

    rows = sum(a.shape[0] for a in pieces)
    return call(kernel, name, [shape((rows, pieces[0].shape[1]), BF)], [VMEM] * n, [], list(pieces), 0, 16, after)[0]


def plane_blocks(name, flags, left, right, after=()):
    rows = left[0].shape[0]
    part = right[0].shape[1] // 2
    span = left[0].shape[1] // 2
    h = span // 2
    cut = half_cut(h)

    def kernel(flag_ref, l0, l1, r0, r1, *refs):
        outs, ls, rs = refs[:5], refs[5], refs[6]
        for a, b, c in ((l0, l1, ls), (r0, r1, rs)):
            c[:rows] = a[...]
            c[rows:] = b[...]
        first = flag_ref[0] == 0
        lo, hi = rs[:, :part], rs[:, part:]
        shares = (jnp.where(first, lo, hi), jnp.where(first, hi, lo))
        for yr in (0, 1):
            for xr in (0, 1):
                got = t_dot(ls[:, xr * span : (xr + 1) * span], shares[yr])
                if yr == 0 and xr == 0:
                    outs[0][...] = got
                    continue
                for side in (0, 1):
                    cols = slice(side * part, (side + 1) * part)
                    top, bottom = low16(got[side * h : side * h + cut]), low16(got[side * h + cut : (side + 1) * h])
                    if xr and yr:
                        outs[1][cut:, cols] = top
                        outs[2][h - cut :, cols] = bottom
                    elif xr:
                        outs[1][:cut, cols] = top
                        outs[3][:, cols] = bottom
                    else:
                        outs[2][: h - cut, cols] = bottom
                        outs[4][:, cols] = top

    outs = [shape((span, part), F32)]
    outs += [shape((n, 2 * part), BF) for n in (2 * cut, 2 * (h - cut), h - cut, cut)]
    scratch = [pltpu.VMEM((2 * rows, 2 * span), BF), pltpu.VMEM((2 * rows, 2 * part), BF)]
    args = [flags, *left, *right]
    flops = 16 * rows * span * part
    return call(kernel, name, outs, [SMEM] + [VMEM] * 4, scratch, args, flops, 40, after)


def scatter_middle(name, beside, above, via_x, via_y, after=()):
    rest, double = beside.shape
    cut = above.shape[0]

    def kernel(beside_ref, above_ref, vx, vy, to_y, to_x):
        to_y[...] = low16(up32(above_ref[...]) + up32(vx[cut:, :]))
        to_x[...] = low16(up32(beside_ref[...]) + up32(vy[rest:, :]))

    outs = [shape((cut, double), BF), shape((rest, double), BF)]
    to_y, to_x = call(kernel, name, outs, [VMEM] * 4, [], [beside, above, via_x, via_y], 0, 16, after)
    return swap_y(to_y), swap_x(to_x)


def scatter_end(name, own, via_x, via_y, over_y, over_x, count, after=()):
    span, part = own.shape
    h = span // 2
    cut = half_cut(h)
    rest = h - cut
    each = span // count

    def kernel(own_ref, vx, vy, oy, ox, *refs):
        outs, total = refs[:count], refs[count]
        for side in (0, 1):
            cols = slice(side * part, (side + 1) * part)
            base = side * h
            total[base : base + cut] = own_ref[base : base + cut, :] + up32(vx[:cut, cols]) + up32(oy[:, cols])
            total[base + cut : base + h] = own_ref[base + cut : base + h, :] + up32(vy[:rest, cols]) + up32(ox[:, cols])
        for i, out in enumerate(outs):
            out[...] = total[i * each : (i + 1) * each]

    outs = [shape((each, part), F32)] * count
    scratch = [pltpu.VMEM((span, part), F32)]
    return call(kernel, name, outs, [VMEM] * 5, scratch, [own, via_x, via_y, over_y, over_x], 0, 24, after)


def gather_gains(shard, moves, dp_idx, x_idx, core):
    if not two_rows():
        return lax.all_gather(shard, ("dp", "tensor"), axis=1, tiled=True)
    beside, above, across = moves

    def pair(index, a, b):
        return jnp.where(index == 0, jnp.concatenate((a, b), axis=1), jnp.concatenate((b, a), axis=1))

    four = jnp.concatenate((shard, beside, above, across), axis=1)
    other = swap_core(four)
    n = shard.shape[1]
    by_core = [pair(core, four[:, i * n : (i + 1) * n], other[:, i * n : (i + 1) * n]) for i in range(4)]
    return pair(dp_idx, pair(x_idx, *by_core[:2]), pair(x_idx, *by_core[2:]))


def ties(*arrays):
    return list(lax.optimization_barrier(arrays))


def tie(a, *others):
    return ties(a, *others)[0]


def local(images, valid_len, query_weight, key_weight, value_weight, output_weight, up_weight, down_weight, norm_gains, cotangent):
    section = lax.axis_index("section")
    sections = lax.axis_size("section")
    dp_idx = lax.axis_index("dp")
    dp = lax.axis_size("dp")
    tensor_idx = lax.axis_index("tensor")
    x_idx, core = tensor_idx // 2, tensor_idx % 2
    per_dp, quarter, width = images.shape
    assert per_dp == 2 and lax.axis_size("tensor") == 4
    padded_quarter = (quarter + 7) // 8 * 8
    flags = jnp.stack((dp_idx, core, section, x_idx)).astype(jnp.int32)

    def pad_rows(a):
        return jnp.pad(a, ((0, padded_quarter - quarter), (0, 0)))

    def mine(a):
        return pad_rows(lax.dynamic_index_in_dim(a, x_idx, 0, keepdims=False))

    def theirs(a):
        return pad_rows(low16(lax.dynamic_index_in_dim(a, 1 - x_idx, 0, keepdims=False)))

    def give_back(rows):
        return swap_x(low16(rows[padded_quarter:]))

    def both_images(rows, got, after=()):
        def kernel(flag_ref, own_ref, got_ref, out):
            first = flag_ref[3] == 0
            own, other = own_ref[:quarter], up32(got_ref[...])[:quarter]
            out[:, 0, :] = jnp.where(first, own, other)
            out[:, 1, :] = jnp.where(first, other, own)

        outs = [shape((quarter, 2, width), F32)]
        pair = call(kernel, "both_images", outs, [SMEM, VMEM, VMEM], [], [flags, rows, got], 0, 16, after)[0]
        return pair

    rows = 2 * padded_quarter
    valid = lax.dynamic_index_in_dim(valid_len, x_idx, 0, keepdims=False)
    spot = jnp.arange(padded_quarter)
    live = [
        (spot < quarter) & ((2 * xx + cc) * quarter + spot < valid) for cc in (core, 1 - core) for xx in (x_idx, 1 - x_idx)
    ]
    bias = jnp.where(jnp.concatenate(live), 0.0, -1e30).astype(F32)[None, :]
    bias = jnp.broadcast_to(bias, (8, bias.shape[1]))

    span = query_weight.shape[2]
    units = up_weight.shape[2]
    part = width // dp
    plane = two_rows()

    gain_moves = [move(norm_gains[0]) for move in (swap_x, swap_y, swap_both)] if plane else []
    turned = [jnp.transpose(w[0]) for w in (query_weight, key_weight, value_weight)]
    packed, packed_x, keep_rows, (at_heads, at_up, at_down), h_units = pack(
        flags, [*turned, output_weight[0]], up_weight[0], jnp.transpose(down_weight[0]), jnp.transpose(images, (1, 0, 2)),
        padded_quarter,
    )
    h_heads = span // 2
    if plane:
        from_x, from_y = swap_x(packed_x), swap_y(packed)
        img_got = from_x[-padded_quarter:]
        at = 2 * h_heads
        over_heads = [(swap_x(from_y[:at]), 0, at), (swap_y(from_x[at:at_up]), 0, at)]
        over_up = [(swap_x(from_y[at_up:at_down]), 0, h_units)]
        over_down = [(swap_y(from_x[at_down : at_down + h_units]), 0, h_units)]
        near = lambda row, rows: [[(packed, row, rows)], [(from_y, row, rows)]]
        far = lambda row, rows, over: [[(from_x, row, rows)], over]
    else:
        whole = lax.all_gather(packed, "dp")
        other = swap_x(whole)
        over_heads = over_up = over_down = None
        img_got = swap_x(theirs(images))
        near = lambda row, rows: [[(whole[i], row, rows)] for i in range(dp)]
        far = lambda row, rows, over: [[(other[i], row, rows)] for i in range(dp)]
    gains = gather_gains(norm_gains[0], gain_moves, dp_idx, x_idx, core)
    first_rows = jnp.concatenate((keep_rows, up32(img_got)), axis=0)
    first_far = swap_core(low16(first_rows))
    heads_near = put_together("heads_near", near(at_heads, 4 * h_heads), flags, 4, h_heads)
    up_near = put_together("up_near", near(at_up, h_units), flags, 1, h_units, [heads_near])[0]
    down_near = put_together("down_near", near(at_down, h_units), flags, 1, h_units, [heads_near])[0]
    heads_far = put_together("heads_far", far(at_heads, 4 * h_heads, over_heads), flags, 4, h_heads, [up_near, down_near, first_rows])
    heads = [heads_near, heads_far, swap_core(heads_near), swap_core(heads_far)]
    hidden, normed_b = layer_first(flags, first_rows, first_far, bias, gains, heads)
    up_near = [up_near, swap_core(up_near)]
    down_near = [down_near, swap_core(down_near)]
    act_near = feed_up(normed_b, up_near)
    half_out = feed_down(hidden, act_near, down_near, F32)
    up_far = put_together("up_far", far(at_up, h_units, over_up), flags, 1, h_units, [normed_b])[0]
    up_far = [up_far, swap_core(up_far)]
    down_far = put_together("down_far", far(at_down, h_units, over_down), flags, 1, h_units, [normed_b])[0]
    down_far = [down_far, swap_core(down_far)]
    act_far = feed_up(normed_b, up_far)
    out = feed_down(half_out, act_far, down_far, BF)

    def fetch(after):
        return settle(flags, after, heads, up_near + up_far, down_near + down_far)

    sources = [first_rows, first_far]
    for tick in range(1, sections):
        got = shift(out, 1)
        if tick == 1:
            weights, token = fetch(out)
            got, token = ties(got, token)
        sources += [got, swap_core(got)]
        if tick + 1 < sections:
            out = layer_mid(flags, *sources[-2:], bias, gains, *weights, [token] if tick == 1 else [])
            if tick == 1:
                cot_got = swap_x(theirs(cotangent))
    x, normed_a, q, kv = last_project(flags, sources, gains, weights[0])
    mix, mix_rest, lse, hidden, normed_b = last_attention(q, kv, bias, x, gains, weights[0])
    out, slope, hidden_grad, do, dy = feed_turn(hidden, normed_b, mine(cotangent), cot_got, gains, *weights)

    sources = [dy]
    acts_got = give_back(out)

    def core_halves(a):
        lo = jnp.concatenate((a[:, :span], a[:, 2 * span : 3 * span]), axis=1)
        hi = jnp.concatenate((a[:, span : 2 * span], a[:, 3 * span :]), axis=1)
        return jnp.where(core == 0, lo, hi), jnp.where(core == 0, hi, lo)

    at = half_cut(rows)

    at = half_cut(rows)
    for tick in range(sections):
        last = tick + 1 == sections
        if last:
            dy_low = low16(sources[0])
            for i, a in enumerate(sources[1:]):
                dy_low = jnp.where(section == sections - 2 - i, a, dy_low)
            if plane:
                dy_x0, dy_y1 = swap_x(dy_low[:at]), swap_y(dy_low[at:])
        if tick:
            mode = "last" if last else "mid"
            used, after = (sources, [act_all]) if last else (sources[-1:], [acts] if tick == 2 else [])
            results = feed_back(mode, flags, used, slope, hidden, gains, *weights, after)
            hidden_grad, do = results[:2]
        if last:
            mix_low, gain_sum_b = results[2:]
            mix_got, ml_far = swap_core(mix_give), swap_core(mix_low)
        after = []
        if plane and tick == 2:
            after = [nb_d0, nb_d1]
        if plane and last:
            dy_d0, dy_d1 = swap_y(dy_x0), swap_x(dy_y1)
            after = [dy_x0, dy_y1]
        dq, dkv, dkv_far = attention_back(q, kv, do, mix, mix_rest, lse, bias, after)
        dkv_got = swap_core(dkv_far)
        after = []
        if plane and last:
            o_parts = plane_blocks("output_grads", flags, (mix_keep, mix_got), (mix_low, ml_far), [dq])
            dy_rest = tie(dy_low, o_parts[0])
            dy_x1, dy_y0 = swap_x(dy_rest[at:]), swap_y(dy_rest[:at])
            after = [o_parts[0]]
        back = qkv_back(last, flags, dq, dkv, dkv_got, x, hidden_grad, gains, weights[0], after)
        if last:
            break
        got = shift(back[0], -1)
        if tick == 0:
            nb_x, nb_y = (swap_x(normed_b), swap_y(normed_b)) if plane else (normed_b, normed_b)
        elif tick == 1:
            if plane:
                nb_d0, nb_d1 = swap_x(nb_y[:at]), swap_y(nb_x[at:])
            acts = both_images(out, acts_got)
            mix_keep, mix_give = core_halves(mix)
            na_far = swap_core(normed_a)
        elif tick == 2:
            if plane:
                pieces = [normed_b, nb_x[:at], nb_x[at:], nb_y[:at], nb_y[at:], nb_d0, nb_d1]
                nb_four = join("join_normed", pieces, [back[0]])
                nb_far = swap_core(nb_four)
            else:
                nb_all = lax.all_gather(normed_b, ("dp", "tensor"), axis=0, tiled=True)
                nb_four, nb_far = jnp.split(nb_all, 2)
            act_all, slope_all = unit_forward(nb_four, nb_far, up_near[0], [mix_keep, mix_give, na_far])
            got, act_all = ties(got, act_all)
        sources.append(got)
    dx, _, keep, give, gain_sum_a = back

    got = swap_core(give)
    grads_got = give_back(dx)
    gain_sums = jnp.concatenate((gain_sum_a, gain_sum_b), axis=0)
    if plane:
        gain_moves = [move(gain_sums) for move in (swap_x, swap_y, swap_both)]
        o_via = swap_x(o_parts[1]), swap_y(o_parts[2])
        qkv_parts = plane_blocks("qkv_grads", flags, (keep, got), (normed_a, na_far))
        via = swap_x(qkv_parts[1]), swap_y(qkv_parts[2])
        dy_four = join("join_dy", [dy_low, dy_x0, dy_x1, dy_y0, dy_y1, dy_d0, dy_d1], [qkv_parts[0]])
        dy_far = swap_core(dy_four)
        grad_up = up_grads(nb_four, nb_far, dy_four, dy_far, slope_all, down_near[0], flags, units, part, [qkv_parts[0]])
        o_over = scatter_middle("output_middle", *o_parts[3:], *o_via, [grad_up])
        over = scatter_middle("qkv_middle", *qkv_parts[3:], *via, [grad_up])
        grad_down = down_grads(dy_four, dy_far, act_all, flags, units, part, [grad_up, *gain_moves])
        gain_sums = gain_sums + gain_moves[0] + gain_moves[1] + gain_moves[2]
        gain_sums = gain_sums + swap_core(gain_sums)
        (grad_o,) = scatter_end("output_end", o_parts[0], *o_via, *o_over, 1, [grad_down])
        grad_heads = scatter_end("qkv_end", qkv_parts[0], *via, *over, 3, [grad_down])
        gain_shard = lax.dynamic_slice_in_dim(gain_sums, (dp_idx * 4 + tensor_idx) * (width // 8), width // 8, 1)
    else:
        dy_all = lax.all_gather(dy_low, ("dp", "tensor"), axis=0, tiled=True)
        dy_four, dy_far = jnp.split(dy_all, 2)
        grad_up = up_grads(nb_four, nb_far, dy_four, dy_far, slope_all, down_near[0], flags, units, part)
        grad_down = down_grads(dy_four, dy_far, act_all, flags, units, part)
        both = lambda a, b: jnp.concatenate((a, b), axis=0)
        g = t_dot(both(keep, got), both(normed_a, na_far))
        g = g[: 3 * span] + up32(swap_x(low16(g[3 * span :])))
        g = up32(lax.psum_scatter(low16(g), "dp", scatter_dimension=1, tiled=True))
        grad_heads = [g[i * span : (i + 1) * span] for i in range(3)]
        g = t_dot(both(mix_keep, swap_core(mix_give)), both(mix_low, swap_core(mix_low)))
        g = g[:span] + up32(swap_x(low16(g[span:])))
        grad_o = up32(lax.psum_scatter(low16(g), "dp", scatter_dimension=1, tiled=True))
        gain_shard = lax.psum_scatter(gain_sums, ("dp", "tensor"), scatter_dimension=1, tiled=True)
    grads = both_images(dx, grads_got)

    return (
        jnp.transpose(acts, (1, 0, 2))[None],
        jnp.transpose(grads, (1, 0, 2))[None],
        *[jnp.transpose(g)[None] for g in grad_heads],
        grad_o[None],
        grad_up[None],
        jnp.transpose(grad_down)[None],
        gain_shard[None],
    )


def solution(mesh):
    return jax.shard_map(
        local,
        mesh=mesh,
        in_specs=(
            P("dp", "tensor", None),
            P("dp"),
            P("section", "dp", "tensor"),
            P("section", "dp", "tensor"),
            P("section", "dp", "tensor"),
            P("section", "tensor", "dp"),
            P("section", "dp", "tensor"),
            P("section", "tensor", "dp"),
            P("section", None, ("dp", "tensor")),
            P("dp", "tensor", None),
        ),
        out_specs=(
            P("section", "dp", "tensor", None),
            P("section", "dp", "tensor", None),
            P("section", "dp", "tensor"),
            P("section", "dp", "tensor"),
            P("section", "dp", "tensor"),
            P("section", "tensor", "dp"),
            P("section", "dp", "tensor"),
            P("section", "tensor", "dp"),
            P("section", None, ("dp", "tensor")),
        ),
        check_vma=False,
    )
```

time: 2010 us -> 742 us (0.37)
  waiting for transfers between devices: 714 us -> 218 us
  matrix products: 391 us -> 0 us
  Pallas kernels: 0 us -> 363 us
  blocking collectives: 347 us -> 0 us
  local copies, waits for them, and re-layouts: 331 us -> 80.8 us
  other arithmetic: 143 us -> 6.7 us
    dot_general x79 -> x0, matrix products: 391 us -> none  [the longest x5 52.4 us: backward_pass(): jnp.einsum('bsd,fd->bsf', down_low, w_lower, preferred_element_type=jnp.f...]
    pallas_call x0 -> x42, Pallas kernels: none -> 363 us  [the longest x38 297 us: call(): pl.pallas_call(past(kernel, len(args), after), out_shape=tuple(outs), in_...]
    unnamed x39 -> x0, waiting for transfers between devices: 290 us -> none
    all_gather x15 -> x0, waiting for transfers between devices: 278 us -> none  [the longest x6 109 us: widen(): return lax.all_gather(token_rows, 'tensor', axis=1, tiled=True)]
    unnamed x10 -> x0, blocking collectives: 222 us -> none
    ppermute x8 -> x61, waiting for transfers between devices: 79.9 us -> 218 us  [the longest x14 99.7 us: swap_y(): return lax.ppermute(a, 'dp', [(0, 1), (1, 0)])]
    all_gather x5 -> x0, blocking collectives: 125 us -> none  [the longest x1 29.3 us: local(): lax.all_gather(key_weight[0], 'dp', axis=0, tiled=True)]
    reduce_scatter x2 -> x0, waiting for transfers between devices: 65.9 us -> none  [the longest x1 65.9 us: local(): lax.psum_scatter(grad_lower.astype(jnp.bfloat16), 'dp', scatter_dimension...]
  transfers between devices with their start and end apart: 41 -> 61, of which waited for: 30 -> 25; matrix products, arithmetic and copies ran while one was open for 26% -> 2% of each run, Pallas kernels for 0% -> 26%
where the time goes in v2:
time: 742 us; the launch traced here: 732 us
  Pallas kernels  363 us (49%)
  waiting for transfers between devices  218 us (29%)
  local copies, waits for them, and re-layouts  80.8 us (11%)
  starting transfers between devices  60.6 us (8%)
    pallas_call x38, Pallas kernels, call(): pl.pallas_call(past(kernel, len(args), after), out_shape=tuple(outs), in_...  297 us
    ppermute x14, waiting for transfers between devices, swap_y(): return lax.ppermute(a, 'dp', [(0, 1), (1, 0)])  99.7 us
    unnamed x310, local copies, waits for them, and re-layouts  69.7 us
    ppermute x6, waiting for transfers between devices, shift(): return lax.ppermute(a, 'section', pairs)  64.9 us
    ppermute x17, waiting for transfers between devices, swap_x(): return lax.ppermute(a, 'tensor', [(i, i ^ 2) for i in range(n)])  31.2 us
    pallas_call x1, Pallas kernels, up_grads(): pl.pallas_call(past(kernel, 7, after), grid=(2 * half,), in_specs=[SMEM,...  26.9 us
    ppermute x22, waiting for transfers between devices, swap_core(): return lax.ppermute(a, 'tensor', [(i, i ^ 1) for i in range(n)])  22.4 us
    ppermute x17, starting transfers between devices, swap_x(): return lax.ppermute(a, 'tensor', [(i, i ^ 2) for i in range(n)])  20.1 us
  transfers between devices with their start and end apart: 61, of which 25 were waited for; matrix products, arithmetic and copies ran while one was open for 2% of the time, Pallas kernels for 26%

profile of v2, /device:TPU:0, one launch (start us, length us, event | category | flops | bytes accessed | tf_op | source)
XLA Modules:
  0.0 732.1 jit_solution(1986092515414111285)
XLA Ops:
  16.7 82.9 %collective-permute-done.4.refs_2_ = bf16[1664,1152]{1,0:T(8,128)(2,1)} collective-permute-done((bf16[1664,1152]{1,0:T(8,128)(2,1)S(1)}, bf16[1664,1152]{1,0:T(8,128)(2,1)}, u32[]{:S(2)}, u32[]{:S(2)}) %collective-permute-start.4) | collective-permute-done | bytes 3833888 | tf_op jit(solution)/shard_map/ppermute | solution.py:36
  101.1 4.4 heads_near.1.refs_3_.refs_5_.refs_0_
  114.7 6.6 collective-permute-done.6.refs_2_
  121.3 7.8 %collective-permute-done.7.refs_3_ = bf16[288,1152]{1,0:T(8,128)(2,1)S(1)} collective-permute-done((bf16[288,1152]{1,0:T(8,128)(2,1)S(1)}, bf16[288,1152]{1,0:T(8,128)(2,1)S(1)}, u32[]{:S(2)}, u32[]{:S(2)}) %collective-permute-start.7) | collective-permute-done | bytes 663584 | tf_op jit(solution)/shard_map/ppermute | solution.py:36
  129.9 4.3 heads_far.1.refs_6_.refs_1_
  149.6 19.4 %layer_first.1 = (f32[368,1152]{1,0:T(8,128)S(1)}, bf16[368,1152]{1,0:T(8,128)(2,1)S(1)}) custom-call(s32[4]{0:T(128)S(1)} %pad_add_fusion.refs_0_.flag_ref, f32[8,736]{1,0:T(8,128)S(1)} %broadcast_in_dim.43.refs_1_.refs_0_.refs_2_.refs_6_, f32[2,1152]{1,0:T(2,128)S(1)} %maximum_select_fusion.refs_2_.refs_1_.refs_4_, ...), custom_call_target="tpu_custom_call" | custom-call | flops 1029806464 | bytes 1573684 | tf_op jit(solution)/shard_map/layer_first/pallas_call | solution.py:154
  181.2 4.0 feed_up.2.refs_1_
  185.2 4.5 feed_down.2.refs_0_
  189.7 3.9 feed_up.3.refs_1_
  196.8 3.9 collective-permute-start.17
  200.7 11.4 %settle.1 = (bf16[4608,1152]{1,0:T(8,128)(2,1)S(1)}, bf16[4352,1152]{1,0:T(8,128)(2,1)S(1)}, bf16[4352,1152]{1,0:T(8,128)(2,1)S(1)}, f32[8,128]{1,0:T(8,128)}) custom-call(s32[4]{0:T(128)} %copy-done.115, bf16[4,288,1152]{2,1,0:T(8,128)(2,1)} %heads_near.1.refs_3_.refs_5_.refs_0_, bf16[4,288,1152]{2,1,0:T(8,128)(2,1)} %heads_far.1.refs_6_.refs_1_, ...), custom_call_target="tpu_custom_call" | custom-call | bytes 6291456 | tf_op jit(solution)/shard_map/settle/pallas_call | solution.py:362
  212.1 6.6 collective-permute-done.17.refs_5_
  222.8 25.5 %layer_mid.2 = bf16[368,1152]{1,0:T(8,128)(2,1)} custom-call(f32[8,736]{1,0:T(8,128)} %copy-done.79, f32[2,1152]{1,0:T(2,128)} %copy-done.84, bf16[4608,1152]{1,0:T(8,128)(2,1)S(1)} %get-tuple-element.85.refs_2_.refs_5_.refs_7_.refs_4_, bf16[4352,1152]{1,0:T(8,128)(2,1)S(1)} %get-tuple-element.88.refs_3_.refs_6_.refs_5_, ...), custom_call_target="tpu_custom_call" | custom-call | flops 1767794304 | bytes 3324723 | tf_op jit(solution)/shard_map/layer_mid/pallas_call | solution.py:154
  248.2 3.9 collective-permute-start.19
  252.1 18.5 %collective-permute-done.19.refs_5_.refs_7_ = bf16[368,1152]{1,0:T(8,128)(2,1)S(1)} collective-permute-done((bf16[368,1152]{1,0:T(8,128)(2,1)}, bf16[368,1152]{1,0:T(8,128)(2,1)S(1)}, u32[]{:S(2)}, u32[]{:S(2)}) %collective-permute-start.19) | collective-permute-done | bytes 847904 | tf_op jit(solution)/shard_map/ppermute | solution.py:48
  273.9 25.7 %layer_mid.3 = bf16[368,1152]{1,0:T(8,128)(2,1)} custom-call(f32[8,736]{1,0:T(8,128)} %copy-done.79, f32[2,1152]{1,0:T(2,128)} %copy-done.84, bf16[4608,1152]{1,0:T(8,128)(2,1)S(1)} %get-tuple-element.85.refs_2_.refs_5_.refs_7_.refs_4_, bf16[4352,1152]{1,0:T(8,128)(2,1)S(1)} %get-tuple-element.88.refs_3_.refs_6_.refs_5_, ...), custom_call_target="tpu_custom_call" | custom-call | flops 1767794304 | bytes 3324723 | tf_op jit(solution)/shard_map/layer_mid/pallas_call | solution.py:154
  299.6 5.2 collective-permute-start.21
  304.8 17.8 %collective-permute-done.21.refs_9_ = bf16[368,1152]{1,0:T(8,128)(2,1)} collective-permute-done((bf16[368,1152]{1,0:T(8,128)(2,1)}, bf16[368,1152]{1,0:T(8,128)(2,1)}, u32[]{:S(2)}, u32[]{:S(2)}) %collective-permute-start.21) | collective-permute-done | bytes 847904 | tf_op jit(solution)/shard_map/ppermute | solution.py:48
  325.9 4.0 copy-done.3
  329.9 8.7 %last_project.1 = (f32[368,1152]{1,0:T(8,128)S(1)}, bf16[368,1152]{1,0:T(8,128)(2,1)}, bf16[368,1152]{1,0:T(8,128)(2,1)S(1)}, bf16[736,2304]{1,0:T(8,128)(2,1)S(1)}) custom-call(s32[4]{0:T(128)S(1)} %copy-done.116, f32[2,1152]{1,0:T(2,128)S(1)} %copy-done.85, bf16[4608,1152]{1,0:T(8,128)(2,1)S(1)} %copy-done.3, f32[368,1152]{1,0:T(8,128)} %copy-done.36, ...), custom_call_target="tpu_custom_call" | custom-call | flops 488374272 | bytes 2503988 | tf_op jit(solution)/shard_map/last_project/pallas_call | solution.py:154
  338.8 10.7 %last_attention.1 = (bf16[368,1152]{1,0:T(8,128)(2,1)S(1)}, bf16[368,1152]{1,0:T(8,128)(2,1)S(1)}, f32[368,128]{1,0:T(8,128)S(1)}, f32[368,1152]{1,0:T(8,128)S(1)}, bf16[368,1152]{1,0:T(8,128)(2,1)S(1)}) custom-call(bf16[368,1152]{1,0:T(8,128)(2,1)S(1)} %get-tuple-element.91.refs_0_, bf16[736,2304]{1,0:T(8,128)(2,1)S(1)} %get-tuple-element.92.refs_1_, ...), custom_call_target="tpu_custom_call" | custom-call | flops 541432192 | bytes 2101248 | tf_op jit(solution)/shard_map/last_attention/pallas_call | solution.py:154
  350.7 4.7 copy-done.6
  355.4 23.1 %feed_turn.1 = (f32[368,1152]{1,0:T(8,128)}, bf16[368,4352]{1,0:T(8,128)(2,1)}, f32[368,1152]{1,0:T(8,128)}, bf16[368,1152]{1,0:T(8,128)(2,1)S(1)}, f32[368,1152]{1,0:T(8,128)}) custom-call(f32[368,1152]{1,0:T(8,128)} %copy-done.32, bf16[368,1152]{1,0:T(8,128)(2,1)S(1)} %get-tuple-element.95.refs_1_.refs_0_, f32[184,1152]{1,0:T(8,128)} %pad.8.refs_2_, ...), custom_call_target="tpu_custom_call" | custom-call | flops 1475975552 | bytes 4363366 | tf_op jit(solution)/shard_map/feed_turn/pallas_call | solution.py:154
  378.5 13.6 %attention_back.4 = (bf16[368,1152]{1,0:T(8,128)(2,1)S(1)}, bf16[368,2304]{1,0:T(8,128)(2,1)S(1)}, bf16[368,2304]{1,0:T(8,128)(2,1)S(1)}) custom-call(bf16[368,1152]{1,0:T(8,128)(2,1)S(1)} %get-tuple-element.91.refs_0_, bf16[736,2304]{1,0:T(8,128)(2,1)S(1)} %get-tuple-element.92.refs_1_, bf16[368,1152]{1,0:T(8,128)(2,1)S(1)} %get-tuple-element.99.refs_2_, ...), custom_call_target="tpu_custom_call" | custom-call | flops 1109393408 | bytes 1123430 | tf_op jit(solution)/shard_map/attention_back/pallas_call | solution.py:154
  395.9 4.9 qkv_back.4
  402.3 22.0 %collective-permute-done.26.refs_7_.refs_8_ = bf16[368,1152]{1,0:T(8,128)(2,1)S(1)} collective-permute-done((bf16[368,1152]{1,0:T(8,128)(2,1)S(1)}, bf16[368,1152]{1,0:T(8,128)(2,1)S(1)}, u32[]{:S(2)}, u32[]{:S(2)}) %collective-permute-start.26) | collective-permute-done | bytes 847904 | tf_op jit(solution)/shard_map/ppermute | solution.py:48
  424.4 4.1 copy-done.7
  428.5 12.4 %feed_back_mid.2 = (f32[368,1152]{1,0:T(8,128)S(1)}, bf16[368,1152]{1,0:T(8,128)(2,1)S(1)}) custom-call(s32[4]{0:T(128)S(1)} %copy-done.116, f32[2,1152]{1,0:T(2,128)S(1)} %copy-done.85, f32[368,1152]{1,0:T(8,128)S(1)} %copy-done.33, bf16[368,4352]{1,0:T(8,128)(2,1)S(1)} %copy-done.30, bf16[4608,1152]{1,0:T(8,128)(2,1)S(1)} %copy-done.4, ...), custom_call_target="tpu_custom_call" | custom-call | flops 835662656 | bytes 3897038 | tf_op jit(solution)/shard_map/feed_back_mid/pallas_call | solution.py:154
  443.3 13.8 %attention_back.5 = (bf16[368,1152]{1,0:T(8,128)(2,1)S(1)}, bf16[368,2304]{1,0:T(8,128)(2,1)S(1)}, bf16[368,2304]{1,0:T(8,128)(2,1)S(1)}) custom-call(bf16[368,1152]{1,0:T(8,128)(2,1)S(1)} %copy-done.45, bf16[736,2304]{1,0:T(8,128)(2,1)S(1)} %copy-done.13, bf16[368,1152]{1,0:T(8,128)(2,1)S(1)} %get-tuple-element.107.refs_2_, ...), custom_call_target="tpu_custom_call" | custom-call | flops 1109393408 | bytes 1123430 | tf_op jit(solution)/shard_map/attention_back/pallas_call | solution.py:154
  463.4 4.9 qkv_back.5
  471.4 8.2 %collective-permute-done.29 = bf16[368,1152]{1,0:T(8,128)(2,1)S(1)} collective-permute-done((bf16[368,1152]{1,0:T(8,128)(2,1)S(1)}, bf16[368,1152]{1,0:T(8,128)(2,1)S(1)}, u32[]{:S(2)}, u32[]{:S(2)}) %collective-permute-start.29) | collective-permute-done | bytes 847904 | tf_op jit(solution)/shard_map/ppermute | solution.py:36
  482.9 7.8 %collective-permute-done.24.refs_2_ = bf16[184,1152]{1,0:T(8,128)(2,1)S(1)} collective-permute-done((bf16[184,1152]{1,0:T(8,128)(2,1)S(1)}, bf16[184,1152]{1,0:T(8,128)(2,1)S(1)}, u32[]{:S(2)}, u32[]{:S(2)}) %collective-permute-start.24) | collective-permute-done | bytes 423968 | tf_op jit(solution)/shard_map/ppermute | solution.py:32
  492.9 3.8 copy-done.8
  498.1 12.4 %feed_back_mid.3 = (f32[368,1152]{1,0:T(8,128)S(1)}, bf16[368,1152]{1,0:T(8,128)(2,1)S(1)}) custom-call(s32[4]{0:T(128)S(1)} %copy-done.116, f32[2,1152]{1,0:T(2,128)S(1)} %copy-done.85, f32[368,1152]{1,0:T(8,128)S(1)} %copy-done.33, bf16[368,4352]{1,0:T(8,128)(2,1)S(1)} %copy-done.30, bf16[4608,1152]{1,0:T(8,128)(2,1)S(1)} %copy-done.4, ...), custom_call_target="tpu_custom_call" | custom-call | flops 835662656 | bytes 3897038 | tf_op jit(solution)/shard_map/feed_back_mid/pallas_call | solution.py:154
  513.2 13.8 %attention_back.6 = (bf16[368,1152]{1,0:T(8,128)(2,1)S(1)}, bf16[368,2304]{1,0:T(8,128)(2,1)S(1)}, bf16[368,2304]{1,0:T(8,128)(2,1)S(1)}) custom-call(bf16[368,1152]{1,0:T(8,128)(2,1)S(1)} %copy-done.46, bf16[736,2304]{1,0:T(8,128)(2,1)S(1)} %copy-done.13, bf16[368,1152]{1,0:T(8,128)(2,1)S(1)} %get-tuple-element.112.refs_2_, ...), custom_call_target="tpu_custom_call" | custom-call | flops 1109393408 | bytes 1123430 | tf_op jit(solution)/shard_map/attention_back/pallas_call | solution.py:154
  530.7 6.0 qkv_back.6.refs_7_
  541.4 4.9 collective-permute-done.36.refs_5_.refs_4_
  546.3 15.9 %unit_forward.1 = (bf16[2944,1088]{1,0:T(8,128)(2,1)S(1)}, bf16[2944,1088]{1,0:T(8,128)(2,1)S(1)}) custom-call(bf16[1472,1152]{1,0:T(8,128)(2,1)} %join_normed.1.refs_0_.refs_1_, bf16[1472,1152]{1,0:T(8,128)(2,1)} %collective-permute-done.35.refs_1_.refs_2_, bf16[1088,1152]{1,0:T(8,128)(2,1)S(1)} %bitcast.68, ...), custom_call_target="tpu_custom_call" | custom-call | flops 1033182912 | bytes 2034892 | tf_op jit(solution)/shard_map/unit_forward/pallas_call | solution.py:684
  576.1 3.8 copy-done.11
  579.9 13.8 %feed_back_last.1 = (f32[368,1152]{1,0:T(8,128)S(1)}, bf16[368,1152]{1,0:T(8,128)(2,1)S(1)}, bf16[368,1152]{1,0:T(8,128)(2,1)S(1)}, f32[1,1152]{1,0:T(1,128)S(1)}) custom-call(s32[4]{0:T(128)S(1)} %copy-done.117, f32[2,1152]{1,0:T(2,128)S(1)} %copy-done.85, f32[368,1152]{1,0:T(8,128)S(1)} %copy-done.34, bf16[368,4352]{1,0:T(8,128)(2,1)S(1)} %copy-done.31, ...), custom_call_target="tpu_custom_call" | custom-call | flops 835662656 | bytes 4321435 | tf_op jit(solution)/shard_map/feed_back_last/pallas_call | solution.py:154
  593.9 14.9 %attention_back.7 = (bf16[368,1152]{1,0:T(8,128)(2,1)S(1)}, bf16[368,2304]{1,0:T(8,128)(2,1)S(1)}, bf16[368,2304]{1,0:T(8,128)(2,1)}) custom-call(bf16[368,1152]{1,0:T(8,128)(2,1)S(1)} %copy-done.47, bf16[736,2304]{1,0:T(8,128)(2,1)S(1)} %copy-done.14, bf16[368,1152]{1,0:T(8,128)(2,1)S(1)} %get-tuple-element.121.refs_2_, bf16[368,1152]{1,0:T(8,128)(2,1)S(1)} %copy-done.39, ...), custom_call_target="tpu_custom_call" | custom-call | flops 1109393408 | bytes 1123430 | tf_op jit(solution)/shard_map/attention_back/pallas_call | solution.py:154
  609.4 4.5 collective-permute-done.40.refs_2_
  617.1 4.0 output_grads.1
  621.2 6.2 qkv_back.7
  633.1 7.9 %qkv_grads.1 = (f32[864,576]{1,0:T(8,128)S(1)}, bf16[448,1152]{1,0:T(8,128)(2,1)}, bf16[416,1152]{1,0:T(8,128)(2,1)}, bf16[208,1152]{1,0:T(8,128)(2,1)S(1)}, bf16[224,1152]{1,0:T(8,128)(2,1)S(1)}) custom-call(s32[4]{0:T(128)S(1)} %copy-done.117, bf16[368,1728]{1,0:T(8,128)(2,1)S(1)} %copy-done.99, bf16[368,1728]{1,0:T(8,128)(2,1)S(1)} %collective-permute-done.43.refs_2_, ...), custom_call_target="tpu_custom_call" | custom-call | flops 293024576 | bytes 921601 | tf_op jit(solution)/shard_map/qkv_grads/pallas_call | solution.py:154
  643.5 7.2 collective-permute-done.46.refs_2_
  660.3 26.9 %up_grads.1.refs_4_ = f32[576,1076]{1,0:T(8,128)} custom-call(s32[4]{0:T(128)S(1)} %copy-done.117, bf16[1472,1152]{1,0:T(8,128)(2,1)} %join_normed.1.refs_0_.refs_1_, bf16[1472,1152]{1,0:T(8,128)(2,1)} %collective-permute-done.35.refs_1_.refs_2_, bf16[1472,1152]{1,0:T(8,128)(2,1)} %copy-done.28, bf16[1472,1152]{1,0:T(8,128)(2,1)} %copy-done.54, ...), custom_call_target="tpu_custom_call" | custom-call | flops 1549774336 | bytes 2034892 | tf_op jit(solution)/shard_map/up_grads/pallas_call | solution.py:723
  712.4 12.2 %down_grads.1.refs_5_ = f32[576,1076]{1,0:T(8,128)} custom-call(s32[4]{0:T(128)S(1)} %copy-done.118, bf16[1472,1152]{1,0:T(8,128)(2,1)S(1)} %copy-done.29, bf16[1472,1152]{1,0:T(8,128)(2,1)S(1)} %copy-done.55, bf16[2944,1088]{1,0:T(8,128)(2,1)} %copy-done.35, f32[576,1076]{1,0:T(8,128)S(1)} %copy-done.22, f32[2,1152]{1,0:T(2,128)S(1)} %collective-permute-done.53.refs_5_, ...), custom_call_target="tpu_custom_call" | custom-call | flops 774887168 | bytes 1356595 | tf_op jit(solution)/shard_map/down_grads/pallas_call | solution.py:754
  (469 shorter events, 171.8 us)
Async XLA Ops:
  12.1 99.5 %collective-permute-start.5 = (bf16[1848,1152]{1,0:T(8,128)(2,1)S(1)}, bf16[1848,1152]{1,0:T(8,128)(2,1)S(1)}, u32[]{:S(2)}, u32[]{:S(2)}) collective-permute-start(bf16[1848,1152]{1,0:T(8,128)(2,1)S(1)} %get-tuple-element.81), channel_id=1, source_target_pairs={{0,2},{1,3},{2,0},{3,1},{4,6},{5,7},{6,4},{7,5},{8,10},{9,11},{10,... | collective-permute-start | bytes 12773384 | tf_op jit(solution)/shard_map/ppermute | solution.py:32
  15.1 84.4 %collective-permute-start.4 = (bf16[1664,1152]{1,0:T(8,128)(2,1)S(1)}, bf16[1664,1152]{1,0:T(8,128)(2,1)}, u32[]{:S(2)}, u32[]{:S(2)}) collective-permute-start(bf16[1664,1152]{1,0:T(8,128)(2,1)S(1)} %get-tuple-element.80.refs_1_), channel_id=1, source_target_pairs={{0,4},{4,0},{1,5},{5,1},{2,6},{6,2},{3,7},{7,3},{8,12},{12,8},{9,1... | collective-permute-start | bytes 11501576 | tf_op jit(solution)/shard_map/ppermute | solution.py:36
  100.7 20.6 %collective-permute-start.6 = (bf16[288,1152]{1,0:T(8,128)(2,1)S(1)}, bf16[288,1152]{1,0:T(8,128)(2,1)S(1)}, u32[]{:S(2)}, u32[]{:S(2)}) collective-permute-start(bf16[288,1152]{1,0:T(8,128)(2,1)S(1)} %slice.100), channel_id=1, source_target_pairs={{0,2},{1,3},{2,0},{3,1},{4,6},{5,7},{6,4},{7,5},{8,10},{9,11},{10,... | collective-permute-start | bytes 1990664 | tf_op jit(solution)/shard_map/ppermute | solution.py:32
  105.5 43.7 %collective-permute-start.8 = (bf16[4,288,1152]{2,1,0:T(8,128)(2,1)}, bf16[4,288,1152]{2,1,0:T(8,128)(2,1)}, u32[]{:S(2)}, u32[]{:S(2)}) collective-permute-start(bf16[4,288,1152]{2,1,0:T(8,128)(2,1)} %heads_near.1.refs_3_.refs_5_.refs_0_), channel_id=1, source_target_pairs={{0,1},{1,0},{2,3},{3,2},{4,5},{5,4},{6,7},{7,6},{8,9},{9,8},{10,11... | collective-permute-start | bytes 7962632 | tf_op jit(solution)/shard_map/ppermute | solution.py:27
  111.7 17.4 %collective-permute-start.7 = (bf16[288,1152]{1,0:T(8,128)(2,1)S(1)}, bf16[288,1152]{1,0:T(8,128)(2,1)S(1)}, u32[]{:S(2)}, u32[]{:S(2)}) collective-permute-start(bf16[288,1152]{1,0:T(8,128)(2,1)S(1)} %slice.101), channel_id=1, source_target_pairs={{0,4},{4,0},{1,5},{5,1},{2,6},{6,2},{3,7},{7,3},{8,12},{12,8},{9,1... | collective-permute-start | bytes 1990664 | tf_op jit(solution)/shard_map/ppermute | solution.py:36
  134.2 15.3 %collective-permute-start.9 = (bf16[4,288,1152]{2,1,0:T(8,128)(2,1)}, bf16[4,288,1152]{2,1,0:T(8,128)(2,1)}, u32[]{:S(2)}, u32[]{:S(2)}) collective-permute-start(bf16[4,288,1152]{2,1,0:T(8,128)(2,1)} %heads_far.1.refs_6_.refs_1_), channel_id=1, source_target_pairs={{0,1},{1,0},{2,3},{3,2},{4,5},{5,4},{6,7},{7,6},{8,9},{9,8},{10,11... | collective-permute-start | bytes 7962632 | tf_op jit(solution)/shard_map/ppermute | solution.py:27
  134.3 5.5 collective-permute-start.2
  141.2 5.4 collective-permute-start.3
  142.8 30.0 %collective-permute-start.11 = (bf16[544,1152]{1,0:T(8,128)(2,1)S(1)}, bf16[544,1152]{1,0:T(8,128)(2,1)S(1)}, u32[]{:S(2)}, u32[]{:S(2)}) collective-permute-start(bf16[544,1152]{1,0:T(8,128)(2,1)S(1)} %slice.103), channel_id=1, source_target_pairs={{0,2},{1,3},{2,0},{3,1},{4,6},{5,7},{6,4},{7,5},{8,10},{9,11},{10,... | collective-permute-start | bytes 3760136 | tf_op jit(solution)/shard_map/ppermute | solution.py:32
  144.8 31.9 %collective-permute-start.15 = (bf16[544,1152]{1,0:T(8,128)(2,1)S(1)}, bf16[544,1152]{1,0:T(8,128)(2,1)S(1)}, u32[]{:S(2)}, u32[]{:S(2)}) collective-permute-start(bf16[544,1152]{1,0:T(8,128)(2,1)S(1)} %slice.104), channel_id=1, source_target_pairs={{0,4},{4,0},{1,5},{5,1},{2,6},{6,2},{3,7},{7,3},{8,12},{12,8},{9,1... | collective-permute-start | bytes 3760136 | tf_op jit(solution)/shard_map/ppermute | solution.py:36
  149.1 32.1 %collective-permute-start.10 = (bf16[1088,1152]{1,0:T(8,128)(2,1)S(1)}, bf16[1088,1152]{1,0:T(8,128)(2,1)}, u32[]{:S(2)}, u32[]{:S(2)}) collective-permute-start(bf16[1088,1152]{1,0:T(8,128)(2,1)S(1)} %bitcast.66), channel_id=1, source_target_pairs={{0,1},{1,0},{2,3},{3,2},{4,5},{5,4},{6,7},{7,6},{8,9},{9,8},{10,11... | collective-permute-start | bytes 7520264 | tf_op jit(solution)/shard_map/ppermute | solution.py:27
  149.2 36.0 %collective-permute-start.14 = (bf16[1088,1152]{1,0:T(8,128)(2,1)S(1)}, bf16[1088,1152]{1,0:T(8,128)(2,1)}, u32[]{:S(2)}, u32[]{:S(2)}) collective-permute-start(bf16[1088,1152]{1,0:T(8,128)(2,1)S(1)} %bitcast.61), channel_id=1, source_target_pairs={{0,1},{1,0},{2,3},{3,2},{4,5},{5,4},{6,7},{7,6},{8,9},{9,8},{10,11... | collective-permute-start | bytes 7520264 | tf_op jit(solution)/shard_map/ppermute | solution.py:27
  176.6 13.0 %collective-permute-start.13 = (bf16[1088,1152]{1,0:T(8,128)(2,1)S(1)}, bf16[1088,1152]{1,0:T(8,128)(2,1)S(1)}, u32[]{:S(2)}, u32[]{:S(2)}) collective-permute-start(bf16[1088,1152]{1,0:T(8,128)(2,1)S(1)} %bitcast.74), channel_id=1, source_target_pairs={{0,1},{1,0},{2,3},{3,2},{4,5},{5,4},{6,7},{7,6},{8,9},{9,8},{10,11... | collective-permute-start | bytes 7520264 | tf_op jit(solution)/shard_map/ppermute | solution.py:27
  180.7 12.9 %collective-permute-start.16 = (bf16[1088,1152]{1,0:T(8,128)(2,1)S(1)}, bf16[1088,1152]{1,0:T(8,128)(2,1)S(1)}, u32[]{:S(2)}, u32[]{:S(2)}) collective-permute-start(bf16[1088,1152]{1,0:T(8,128)(2,1)S(1)} %bitcast.71), channel_id=1, source_target_pairs={{0,1},{1,0},{2,3},{3,2},{4,5},{5,4},{6,7},{7,6},{8,9},{9,8},{10,11... | collective-permute-start | bytes 7520264 | tf_op jit(solution)/shard_map/ppermute | solution.py:27
  196.8 22.0 %collective-permute-start.17 = (bf16[368,1152]{1,0:T(8,128)(2,1)S(1)}, bf16[368,1152]{1,0:T(8,128)(2,1)S(1)}, u32[]{:S(2)}, u32[]{:S(2)}) collective-permute-start(bf16[368,1152]{1,0:T(8,128)(2,1)S(1)} %feed_down.3.refs_12_), channel_id=1, source_target_pairs={{0,8},{8,16},{16,24},{1,9},{9,17},{17,25},{2,10},{10,18},{18,26},{... | collective-permute-start | bytes 2543624 | tf_op jit(solution)/shard_map/ppermute | solution.py:48
  248.2 22.4 %collective-permute-start.19 = (bf16[368,1152]{1,0:T(8,128)(2,1)}, bf16[368,1152]{1,0:T(8,128)(2,1)S(1)}, u32[]{:S(2)}, u32[]{:S(2)}) collective-permute-start(bf16[368,1152]{1,0:T(8,128)(2,1)} %layer_mid.2), channel_id=1, source_target_pairs={{0,8},{8,16},{16,24},{1,9},{9,17},{17,25},{2,10},{10,18},{18,26},{... | collective-permute-start | bytes 2543624 | tf_op jit(solution)/shard_map/ppermute | solution.py:48
  299.6 23.0 %collective-permute-start.21 = (bf16[368,1152]{1,0:T(8,128)(2,1)}, bf16[368,1152]{1,0:T(8,128)(2,1)}, u32[]{:S(2)}, u32[]{:S(2)}) collective-permute-start(bf16[368,1152]{1,0:T(8,128)(2,1)} %layer_mid.3), channel_id=1, source_target_pairs={{0,8},{8,16},{16,24},{1,9},{9,17},{17,25},{2,10},{10,18},{18,26},{... | collective-permute-start | bytes 2543624 | tf_op jit(solution)/shard_map/ppermute | solution.py:48
  323.5 27.2 %collective-permute-start.23 = (bf16[184,1152]{1,0:T(8,128)(2,1)S(1)}, bf16[184,1152]{1,0:T(8,128)(2,1)S(1)}, u32[]{:S(2)}, u32[]{:S(2)}) collective-permute-start(bf16[184,1152]{1,0:T(8,128)(2,1)S(1)} %pad.9), channel_id=1, source_target_pairs={{0,2},{1,3},{2,0},{3,1},{4,6},{5,7},{6,4},{7,5},{8,10},{9,11},{10,... | collective-permute-start | bytes 1271816 | tf_op jit(solution)/shard_map/ppermute | solution.py:32
  400.8 23.5 %collective-permute-start.26 = (bf16[368,1152]{1,0:T(8,128)(2,1)S(1)}, bf16[368,1152]{1,0:T(8,128)(2,1)S(1)}, u32[]{:S(2)}, u32[]{:S(2)}) collective-permute-start(bf16[368,1152]{1,0:T(8,128)(2,1)S(1)} %qkv_back.4), channel_id=1, source_target_pairs={{8,0},{16,8},{24,16},{9,1},{17,9},{25,17},{10,2},{18,10},{26,18},{... | collective-permute-start | bytes 2543624 | tf_op jit(solution)/shard_map/ppermute | solution.py:48
  458.4 21.3 %collective-permute-start.29 = (bf16[368,1152]{1,0:T(8,128)(2,1)S(1)}, bf16[368,1152]{1,0:T(8,128)(2,1)S(1)}, u32[]{:S(2)}, u32[]{:S(2)}) collective-permute-start(bf16[368,1152]{1,0:T(8,128)(2,1)S(1)} %copy-done.71), channel_id=1, source_target_pairs={{0,4},{4,0},{1,5},{5,1},{2,6},{6,2},{3,7},{7,3},{8,12},{12,8},{9,1... | collective-permute-start | bytes 2543624 | tf_op jit(solution)/shard_map/ppermute | solution.py:36
  459.9 21.7 %collective-permute-start.31 = (bf16[368,1152]{1,0:T(8,128)(2,1)S(1)}, bf16[368,1152]{1,0:T(8,128)(2,1)S(1)}, u32[]{:S(2)}, u32[]{:S(2)}) collective-permute-start(bf16[368,1152]{1,0:T(8,128)(2,1)S(1)} %copy-done.71), channel_id=1, source_target_pairs={{0,2},{1,3},{2,0},{3,1},{4,6},{5,7},{6,4},{7,5},{8,10},{9,11},{10,... | collective-permute-start | bytes 2543624 | tf_op jit(solution)/shard_map/ppermute | solution.py:32
  468.3 24.5 %collective-permute-start.28 = (bf16[368,1152]{1,0:T(8,128)(2,1)S(1)}, bf16[368,1152]{1,0:T(8,128)(2,1)S(1)}, u32[]{:S(2)}, u32[]{:S(2)}) collective-permute-start(bf16[368,1152]{1,0:T(8,128)(2,1)S(1)} %qkv_back.5), channel_id=1, source_target_pairs={{8,0},{16,8},{24,16},{9,1},{17,9},{25,17},{10,2},{18,10},{26,18},{... | collective-permute-start | bytes 2543624 | tf_op jit(solution)/shard_map/ppermute | solution.py:48
  469.9 20.8 %collective-permute-start.24 = (bf16[184,1152]{1,0:T(8,128)(2,1)S(1)}, bf16[184,1152]{1,0:T(8,128)(2,1)S(1)}, u32[]{:S(2)}, u32[]{:S(2)}) collective-permute-start(bf16[184,1152]{1,0:T(8,128)(2,1)S(1)} %slice.117), channel_id=1, source_target_pairs={{0,2},{1,3},{2,0},{3,1},{4,6},{5,7},{6,4},{7,5},{8,10},{9,11},{10,... | collective-permute-start | bytes 1271816 | tf_op jit(solution)/shard_map/ppermute | solution.py:32
  479.7 30.9 %collective-permute-start.30 = (bf16[192,1152]{1,0:T(8,128)(2,1)S(1)}, bf16[192,1152]{1,0:T(8,128)(2,1)S(1)}, u32[]{:S(2)}, u32[]{:S(2)}) collective-permute-start(bf16[192,1152]{1,0:T(8,128)(2,1)S(1)} %slice.106.refs_3_), channel_id=1, source_target_pairs={{0,2},{1,3},{2,0},{3,1},{4,6},{5,7},{6,4},{7,5},{8,10},{9,11},{10,... | collective-permute-start | bytes 1327112 | tf_op jit(solution)/shard_map/ppermute | solution.py:32
  481.6 29.0 %collective-permute-start.32 = (bf16[176,1152]{1,0:T(8,128)(2,1)S(1)}, bf16[176,1152]{1,0:T(8,128)(2,1)S(1)}, u32[]{:S(2)}, u32[]{:S(2)}) collective-permute-start(bf16[176,1152]{1,0:T(8,128)(2,1)S(1)} %slice.107.refs_2_), channel_id=1, source_target_pairs={{0,4},{4,0},{1,5},{5,1},{2,6},{6,2},{3,7},{7,3},{8,12},{12,8},{9,1... | collective-permute-start | bytes 1216520 | tf_op jit(solution)/shard_map/ppermute | solution.py:36
  538.7 7.6 %collective-permute-start.35 = (bf16[1472,1152]{1,0:T(8,128)(2,1)}, bf16[1472,1152]{1,0:T(8,128)(2,1)}, u32[]{:S(2)}, u32[]{:S(2)}) collective-permute-start(bf16[1472,1152]{1,0:T(8,128)(2,1)} %join_normed.1.refs_0_.refs_1_), channel_id=1, source_target_pairs={{0,1},{1,0},{2,3},{3,2},{4,5},{5,4},{6,7},{7,6},{8,9},{9,8},{10,11... | collective-permute-start | bytes 10174472 | tf_op jit(solution)/shard_map/ppermute | solution.py:27
  538.9 7.4 %collective-permute-start.36 = (bf16[368,1152]{1,0:T(8,128)(2,1)}, bf16[368,1152]{1,0:T(8,128)(2,1)}, u32[]{:S(2)}, u32[]{:S(2)}) collective-permute-start(bf16[368,1152]{1,0:T(8,128)(2,1)} %get-tuple-element.117.refs_3_), channel_id=1, source_target_pairs={{0,1},{1,0},{2,3},{3,2},{4,5},{5,4},{6,7},{7,6},{8,9},{9,8},{10,11... | collective-permute-start | bytes 2543624 | tf_op jit(solution)/shard_map/ppermute | solution.py:27
  539.2 28.6 %collective-permute-start.34 = (bf16[368,1152]{1,0:T(8,128)(2,1)}, bf16[368,1152]{1,0:T(8,128)(2,1)}, u32[]{:S(2)}, u32[]{:S(2)}) collective-permute-start(bf16[368,1152]{1,0:T(8,128)(2,1)} %qkv_back.6.refs_7_), channel_id=1, source_target_pairs={{8,0},{16,8},{24,16},{9,1},{17,9},{25,17},{10,2},{18,10},{26,18},{... | collective-permute-start | bytes 2543624 | tf_op jit(solution)/shard_map/ppermute | solution.py:48
  570.0 23.8 %collective-permute-start.37 = (bf16[192,1152]{1,0:T(8,128)(2,1)S(1)}, bf16[192,1152]{1,0:T(8,128)(2,1)}, u32[]{:S(2)}, u32[]{:S(2)}) collective-permute-start(bf16[192,1152]{1,0:T(8,128)(2,1)S(1)} %slice.110), channel_id=1, source_target_pairs={{0,2},{1,3},{2,0},{3,1},{4,6},{5,7},{6,4},{7,5},{8,10},{9,11},{10,... | collective-permute-start | bytes 1327112 | tf_op jit(solution)/shard_map/ppermute | solution.py:32
  571.6 22.1 %collective-permute-start.38 = (bf16[176,1152]{1,0:T(8,128)(2,1)S(1)}, bf16[176,1152]{1,0:T(8,128)(2,1)}, u32[]{:S(2)}, u32[]{:S(2)}) collective-permute-start(bf16[176,1152]{1,0:T(8,128)(2,1)S(1)} %slice.111), channel_id=1, source_target_pairs={{0,4},{4,0},{1,5},{5,1},{2,6},{6,2},{3,7},{7,3},{8,12},{12,8},{9,1... | collective-permute-start | bytes 1216520 | tf_op jit(solution)/shard_map/ppermute | solution.py:36
  608.8 12.4 %collective-permute-start.39 = (bf16[368,2304]{1,0:T(8,128)(2,1)}, bf16[368,2304]{1,0:T(8,128)(2,1)S(1)}, u32[]{:S(2)}, u32[]{:S(2)}) collective-permute-start(bf16[368,2304]{1,0:T(8,128)(2,1)} %get-tuple-element.124), channel_id=1, source_target_pairs={{0,1},{1,0},{2,3},{3,2},{4,5},{5,4},{6,7},{7,6},{8,9},{9,8},{10,11... | collective-permute-start | bytes 5087240 | tf_op jit(solution)/shard_map/ppermute | solution.py:27
  628.9 14.7 %collective-permute-start.48 = (bf16[192,1152]{1,0:T(8,128)(2,1)}, bf16[192,1152]{1,0:T(8,128)(2,1)S(1)}, u32[]{:S(2)}, u32[]{:S(2)}) collective-permute-start(bf16[192,1152]{1,0:T(8,128)(2,1)} %collective-permute-done.37.refs_7_.refs_1_), channel_id=1, source_target_pairs={{0,4},{4,0},{1,5},{5,1},{2,6},{6,2},{3,7},{7,3},{8,12},{12,8},{9,1... | collective-permute-start | bytes 1327112 | tf_op jit(solution)/shard_map/ppermute | solution.py:36
  630.4 20.4 %collective-permute-start.47 = (bf16[192,1152]{1,0:T(8,128)(2,1)S(1)}, bf16[192,1152]{1,0:T(8,128)(2,1)S(1)}, u32[]{:S(2)}, u32[]{:S(2)}) collective-permute-start(bf16[192,1152]{1,0:T(8,128)(2,1)S(1)} %slice.95), channel_id=1, source_target_pairs={{0,4},{4,0},{1,5},{5,1},{2,6},{6,2},{3,7},{7,3},{8,12},{12,8},{9,1... | collective-permute-start | bytes 1327112 | tf_op jit(solution)/shard_map/ppermute | solution.py:36
  631.0 12.5 %collective-permute-start.49 = (bf16[176,1152]{1,0:T(8,128)(2,1)}, bf16[176,1152]{1,0:T(8,128)(2,1)S(1)}, u32[]{:S(2)}, u32[]{:S(2)}) collective-permute-start(bf16[176,1152]{1,0:T(8,128)(2,1)} %collective-permute-done.38.refs_8_.refs_4_), channel_id=1, source_target_pairs={{0,2},{1,3},{2,0},{3,1},{4,6},{5,7},{6,4},{7,5},{8,10},{9,11},{10,... | collective-permute-start | bytes 1216520 | tf_op jit(solution)/shard_map/ppermute | solution.py:32
  631.6 19.2 %collective-permute-start.46 = (bf16[176,1152]{1,0:T(8,128)(2,1)S(1)}, bf16[176,1152]{1,0:T(8,128)(2,1)S(1)}, u32[]{:S(2)}, u32[]{:S(2)}) collective-permute-start(bf16[176,1152]{1,0:T(8,128)(2,1)S(1)} %slice.94), channel_id=1, source_target_pairs={{0,2},{1,3},{2,0},{3,1},{4,6},{5,7},{6,4},{7,5},{8,10},{9,11},{10,... | collective-permute-start | bytes 1216520 | tf_op jit(solution)/shard_map/ppermute | solution.py:32
  652.3 6.2 collective-permute-start.50
  652.4 36.2 %collective-permute-start.44 = (bf16[448,1152]{1,0:T(8,128)(2,1)}, bf16[448,1152]{1,0:T(8,128)(2,1)S(1)}, u32[]{:S(2)}, u32[]{:S(2)}) collective-permute-start(bf16[448,1152]{1,0:T(8,128)(2,1)} %get-tuple-element.132), channel_id=1, source_target_pairs={{0,2},{1,3},{2,0},{3,1},{4,6},{5,7},{6,4},{7,5},{8,10},{9,11},{10,... | collective-permute-start | bytes 3096584 | tf_op jit(solution)/shard_map/ppermute | solution.py:32
  653.0 34.2 %collective-permute-start.45 = (bf16[416,1152]{1,0:T(8,128)(2,1)}, bf16[416,1152]{1,0:T(8,128)(2,1)S(1)}, u32[]{:S(2)}, u32[]{:S(2)}) collective-permute-start(bf16[416,1152]{1,0:T(8,128)(2,1)} %get-tuple-element.133), channel_id=1, source_target_pairs={{0,4},{4,0},{1,5},{5,1},{2,6},{6,2},{3,7},{7,3},{8,12},{12,8},{9,1... | collective-permute-start | bytes 2875400 | tf_op jit(solution)/shard_map/ppermute | solution.py:36
  654.5 39.7 %collective-permute-start.53 = (f32[2,1152]{1,0:T(2,128)S(1)}, f32[2,1152]{1,0:T(2,128)S(1)}, u32[]{:S(2)}, u32[]{:S(2)}) collective-permute-start(f32[2,1152]{1,0:T(2,128)S(1)} %pad_maximum_fusion.3), channel_id=1, source_target_pairs={{0,2},{1,3},{2,0},{3,1},{4,6},{5,7},{6,4},{7,5},{8,10},{9,11},{10,... | collective-permute-start | bytes 27656 | tf_op jit(solution)/shard_map/ppermute | solution.py:32
  656.1 39.7 %collective-permute-start.54 = (f32[2,1152]{1,0:T(2,128)S(1)}, f32[2,1152]{1,0:T(2,128)S(1)}, u32[]{:S(2)}, u32[]{:S(2)}) collective-permute-start(f32[2,1152]{1,0:T(2,128)S(1)} %pad_maximum_fusion.3), channel_id=1, source_target_pairs={{0,4},{4,0},{1,5},{5,1},{2,6},{6,2},{3,7},{7,3},{8,12},{12,8},{9,1... | collective-permute-start | bytes 27656 | tf_op jit(solution)/shard_map/ppermute | solution.py:36
  658.6 37.8 %collective-permute-start.55 = (f32[2,1152]{1,0:T(2,128)S(1)}, f32[2,1152]{1,0:T(2,128)S(1)}, u32[]{:S(2)}, u32[]{:S(2)}) collective-permute-start(f32[2,1152]{1,0:T(2,128)S(1)} %pad_maximum_fusion.3), channel_id=1, source_target_pairs={{0,6},{1,7},{2,4},{3,5},{4,2},{5,3},{6,0},{7,1},{8,14},{9,15},{10,... | collective-permute-start | bytes 27656 | tf_op jit(solution)/shard_map/ppermute | solution.py:42
  687.2 11.8 %collective-permute-start.56 = (bf16[160,1152]{1,0:T(8,128)(2,1)}, bf16[160,1152]{1,0:T(8,128)(2,1)}, u32[]{:S(2)}, u32[]{:S(2)}) collective-permute-start(bf16[160,1152]{1,0:T(8,128)(2,1)} %get-tuple-element.145), channel_id=1, source_target_pairs={{0,2},{1,3},{2,0},{3,1},{4,6},{5,7},{6,4},{7,5},{8,10},{9,11},{10,... | collective-permute-start | bytes 1105928 | tf_op jit(solution)/shard_map/ppermute | solution.py:32
  688.6 9.7 %collective-permute-start.57 = (bf16[128,1152]{1,0:T(8,128)(2,1)}, bf16[128,1152]{1,0:T(8,128)(2,1)S(1)}, u32[]{:S(2)}, u32[]{:S(2)}) collective-permute-start(bf16[128,1152]{1,0:T(8,128)(2,1)} %get-tuple-element.146), channel_id=1, source_target_pairs={{0,4},{4,0},{1,5},{5,1},{2,6},{6,2},{3,7},{7,3},{8,12},{12,8},{9,1... | collective-permute-start | bytes 884744 | tf_op jit(solution)/shard_map/ppermute | solution.py:36
  694.3 13.9 %collective-permute-start.42 = (bf16[184,1152]{1,0:T(8,128)(2,1)}, bf16[184,1152]{1,0:T(8,128)(2,1)}, u32[]{:S(2)}, u32[]{:S(2)}) collective-permute-start(bf16[184,1152]{1,0:T(8,128)(2,1)} %slice.116), channel_id=1, source_target_pairs={{0,2},{1,3},{2,0},{3,1},{4,6},{5,7},{6,4},{7,5},{8,10},{9,11},{10,... | collective-permute-start | bytes 1271816 | tf_op jit(solution)/shard_map/ppermute | solution.py:32
  695.8 32.8 %collective-permute-start.51 = (bf16[224,1152]{1,0:T(8,128)(2,1)}, bf16[224,1152]{1,0:T(8,128)(2,1)}, u32[]{:S(2)}, u32[]{:S(2)}) collective-permute-start(bf16[224,1152]{1,0:T(8,128)(2,1)} %get-tuple-element.138), channel_id=1, source_target_pairs={{0,4},{4,0},{1,5},{5,1},{2,6},{6,2},{3,7},{7,3},{8,12},{12,8},{9,1... | collective-permute-start | bytes 1548296 | tf_op jit(solution)/shard_map/ppermute | solution.py:36
  696.3 32.3 %collective-permute-start.52 = (bf16[208,1152]{1,0:T(8,128)(2,1)}, bf16[208,1152]{1,0:T(8,128)(2,1)}, u32[]{:S(2)}, u32[]{:S(2)}) collective-permute-start(bf16[208,1152]{1,0:T(8,128)(2,1)} %get-tuple-element.139), channel_id=1, source_target_pairs={{0,2},{1,3},{2,0},{3,1},{4,6},{5,7},{6,4},{7,5},{8,10},{9,11},{10,... | collective-permute-start | bytes 1437704 | tf_op jit(solution)/shard_map/ppermute | solution.py:32
  702.2 22.4 %collective-permute-start.58 = (bf16[80,1152]{1,0:T(8,128)(2,1)S(1)}, bf16[80,1152]{1,0:T(8,128)(2,1)S(1)}, u32[]{:S(2)}, u32[]{:S(2)}) collective-permute-start(bf16[80,1152]{1,0:T(8,128)(2,1)S(1)} %get-tuple-element.149), channel_id=1, source_target_pairs={{0,4},{4,0},{1,5},{5,1},{2,6},{6,2},{3,7},{7,3},{8,12},{12,8},{9,1... | collective-permute-start | bytes 552968 | tf_op jit(solution)/shard_map/ppermute | solution.py:36
  703.8 20.8 %collective-permute-start.59 = (bf16[64,1152]{1,0:T(8,128)(2,1)S(1)}, bf16[64,1152]{1,0:T(8,128)(2,1)S(1)}, u32[]{:S(2)}, u32[]{:S(2)}) collective-permute-start(bf16[64,1152]{1,0:T(8,128)(2,1)S(1)} %get-tuple-element.150), channel_id=1, source_target_pairs={{0,2},{1,3},{2,0},{3,1},{4,6},{5,7},{6,4},{7,5},{8,10},{9,11},{10,... | collective-permute-start | bytes 442376 | tf_op jit(solution)/shard_map/ppermute | solution.py:32
  (167 other events, 2439.7 us)

commit v3 on v2

--- a/solution.py
+++ b/solution.py
@@ -149,7 +149,7 @@
     return lambda *refs: kernel(*refs[:inputs], *refs[inputs + len(after) :])
 
 
-def call(kernel, name, outs, ins, scratch, args, flops, limit=60, after=()):
+def call(kernel, name, outs, ins, scratch, args, flops, limit=60, after=(), cost=None):
     moved = sum(a.size * a.dtype.itemsize for a in args) + sum(o.size * o.dtype.itemsize for o in outs)
     return pl.pallas_call(
         past(kernel, len(args), after),
@@ -158,7 +158,7 @@
         out_specs=tuple([VMEM] * len(outs)),
         scratch_shapes=scratch,
         compiler_params=pltpu.CompilerParams(vmem_limit_bytes=limit * 2**20),
-        cost_estimate=pl.CostEstimate(flops=int(flops * COST), bytes_accessed=int(moved * COST), transcendentals=0),
+        cost_estimate=pl.CostEstimate(flops=int(flops * (cost or COST)), bytes_accessed=int(moved * (cost or COST)), transcendentals=0),
         name=name,
     )(*args, *after)
 
@@ -170,7 +170,7 @@
     hu = (units + 31) // 32 * 16
 
     def kernel(flag_ref, *refs):
-        pair_ref, out, out_x, mine_ref = refs[6:]
+        pair_ref, out, give_ref, mine_ref = refs[6:]
         got = pair_ref.shape[0]
         first = flag_ref[3] == 0
         one, two = pair_ref[:, 0, :], pair_ref[:, 1, :]
@@ -185,15 +185,12 @@
             out[base : base + hu, :part] = rows[:hu]
             out[base : base + units - hu, part:] = rows[hu:]
             out[base + units - hu : base + hu, part:] = jnp.zeros((2 * hu - units, part), BF)
-        if ride:
-            out_x[:total] = out[...]
-            out_x[total : total + quarter] = low16(jnp.concatenate((jnp.where(first, two, one), jnp.zeros((spare, width), F32)), axis=0))
+        give_ref[...] = jnp.zeros_like(give_ref)
+        give_ref[:got] = low16(jnp.where(first, two, one))
 
     total = 4 * h + 2 * hu
-    spare = quarter - pair.shape[0]
     width = pair.shape[2]
-    ride = 2 * part == width
-    outs = [shape((total, 2 * part), BF), shape((total + quarter if ride else 16, 2 * part), BF), shape((quarter, width), F32)]
+    outs = [shape((total, 2 * part), BF), shape((quarter, width), BF), shape((quarter, width), F32)]
     got = call(kernel, "pack", outs, [SMEM] + [VMEM] * 7, [], [flags, *heads, up, down, pair], 0, 30)
     return *got, (0, 4 * h, 4 * h + hu), hu
 
@@ -342,7 +339,7 @@
     outs = [shape((rows, width), F32), shape((rows, width), BF)]
     ins = [SMEM] + [VMEM] * 4 + [ANY] * 4
     flops = 16 * rows * 2 * rows * WIN * 4 + 12 * rows * width * width
-    return call(kernel, "layer_first", outs, ins, scratch, [flags, bias, gains, rows32, far, *heads], flops, 44)
+    return call(kernel, "layer_first", outs, ins, scratch, [flags, bias, gains, rows32, far, *heads], flops, 44, (), 0.001)
 
 
 def settle(flags, after, heads, ups, downs):
@@ -500,19 +497,26 @@
     return call(kernel, "feed_turn", outs, [VMEM] * 8, scratch, args, flops, 22)
 
 
-def feed_grads(low, slope_ref, w_up, w_down, inner, out):
+def feed_grads(low, slope_ref, w_up, w_down, inner, out, ups=()):
     for at, n in spans(w_up.shape[0], 512):
         inner[:, at : at + n] = low16(dot_t(low, w_down[at : at + n, :]) * up32(slope_ref[:, at : at + n]))
+    wait_all(ups)
     for at, n in spans(w_up.shape[1], 256):
         out[:, at : at + n] = dot(inner[...], w_up[:, at : at + n])
 
 
-def feed_back(mode, flags, sources, slope, hidden, gains, w_heads, w_up, w_down, after=()):
+def feed_back(mode, flags, sources, slope, hidden, gains, w_heads, w_ups, w_down, after=()):
     last = mode == "last"
     rows, width = hidden.shape
-    units = w_up.shape[0]
-
-    def kernel(flag_ref, gain_ref, hid_ref, slope_ref, wh, wu, wd, *refs):
+    units = w_down.shape[0]
+    n_up = len(w_ups)
+
+    def kernel(flag_ref, gain_ref, hid_ref, slope_ref, wh, wd, *refs):
+        *refs, wu, up_sem = refs
+        ups = [copy for copy, _ in span_copies(refs[:n_up], wu, up_sem, 0)]
+        for copy in ups:
+            copy.start()
+        refs = refs[n_up:]
         src, refs = refs[: len(sources)], refs[len(sources) :]
         hg_ref, do_ref, refs = refs[0], refs[1], refs[2:]
         if last:
@@ -536,7 +540,7 @@
             ig, nbg, dy_ref, low = refs
             dy_ref[...] = src[0][...].astype(F32)
             low[...] = low16(src[0][...])
-        feed_grads(low[...], slope_ref, wu, wd, ig, nbg)
+        feed_grads(low[...], slope_ref, wu, wd, ig, nbg, ups)
         unit, inverse = norm_parts(hid_ref[...])
         grad = nbg[...]
         if last:
@@ -549,7 +553,7 @@
         do_ref[...] = low16(dot_t(mix_low, wh[:width, :]))
 
     sources = [in_hbm(a) if last else a for a in sources]
-    args = [flags, gains, hidden, slope, w_heads, w_up, w_down, *sources]
+    args = [flags, gains, hidden, slope, w_heads, w_down, *[in_hbm(a) for a in w_ups], *sources]
     outs = [shape((rows, width), F32), shape((rows, width), BF)]
     if last:
         outs += [shape((rows, width), BF), shape((1, width), F32)]
@@ -561,9 +565,10 @@
     ]
     if last:
         scratch.append(pltpu.SemaphoreType.DMA((1,)))
-    ins = [SMEM] + [VMEM] * 6 + [ANY if last else VMEM] * len(sources)
+    scratch += [pltpu.VMEM((units, width), BF), pltpu.SemaphoreType.DMA((n_up,))]
+    ins = [SMEM] + [VMEM] * 5 + [ANY] * n_up + [ANY if last else VMEM] * len(sources)
     flops = 4 * rows * width * units + 2 * rows * width * width
-    return call(kernel, "feed_back_" + mode, outs, ins, scratch, args, flops, 13, after)
+    return call(kernel, "feed_back_" + mode, outs, ins, scratch, args, flops, 24, after)
 
 
 def attention_back(q, kv_all, do, mix, mix_rest, lse, bias, after=()):
@@ -674,11 +679,14 @@
     half, block = halves_of(total)
 
     def kernel(a_ref, b_ref, wu_ref, act_ref, slope_ref):
-        nb = jnp.where(pl.program_id(0) < half, a_ref[...], b_ref[...])
-        for at, k in spans(n, 512):
-            act, slope = gelu_both(dot_t(nb, wu_ref[at : at + k, :]))
-            act_ref[:, at : at + k] = low16(act)
-            slope_ref[:, at : at + k] = low16(slope)
+        def rows(nb_ref):
+            for at, k in spans(n, 512):
+                act, slope = gelu_both(dot_t(nb_ref[...], wu_ref[at : at + k, :]))
+                act_ref[:, at : at + k] = low16(act)
+                slope_ref[:, at : at + k] = low16(slope)
+
+        pl.when(pl.program_id(0) < half)(lambda: rows(a_ref))
+        pl.when(pl.program_id(0) >= half)(lambda: rows(b_ref))
 
     by_rows = pl.BlockSpec((block, n), lambda i: (i, 0))
     return pl.pallas_call(
@@ -686,8 +694,8 @@
         grid=(2 * half,),
         in_specs=[*halves_specs(half, block, width), VMEM, *[ANY] * len(after)],
         out_specs=(by_rows, by_rows),
-        out_shape=(shape((2 * total, n), BF), shape((2 * total, n), BF)),
-        compiler_params=pltpu.CompilerParams(vmem_limit_bytes=26 * 2**20),
+        out_shape=(pltpu.HBM((2 * total, n), BF), pltpu.HBM((2 * total, n), BF)),
+        compiler_params=pltpu.CompilerParams(vmem_limit_bytes=18 * 2**20),
         cost_estimate=pl.CostEstimate(flops=int(5.6 * COST * total * width * n), bytes_accessed=int(12 * COST * total * width), transcendentals=0),
         name="unit_forward",
     )(normed_four, normed_far, w_up, *after)
@@ -700,69 +708,52 @@
     return picked
 
 
-def up_grads(normed_four, normed_far, dy_four, dy_far, slope_all, w_down, flags, units, part, after=()):
-    total, width = normed_four.shape
-    n = w_down.shape[0]
-    half, block = halves_of(total)
-
-    def kernel(flag_ref, na_ref, nb_ref, da_ref, db_ref, slope_ref, wd_ref, gu_ref):
-        step = pl.program_id(0)
-        dy = jnp.where(step < half, da_ref[...], db_ref[...])
-        turned = pick_cols(jnp.where(step < half, na_ref[...], nb_ref[...]), flag_ref[0], part).T
-
-        @pl.when(step == 0)
-        def _():
-            gu_ref[...] = jnp.zeros_like(gu_ref)
-
-        for at, k in spans(n, 512):
-            inner = low16(dot_t(dy, wd_ref[at : at + k, :]) * up32(slope_ref[:, at : at + k]))
-            real = min(k, units - at)
-            gu_ref[:, at : at + real] += dot(turned, inner)[:, :real]
-
-    by_rows = pl.BlockSpec((block, n), lambda i: (i, 0))
-    return pl.pallas_call(
-        past(kernel, 7, after),
-        grid=(2 * half,),
-        in_specs=[
-            SMEM, *halves_specs(half, block, width), *halves_specs(half, block, width), by_rows, VMEM, *[ANY] * len(after)
-        ],
-        out_specs=VMEM,
-        out_shape=shape((part, units), F32),
-        compiler_params=pltpu.CompilerParams(vmem_limit_bytes=48 * 2**20),
-        cost_estimate=pl.CostEstimate(flops=int(8.4 * COST * total * width * n), bytes_accessed=int(12 * COST * total * width), transcendentals=0),
-        name="up_grads",
-    )(flags, normed_four, normed_far, dy_four, dy_far, slope_all, w_down, *after)
-
-
-def down_grads(dy_four, dy_far, act_all, flags, units, part, after=()):
-    total, width = dy_four.shape
-    n = act_all.shape[1]
-    half, block = halves_of(total)
-
-    def kernel(flag_ref, da_ref, db_ref, act_ref, gdt):
-        step = pl.program_id(0)
-        turned = pick_cols(jnp.where(step < half, da_ref[...], db_ref[...]), flag_ref[0], part).T
-
-        @pl.when(step == 0)
-        def _():
-            gdt[...] = jnp.zeros_like(gdt)
-
-        for at, k in spans(n, 512):
-            real = min(k, units - at)
-            gdt[:, at : at + real] += dot(turned, act_ref[:, at : at + k])[:, :real]
-
-    return pl.pallas_call(
-        past(kernel, 4, after),
-        grid=(2 * half,),
-        in_specs=[
-            SMEM, *halves_specs(half, block, width), pl.BlockSpec((block, n), lambda i: (i, 0)), *[ANY] * len(after)
-        ],
-        out_specs=VMEM,
-        out_shape=shape((part, units), F32),
-        compiler_params=pltpu.CompilerParams(vmem_limit_bytes=44 * 2**20),
-        cost_estimate=pl.CostEstimate(flops=int(4.2 * COST * total * width * n), bytes_accessed=int(8 * COST * total * width), transcendentals=0),
-        name="down_grads",
-    )(flags, dy_four, dy_far, act_all, *after)
+def unit_sums(name, flags, sides, saved, w_down, units, part, after=()):
+    total, width = sides[0][0].shape
+    n = saved.shape[1]
+    steps = max(1, total // 736)
+    block = total // steps
+    all_steps = steps * len(sides)
+    kinds = len(sides[0])
+    flat = [a for side in sides for a in side]
+    with_w = w_down is not None
+
+    def kernel(flag_ref, *refs):
+        if with_w:
+            wd_ref, refs = refs[0], refs[1:]
+        saved_hbm, refs = refs[0], refs[1:]
+        rows_hbm, refs = refs[: len(flat)], refs[len(flat) :]
+        out, held, sems = refs[0], refs[1 : 2 + kinds], refs[2 + kinds]
+
+        def into(i):
+            rows = slice(i % steps * block, (i % steps + 1) * block)
+            sources = [rows_hbm[i // steps * kinds + j].at[rows] for j in range(kinds)]
+            sources.append(saved_hbm.at[i * block : (i + 1) * block])
+            return [pltpu.make_async_copy(a, b.at[i % 2], sems.at[j, i % 2]) for j, (a, b) in enumerate(zip(sources, held))]
+
+        for copy in into(0):
+            copy.start()
+        for i in range(all_steps):
+            if i + 1 < all_steps:
+                for copy in into(i + 1):
+                    copy.start()
+            wait_all(into(i))
+            turned = pick_cols(held[0][i % 2], flag_ref[0], part).T
+            for at, k in spans(n, 512):
+                right = held[kinds][i % 2, :, at : at + k]
+                if with_w:
+                    right = low16(dot_t(held[1][i % 2], wd_ref[at : at + k, :]) * up32(right))
+                real = min(k, units - at)
+                cols = slice(at, at + real)
+                got = dot(turned, right)[:, :real]
+                out[:, cols] = got if i == 0 else out[:, cols] + got
+
+    scratch = [pltpu.VMEM((2, block, width), BF)] * kinds + [pltpu.VMEM((2, block, n), BF)]
+    scratch.append(pltpu.SemaphoreType.DMA((kinds + 1, 2)))
+    args = [flags, *([w_down] if with_w else []), in_hbm(saved), *flat]
+    ins = [SMEM] + [VMEM] * with_w + [ANY] * (1 + len(flat))
+    flops = (4 if with_w else 2) * total * len(sides) * width * n
+    return call(kernel, name, [shape((part, units), F32)], ins, scratch, args, flops, 40, after, 0.2)[0]
 
 
 def join(name, pieces, after=()):
@@ -786,10 +777,14 @@
     cut = half_cut(h)
 
     def kernel(flag_ref, l0, l1, r0, r1, *refs):
-        outs, ls, rs = refs[:5], refs[5], refs[6]
-        for a, b, c in ((l0, l1, ls), (r0, r1, rs)):
-            c[:rows] = a[...]
-            c[rows:] = b[...]
+        outs, ls, rs, sem = refs[:5], *refs[5:]
+        copies = [
+            pltpu.make_async_copy(a, c.at[at : at + rows], sem.at[i])
+            for i, (a, c, at) in enumerate(((l0, ls, 0), (l1, ls, rows), (r0, rs, 0), (r1, rs, rows)))
+        ]
+        for copy in copies:
+            copy.start()
+        wait_all(copies)
         first = flag_ref[0] == 0
         lo, hi = rs[:, :part], rs[:, part:]
         shares = (jnp.where(first, lo, hi), jnp.where(first, hi, lo))
@@ -814,10 +809,10 @@
 
     outs = [shape((span, part), F32)]
     outs += [shape((n, 2 * part), BF) for n in (2 * cut, 2 * (h - cut), h - cut, cut)]
-    scratch = [pltpu.VMEM((2 * rows, 2 * span), BF), pltpu.VMEM((2 * rows, 2 * part), BF)]
+    scratch = [pltpu.VMEM((2 * rows, 2 * span), BF), pltpu.VMEM((2 * rows, 2 * part), BF), pltpu.SemaphoreType.DMA((4,))]
     args = [flags, *left, *right]
     flops = 16 * rows * span * part
-    return call(kernel, name, outs, [SMEM] + [VMEM] * 4, scratch, args, flops, 40, after)
+    return call(kernel, name, outs, [SMEM] + [ANY] * 4, scratch, args, flops, 24, after)
 
 
 def scatter_middle(name, beside, above, via_x, via_y, after=()):
@@ -929,25 +924,27 @@
 
     gain_moves = [move(norm_gains[0]) for move in (swap_x, swap_y, swap_both)] if plane else []
     turned = [jnp.transpose(w[0]) for w in (query_weight, key_weight, value_weight)]
-    packed, packed_x, keep_rows, (at_heads, at_up, at_down), h_units = pack(
+    packed, give_rows, keep_rows, (at_heads, at_up, at_down), h_units = pack(
         flags, [*turned, output_weight[0]], up_weight[0], jnp.transpose(down_weight[0]), jnp.transpose(images, (1, 0, 2)),
         padded_quarter,
     )
     h_heads = span // 2
     if plane:
-        from_x, from_y = swap_x(packed_x), swap_y(packed)
-        img_got = from_x[-padded_quarter:]
+        from_x, from_y = swap_x(packed), swap_y(packed)
+        img_got = swap_x(give_rows)
         at = 2 * h_heads
         over_heads = [(swap_x(from_y[:at]), 0, at), (swap_y(from_x[at:at_up]), 0, at)]
-        over_up = [(swap_x(from_y[at_up:at_down]), 0, h_units)]
-        over_down = [(swap_y(from_x[at_down : at_down + h_units]), 0, h_units)]
+        up_on, down_on = from_y[at_up:at_down], from_x[at_down:]
+        over_up, over_down = [(swap_x(up_on), 0, h_units)], [(swap_y(down_on), 0, h_units)]
+        cuts = [up_on, down_on]
         near = lambda row, rows: [[(packed, row, rows)], [(from_y, row, rows)]]
         far = lambda row, rows, over: [[(from_x, row, rows)], over]
     else:
         whole = lax.all_gather(packed, "dp")
         other = swap_x(whole)
         over_heads = over_up = over_down = None
-        img_got = swap_x(theirs(images))
+        cuts = []
+        img_got = swap_x(give_rows)
         near = lambda row, rows: [[(whole[i], row, rows)] for i in range(dp)]
         far = lambda row, rows, over: [[(other[i], row, rows)] for i in range(dp)]
     gains = gather_gains(norm_gains[0], gain_moves, dp_idx, x_idx, core)
@@ -956,7 +953,7 @@
     heads_near = put_together("heads_near", near(at_heads, 4 * h_heads), flags, 4, h_heads)
     up_near = put_together("up_near", near(at_up, h_units), flags, 1, h_units, [heads_near])[0]
     down_near = put_together("down_near", near(at_down, h_units), flags, 1, h_units, [heads_near])[0]
-    heads_far = put_together("heads_far", far(at_heads, 4 * h_heads, over_heads), flags, 4, h_heads, [up_near, down_near, first_rows])
+    heads_far = put_together("heads_far", far(at_heads, 4 * h_heads, over_heads), flags, 4, h_heads, [up_near, down_near, *cuts])
     heads = [heads_near, heads_far, swap_core(heads_near), swap_core(heads_far)]
     hidden, normed_b = layer_first(flags, first_rows, first_far, bias, gains, heads)
     up_near = [up_near, swap_core(up_near)]
@@ -1009,13 +1006,15 @@
                 dy_x0, dy_y1 = swap_x(dy_low[:at]), swap_y(dy_low[at:])
         if tick:
             mode = "last" if last else "mid"
-            used, after = (sources, [act_all]) if last else (sources[-1:], [acts] if tick == 2 else [])
-            results = feed_back(mode, flags, used, slope, hidden, gains, *weights, after)
+            used, after = (sources, [act_all]) if last else (sources[-1:], [acts_got] if tick == 1 else [acts, nb_x1, nb_y0])
+            results = feed_back(mode, flags, used, slope, hidden, gains, weights[0], up_near + up_far, weights[2], after)
             hidden_grad, do = results[:2]
         if last:
             mix_low, gain_sum_b = results[2:]
             mix_got, ml_far = swap_core(mix_give), swap_core(mix_low)
         after = []
+        if plane and tick == 1:
+            after = [nb_x0, nb_y1]
         if plane and tick == 2:
             after = [nb_d0, nb_d1]
         if plane and last:
@@ -1026,25 +1025,33 @@
         after = []
         if plane and last:
             o_parts = plane_blocks("output_grads", flags, (mix_keep, mix_got), (mix_low, ml_far), [dq])
-            dy_rest = tie(dy_low, o_parts[0])
+            o_via = swap_x(o_parts[1]), swap_y(o_parts[2])
+            dy_rest = tie(dy_low, dq)
             dy_x1, dy_y0 = swap_x(dy_rest[at:]), swap_y(dy_rest[:at])
-            after = [o_parts[0]]
+            after = [o_parts[0], dy_d0, dy_d1]
+        if plane and tick == 2:
+            nb_four = join("join_normed", [normed_b, nb_x0, nb_x1, nb_y0, nb_y1, nb_d0, nb_d1], [dq])
+            after = [nb_four]
         back = qkv_back(last, flags, dq, dkv, dkv_got, x, hidden_grad, gains, weights[0], after)
         if last:
             break
-        got = shift(back[0], -1)
+        low = back[0]
+        if plane and tick == 2:
+            nb_four, low = ties(nb_four, low)
+        got = shift(low, -1)
         if tick == 0:
-            nb_x, nb_y = (swap_x(normed_b), swap_y(normed_b)) if plane else (normed_b, normed_b)
+            nb_x0 = nb_x1 = nb_y0 = nb_y1 = normed_b
+            if plane:
+                nb_x0, nb_y1 = swap_x(normed_b[:at]), swap_y(normed_b[at:])
         elif tick == 1:
             if plane:
-                nb_d0, nb_d1 = swap_x(nb_y[:at]), swap_y(nb_x[at:])
+                nb_x1, nb_y0 = swap_x(normed_b[at:]), swap_y(normed_b[:at])
+                nb_d0, nb_d1 = swap_y(nb_x0), swap_x(nb_y1)
             acts = both_images(out, acts_got)
             mix_keep, mix_give = core_halves(mix)
             na_far = swap_core(normed_a)
         elif tick == 2:
             if plane:
-                pieces = [normed_b, nb_x[:at], nb_x[at:], nb_y[:at], nb_y[at:], nb_d0, nb_d1]
-                nb_four = join("join_normed", pieces, [back[0]])
                 nb_far = swap_core(nb_four)
             else:
                 nb_all = lax.all_gather(normed_b, ("dp", "tensor"), axis=0, tiled=True)
@@ -1059,25 +1066,27 @@
     gain_sums = jnp.concatenate((gain_sum_a, gain_sum_b), axis=0)
     if plane:
         gain_moves = [move(gain_sums) for move in (swap_x, swap_y, swap_both)]
-        o_via = swap_x(o_parts[1]), swap_y(o_parts[2])
         qkv_parts = plane_blocks("qkv_grads", flags, (keep, got), (normed_a, na_far))
         via = swap_x(qkv_parts[1]), swap_y(qkv_parts[2])
         dy_four = join("join_dy", [dy_low, dy_x0, dy_x1, dy_y0, dy_y1, dy_d0, dy_d1], [qkv_parts[0]])
         dy_far = swap_core(dy_four)
-        grad_up = up_grads(nb_four, nb_far, dy_four, dy_far, slope_all, down_near[0], flags, units, part, [qkv_parts[0]])
+        sides = [(nb_four, dy_four), (nb_far, dy_far)]
+        grad_up = unit_sums("up_grads", flags, sides, slope_all, down_near[0], units, part, [qkv_parts[0]])
+        over = scatter_middle("qkv_middle", *qkv_parts[3:], *via, [grad_up])
         o_over = scatter_middle("output_middle", *o_parts[3:], *o_via, [grad_up])
-        over = scatter_middle("qkv_middle", *qkv_parts[3:], *via, [grad_up])
-        grad_down = down_grads(dy_four, dy_far, act_all, flags, units, part, [grad_up, *gain_moves])
+        grad_down = unit_sums("down_grads", flags, [(dy_four,), (dy_far,)], act_all, None, units, part, [grad_up, *gain_moves])
         gain_sums = gain_sums + gain_moves[0] + gain_moves[1] + gain_moves[2]
         gain_sums = gain_sums + swap_core(gain_sums)
         (grad_o,) = scatter_end("output_end", o_parts[0], *o_via, *o_over, 1, [grad_down])
         grad_heads = scatter_end("qkv_end", qkv_parts[0], *via, *over, 3, [grad_down])
         gain_shard = lax.dynamic_slice_in_dim(gain_sums, (dp_idx * 4 + tensor_idx) * (width // 8), width // 8, 1)
+        grads_after = [grad_down]
     else:
         dy_all = lax.all_gather(dy_low, ("dp", "tensor"), axis=0, tiled=True)
         dy_four, dy_far = jnp.split(dy_all, 2)
-        grad_up = up_grads(nb_four, nb_far, dy_four, dy_far, slope_all, down_near[0], flags, units, part)
-        grad_down = down_grads(dy_four, dy_far, act_all, flags, units, part)
+        grad_up = unit_sums("up_grads", flags, [(nb_four, dy_four), (nb_far, dy_far)], slope_all, down_near[0], units, part)
+        grad_down = unit_sums("down_grads", flags, [(dy_four,), (dy_far,)], act_all, None, units, part)
+        grads_after = []
         both = lambda a, b: jnp.concatenate((a, b), axis=0)
         g = t_dot(both(keep, got), both(normed_a, na_far))
         g = g[: 3 * span] + up32(swap_x(low16(g[3 * span :])))
@@ -1087,7 +1096,7 @@
         g = g[:span] + up32(swap_x(low16(g[span:])))
         grad_o = up32(lax.psum_scatter(low16(g), "dp", scatter_dimension=1, tiled=True))
         gain_shard = lax.psum_scatter(gain_sums, ("dp", "tensor"), scatter_dimension=1, tiled=True)
-    grads = both_images(dx, grads_got)
+    grads = both_images(dx, grads_got, grads_after)
 
     return (
         jnp.transpose(acts, (1, 0, 2))[None],

time: 742 us -> 704 us (0.949)
  local copies, waits for them, and re-layouts: 80.8 us -> 55.9 us
  waiting for transfers between devices: 218 us -> 202 us
    pallas_call x38 -> x40, Pallas kernels: 297 us -> 337 us  [call(): pl.pallas_call(past(kernel, len(args), after), out_shape=tuple(outs), in_...]
    pallas_call x2 -> x0, Pallas kernels: 39.2 us -> none  [the longest x1 26.9 us: up_grads(): pl.pallas_call(past(kernel, 7, after), grid=(2 * half,), in_specs=[SMEM,...]
    unnamed x310 -> x232, local copies, waits for them, and re-layouts: 69.7 us -> 45.4 us
    ppermute x14 -> x15, waiting for transfers between devices: 99.7 us -> 84.4 us  [swap_y(): return lax.ppermute(a, 'dp', [(0, 1), (1, 0)])]
    ppermute x17 -> x19, starting transfers between devices: 20.1 us -> 23 us  [swap_x(): return lax.ppermute(a, 'tensor', [(i, i ^ 2) for i in range(n)])]
    ppermute x17 -> x19, waiting for transfers between devices: 31.2 us -> 32.8 us  [swap_x(): return lax.ppermute(a, 'tensor', [(i, i ^ 2) for i in range(n)])]
    ppermute x14 -> x15, starting transfers between devices: 15.8 us -> 16.8 us  [swap_y(): return lax.ppermute(a, 'dp', [(0, 1), (1, 0)])]
  transfers between devices with their start and end apart: 61 -> 64, of which waited for: 25 -> 25; matrix products, arithmetic and copies ran while one was open for 2% -> 2% of each run, Pallas kernels for 26% -> 30%
where the time goes in v3:
time: 704 us; the launch traced here: 694 us
  Pallas kernels  366 us (52%)
  waiting for transfers between devices  202 us (29%)
  starting transfers between devices  62.5 us (9%)
  local copies, waits for them, and re-layouts  55.9 us (8%)
    pallas_call x40, Pallas kernels, call(): pl.pallas_call(past(kernel, len(args), after), out_shape=tuple(outs), in_...  337 us
    ppermute x15, waiting for transfers between devices, swap_y(): return lax.ppermute(a, 'dp', [(0, 1), (1, 0)])  84.4 us
    ppermute x6, waiting for transfers between devices, shift(): return lax.ppermute(a, 'section', pairs)  61.3 us
    unnamed x232, local copies, waits for them, and re-layouts  45.4 us
    ppermute x19, waiting for transfers between devices, swap_x(): return lax.ppermute(a, 'tensor', [(i, i ^ 2) for i in range(n)])  32.8 us
    ppermute x22, waiting for transfers between devices, swap_core(): return lax.ppermute(a, 'tensor', [(i, i ^ 1) for i in range(n)])  23.7 us
    ppermute x19, starting transfers between devices, swap_x(): return lax.ppermute(a, 'tensor', [(i, i ^ 2) for i in range(n)])  23 us
    pallas_call x1, Pallas kernels, unit_forward(): pl.pallas_call(past(kernel, 3, after), grid=(2 * half,), in_specs=[*halve...  17.7 us
  transfers between devices with their start and end apart: 64, of which 25 were waited for; matrix products, arithmetic and copies ran while one was open for 2% of the time, Pallas kernels for 30%

profile of v3, /device:TPU:0, one launch (start us, length us, event | category | flops | bytes accessed | tf_op | source)
XLA Modules:
  0.0 694.0 jit_solution(18234600419213999906)
XLA Ops:
  8.9 4.0 pack.1
  17.4 81.4 %collective-permute-done.4.refs_2_ = bf16[1664,1152]{1,0:T(8,128)(2,1)S(1)} collective-permute-done((bf16[1664,1152]{1,0:T(8,128)(2,1)S(1)}, bf16[1664,1152]{1,0:T(8,128)(2,1)S(1)}, u32[]{:S(2)}, u32[]{:S(2)}) %collective-permute-start.4) | collective-permute-done | bytes 3833888 | tf_op jit(solution)/shard_map/ppermute | solution.py:36
  102.3 4.4 heads_near.1.refs_3_.refs_5_.refs_0_
  112.8 3.3 slice.90.refs_6_
  118.3 4.3 heads_far.1.refs_6_.refs_1_
  129.3 7.2 %collective-permute-done = f32[2,144]{1,0:T(2,128)S(1)} collective-permute-done((f32[2,144]{1,0:T(2,128)S(1)}, f32[2,144]{1,0:T(2,128)S(1)}, u32[]{:S(2)}, u32[]{:S(2)}) %collective-permute-start) | collective-permute-done | bytes 1184 | tf_op jit(solution)/shard_map/ppermute | solution.py:32
  142.3 19.4 %layer_first.1 = (f32[368,1152]{1,0:T(8,128)S(1)}, bf16[368,1152]{1,0:T(8,128)(2,1)S(1)}) custom-call(s32[4]{0:T(128)S(1)} %pad_add_fusion.refs_0_.flag_ref, f32[8,736]{1,0:T(8,128)S(1)} %broadcast_in_dim.43.refs_1_.refs_0_.refs_2_.refs_6_, f32[2,1152]{1,0:T(2,128)S(1)} %maximum_select_fusion.refs_2_.refs_1_.refs_4_, ...), custom_call_target="tpu_custom_call" | custom-call | flops 10298064 | bytes 15736 | tf_op jit(solution)/shard_map/layer_first/pallas_call | solution.py:154
  161.7 5.2 collective-permute-done.11.refs_2_
  173.3 4.0 feed_up.2.refs_1_
  180.5 3.9 feed_up.3.refs_1_
  187.6 4.0 collective-permute-start.18
  191.5 11.3 %settle.1 = (bf16[4608,1152]{1,0:T(8,128)(2,1)S(1)}, bf16[4352,1152]{1,0:T(8,128)(2,1)S(1)}, bf16[4352,1152]{1,0:T(8,128)(2,1)S(1)}, f32[8,128]{1,0:T(8,128)}) custom-call(s32[4]{0:T(128)} %copy-done.90, bf16[4,288,1152]{2,1,0:T(8,128)(2,1)} %heads_near.1.refs_3_.refs_5_.refs_0_, bf16[4,288,1152]{2,1,0:T(8,128)(2,1)} %heads_far.1.refs_6_.refs_1_, ...), custom_call_target="tpu_custom_call" | custom-call | bytes 6291456 | tf_op jit(solution)/shard_map/settle/pallas_call | solution.py:359
  202.9 6.7 collective-permute-done.18.refs_5_
  213.6 25.5 %layer_mid.2 = bf16[368,1152]{1,0:T(8,128)(2,1)} custom-call(f32[8,736]{1,0:T(8,128)} %copy-done.66, f32[2,1152]{1,0:T(2,128)} %copy-done.68, bf16[4608,1152]{1,0:T(8,128)(2,1)S(1)} %get-tuple-element.87.refs_2_.refs_5_.refs_7_.refs_4_, bf16[4352,1152]{1,0:T(8,128)(2,1)S(1)} %get-tuple-element.90.refs_3_.refs_6_, ...), custom_call_target="tpu_custom_call" | custom-call | flops 1767794304 | bytes 3324723 | tf_op jit(solution)/shard_map/layer_mid/pallas_call | solution.py:154
  239.0 3.9 collective-permute-start.20
  242.9 18.5 %collective-permute-done.20.refs_5_.refs_7_ = bf16[368,1152]{1,0:T(8,128)(2,1)S(1)} collective-permute-done((bf16[368,1152]{1,0:T(8,128)(2,1)}, bf16[368,1152]{1,0:T(8,128)(2,1)S(1)}, u32[]{:S(2)}, u32[]{:S(2)}) %collective-permute-start.20) | collective-permute-done | bytes 847904 | tf_op jit(solution)/shard_map/ppermute | solution.py:48
  264.7 25.7 %layer_mid.3 = bf16[368,1152]{1,0:T(8,128)(2,1)} custom-call(f32[8,736]{1,0:T(8,128)} %copy-done.66, f32[2,1152]{1,0:T(2,128)} %copy-done.68, bf16[4608,1152]{1,0:T(8,128)(2,1)S(1)} %get-tuple-element.87.refs_2_.refs_5_.refs_7_.refs_4_, bf16[4352,1152]{1,0:T(8,128)(2,1)S(1)} %get-tuple-element.90.refs_3_.refs_6_, ...), custom_call_target="tpu_custom_call" | custom-call | flops 1767794304 | bytes 3324723 | tf_op jit(solution)/shard_map/layer_mid/pallas_call | solution.py:154
  290.4 4.3 collective-permute-start.22
  294.7 18.7 %collective-permute-done.22.refs_9_ = bf16[368,1152]{1,0:T(8,128)(2,1)S(1)} collective-permute-done((bf16[368,1152]{1,0:T(8,128)(2,1)}, bf16[368,1152]{1,0:T(8,128)(2,1)S(1)}, u32[]{:S(2)}, u32[]{:S(2)}) %collective-permute-start.22) | collective-permute-done | bytes 847904 | tf_op jit(solution)/shard_map/ppermute | solution.py:48
  317.7 4.0 copy-done.3
  321.7 8.8 %last_project.1 = (f32[368,1152]{1,0:T(8,128)S(1)}, bf16[368,1152]{1,0:T(8,128)(2,1)}, bf16[368,1152]{1,0:T(8,128)(2,1)S(1)}, bf16[736,2304]{1,0:T(8,128)(2,1)S(1)}) custom-call(s32[4]{0:T(128)S(1)} %copy-done.91, f32[2,1152]{1,0:T(2,128)S(1)} %copy-done.69, bf16[4608,1152]{1,0:T(8,128)(2,1)S(1)} %copy-done.3, f32[368,1152]{1,0:T(8,128)} %copy-done.41, ...), custom_call_target="tpu_custom_call" | custom-call | flops 488374272 | bytes 2503988 | tf_op jit(solution)/shard_map/last_project/pallas_call | solution.py:154
  330.5 10.6 %last_attention.1 = (bf16[368,1152]{1,0:T(8,128)(2,1)S(1)}, bf16[368,1152]{1,0:T(8,128)(2,1)S(1)}, f32[368,128]{1,0:T(8,128)S(1)}, f32[368,1152]{1,0:T(8,128)S(1)}, bf16[368,1152]{1,0:T(8,128)(2,1)S(1)}) custom-call(bf16[368,1152]{1,0:T(8,128)(2,1)S(1)} %get-tuple-element.93.refs_0_, bf16[736,2304]{1,0:T(8,128)(2,1)S(1)} %get-tuple-element.94.refs_1_, ...), custom_call_target="tpu_custom_call" | custom-call | flops 541432192 | bytes 2101248 | tf_op jit(solution)/shard_map/last_attention/pallas_call | solution.py:154
  342.4 4.5 copy-done.11
  346.9 22.8 %feed_turn.1 = (f32[368,1152]{1,0:T(8,128)}, bf16[368,4352]{1,0:T(8,128)(2,1)}, f32[368,1152]{1,0:T(8,128)}, bf16[368,1152]{1,0:T(8,128)(2,1)S(1)}, f32[368,1152]{1,0:T(8,128)}) custom-call(f32[368,1152]{1,0:T(8,128)} %copy-done.31, bf16[368,1152]{1,0:T(8,128)(2,1)S(1)} %get-tuple-element.97.refs_1_.refs_0_, f32[184,1152]{1,0:T(8,128)} %pad.8.refs_2_, ...), custom_call_target="tpu_custom_call" | custom-call | flops 1475975552 | bytes 4363366 | tf_op jit(solution)/shard_map/feed_turn/pallas_call | solution.py:154
  369.7 13.6 %attention_back.4 = (bf16[368,1152]{1,0:T(8,128)(2,1)S(1)}, bf16[368,2304]{1,0:T(8,128)(2,1)S(1)}, bf16[368,2304]{1,0:T(8,128)(2,1)S(1)}) custom-call(bf16[368,1152]{1,0:T(8,128)(2,1)S(1)} %get-tuple-element.93.refs_0_, bf16[736,2304]{1,0:T(8,128)(2,1)S(1)} %get-tuple-element.94.refs_1_, bf16[368,1152]{1,0:T(8,128)(2,1)S(1)} %get-tuple-element.101.refs_2_, ...), custom_call_target="tpu_custom_call" | custom-call | flops 1109393408 | bytes 1123430 | tf_op jit(solution)/shard_map/attention_back/pallas_call | solution.py:154
  383.6 3.3 collective-permute-done.26.refs_4_
  387.0 4.8 qkv_back.4
  397.1 9.1 %collective-permute-done.25.refs_2_.refs_11_ = bf16[184,1152]{1,0:T(8,128)(2,1)S(1)} collective-permute-done((bf16[184,1152]{1,0:T(8,128)(2,1)S(1)}, bf16[184,1152]{1,0:T(8,128)(2,1)S(1)}, u32[]{:S(2)}, u32[]{:S(2)}) %collective-permute-start.25) | collective-permute-done | bytes 423968 | tf_op jit(solution)/shard_map/ppermute | solution.py:32
  406.2 9.2 %collective-permute-done.27.refs_10_.refs_11_ = bf16[368,1152]{1,0:T(8,128)(2,1)S(1)} collective-permute-done((bf16[368,1152]{1,0:T(8,128)(2,1)S(1)}, bf16[368,1152]{1,0:T(8,128)(2,1)S(1)}, u32[]{:S(2)}, u32[]{:S(2)}) %collective-permute-start.27) | collective-permute-done | bytes 847904 | tf_op jit(solution)/shard_map/ppermute | solution.py:48
  415.5 14.1 %feed_back_mid.2 = (f32[368,1152]{1,0:T(8,128)S(1)}, bf16[368,1152]{1,0:T(8,128)(2,1)S(1)}) custom-call(s32[4]{0:T(128)S(1)} %copy-done.91, f32[2,1152]{1,0:T(2,128)S(1)} %copy-done.69, f32[368,1152]{1,0:T(8,128)S(1)} %copy-done.32, bf16[368,4352]{1,0:T(8,128)(2,1)S(1)} %copy-done.29, bf16[4608,1152]{1,0:T(8,128)(2,1)S(1)} %copy-done.4, ...), custom_call_target="tpu_custom_call" | custom-call | flops 835662656 | bytes 3897038 | tf_op jit(solution)/shard_map/feed_back_mid/pallas_call | solution.py:154
  429.7 13.9 %attention_back.5 = (bf16[368,1152]{1,0:T(8,128)(2,1)S(1)}, bf16[368,2304]{1,0:T(8,128)(2,1)S(1)}, bf16[368,2304]{1,0:T(8,128)(2,1)S(1)}) custom-call(bf16[368,1152]{1,0:T(8,128)(2,1)S(1)} %get-tuple-element.93.refs_0_, bf16[736,2304]{1,0:T(8,128)(2,1)S(1)} %copy-done.14, bf16[368,1152]{1,0:T(8,128)(2,1)S(1)} %get-tuple-element.109.refs_2_, ...), custom_call_target="tpu_custom_call" | custom-call | flops 1109393408 | bytes 1123430 | tf_op jit(solution)/shard_map/attention_back/pallas_call | solution.py:154
  443.7 3.6 collective-permute-done.30.refs_4_
  448.7 4.9 qkv_back.5
  461.2 6.8 collective-permute-done.32.refs_12_.refs_2_
  468.1 8.3 %collective-permute-done.31.refs_10_.refs_12_ = bf16[368,1152]{1,0:T(8,128)(2,1)S(1)} collective-permute-done((bf16[368,1152]{1,0:T(8,128)(2,1)S(1)}, bf16[368,1152]{1,0:T(8,128)(2,1)S(1)}, u32[]{:S(2)}, u32[]{:S(2)}) %collective-permute-start.31) | collective-permute-done | bytes 847904 | tf_op jit(solution)/shard_map/ppermute | solution.py:48
  477.9 18.0 %feed_back_mid.3 = (f32[368,1152]{1,0:T(8,128)S(1)}, bf16[368,1152]{1,0:T(8,128)(2,1)S(1)}) custom-call(s32[4]{0:T(128)S(1)} %copy-done.91, f32[2,1152]{1,0:T(2,128)S(1)} %copy-done.69, f32[368,1152]{1,0:T(8,128)S(1)} %copy-done.32, bf16[368,4352]{1,0:T(8,128)(2,1)} %get-tuple-element.99.refs_3_, bf16[4608,1152]{1,0:T(8,128)(2,1)S(1)} %copy-done.4, ...), custom_call_target="tpu_custom_call" | custom-call | flops 835662656 | bytes 3897038 | tf_op jit(solution)/shard_map/feed_back_mid/pallas_call | solution.py:154
  497.7 13.6 %attention_back.6 = (bf16[368,1152]{1,0:T(8,128)(2,1)S(1)}, bf16[368,2304]{1,0:T(8,128)(2,1)S(1)}, bf16[368,2304]{1,0:T(8,128)(2,1)S(1)}) custom-call(bf16[368,1152]{1,0:T(8,128)(2,1)S(1)} %get-tuple-element.93.refs_0_, bf16[736,2304]{1,0:T(8,128)(2,1)S(1)} %copy-done.14, bf16[368,1152]{1,0:T(8,128)(2,1)S(1)} %get-tuple-element.114.refs_2_, ...), custom_call_target="tpu_custom_call" | custom-call | flops 1109393408 | bytes 1123430 | tf_op jit(solution)/shard_map/attention_back/pallas_call | solution.py:154
  514.9 6.0 qkv_back.6
  524.9 3.2 collective-permute-done.39.refs_5_.refs_4_
  530.2 17.7 %unit_forward.1 = (bf16[2944,1088]{1,0:T(8,128)(2,1)}, bf16[2944,1088]{1,0:T(8,128)(2,1)}) custom-call(bf16[1472,1152]{1,0:T(8,128)(2,1)} %join_normed.1.refs_8_.refs_0_.refs_3_, bf16[1472,1152]{1,0:T(8,128)(2,1)} %collective-permute-done.38.refs_1_.refs_5_, bf16[1088,1152]{1,0:T(8,128)(2,1)S(1)} %bitcast.66, ...), custom_call_target="tpu_custom_call" | custom-call | flops 1033182912 | bytes 2034892 | tf_op jit(solution)/shard_map/unit_forward/pallas_call | solution.py:692
  551.5 3.8 copy-done.6
  555.4 17.3 %feed_back_last.1 = (f32[368,1152]{1,0:T(8,128)S(1)}, bf16[368,1152]{1,0:T(8,128)(2,1)S(1)}, bf16[368,1152]{1,0:T(8,128)(2,1)S(1)}, f32[1,1152]{1,0:T(1,128)S(1)}) custom-call(s32[4]{0:T(128)S(1)} %copy-done.91, f32[2,1152]{1,0:T(2,128)S(1)} %copy-done.69, f32[368,1152]{1,0:T(8,128)S(1)} %copy-done.33, bf16[368,4352]{1,0:T(8,128)(2,1)S(1)} %copy-done.30, ...), custom_call_target="tpu_custom_call" | custom-call | flops 835662656 | bytes 4321435 | tf_op jit(solution)/shard_map/feed_back_last/pallas_call | solution.py:154
  572.8 13.7 %attention_back.7 = (bf16[368,1152]{1,0:T(8,128)(2,1)S(1)}, bf16[368,2304]{1,0:T(8,128)(2,1)S(1)}, bf16[368,2304]{1,0:T(8,128)(2,1)S(1)}) custom-call(bf16[368,1152]{1,0:T(8,128)(2,1)S(1)} %copy-done.38, bf16[736,2304]{1,0:T(8,128)(2,1)S(1)} %copy-done.15, bf16[368,1152]{1,0:T(8,128)(2,1)S(1)} %get-tuple-element.125.refs_2_, ...), custom_call_target="tpu_custom_call" | custom-call | flops 1109393408 | bytes 1123430 | tf_op jit(solution)/shard_map/attention_back/pallas_call | solution.py:154
  593.1 5.2 output_grads.1
  599.6 5.8 qkv_back.7
  608.5 7.1 %qkv_grads.1 = (f32[864,576]{1,0:T(8,128)S(1)}, bf16[448,1152]{1,0:T(8,128)(2,1)S(1)}, bf16[416,1152]{1,0:T(8,128)(2,1)S(1)}, bf16[208,1152]{1,0:T(8,128)(2,1)S(1)}, bf16[224,1152]{1,0:T(8,128)(2,1)S(1)}) custom-call(s32[4]{0:T(128)S(1)} %copy-done.91, bf16[368,1728]{1,0:T(8,128)(2,1)S(1)} %get-tuple-element.134.refs_1_, ...), custom_call_target="tpu_custom_call" | custom-call | flops 293024576 | bytes 921601 | tf_op jit(solution)/shard_map/qkv_grads/pallas_call | solution.py:154
  626.6 21.7 %up_grads.1.refs_4_ = f32[576,1076]{1,0:T(8,128)} custom-call(s32[4]{0:T(128)S(1)} %copy-done.91, bf16[1088,1152]{1,0:T(8,128)(2,1)S(1)} %bitcast.77, bf16[2944,1088]{1,0:T(8,128)(2,1)} %get-tuple-element.137.refs_2_, bf16[1472,1152]{1,0:T(8,128)(2,1)} %join_normed.1.refs_8_.refs_0_.refs_3_, bf16[1472,1152]{1,0:T(8,128)(2,1)S(1)} %join_dy.1.refs_4_.refs_2_, ...), custom_call_target="tpu_custom_call" | custom-call | flops 2951951104 | bytes 4991593 | tf_op jit(solution)/shard_map/up_grads/pallas_call | solution.py:154
  668.8 14.0 %down_grads.1.refs_3_.refs_5_ = f32[576,1076]{1,0:T(8,128)} custom-call(s32[4]{0:T(128)S(1)} %copy-done.91, bf16[2944,1088]{1,0:T(8,128)(2,1)} %get-tuple-element.124.refs_14_.refs_1_, bf16[1472,1152]{1,0:T(8,128)(2,1)S(1)} %copy-done.28, bf16[1472,1152]{1,0:T(8,128)(2,1)S(1)} %copy-done.45, f32[576,1076]{1,0:T(8,128)S(1)} %copy-done.23, ...), custom_call_target="tpu_custom_call" | custom-call | flops 1475975552 | bytes 3133648 | tf_op jit(solution)/shard_map/down_grads/pallas_call | solution.py:154
  (395 shorter events, 146.7 us)
Async XLA Ops:
  12.9 85.9 %collective-permute-start.4 = (bf16[1664,1152]{1,0:T(8,128)(2,1)S(1)}, bf16[1664,1152]{1,0:T(8,128)(2,1)S(1)}, u32[]{:S(2)}, u32[]{:S(2)}) collective-permute-start(bf16[1664,1152]{1,0:T(8,128)(2,1)S(1)} %get-tuple-element.82.refs_1_), channel_id=1, source_target_pairs={{0,4},{4,0},{1,5},{5,1},{2,6},{6,2},{3,7},{7,3},{8,12},{12,8},{9,1... | collective-permute-start | bytes 11501576 | tf_op jit(solution)/shard_map/ppermute | solution.py:36
  15.9 84.7 %collective-permute-start.5 = (bf16[1664,1152]{1,0:T(8,128)(2,1)S(1)}, bf16[1664,1152]{1,0:T(8,128)(2,1)S(1)}, u32[]{:S(2)}, u32[]{:S(2)}) collective-permute-start(bf16[1664,1152]{1,0:T(8,128)(2,1)S(1)} %get-tuple-element.82.refs_1_), channel_id=1, source_target_pairs={{0,2},{1,3},{2,0},{3,1},{4,6},{5,7},{6,4},{7,5},{8,10},{9,11},{10,... | collective-permute-start | bytes 11501576 | tf_op jit(solution)/shard_map/ppermute | solution.py:32
  98.8 18.4 %collective-permute-start.6 = (bf16[288,1152]{1,0:T(8,128)(2,1)S(1)}, bf16[288,1152]{1,0:T(8,128)(2,1)S(1)}, u32[]{:S(2)}, u32[]{:S(2)}) collective-permute-start(bf16[288,1152]{1,0:T(8,128)(2,1)S(1)} %slice.88), channel_id=1, source_target_pairs={{0,2},{1,3},{2,0},{3,1},{4,6},{5,7},{6,4},{7,5},{8,10},{9,11},{10,... | collective-permute-start | bytes 1990664 | tf_op jit(solution)/shard_map/ppermute | solution.py:32
  100.7 16.6 %collective-permute-start.7 = (bf16[288,1152]{1,0:T(8,128)(2,1)S(1)}, bf16[288,1152]{1,0:T(8,128)(2,1)S(1)}, u32[]{:S(2)}, u32[]{:S(2)}) collective-permute-start(bf16[288,1152]{1,0:T(8,128)(2,1)S(1)} %slice.89), channel_id=1, source_target_pairs={{0,4},{4,0},{1,5},{5,1},{2,6},{6,2},{3,7},{7,3},{8,12},{12,8},{9,1... | collective-permute-start | bytes 1990664 | tf_op jit(solution)/shard_map/ppermute | solution.py:36
  106.6 34.9 %collective-permute-start.8 = (bf16[4,288,1152]{2,1,0:T(8,128)(2,1)}, bf16[4,288,1152]{2,1,0:T(8,128)(2,1)}, u32[]{:S(2)}, u32[]{:S(2)}) collective-permute-start(bf16[4,288,1152]{2,1,0:T(8,128)(2,1)} %heads_near.1.refs_3_.refs_5_.refs_0_), channel_id=1, source_target_pairs={{0,1},{1,0},{2,3},{3,2},{4,5},{5,4},{6,7},{7,6},{8,9},{9,8},{10,11... | collective-permute-start | bytes 7962632 | tf_op jit(solution)/shard_map/ppermute | solution.py:27
  122.6 19.4 %collective-permute-start.9 = (bf16[4,288,1152]{2,1,0:T(8,128)(2,1)}, bf16[4,288,1152]{2,1,0:T(8,128)(2,1)}, u32[]{:S(2)}, u32[]{:S(2)}) collective-permute-start(bf16[4,288,1152]{2,1,0:T(8,128)(2,1)} %heads_far.1.refs_6_.refs_1_), channel_id=1, source_target_pairs={{0,1},{1,0},{2,3},{3,2},{4,5},{5,4},{6,7},{7,6},{8,9},{9,8},{10,11... | collective-permute-start | bytes 7962632 | tf_op jit(solution)/shard_map/ppermute | solution.py:27
  125.2 11.4 %collective-permute-start.12 = (bf16[184,1152]{1,0:T(8,128)(2,1)S(1)}, bf16[184,1152]{1,0:T(8,128)(2,1)S(1)}, u32[]{:S(2)}, u32[]{:S(2)}) collective-permute-start(bf16[184,1152]{1,0:T(8,128)(2,1)S(1)} %get-tuple-element.84), channel_id=1, source_target_pairs={{0,2},{1,3},{2,0},{3,1},{4,6},{5,7},{6,4},{7,5},{8,10},{9,11},{10,... | collective-permute-start | bytes 1271816 | tf_op jit(solution)/shard_map/ppermute | solution.py:32
  128.6 7.8 %collective-permute-start = (f32[2,144]{1,0:T(2,128)S(1)}, f32[2,144]{1,0:T(2,128)S(1)}, u32[]{:S(2)}, u32[]{:S(2)}) collective-permute-start(f32[2,144]{1,0:T(2,128)S(1)} %bitcast.97), channel_id=1, source_target_pairs={{0,2},{1,3},{2,0},{3,1},{4,6},{5,7},{6,4},{7,5},{8,10},{9,11},{10,... | collective-permute-start | bytes 3464 | tf_op jit(solution)/shard_map/ppermute | solution.py:32
  136.6 30.3 %collective-permute-start.11 = (bf16[544,1152]{1,0:T(8,128)(2,1)}, bf16[544,1152]{1,0:T(8,128)(2,1)}, u32[]{:S(2)}, u32[]{:S(2)}) collective-permute-start(bf16[544,1152]{1,0:T(8,128)(2,1)} %slice.90.refs_6_), channel_id=1, source_target_pairs={{0,2},{1,3},{2,0},{3,1},{4,6},{5,7},{6,4},{7,5},{8,10},{9,11},{10,... | collective-permute-start | bytes 3760136 | tf_op jit(solution)/shard_map/ppermute | solution.py:32
  138.2 31.7 %collective-permute-start.16 = (bf16[544,1152]{1,0:T(8,128)(2,1)}, bf16[544,1152]{1,0:T(8,128)(2,1)}, u32[]{:S(2)}, u32[]{:S(2)}) collective-permute-start(bf16[544,1152]{1,0:T(8,128)(2,1)} %slice.91.refs_7_), channel_id=1, source_target_pairs={{0,4},{4,0},{1,5},{5,1},{2,6},{6,2},{3,7},{7,3},{8,12},{12,8},{9,1... | collective-permute-start | bytes 3760136 | tf_op jit(solution)/shard_map/ppermute | solution.py:36
  141.4 31.9 %collective-permute-start.10 = (bf16[1088,1152]{1,0:T(8,128)(2,1)S(1)}, bf16[1088,1152]{1,0:T(8,128)(2,1)S(1)}, u32[]{:S(2)}, u32[]{:S(2)}) collective-permute-start(bf16[1088,1152]{1,0:T(8,128)(2,1)S(1)} %bitcast.64), channel_id=1, source_target_pairs={{0,1},{1,0},{2,3},{3,2},{4,5},{5,4},{6,7},{7,6},{8,9},{9,8},{10,11... | collective-permute-start | bytes 7520264 | tf_op jit(solution)/shard_map/ppermute | solution.py:27
  141.5 35.8 %collective-permute-start.15 = (bf16[1088,1152]{1,0:T(8,128)(2,1)}, bf16[1088,1152]{1,0:T(8,128)(2,1)S(1)}, u32[]{:S(2)}, u32[]{:S(2)}) collective-permute-start(bf16[1088,1152]{1,0:T(8,128)(2,1)} %bitcast.74), channel_id=1, source_target_pairs={{0,1},{1,0},{2,3},{3,2},{4,5},{5,4},{6,7},{7,6},{8,9},{9,8},{10,11... | collective-permute-start | bytes 7520264 | tf_op jit(solution)/shard_map/ppermute | solution.py:27
  169.8 10.7 %collective-permute-start.14 = (bf16[1088,1152]{1,0:T(8,128)(2,1)S(1)}, bf16[1088,1152]{1,0:T(8,128)(2,1)S(1)}, u32[]{:S(2)}, u32[]{:S(2)}) collective-permute-start(bf16[1088,1152]{1,0:T(8,128)(2,1)S(1)} %bitcast.67), channel_id=1, source_target_pairs={{0,1},{1,0},{2,3},{3,2},{4,5},{5,4},{6,7},{7,6},{8,9},{9,8},{10,11... | collective-permute-start | bytes 7520264 | tf_op jit(solution)/shard_map/ppermute | solution.py:27
  173.0 11.4 %collective-permute-start.17 = (bf16[1088,1152]{1,0:T(8,128)(2,1)S(1)}, bf16[1088,1152]{1,0:T(8,128)(2,1)S(1)}, u32[]{:S(2)}, u32[]{:S(2)}) collective-permute-start(bf16[1088,1152]{1,0:T(8,128)(2,1)S(1)} %bitcast.80), channel_id=1, source_target_pairs={{0,1},{1,0},{2,3},{3,2},{4,5},{5,4},{6,7},{7,6},{8,9},{9,8},{10,11... | collective-permute-start | bytes 7520264 | tf_op jit(solution)/shard_map/ppermute | solution.py:27
  187.6 22.0 %collective-permute-start.18 = (bf16[368,1152]{1,0:T(8,128)(2,1)S(1)}, bf16[368,1152]{1,0:T(8,128)(2,1)S(1)}, u32[]{:S(2)}, u32[]{:S(2)}) collective-permute-start(bf16[368,1152]{1,0:T(8,128)(2,1)S(1)} %feed_down.3.refs_12_), channel_id=1, source_target_pairs={{0,8},{8,16},{16,24},{1,9},{9,17},{17,25},{2,10},{10,18},{18,26},{... | collective-permute-start | bytes 2543624 | tf_op jit(solution)/shard_map/ppermute | solution.py:48
  239.0 22.4 %collective-permute-start.20 = (bf16[368,1152]{1,0:T(8,128)(2,1)}, bf16[368,1152]{1,0:T(8,128)(2,1)S(1)}, u32[]{:S(2)}, u32[]{:S(2)}) collective-permute-start(bf16[368,1152]{1,0:T(8,128)(2,1)} %layer_mid.2), channel_id=1, source_target_pairs={{0,8},{8,16},{16,24},{1,9},{9,17},{17,25},{2,10},{10,18},{18,26},{... | collective-permute-start | bytes 2543624 | tf_op jit(solution)/shard_map/ppermute | solution.py:48
  290.4 23.0 %collective-permute-start.22 = (bf16[368,1152]{1,0:T(8,128)(2,1)}, bf16[368,1152]{1,0:T(8,128)(2,1)S(1)}, u32[]{:S(2)}, u32[]{:S(2)}) collective-permute-start(bf16[368,1152]{1,0:T(8,128)(2,1)} %layer_mid.3), channel_id=1, source_target_pairs={{0,8},{8,16},{16,24},{1,9},{9,17},{17,25},{2,10},{10,18},{18,26},{... | collective-permute-start | bytes 2543624 | tf_op jit(solution)/shard_map/ppermute | solution.py:48
  314.3 28.1 %collective-permute-start.24 = (bf16[184,1152]{1,0:T(8,128)(2,1)S(1)}, bf16[184,1152]{1,0:T(8,128)(2,1)S(1)}, u32[]{:S(2)}, u32[]{:S(2)}) collective-permute-start(bf16[184,1152]{1,0:T(8,128)(2,1)S(1)} %pad.9), channel_id=1, source_target_pairs={{0,2},{1,3},{2,0},{3,1},{4,6},{5,7},{6,4},{7,5},{8,10},{9,11},{10,... | collective-permute-start | bytes 1271816 | tf_op jit(solution)/shard_map/ppermute | solution.py:32
  391.8 23.6 %collective-permute-start.27 = (bf16[368,1152]{1,0:T(8,128)(2,1)S(1)}, bf16[368,1152]{1,0:T(8,128)(2,1)S(1)}, u32[]{:S(2)}, u32[]{:S(2)}) collective-permute-start(bf16[368,1152]{1,0:T(8,128)(2,1)S(1)} %qkv_back.4), channel_id=1, source_target_pairs={{8,0},{16,8},{24,16},{9,1},{17,9},{25,17},{10,2},{18,10},{26,18},{... | collective-permute-start | bytes 2543624 | tf_op jit(solution)/shard_map/ppermute | solution.py:48
  393.6 12.7 %collective-permute-start.25 = (bf16[184,1152]{1,0:T(8,128)(2,1)S(1)}, bf16[184,1152]{1,0:T(8,128)(2,1)S(1)}, u32[]{:S(2)}, u32[]{:S(2)}) collective-permute-start(bf16[184,1152]{1,0:T(8,128)(2,1)S(1)} %slice.99), channel_id=1, source_target_pairs={{0,2},{1,3},{2,0},{3,1},{4,6},{5,7},{6,4},{7,5},{8,10},{9,11},{10,... | collective-permute-start | bytes 1271816 | tf_op jit(solution)/shard_map/ppermute | solution.py:32
  394.2 35.5 %collective-permute-start.28 = (bf16[192,1152]{1,0:T(8,128)(2,1)S(1)}, bf16[192,1152]{1,0:T(8,128)(2,1)S(1)}, u32[]{:S(2)}, u32[]{:S(2)}) collective-permute-start(bf16[192,1152]{1,0:T(8,128)(2,1)S(1)} %slice.73), channel_id=1, source_target_pairs={{0,2},{1,3},{2,0},{3,1},{4,6},{5,7},{6,4},{7,5},{8,10},{9,11},{10,... | collective-permute-start | bytes 1327112 | tf_op jit(solution)/shard_map/ppermute | solution.py:32
  396.5 33.1 %collective-permute-start.29 = (bf16[176,1152]{1,0:T(8,128)(2,1)}, bf16[176,1152]{1,0:T(8,128)(2,1)S(1)}, u32[]{:S(2)}, u32[]{:S(2)}) collective-permute-start(bf16[176,1152]{1,0:T(8,128)(2,1)} %slice.74), channel_id=1, source_target_pairs={{0,4},{4,0},{1,5},{5,1},{2,6},{6,2},{3,7},{7,3},{8,12},{12,8},{9,1... | collective-permute-start | bytes 1216520 | tf_op jit(solution)/shard_map/ppermute | solution.py:36
  453.6 22.8 %collective-permute-start.31 = (bf16[368,1152]{1,0:T(8,128)(2,1)S(1)}, bf16[368,1152]{1,0:T(8,128)(2,1)S(1)}, u32[]{:S(2)}, u32[]{:S(2)}) collective-permute-start(bf16[368,1152]{1,0:T(8,128)(2,1)S(1)} %qkv_back.5), channel_id=1, source_target_pairs={{8,0},{16,8},{24,16},{9,1},{17,9},{25,17},{10,2},{18,10},{26,18},{... | collective-permute-start | bytes 2543624 | tf_op jit(solution)/shard_map/ppermute | solution.py:48
  454.9 13.2 %collective-permute-start.33 = (bf16[192,1152]{1,0:T(8,128)(2,1)S(1)}, bf16[192,1152]{1,0:T(8,128)(2,1)S(1)}, u32[]{:S(2)}, u32[]{:S(2)}) collective-permute-start(bf16[192,1152]{1,0:T(8,128)(2,1)S(1)} %slice.73), channel_id=1, source_target_pairs={{0,4},{4,0},{1,5},{5,1},{2,6},{6,2},{3,7},{7,3},{8,12},{12,8},{9,1... | collective-permute-start | bytes 1327112 | tf_op jit(solution)/shard_map/ppermute | solution.py:36
  455.6 12.5 %collective-permute-start.32 = (bf16[176,1152]{1,0:T(8,128)(2,1)}, bf16[176,1152]{1,0:T(8,128)(2,1)S(1)}, u32[]{:S(2)}, u32[]{:S(2)}) collective-permute-start(bf16[176,1152]{1,0:T(8,128)(2,1)} %slice.74), channel_id=1, source_target_pairs={{0,2},{1,3},{2,0},{3,1},{4,6},{5,7},{6,4},{7,5},{8,10},{9,11},{10,... | collective-permute-start | bytes 1216520 | tf_op jit(solution)/shard_map/ppermute | solution.py:32
  456.7 40.0 %collective-permute-start.34 = (bf16[192,1152]{1,0:T(8,128)(2,1)S(1)}, bf16[192,1152]{1,0:T(8,128)(2,1)S(1)}, u32[]{:S(2)}, u32[]{:S(2)}) collective-permute-start(bf16[192,1152]{1,0:T(8,128)(2,1)S(1)} %collective-permute-done.28.refs_7_.refs_1_), channel_id=1, source_target_pairs={{0,4},{4,0},{1,5},{5,1},{2,6},{6,2},{3,7},{7,3},{8,12},{12,8},{9,1... | collective-permute-start | bytes 1327112 | tf_op jit(solution)/shard_map/ppermute | solution.py:36
  457.5 38.5 %collective-permute-start.35 = (bf16[176,1152]{1,0:T(8,128)(2,1)S(1)}, bf16[176,1152]{1,0:T(8,128)(2,1)S(1)}, u32[]{:S(2)}, u32[]{:S(2)}) collective-permute-start(bf16[176,1152]{1,0:T(8,128)(2,1)S(1)} %collective-permute-done.29.refs_8_.refs_4_), channel_id=1, source_target_pairs={{0,2},{1,3},{2,0},{3,1},{4,6},{5,7},{6,4},{7,5},{8,10},{9,11},{10,... | collective-permute-start | bytes 1216520 | tf_op jit(solution)/shard_map/ppermute | solution.py:32
  520.9 7.6 %collective-permute-start.38 = (bf16[1472,1152]{1,0:T(8,128)(2,1)}, bf16[1472,1152]{1,0:T(8,128)(2,1)}, u32[]{:S(2)}, u32[]{:S(2)}) collective-permute-start(bf16[1472,1152]{1,0:T(8,128)(2,1)} %join_normed.1.refs_8_.refs_0_.refs_3_), channel_id=1, source_target_pairs={{0,1},{1,0},{2,3},{3,2},{4,5},{5,4},{6,7},{7,6},{8,9},{9,8},{10,11... | collective-permute-start | bytes 10174472 | tf_op jit(solution)/shard_map/ppermute | solution.py:27
  521.4 26.5 %collective-permute-start.37 = (bf16[368,1152]{1,0:T(8,128)(2,1)}, bf16[368,1152]{1,0:T(8,128)(2,1)}, u32[]{:S(2)}, u32[]{:S(2)}) collective-permute-start(bf16[368,1152]{1,0:T(8,128)(2,1)} %qkv_back.6), channel_id=1, source_target_pairs={{8,0},{16,8},{24,16},{9,1},{17,9},{25,17},{10,2},{18,10},{26,18},{... | collective-permute-start | bytes 2543624 | tf_op jit(solution)/shard_map/ppermute | solution.py:48
  549.6 23.1 %collective-permute-start.40 = (bf16[192,1152]{1,0:T(8,128)(2,1)S(1)}, bf16[192,1152]{1,0:T(8,128)(2,1)S(1)}, u32[]{:S(2)}, u32[]{:S(2)}) collective-permute-start(bf16[192,1152]{1,0:T(8,128)(2,1)S(1)} %slice.93), channel_id=1, source_target_pairs={{0,2},{1,3},{2,0},{3,1},{4,6},{5,7},{6,4},{7,5},{8,10},{9,11},{10,... | collective-permute-start | bytes 1327112 | tf_op jit(solution)/shard_map/ppermute | solution.py:32
  550.2 22.5 %collective-permute-start.41 = (bf16[176,1152]{1,0:T(8,128)(2,1)S(1)}, bf16[176,1152]{1,0:T(8,128)(2,1)S(1)}, u32[]{:S(2)}, u32[]{:S(2)}) collective-permute-start(bf16[176,1152]{1,0:T(8,128)(2,1)S(1)} %slice.94), channel_id=1, source_target_pairs={{0,4},{4,0},{1,5},{5,1},{2,6},{6,2},{3,7},{7,3},{8,12},{12,8},{9,1... | collective-permute-start | bytes 1216520 | tf_op jit(solution)/shard_map/ppermute | solution.py:36
  586.4 13.2 %collective-permute-start.42 = (bf16[368,2304]{1,0:T(8,128)(2,1)S(1)}, bf16[368,2304]{1,0:T(8,128)(2,1)S(1)}, u32[]{:S(2)}, u32[]{:S(2)}) collective-permute-start(bf16[368,2304]{1,0:T(8,128)(2,1)S(1)} %get-tuple-element.128), channel_id=1, source_target_pairs={{0,1},{1,0},{2,3},{3,2},{4,5},{5,4},{6,7},{7,6},{8,9},{9,8},{10,11... | collective-permute-start | bytes 5087240 | tf_op jit(solution)/shard_map/ppermute | solution.py:27
  587.0 12.6 %collective-permute-start.45 = (bf16[192,1152]{1,0:T(8,128)(2,1)S(1)}, bf16[192,1152]{1,0:T(8,128)(2,1)S(1)}, u32[]{:S(2)}, u32[]{:S(2)}) collective-permute-start(bf16[192,1152]{1,0:T(8,128)(2,1)S(1)} %collective-permute-done.40.refs_7_.refs_1_), channel_id=1, source_target_pairs={{0,4},{4,0},{1,5},{5,1},{2,6},{6,2},{3,7},{7,3},{8,12},{12,8},{9,1... | collective-permute-start | bytes 1327112 | tf_op jit(solution)/shard_map/ppermute | solution.py:36
  587.8 11.8 %collective-permute-start.46 = (bf16[176,1152]{1,0:T(8,128)(2,1)S(1)}, bf16[176,1152]{1,0:T(8,128)(2,1)S(1)}, u32[]{:S(2)}, u32[]{:S(2)}) collective-permute-start(bf16[176,1152]{1,0:T(8,128)(2,1)S(1)} %collective-permute-done.41.refs_8_.refs_4_), channel_id=1, source_target_pairs={{0,2},{1,3},{2,0},{3,1},{4,6},{5,7},{6,4},{7,5},{8,10},{9,11},{10,... | collective-permute-start | bytes 1216520 | tf_op jit(solution)/shard_map/ppermute | solution.py:32
  605.6 12.9 %collective-permute-start.49 = (bf16[192,1152]{1,0:T(8,128)(2,1)S(1)}, bf16[192,1152]{1,0:T(8,128)(2,1)S(1)}, u32[]{:S(2)}, u32[]{:S(2)}) collective-permute-start(bf16[192,1152]{1,0:T(8,128)(2,1)S(1)} %slice.83), channel_id=1, source_target_pairs={{0,4},{4,0},{1,5},{5,1},{2,6},{6,2},{3,7},{7,3},{8,12},{12,8},{9,1... | collective-permute-start | bytes 1327112 | tf_op jit(solution)/shard_map/ppermute | solution.py:36
  606.9 11.6 %collective-permute-start.48 = (bf16[176,1152]{1,0:T(8,128)(2,1)S(1)}, bf16[176,1152]{1,0:T(8,128)(2,1)S(1)}, u32[]{:S(2)}, u32[]{:S(2)}) collective-permute-start(bf16[176,1152]{1,0:T(8,128)(2,1)S(1)} %slice.82), channel_id=1, source_target_pairs={{0,2},{1,3},{2,0},{3,1},{4,6},{5,7},{6,4},{7,5},{8,10},{9,11},{10,... | collective-permute-start | bytes 1216520 | tf_op jit(solution)/shard_map/ppermute | solution.py:32
  618.8 30.9 %collective-permute-start.55 = (bf16[448,1152]{1,0:T(8,128)(2,1)S(1)}, bf16[448,1152]{1,0:T(8,128)(2,1)S(1)}, u32[]{:S(2)}, u32[]{:S(2)}) collective-permute-start(bf16[448,1152]{1,0:T(8,128)(2,1)S(1)} %get-tuple-element.140), channel_id=1, source_target_pairs={{0,2},{1,3},{2,0},{3,1},{4,6},{5,7},{6,4},{7,5},{8,10},{9,11},{10,... | collective-permute-start | bytes 3096584 | tf_op jit(solution)/shard_map/ppermute | solution.py:32
  620.1 28.2 %collective-permute-start.56 = (bf16[416,1152]{1,0:T(8,128)(2,1)S(1)}, bf16[416,1152]{1,0:T(8,128)(2,1)S(1)}, u32[]{:S(2)}, u32[]{:S(2)}) collective-permute-start(bf16[416,1152]{1,0:T(8,128)(2,1)S(1)} %get-tuple-element.141), channel_id=1, source_target_pairs={{0,4},{4,0},{1,5},{5,1},{2,6},{6,2},{3,7},{7,3},{8,12},{12,8},{9,1... | collective-permute-start | bytes 2875400 | tf_op jit(solution)/shard_map/ppermute | solution.py:36
  621.2 32.3 %collective-permute-start.52 = (f32[2,1152]{1,0:T(2,128)S(1)}, f32[2,1152]{1,0:T(2,128)S(1)}, u32[]{:S(2)}, u32[]{:S(2)}) collective-permute-start(f32[2,1152]{1,0:T(2,128)S(1)} %pad_maximum_fusion.3), channel_id=1, source_target_pairs={{0,2},{1,3},{2,0},{3,1},{4,6},{5,7},{6,4},{7,5},{8,10},{9,11},{10,... | collective-permute-start | bytes 27656 | tf_op jit(solution)/shard_map/ppermute | solution.py:32
  621.9 32.3 %collective-permute-start.53 = (f32[2,1152]{1,0:T(2,128)S(1)}, f32[2,1152]{1,0:T(2,128)S(1)}, u32[]{:S(2)}, u32[]{:S(2)}) collective-permute-start(f32[2,1152]{1,0:T(2,128)S(1)} %pad_maximum_fusion.3), channel_id=1, source_target_pairs={{0,4},{4,0},{1,5},{5,1},{2,6},{6,2},{3,7},{7,3},{8,12},{12,8},{9,1... | collective-permute-start | bytes 27656 | tf_op jit(solution)/shard_map/ppermute | solution.py:36
  624.8 30.5 %collective-permute-start.54 = (f32[2,1152]{1,0:T(2,128)S(1)}, f32[2,1152]{1,0:T(2,128)S(1)}, u32[]{:S(2)}, u32[]{:S(2)}) collective-permute-start(f32[2,1152]{1,0:T(2,128)S(1)} %pad_maximum_fusion.3), channel_id=1, source_target_pairs={{0,6},{1,7},{2,4},{3,5},{4,2},{5,3},{6,0},{7,1},{8,14},{9,15},{10,... | collective-permute-start | bytes 27656 | tf_op jit(solution)/shard_map/ppermute | solution.py:42
  648.3 11.7 %collective-permute-start.59 = (bf16[160,1152]{1,0:T(8,128)(2,1)}, bf16[160,1152]{1,0:T(8,128)(2,1)S(1)}, u32[]{:S(2)}, u32[]{:S(2)}) collective-permute-start(bf16[160,1152]{1,0:T(8,128)(2,1)} %get-tuple-element.149), channel_id=1, source_target_pairs={{0,2},{1,3},{2,0},{3,1},{4,6},{5,7},{6,4},{7,5},{8,10},{9,11},{10,... | collective-permute-start | bytes 1105928 | tf_op jit(solution)/shard_map/ppermute | solution.py:32
  649.7 9.9 %collective-permute-start.60 = (bf16[128,1152]{1,0:T(8,128)(2,1)S(1)}, bf16[128,1152]{1,0:T(8,128)(2,1)S(1)}, u32[]{:S(2)}, u32[]{:S(2)}) collective-permute-start(bf16[128,1152]{1,0:T(8,128)(2,1)S(1)} %get-tuple-element.150), channel_id=1, source_target_pairs={{0,4},{4,0},{1,5},{5,1},{2,6},{6,2},{3,7},{7,3},{8,12},{12,8},{9,1... | collective-permute-start | bytes 884744 | tf_op jit(solution)/shard_map/ppermute | solution.py:36
  653.5 29.3 %collective-permute-start.47 = (bf16[184,1152]{1,0:T(8,128)(2,1)S(1)}, bf16[184,1152]{1,0:T(8,128)(2,1)S(1)}, u32[]{:S(2)}, u32[]{:S(2)}) collective-permute-start(bf16[184,1152]{1,0:T(8,128)(2,1)S(1)} %slice.98), channel_id=1, source_target_pairs={{0,2},{1,3},{2,0},{3,1},{4,6},{5,7},{6,4},{7,5},{8,10},{9,11},{10,... | collective-permute-start | bytes 1271816 | tf_op jit(solution)/shard_map/ppermute | solution.py:32
  654.2 35.5 %collective-permute-start.57 = (bf16[224,1152]{1,0:T(8,128)(2,1)}, bf16[224,1152]{1,0:T(8,128)(2,1)}, u32[]{:S(2)}, u32[]{:S(2)}) collective-permute-start(bf16[224,1152]{1,0:T(8,128)(2,1)} %get-tuple-element.144), channel_id=1, source_target_pairs={{0,4},{4,0},{1,5},{5,1},{2,6},{6,2},{3,7},{7,3},{8,12},{12,8},{9,1... | collective-permute-start | bytes 1548296 | tf_op jit(solution)/shard_map/ppermute | solution.py:36
  655.3 34.4 %collective-permute-start.58 = (bf16[208,1152]{1,0:T(8,128)(2,1)}, bf16[208,1152]{1,0:T(8,128)(2,1)}, u32[]{:S(2)}, u32[]{:S(2)}) collective-permute-start(bf16[208,1152]{1,0:T(8,128)(2,1)} %get-tuple-element.145), channel_id=1, source_target_pairs={{0,2},{1,3},{2,0},{3,1},{4,6},{5,7},{6,4},{7,5},{8,10},{9,11},{10,... | collective-permute-start | bytes 1437704 | tf_op jit(solution)/shard_map/ppermute | solution.py:32
  661.9 26.7 %collective-permute-start.61 = (bf16[80,1152]{1,0:T(8,128)(2,1)S(1)}, bf16[80,1152]{1,0:T(8,128)(2,1)S(1)}, u32[]{:S(2)}, u32[]{:S(2)}) collective-permute-start(bf16[80,1152]{1,0:T(8,128)(2,1)S(1)} %get-tuple-element.153), channel_id=1, source_target_pairs={{0,4},{4,0},{1,5},{5,1},{2,6},{6,2},{3,7},{7,3},{8,12},{12,8},{9,1... | collective-permute-start | bytes 552968 | tf_op jit(solution)/shard_map/ppermute | solution.py:36
  662.9 25.7 %collective-permute-start.62 = (bf16[64,1152]{1,0:T(8,128)(2,1)S(1)}, bf16[64,1152]{1,0:T(8,128)(2,1)S(1)}, u32[]{:S(2)}, u32[]{:S(2)}) collective-permute-start(bf16[64,1152]{1,0:T(8,128)(2,1)S(1)} %get-tuple-element.154), channel_id=1, source_target_pairs={{0,2},{1,3},{2,0},{3,1},{4,6},{5,7},{6,4},{7,5},{8,10},{9,11},{10,... | collective-permute-start | bytes 442376 | tf_op jit(solution)/shard_map/ppermute | solution.py:32
  (131 other events, 2427.7 us)

commit v4 on v3

--- a/solution.py
+++ b/solution.py
@@ -1,3 +1,5 @@
+import math
+
 import jax
 import jax.numpy as jnp
 from jax import lax
@@ -150,7 +152,7 @@
 
 
 def call(kernel, name, outs, ins, scratch, args, flops, limit=60, after=(), cost=None):
-    moved = sum(a.size * a.dtype.itemsize for a in args) + sum(o.size * o.dtype.itemsize for o in outs)
+    moved = sum(4 * math.prod(a.shape) for a in (*args, *outs))
     return pl.pallas_call(
         past(kernel, len(args), after),
         out_shape=tuple(outs),
@@ -170,12 +172,19 @@
     hu = (units + 31) // 32 * 16
 
     def kernel(flag_ref, *refs):
-        pair_ref, out, give_ref, mine_ref = refs[6:]
+        pair_ref, out, give_ref, mine_ref, *held, sem = refs[6:]
+        copies = [pltpu.make_async_copy(a, b, sem.at[i]) for i, (a, b) in enumerate(zip(refs[:6], held))]
+        for copy in copies:
+            copy.start()
+        refs = held
         got = pair_ref.shape[0]
         first = flag_ref[3] == 0
         one, two = pair_ref[:, 0, :], pair_ref[:, 1, :]
         mine_ref[...] = jnp.zeros_like(mine_ref)
         mine_ref[:got] = jnp.where(first, one, two)
+        give_ref[...] = jnp.zeros_like(give_ref)
+        give_ref[:got] = low16(jnp.where(first, two, one))
+        wait_all(copies)
         for i, ref in enumerate(refs[:4]):
             out[i * h : (i + 1) * h, :part] = ref[:h, :]
             out[i * h : (i + 1) * h, part:] = ref[h:, :]
@@ -185,13 +194,13 @@
             out[base : base + hu, :part] = rows[:hu]
             out[base : base + units - hu, part:] = rows[hu:]
             out[base + units - hu : base + hu, part:] = jnp.zeros((2 * hu - units, part), BF)
-        give_ref[...] = jnp.zeros_like(give_ref)
-        give_ref[:got] = low16(jnp.where(first, two, one))
 
     total = 4 * h + 2 * hu
     width = pair.shape[2]
     outs = [shape((total, 2 * part), BF), shape((quarter, width), BF), shape((quarter, width), F32)]
-    got = call(kernel, "pack", outs, [SMEM] + [VMEM] * 7, [], [flags, *heads, up, down, pair], 0, 30)
+    scratch = [pltpu.VMEM(a.shape, BF) for a in (*heads, up, down)] + [pltpu.SemaphoreType.DMA((6,))]
+    args = [flags, *[in_hbm(a) for a in (*heads, up, down)], pair]
+    got = call(kernel, "pack", outs, [SMEM] + [ANY] * 6 + [VMEM], scratch, args, 0, 34)
     return *got, (0, 4 * h, 4 * h + hu), hu
 
 
@@ -750,7 +759,7 @@
 
     scratch = [pltpu.VMEM((2, block, width), BF)] * kinds + [pltpu.VMEM((2, block, n), BF)]
     scratch.append(pltpu.SemaphoreType.DMA((kinds + 1, 2)))
-    args = [flags, *([w_down] if with_w else []), in_hbm(saved), *flat]
+    args = [flags, *([w_down] if with_w else []), in_hbm(saved), *[in_hbm(a) for a in flat]]
     ins = [SMEM] + [VMEM] * with_w + [ANY] * (1 + len(flat))
     flops = (4 if with_w else 2) * total * len(sides) * width * n
     return call(kernel, name, [shape((part, units), F32)], ins, scratch, args, flops, 40, after, 0.2)[0]
@@ -766,7 +775,7 @@
             at += ref.shape[0]
 
     rows = sum(a.shape[0] for a in pieces)
-    return call(kernel, name, [shape((rows, pieces[0].shape[1]), BF)], [VMEM] * n, [], list(pieces), 0, 16, after)[0]
+    return call(kernel, name, [pltpu.HBM((rows, pieces[0].shape[1]), BF)], [VMEM] * n, [], list(pieces), 0, 16, after)[0]
 
 
 def plane_blocks(name, flags, left, right, after=()):

time: 704 us -> 695 us (0.987)
  local copies, waits for them, and re-layouts: 55.9 us -> 45.7 us
    unnamed x232 -> x220, local copies, waits for them, and re-layouts: 45.4 us -> 35.2 us
where the time goes in v4:
time: 695 us; the launch traced here: 685 us
  Pallas kernels  368 us (53%)
  waiting for transfers between devices  202 us (29%)
  starting transfers between devices  62.6 us (9%)
  local copies, waits for them, and re-layouts  45.7 us (7%)
    pallas_call x40, Pallas kernels, call(): pl.pallas_call(past(kernel, len(args), after), out_shape=tuple(outs), in_...  339 us
    ppermute x15, waiting for transfers between devices, swap_y(): return lax.ppermute(a, 'dp', [(0, 1), (1, 0)])  84.4 us
    ppermute x6, waiting for transfers between devices, shift(): return lax.ppermute(a, 'section', pairs)  61 us
    unnamed x220, local copies, waits for them, and re-layouts  35.2 us
    ppermute x19, waiting for transfers between devices, swap_x(): return lax.ppermute(a, 'tensor', [(i, i ^ 2) for i in range(n)])  33.2 us
    ppermute x22, waiting for transfers between devices, swap_core(): return lax.ppermute(a, 'tensor', [(i, i ^ 1) for i in range(n)])  23.1 us
    ppermute x19, starting transfers between devices, swap_x(): return lax.ppermute(a, 'tensor', [(i, i ^ 2) for i in range(n)])  22.8 us
    pallas_call x1, Pallas kernels, unit_forward(): pl.pallas_call(past(kernel, 3, after), grid=(2 * half,), in_specs=[*halve...  17.7 us
  transfers between devices with their start and end apart: 64, of which 25 were waited for; matrix products, arithmetic and copies ran while one was open for 2% of the time, Pallas kernels for 30%

profile of v4, /device:TPU:0, one launch (start us, length us, event | category | flops | bytes accessed | tf_op | source)
XLA Modules:
  0.0 685.1 jit_solution(1843294864989485908)
XLA Ops:
  2.3 4.3 pack.1
  11.2 81.4 %collective-permute-done.4.refs_2_ = bf16[1664,1152]{1,0:T(8,128)(2,1)S(1)} collective-permute-done((bf16[1664,1152]{1,0:T(8,128)(2,1)S(1)}, bf16[1664,1152]{1,0:T(8,128)(2,1)S(1)}, u32[]{:S(2)}, u32[]{:S(2)}) %collective-permute-start.4) | collective-permute-done | bytes 3833888 | tf_op jit(solution)/shard_map/ppermute | solution.py:38
  96.0 4.4 heads_near.1.refs_3_.refs_5_.refs_0_
  106.5 3.3 slice.90.refs_6_
  112.0 4.3 heads_far.1.refs_6_.refs_1_
  123.0 7.2 %collective-permute-done = f32[2,144]{1,0:T(2,128)S(1)} collective-permute-done((f32[2,144]{1,0:T(2,128)S(1)}, f32[2,144]{1,0:T(2,128)S(1)}, u32[]{:S(2)}, u32[]{:S(2)}) %collective-permute-start) | collective-permute-done | bytes 1184 | tf_op jit(solution)/shard_map/ppermute | solution.py:34
  136.0 19.4 %layer_first.1 = (f32[368,1152]{1,0:T(8,128)S(1)}, bf16[368,1152]{1,0:T(8,128)(2,1)S(1)}) custom-call(s32[4]{0:T(128)S(1)} %pad_add_fusion.refs_0_.flag_ref, f32[8,736]{1,0:T(8,128)S(1)} %broadcast_in_dim.43.refs_1_.refs_0_.refs_2_.refs_6_, f32[2,1152]{1,0:T(2,128)S(1)} %maximum_select_fusion.refs_2_.refs_1_.refs_4_, ...), custom_call_target="tpu_custom_call" | custom-call | flops 10298064 | bytes 28049 | tf_op jit(solution)/shard_map/layer_first/pallas_call | solution.py:156
  155.5 5.2 collective-permute-done.11.refs_2_
  168.1 4.3 feed_up.2.refs_1_
  175.5 3.9 feed_up.3.refs_1_
  182.6 3.7 collective-permute-start.18
  186.3 11.3 %settle.1 = (bf16[4608,1152]{1,0:T(8,128)(2,1)S(1)}, bf16[4352,1152]{1,0:T(8,128)(2,1)S(1)}, bf16[4352,1152]{1,0:T(8,128)(2,1)S(1)}, f32[8,128]{1,0:T(8,128)}) custom-call(s32[4]{0:T(128)} %copy-done.80, bf16[4,288,1152]{2,1,0:T(8,128)(2,1)} %heads_near.1.refs_3_.refs_5_.refs_0_, bf16[4,288,1152]{2,1,0:T(8,128)(2,1)} %heads_far.1.refs_6_.refs_1_, ...), custom_call_target="tpu_custom_call" | custom-call | bytes 6291456 | tf_op jit(solution)/shard_map/settle/pallas_call | solution.py:368
  197.7 6.8 collective-permute-done.18.refs_5_
  208.3 25.5 %layer_mid.2 = bf16[368,1152]{1,0:T(8,128)(2,1)} custom-call(f32[8,736]{1,0:T(8,128)} %copy-done.62, f32[2,1152]{1,0:T(2,128)} %copy-done.64, bf16[4608,1152]{1,0:T(8,128)(2,1)S(1)} %get-tuple-element.87.refs_2_.refs_5_.refs_7_.refs_4_, bf16[4352,1152]{1,0:T(8,128)(2,1)S(1)} %get-tuple-element.90.refs_3_.refs_6_, ...), custom_call_target="tpu_custom_call" | custom-call | flops 1767794304 | bytes 6646169 | tf_op jit(solution)/shard_map/layer_mid/pallas_call | solution.py:156
  233.8 4.2 collective-permute-start.20
  238.1 18.3 %collective-permute-done.20.refs_5_.refs_7_ = bf16[368,1152]{1,0:T(8,128)(2,1)S(1)} collective-permute-done((bf16[368,1152]{1,0:T(8,128)(2,1)}, bf16[368,1152]{1,0:T(8,128)(2,1)S(1)}, u32[]{:S(2)}, u32[]{:S(2)}) %collective-permute-start.20) | collective-permute-done | bytes 847904 | tf_op jit(solution)/shard_map/ppermute | solution.py:50
  259.7 25.5 %layer_mid.3 = bf16[368,1152]{1,0:T(8,128)(2,1)} custom-call(f32[8,736]{1,0:T(8,128)} %copy-done.62, f32[2,1152]{1,0:T(2,128)} %copy-done.64, bf16[4608,1152]{1,0:T(8,128)(2,1)S(1)} %get-tuple-element.87.refs_2_.refs_5_.refs_7_.refs_4_, bf16[4352,1152]{1,0:T(8,128)(2,1)S(1)} %get-tuple-element.90.refs_3_.refs_6_, ...), custom_call_target="tpu_custom_call" | custom-call | flops 1767794304 | bytes 6646169 | tf_op jit(solution)/shard_map/layer_mid/pallas_call | solution.py:156
  285.1 4.3 collective-permute-start.22
  289.4 18.7 %collective-permute-done.22.refs_9_ = bf16[368,1152]{1,0:T(8,128)(2,1)S(1)} collective-permute-done((bf16[368,1152]{1,0:T(8,128)(2,1)}, bf16[368,1152]{1,0:T(8,128)(2,1)S(1)}, u32[]{:S(2)}, u32[]{:S(2)}) %collective-permute-start.22) | collective-permute-done | bytes 847904 | tf_op jit(solution)/shard_map/ppermute | solution.py:50
  312.4 4.0 copy-done.3
  316.4 8.9 %last_project.1 = (f32[368,1152]{1,0:T(8,128)S(1)}, bf16[368,1152]{1,0:T(8,128)(2,1)}, bf16[368,1152]{1,0:T(8,128)(2,1)S(1)}, bf16[736,2304]{1,0:T(8,128)(2,1)S(1)}) custom-call(s32[4]{0:T(128)S(1)} %copy-done.81, f32[2,1152]{1,0:T(2,128)S(1)} %copy-done.65, bf16[4608,1152]{1,0:T(8,128)(2,1)S(1)} %copy-done.3, f32[368,1152]{1,0:T(8,128)} %copy-done.39, ...), custom_call_target="tpu_custom_call" | custom-call | flops 488374272 | bytes 4667905 | tf_op jit(solution)/shard_map/last_project/pallas_call | solution.py:156
  325.3 10.8 %last_attention.1 = (bf16[368,1152]{1,0:T(8,128)(2,1)S(1)}, bf16[368,1152]{1,0:T(8,128)(2,1)S(1)}, f32[368,128]{1,0:T(8,128)S(1)}, f32[368,1152]{1,0:T(8,128)S(1)}, bf16[368,1152]{1,0:T(8,128)(2,1)S(1)}) custom-call(bf16[368,1152]{1,0:T(8,128)(2,1)S(1)} %get-tuple-element.93.refs_0_, bf16[736,2304]{1,0:T(8,128)(2,1)S(1)} %get-tuple-element.94.refs_1_, ...), custom_call_target="tpu_custom_call" | custom-call | flops 541432192 | bytes 3841228 | tf_op jit(solution)/shard_map/last_attention/pallas_call | solution.py:156
  337.3 4.5 copy-done.11
  341.8 22.6 %feed_turn.1 = (f32[368,1152]{1,0:T(8,128)}, bf16[368,4352]{1,0:T(8,128)(2,1)}, f32[368,1152]{1,0:T(8,128)}, bf16[368,1152]{1,0:T(8,128)(2,1)S(1)}, f32[368,1152]{1,0:T(8,128)}) custom-call(f32[368,1152]{1,0:T(8,128)} %copy-done.29, bf16[368,1152]{1,0:T(8,128)(2,1)S(1)} %get-tuple-element.97.refs_1_.refs_0_, f32[184,1152]{1,0:T(8,128)} %pad.8.refs_2_, ...), custom_call_target="tpu_custom_call" | custom-call | flops 1475975552 | bytes 7962726 | tf_op jit(solution)/shard_map/feed_turn/pallas_call | solution.py:156
  364.5 13.6 %attention_back.4 = (bf16[368,1152]{1,0:T(8,128)(2,1)S(1)}, bf16[368,2304]{1,0:T(8,128)(2,1)S(1)}, bf16[368,2304]{1,0:T(8,128)(2,1)S(1)}) custom-call(bf16[368,1152]{1,0:T(8,128)(2,1)S(1)} %get-tuple-element.93.refs_0_, bf16[736,2304]{1,0:T(8,128)(2,1)S(1)} %get-tuple-element.94.refs_1_, bf16[368,1152]{1,0:T(8,128)(2,1)S(1)} %get-tuple-element.101.refs_2_, ...), custom_call_target="tpu_custom_call" | custom-call | flops 1109393408 | bytes 2225664 | tf_op jit(solution)/shard_map/attention_back/pallas_call | solution.py:156
  378.4 3.4 collective-permute-done.26.refs_4_
  381.8 4.8 qkv_back.4
  392.1 9.1 %collective-permute-done.25.refs_2_.refs_11_ = bf16[184,1152]{1,0:T(8,128)(2,1)S(1)} collective-permute-done((bf16[184,1152]{1,0:T(8,128)(2,1)S(1)}, bf16[184,1152]{1,0:T(8,128)(2,1)S(1)}, u32[]{:S(2)}, u32[]{:S(2)}) %collective-permute-start.25) | collective-permute-done | bytes 423968 | tf_op jit(solution)/shard_map/ppermute | solution.py:34
  401.2 9.0 %collective-permute-done.27.refs_10_.refs_11_ = bf16[368,1152]{1,0:T(8,128)(2,1)S(1)} collective-permute-done((bf16[368,1152]{1,0:T(8,128)(2,1)S(1)}, bf16[368,1152]{1,0:T(8,128)(2,1)S(1)}, u32[]{:S(2)}, u32[]{:S(2)}) %collective-permute-start.27) | collective-permute-done | bytes 847904 | tf_op jit(solution)/shard_map/ppermute | solution.py:50
  410.2 14.1 %feed_back_mid.2 = (f32[368,1152]{1,0:T(8,128)S(1)}, bf16[368,1152]{1,0:T(8,128)(2,1)S(1)}) custom-call(s32[4]{0:T(128)S(1)} %copy-done.81, f32[2,1152]{1,0:T(2,128)S(1)} %copy-done.65, f32[368,1152]{1,0:T(8,128)S(1)} %copy-done.30, bf16[368,4352]{1,0:T(8,128)(2,1)S(1)} %copy-done.27, bf16[4608,1152]{1,0:T(8,128)(2,1)S(1)} %copy-done.4, ...), custom_call_target="tpu_custom_call" | custom-call | flops 835662656 | bytes 7454004 | tf_op jit(solution)/shard_map/feed_back_mid/pallas_call | solution.py:156
  424.4 13.6 %attention_back.5 = (bf16[368,1152]{1,0:T(8,128)(2,1)S(1)}, bf16[368,2304]{1,0:T(8,128)(2,1)S(1)}, bf16[368,2304]{1,0:T(8,128)(2,1)S(1)}) custom-call(bf16[368,1152]{1,0:T(8,128)(2,1)S(1)} %get-tuple-element.93.refs_0_, bf16[736,2304]{1,0:T(8,128)(2,1)S(1)} %copy-done.14, bf16[368,1152]{1,0:T(8,128)(2,1)S(1)} %get-tuple-element.109.refs_2_, ...), custom_call_target="tpu_custom_call" | custom-call | flops 1109393408 | bytes 2225664 | tf_op jit(solution)/shard_map/attention_back/pallas_call | solution.py:156
  438.1 3.6 collective-permute-done.30.refs_4_
  443.1 5.1 qkv_back.5
  455.8 6.9 %collective-permute-done.32.refs_12_.refs_2_ = bf16[176,1152]{1,0:T(8,128)(2,1)S(1)} collective-permute-done((bf16[176,1152]{1,0:T(8,128)(2,1)}, bf16[176,1152]{1,0:T(8,128)(2,1)S(1)}, u32[]{:S(2)}, u32[]{:S(2)}) %collective-permute-start.32) | collective-permute-done | bytes 405536 | tf_op jit(solution)/shard_map/ppermute | solution.py:34
  462.7 8.3 %collective-permute-done.31.refs_10_.refs_12_ = bf16[368,1152]{1,0:T(8,128)(2,1)S(1)} collective-permute-done((bf16[368,1152]{1,0:T(8,128)(2,1)S(1)}, bf16[368,1152]{1,0:T(8,128)(2,1)S(1)}, u32[]{:S(2)}, u32[]{:S(2)}) %collective-permute-start.31) | collective-permute-done | bytes 847904 | tf_op jit(solution)/shard_map/ppermute | solution.py:50
  472.5 18.0 %feed_back_mid.3 = (f32[368,1152]{1,0:T(8,128)S(1)}, bf16[368,1152]{1,0:T(8,128)(2,1)S(1)}) custom-call(s32[4]{0:T(128)S(1)} %copy-done.81, f32[2,1152]{1,0:T(2,128)S(1)} %copy-done.65, f32[368,1152]{1,0:T(8,128)S(1)} %copy-done.30, bf16[368,4352]{1,0:T(8,128)(2,1)} %get-tuple-element.99.refs_3_, bf16[4608,1152]{1,0:T(8,128)(2,1)S(1)} %copy-done.4, ...), custom_call_target="tpu_custom_call" | custom-call | flops 835662656 | bytes 7454004 | tf_op jit(solution)/shard_map/feed_back_mid/pallas_call | solution.py:156
  490.6 13.4 %attention_back.6 = (bf16[368,1152]{1,0:T(8,128)(2,1)S(1)}, bf16[368,2304]{1,0:T(8,128)(2,1)S(1)}, bf16[368,2304]{1,0:T(8,128)(2,1)S(1)}) custom-call(bf16[368,1152]{1,0:T(8,128)(2,1)S(1)} %get-tuple-element.93.refs_0_, bf16[736,2304]{1,0:T(8,128)(2,1)S(1)} %copy-done.14, bf16[368,1152]{1,0:T(8,128)(2,1)S(1)} %get-tuple-element.114.refs_2_, ...), custom_call_target="tpu_custom_call" | custom-call | flops 1109393408 | bytes 2225664 | tf_op jit(solution)/shard_map/attention_back/pallas_call | solution.py:156
  507.6 5.8 qkv_back.6
  517.5 3.2 collective-permute-done.39.refs_5_.refs_4_
  522.7 17.7 %unit_forward.1 = (bf16[2944,1088]{1,0:T(8,128)(2,1)}, bf16[2944,1088]{1,0:T(8,128)(2,1)}) custom-call(bf16[1472,1152]{1,0:T(8,128)(2,1)} %join_normed.1.refs_8_.refs_0_.refs_3_, bf16[1472,1152]{1,0:T(8,128)(2,1)} %collective-permute-done.38.refs_1_.refs_5_, bf16[1088,1152]{1,0:T(8,128)(2,1)S(1)} %bitcast.66, ...), custom_call_target="tpu_custom_call" | custom-call | flops 1033182912 | bytes 2034892 | tf_op jit(solution)/shard_map/unit_forward/pallas_call | solution.py:701
  544.1 3.8 copy-done.6
  548.0 17.6 %feed_back_last.1 = (f32[368,1152]{1,0:T(8,128)S(1)}, bf16[368,1152]{1,0:T(8,128)(2,1)S(1)}, bf16[368,1152]{1,0:T(8,128)(2,1)S(1)}, f32[1,1152]{1,0:T(1,128)S(1)}) custom-call(s32[4]{0:T(128)S(1)} %copy-done.81, f32[2,1152]{1,0:T(2,128)S(1)} %copy-done.65, f32[368,1152]{1,0:T(8,128)S(1)} %copy-done.31, bf16[368,4352]{1,0:T(8,128)(2,1)S(1)} %copy-done.28, ...), custom_call_target="tpu_custom_call" | custom-call | flops 835662656 | bytes 8132763 | tf_op jit(solution)/shard_map/feed_back_last/pallas_call | solution.py:156
  565.7 13.6 %attention_back.7 = (bf16[368,1152]{1,0:T(8,128)(2,1)S(1)}, bf16[368,2304]{1,0:T(8,128)(2,1)S(1)}, bf16[368,2304]{1,0:T(8,128)(2,1)S(1)}) custom-call(bf16[368,1152]{1,0:T(8,128)(2,1)S(1)} %copy-done.36, bf16[736,2304]{1,0:T(8,128)(2,1)S(1)} %copy-done.15, bf16[368,1152]{1,0:T(8,128)(2,1)S(1)} %get-tuple-element.125.refs_2_, ...), custom_call_target="tpu_custom_call" | custom-call | flops 1109393408 | bytes 2225664 | tf_op jit(solution)/shard_map/attention_back/pallas_call | solution.py:156
  586.0 4.8 output_grads.1
  592.5 5.8 qkv_back.7
  601.4 7.1 %qkv_grads.1 = (f32[864,576]{1,0:T(8,128)S(1)}, bf16[448,1152]{1,0:T(8,128)(2,1)S(1)}, bf16[416,1152]{1,0:T(8,128)(2,1)S(1)}, bf16[208,1152]{1,0:T(8,128)(2,1)S(1)}, bf16[224,1152]{1,0:T(8,128)(2,1)S(1)}) custom-call(s32[4]{0:T(128)S(1)} %copy-done.81, bf16[368,1728]{1,0:T(8,128)(2,1)S(1)} %get-tuple-element.134.refs_1_, ...), custom_call_target="tpu_custom_call" | custom-call | flops 293024576 | bytes 1644136 | tf_op jit(solution)/shard_map/qkv_grads/pallas_call | solution.py:156
  621.3 22.1 %up_grads.1.refs_4_ = f32[576,1076]{1,0:T(8,128)} custom-call(s32[4]{0:T(128)S(1)} %copy-done.81, bf16[1088,1152]{1,0:T(8,128)(2,1)S(1)} %bitcast.77, bf16[2944,1088]{1,0:T(8,128)(2,1)} %get-tuple-element.137.refs_2_, bf16[1472,1152]{1,0:T(8,128)(2,1)} %join_normed.1.refs_8_.refs_0_.refs_3_, bf16[1472,1152]{1,0:T(8,128)(2,1)} %join_dy.1.refs_4_.refs_2_, ...), custom_call_target="tpu_custom_call" | custom-call | flops 2951951104 | bytes 9487363 | tf_op jit(solution)/shard_map/up_grads/pallas_call | solution.py:156
  660.0 14.0 %down_grads.1.refs_3_.refs_5_ = f32[576,1076]{1,0:T(8,128)} custom-call(s32[4]{0:T(128)S(1)} %copy-done.81, bf16[2944,1088]{1,0:T(8,128)(2,1)} %get-tuple-element.124.refs_14_.refs_1_, bf16[1472,1152]{1,0:T(8,128)(2,1)} %join_dy.1.refs_4_.refs_2_, bf16[1472,1152]{1,0:T(8,128)(2,1)} %copy-done.86, f32[576,1076]{1,0:T(8,128)S(1)} %copy-done.23, ...), custom_call_target="tpu_custom_call" | custom-call | flops 1475975552 | bytes 5771472 | tf_op jit(solution)/shard_map/down_grads/pallas_call | solution.py:156
  (383 shorter events, 137.8 us)
Async XLA Ops:
  6.6 85.9 %collective-permute-start.4 = (bf16[1664,1152]{1,0:T(8,128)(2,1)S(1)}, bf16[1664,1152]{1,0:T(8,128)(2,1)S(1)}, u32[]{:S(2)}, u32[]{:S(2)}) collective-permute-start(bf16[1664,1152]{1,0:T(8,128)(2,1)S(1)} %get-tuple-element.82.refs_1_), channel_id=1, source_target_pairs={{0,4},{4,0},{1,5},{5,1},{2,6},{6,2},{3,7},{7,3},{8,12},{12,8},{9,1... | collective-permute-start | bytes 11501576 | tf_op jit(solution)/shard_map/ppermute | solution.py:38
  9.7 84.7 %collective-permute-start.5 = (bf16[1664,1152]{1,0:T(8,128)(2,1)S(1)}, bf16[1664,1152]{1,0:T(8,128)(2,1)S(1)}, u32[]{:S(2)}, u32[]{:S(2)}) collective-permute-start(bf16[1664,1152]{1,0:T(8,128)(2,1)S(1)} %get-tuple-element.82.refs_1_), channel_id=1, source_target_pairs={{0,2},{1,3},{2,0},{3,1},{4,6},{5,7},{6,4},{7,5},{8,10},{9,11},{10,... | collective-permute-start | bytes 11501576 | tf_op jit(solution)/shard_map/ppermute | solution.py:34
  92.6 18.4 %collective-permute-start.6 = (bf16[288,1152]{1,0:T(8,128)(2,1)S(1)}, bf16[288,1152]{1,0:T(8,128)(2,1)S(1)}, u32[]{:S(2)}, u32[]{:S(2)}) collective-permute-start(bf16[288,1152]{1,0:T(8,128)(2,1)S(1)} %slice.88), channel_id=1, source_target_pairs={{0,2},{1,3},{2,0},{3,1},{4,6},{5,7},{6,4},{7,5},{8,10},{9,11},{10,... | collective-permute-start | bytes 1990664 | tf_op jit(solution)/shard_map/ppermute | solution.py:34
  94.4 16.6 %collective-permute-start.7 = (bf16[288,1152]{1,0:T(8,128)(2,1)S(1)}, bf16[288,1152]{1,0:T(8,128)(2,1)S(1)}, u32[]{:S(2)}, u32[]{:S(2)}) collective-permute-start(bf16[288,1152]{1,0:T(8,128)(2,1)S(1)} %slice.89), channel_id=1, source_target_pairs={{0,4},{4,0},{1,5},{5,1},{2,6},{6,2},{3,7},{7,3},{8,12},{12,8},{9,1... | collective-permute-start | bytes 1990664 | tf_op jit(solution)/shard_map/ppermute | solution.py:38
  100.4 34.9 %collective-permute-start.8 = (bf16[4,288,1152]{2,1,0:T(8,128)(2,1)}, bf16[4,288,1152]{2,1,0:T(8,128)(2,1)}, u32[]{:S(2)}, u32[]{:S(2)}) collective-permute-start(bf16[4,288,1152]{2,1,0:T(8,128)(2,1)} %heads_near.1.refs_3_.refs_5_.refs_0_), channel_id=1, source_target_pairs={{0,1},{1,0},{2,3},{3,2},{4,5},{5,4},{6,7},{7,6},{8,9},{9,8},{10,11... | collective-permute-start | bytes 7962632 | tf_op jit(solution)/shard_map/ppermute | solution.py:29
  116.4 19.4 %collective-permute-start.9 = (bf16[4,288,1152]{2,1,0:T(8,128)(2,1)}, bf16[4,288,1152]{2,1,0:T(8,128)(2,1)}, u32[]{:S(2)}, u32[]{:S(2)}) collective-permute-start(bf16[4,288,1152]{2,1,0:T(8,128)(2,1)} %heads_far.1.refs_6_.refs_1_), channel_id=1, source_target_pairs={{0,1},{1,0},{2,3},{3,2},{4,5},{5,4},{6,7},{7,6},{8,9},{9,8},{10,11... | collective-permute-start | bytes 7962632 | tf_op jit(solution)/shard_map/ppermute | solution.py:29
  118.9 11.4 %collective-permute-start.12 = (bf16[184,1152]{1,0:T(8,128)(2,1)S(1)}, bf16[184,1152]{1,0:T(8,128)(2,1)S(1)}, u32[]{:S(2)}, u32[]{:S(2)}) collective-permute-start(bf16[184,1152]{1,0:T(8,128)(2,1)S(1)} %get-tuple-element.84), channel_id=1, source_target_pairs={{0,2},{1,3},{2,0},{3,1},{4,6},{5,7},{6,4},{7,5},{8,10},{9,11},{10,... | collective-permute-start | bytes 1271816 | tf_op jit(solution)/shard_map/ppermute | solution.py:34
  122.3 7.8 %collective-permute-start = (f32[2,144]{1,0:T(2,128)S(1)}, f32[2,144]{1,0:T(2,128)S(1)}, u32[]{:S(2)}, u32[]{:S(2)}) collective-permute-start(f32[2,144]{1,0:T(2,128)S(1)} %bitcast.97), channel_id=1, source_target_pairs={{0,2},{1,3},{2,0},{3,1},{4,6},{5,7},{6,4},{7,5},{8,10},{9,11},{10,... | collective-permute-start | bytes 3464 | tf_op jit(solution)/shard_map/ppermute | solution.py:34
  130.4 30.3 %collective-permute-start.11 = (bf16[544,1152]{1,0:T(8,128)(2,1)}, bf16[544,1152]{1,0:T(8,128)(2,1)}, u32[]{:S(2)}, u32[]{:S(2)}) collective-permute-start(bf16[544,1152]{1,0:T(8,128)(2,1)} %slice.90.refs_6_), channel_id=1, source_target_pairs={{0,2},{1,3},{2,0},{3,1},{4,6},{5,7},{6,4},{7,5},{8,10},{9,11},{10,... | collective-permute-start | bytes 3760136 | tf_op jit(solution)/shard_map/ppermute | solution.py:34
  131.9 31.7 %collective-permute-start.16 = (bf16[544,1152]{1,0:T(8,128)(2,1)}, bf16[544,1152]{1,0:T(8,128)(2,1)S(1)}, u32[]{:S(2)}, u32[]{:S(2)}) collective-permute-start(bf16[544,1152]{1,0:T(8,128)(2,1)} %slice.91.refs_7_), channel_id=1, source_target_pairs={{0,4},{4,0},{1,5},{5,1},{2,6},{6,2},{3,7},{7,3},{8,12},{12,8},{9,1... | collective-permute-start | bytes 3760136 | tf_op jit(solution)/shard_map/ppermute | solution.py:38
  135.1 33.0 %collective-permute-start.10 = (bf16[1088,1152]{1,0:T(8,128)(2,1)S(1)}, bf16[1088,1152]{1,0:T(8,128)(2,1)S(1)}, u32[]{:S(2)}, u32[]{:S(2)}) collective-permute-start(bf16[1088,1152]{1,0:T(8,128)(2,1)S(1)} %bitcast.64), channel_id=1, source_target_pairs={{0,1},{1,0},{2,3},{3,2},{4,5},{5,4},{6,7},{7,6},{8,9},{9,8},{10,11... | collective-permute-start | bytes 7520264 | tf_op jit(solution)/shard_map/ppermute | solution.py:29
  135.2 37.1 %collective-permute-start.15 = (bf16[1088,1152]{1,0:T(8,128)(2,1)}, bf16[1088,1152]{1,0:T(8,128)(2,1)S(1)}, u32[]{:S(2)}, u32[]{:S(2)}) collective-permute-start(bf16[1088,1152]{1,0:T(8,128)(2,1)} %bitcast.74), channel_id=1, source_target_pairs={{0,1},{1,0},{2,3},{3,2},{4,5},{5,4},{6,7},{7,6},{8,9},{9,8},{10,11... | collective-permute-start | bytes 7520264 | tf_op jit(solution)/shard_map/ppermute | solution.py:29
  163.5 12.0 %collective-permute-start.14 = (bf16[1088,1152]{1,0:T(8,128)(2,1)S(1)}, bf16[1088,1152]{1,0:T(8,128)(2,1)S(1)}, u32[]{:S(2)}, u32[]{:S(2)}) collective-permute-start(bf16[1088,1152]{1,0:T(8,128)(2,1)S(1)} %bitcast.67), channel_id=1, source_target_pairs={{0,1},{1,0},{2,3},{3,2},{4,5},{5,4},{6,7},{7,6},{8,9},{9,8},{10,11... | collective-permute-start | bytes 7520264 | tf_op jit(solution)/shard_map/ppermute | solution.py:29
  167.6 11.8 %collective-permute-start.17 = (bf16[1088,1152]{1,0:T(8,128)(2,1)S(1)}, bf16[1088,1152]{1,0:T(8,128)(2,1)S(1)}, u32[]{:S(2)}, u32[]{:S(2)}) collective-permute-start(bf16[1088,1152]{1,0:T(8,128)(2,1)S(1)} %bitcast.80), channel_id=1, source_target_pairs={{0,1},{1,0},{2,3},{3,2},{4,5},{5,4},{6,7},{7,6},{8,9},{9,8},{10,11... | collective-permute-start | bytes 7520264 | tf_op jit(solution)/shard_map/ppermute | solution.py:29
  182.6 21.9 %collective-permute-start.18 = (bf16[368,1152]{1,0:T(8,128)(2,1)S(1)}, bf16[368,1152]{1,0:T(8,128)(2,1)S(1)}, u32[]{:S(2)}, u32[]{:S(2)}) collective-permute-start(bf16[368,1152]{1,0:T(8,128)(2,1)S(1)} %feed_down.3.refs_12_), channel_id=1, source_target_pairs={{0,8},{8,16},{16,24},{1,9},{9,17},{17,25},{2,10},{10,18},{18,26},{... | collective-permute-start | bytes 2543624 | tf_op jit(solution)/shard_map/ppermute | solution.py:50
  233.8 22.5 %collective-permute-start.20 = (bf16[368,1152]{1,0:T(8,128)(2,1)}, bf16[368,1152]{1,0:T(8,128)(2,1)S(1)}, u32[]{:S(2)}, u32[]{:S(2)}) collective-permute-start(bf16[368,1152]{1,0:T(8,128)(2,1)} %layer_mid.2), channel_id=1, source_target_pairs={{0,8},{8,16},{16,24},{1,9},{9,17},{17,25},{2,10},{10,18},{18,26},{... | collective-permute-start | bytes 2543624 | tf_op jit(solution)/shard_map/ppermute | solution.py:50
  285.1 23.0 %collective-permute-start.22 = (bf16[368,1152]{1,0:T(8,128)(2,1)}, bf16[368,1152]{1,0:T(8,128)(2,1)S(1)}, u32[]{:S(2)}, u32[]{:S(2)}) collective-permute-start(bf16[368,1152]{1,0:T(8,128)(2,1)} %layer_mid.3), channel_id=1, source_target_pairs={{0,8},{8,16},{16,24},{1,9},{9,17},{17,25},{2,10},{10,18},{18,26},{... | collective-permute-start | bytes 2543624 | tf_op jit(solution)/shard_map/ppermute | solution.py:50
  309.0 28.3 %collective-permute-start.24 = (bf16[184,1152]{1,0:T(8,128)(2,1)S(1)}, bf16[184,1152]{1,0:T(8,128)(2,1)S(1)}, u32[]{:S(2)}, u32[]{:S(2)}) collective-permute-start(bf16[184,1152]{1,0:T(8,128)(2,1)S(1)} %pad.9), channel_id=1, source_target_pairs={{0,2},{1,3},{2,0},{3,1},{4,6},{5,7},{6,4},{7,5},{8,10},{9,11},{10,... | collective-permute-start | bytes 1271816 | tf_op jit(solution)/shard_map/ppermute | solution.py:34
  386.6 23.5 %collective-permute-start.27 = (bf16[368,1152]{1,0:T(8,128)(2,1)S(1)}, bf16[368,1152]{1,0:T(8,128)(2,1)S(1)}, u32[]{:S(2)}, u32[]{:S(2)}) collective-permute-start(bf16[368,1152]{1,0:T(8,128)(2,1)S(1)} %qkv_back.4), channel_id=1, source_target_pairs={{8,0},{16,8},{24,16},{9,1},{17,9},{25,17},{10,2},{18,10},{26,18},{... | collective-permute-start | bytes 2543624 | tf_op jit(solution)/shard_map/ppermute | solution.py:50
  388.5 12.7 %collective-permute-start.25 = (bf16[184,1152]{1,0:T(8,128)(2,1)S(1)}, bf16[184,1152]{1,0:T(8,128)(2,1)S(1)}, u32[]{:S(2)}, u32[]{:S(2)}) collective-permute-start(bf16[184,1152]{1,0:T(8,128)(2,1)S(1)} %slice.99), channel_id=1, source_target_pairs={{0,2},{1,3},{2,0},{3,1},{4,6},{5,7},{6,4},{7,5},{8,10},{9,11},{10,... | collective-permute-start | bytes 1271816 | tf_op jit(solution)/shard_map/ppermute | solution.py:34
  389.2 35.2 %collective-permute-start.28 = (bf16[192,1152]{1,0:T(8,128)(2,1)S(1)}, bf16[192,1152]{1,0:T(8,128)(2,1)S(1)}, u32[]{:S(2)}, u32[]{:S(2)}) collective-permute-start(bf16[192,1152]{1,0:T(8,128)(2,1)S(1)} %slice.73), channel_id=1, source_target_pairs={{0,2},{1,3},{2,0},{3,1},{4,6},{5,7},{6,4},{7,5},{8,10},{9,11},{10,... | collective-permute-start | bytes 1327112 | tf_op jit(solution)/shard_map/ppermute | solution.py:34
  391.5 32.9 %collective-permute-start.29 = (bf16[176,1152]{1,0:T(8,128)(2,1)}, bf16[176,1152]{1,0:T(8,128)(2,1)S(1)}, u32[]{:S(2)}, u32[]{:S(2)}) collective-permute-start(bf16[176,1152]{1,0:T(8,128)(2,1)} %slice.74), channel_id=1, source_target_pairs={{0,4},{4,0},{1,5},{5,1},{2,6},{6,2},{3,7},{7,3},{8,12},{12,8},{9,1... | collective-permute-start | bytes 1216520 | tf_op jit(solution)/shard_map/ppermute | solution.py:38
  448.2 22.8 %collective-permute-start.31 = (bf16[368,1152]{1,0:T(8,128)(2,1)S(1)}, bf16[368,1152]{1,0:T(8,128)(2,1)S(1)}, u32[]{:S(2)}, u32[]{:S(2)}) collective-permute-start(bf16[368,1152]{1,0:T(8,128)(2,1)S(1)} %qkv_back.5), channel_id=1, source_target_pairs={{8,0},{16,8},{24,16},{9,1},{17,9},{25,17},{10,2},{18,10},{26,18},{... | collective-permute-start | bytes 2543624 | tf_op jit(solution)/shard_map/ppermute | solution.py:50
  449.5 13.2 %collective-permute-start.33 = (bf16[192,1152]{1,0:T(8,128)(2,1)S(1)}, bf16[192,1152]{1,0:T(8,128)(2,1)S(1)}, u32[]{:S(2)}, u32[]{:S(2)}) collective-permute-start(bf16[192,1152]{1,0:T(8,128)(2,1)S(1)} %copy-done.97), channel_id=1, source_target_pairs={{0,4},{4,0},{1,5},{5,1},{2,6},{6,2},{3,7},{7,3},{8,12},{12,8},{9,1... | collective-permute-start | bytes 1327112 | tf_op jit(solution)/shard_map/ppermute | solution.py:38
  450.2 12.5 %collective-permute-start.32 = (bf16[176,1152]{1,0:T(8,128)(2,1)}, bf16[176,1152]{1,0:T(8,128)(2,1)S(1)}, u32[]{:S(2)}, u32[]{:S(2)}) collective-permute-start(bf16[176,1152]{1,0:T(8,128)(2,1)} %slice.74), channel_id=1, source_target_pairs={{0,2},{1,3},{2,0},{3,1},{4,6},{5,7},{6,4},{7,5},{8,10},{9,11},{10,... | collective-permute-start | bytes 1216520 | tf_op jit(solution)/shard_map/ppermute | solution.py:34
  451.3 39.2 %collective-permute-start.34 = (bf16[192,1152]{1,0:T(8,128)(2,1)S(1)}, bf16[192,1152]{1,0:T(8,128)(2,1)S(1)}, u32[]{:S(2)}, u32[]{:S(2)}) collective-permute-start(bf16[192,1152]{1,0:T(8,128)(2,1)S(1)} %collective-permute-done.28.refs_7_.refs_1_), channel_id=1, source_target_pairs={{0,4},{4,0},{1,5},{5,1},{2,6},{6,2},{3,7},{7,3},{8,12},{12,8},{9,1... | collective-permute-start | bytes 1327112 | tf_op jit(solution)/shard_map/ppermute | solution.py:38
  452.1 38.4 %collective-permute-start.35 = (bf16[176,1152]{1,0:T(8,128)(2,1)S(1)}, bf16[176,1152]{1,0:T(8,128)(2,1)S(1)}, u32[]{:S(2)}, u32[]{:S(2)}) collective-permute-start(bf16[176,1152]{1,0:T(8,128)(2,1)S(1)} %collective-permute-done.29.refs_8_.refs_4_), channel_id=1, source_target_pairs={{0,2},{1,3},{2,0},{3,1},{4,6},{5,7},{6,4},{7,5},{8,10},{9,11},{10,... | collective-permute-start | bytes 1216520 | tf_op jit(solution)/shard_map/ppermute | solution.py:34
  513.4 7.6 %collective-permute-start.38 = (bf16[1472,1152]{1,0:T(8,128)(2,1)}, bf16[1472,1152]{1,0:T(8,128)(2,1)}, u32[]{:S(2)}, u32[]{:S(2)}) collective-permute-start(bf16[1472,1152]{1,0:T(8,128)(2,1)} %join_normed.1.refs_8_.refs_0_.refs_3_), channel_id=1, source_target_pairs={{0,1},{1,0},{2,3},{3,2},{4,5},{5,4},{6,7},{7,6},{8,9},{9,8},{10,11... | collective-permute-start | bytes 10174472 | tf_op jit(solution)/shard_map/ppermute | solution.py:29
  513.9 26.5 %collective-permute-start.37 = (bf16[368,1152]{1,0:T(8,128)(2,1)}, bf16[368,1152]{1,0:T(8,128)(2,1)}, u32[]{:S(2)}, u32[]{:S(2)}) collective-permute-start(bf16[368,1152]{1,0:T(8,128)(2,1)} %qkv_back.6), channel_id=1, source_target_pairs={{8,0},{16,8},{24,16},{9,1},{17,9},{25,17},{10,2},{18,10},{26,18},{... | collective-permute-start | bytes 2543624 | tf_op jit(solution)/shard_map/ppermute | solution.py:50
  542.2 23.4 %collective-permute-start.40 = (bf16[192,1152]{1,0:T(8,128)(2,1)S(1)}, bf16[192,1152]{1,0:T(8,128)(2,1)S(1)}, u32[]{:S(2)}, u32[]{:S(2)}) collective-permute-start(bf16[192,1152]{1,0:T(8,128)(2,1)S(1)} %slice.93), channel_id=1, source_target_pairs={{0,2},{1,3},{2,0},{3,1},{4,6},{5,7},{6,4},{7,5},{8,10},{9,11},{10,... | collective-permute-start | bytes 1327112 | tf_op jit(solution)/shard_map/ppermute | solution.py:34
  542.8 22.8 %collective-permute-start.41 = (bf16[176,1152]{1,0:T(8,128)(2,1)S(1)}, bf16[176,1152]{1,0:T(8,128)(2,1)S(1)}, u32[]{:S(2)}, u32[]{:S(2)}) collective-permute-start(bf16[176,1152]{1,0:T(8,128)(2,1)S(1)} %slice.94), channel_id=1, source_target_pairs={{0,4},{4,0},{1,5},{5,1},{2,6},{6,2},{3,7},{7,3},{8,12},{12,8},{9,1... | collective-permute-start | bytes 1216520 | tf_op jit(solution)/shard_map/ppermute | solution.py:38
  579.3 13.2 %collective-permute-start.42 = (bf16[368,2304]{1,0:T(8,128)(2,1)S(1)}, bf16[368,2304]{1,0:T(8,128)(2,1)S(1)}, u32[]{:S(2)}, u32[]{:S(2)}) collective-permute-start(bf16[368,2304]{1,0:T(8,128)(2,1)S(1)} %get-tuple-element.128), channel_id=1, source_target_pairs={{0,1},{1,0},{2,3},{3,2},{4,5},{5,4},{6,7},{7,6},{8,9},{9,8},{10,11... | collective-permute-start | bytes 5087240 | tf_op jit(solution)/shard_map/ppermute | solution.py:29
  579.9 12.6 %collective-permute-start.45 = (bf16[192,1152]{1,0:T(8,128)(2,1)S(1)}, bf16[192,1152]{1,0:T(8,128)(2,1)S(1)}, u32[]{:S(2)}, u32[]{:S(2)}) collective-permute-start(bf16[192,1152]{1,0:T(8,128)(2,1)S(1)} %collective-permute-done.40.refs_7_.refs_1_), channel_id=1, source_target_pairs={{0,4},{4,0},{1,5},{5,1},{2,6},{6,2},{3,7},{7,3},{8,12},{12,8},{9,1... | collective-permute-start | bytes 1327112 | tf_op jit(solution)/shard_map/ppermute | solution.py:38
  580.7 11.8 %collective-permute-start.46 = (bf16[176,1152]{1,0:T(8,128)(2,1)S(1)}, bf16[176,1152]{1,0:T(8,128)(2,1)S(1)}, u32[]{:S(2)}, u32[]{:S(2)}) collective-permute-start(bf16[176,1152]{1,0:T(8,128)(2,1)S(1)} %collective-permute-done.41.refs_8_.refs_4_), channel_id=1, source_target_pairs={{0,2},{1,3},{2,0},{3,1},{4,6},{5,7},{6,4},{7,5},{8,10},{9,11},{10,... | collective-permute-start | bytes 1216520 | tf_op jit(solution)/shard_map/ppermute | solution.py:34
  598.4 12.9 %collective-permute-start.49 = (bf16[192,1152]{1,0:T(8,128)(2,1)S(1)}, bf16[192,1152]{1,0:T(8,128)(2,1)S(1)}, u32[]{:S(2)}, u32[]{:S(2)}) collective-permute-start(bf16[192,1152]{1,0:T(8,128)(2,1)S(1)} %slice.83), channel_id=1, source_target_pairs={{0,4},{4,0},{1,5},{5,1},{2,6},{6,2},{3,7},{7,3},{8,12},{12,8},{9,1... | collective-permute-start | bytes 1327112 | tf_op jit(solution)/shard_map/ppermute | solution.py:38
  599.7 11.6 %collective-permute-start.48 = (bf16[176,1152]{1,0:T(8,128)(2,1)S(1)}, bf16[176,1152]{1,0:T(8,128)(2,1)S(1)}, u32[]{:S(2)}, u32[]{:S(2)}) collective-permute-start(bf16[176,1152]{1,0:T(8,128)(2,1)S(1)} %slice.82), channel_id=1, source_target_pairs={{0,2},{1,3},{2,0},{3,1},{4,6},{5,7},{6,4},{7,5},{8,10},{9,11},{10,... | collective-permute-start | bytes 1216520 | tf_op jit(solution)/shard_map/ppermute | solution.py:34
  613.3 31.4 %collective-permute-start.55 = (bf16[448,1152]{1,0:T(8,128)(2,1)S(1)}, bf16[448,1152]{1,0:T(8,128)(2,1)S(1)}, u32[]{:S(2)}, u32[]{:S(2)}) collective-permute-start(bf16[448,1152]{1,0:T(8,128)(2,1)S(1)} %get-tuple-element.140), channel_id=1, source_target_pairs={{0,2},{1,3},{2,0},{3,1},{4,6},{5,7},{6,4},{7,5},{8,10},{9,11},{10,... | collective-permute-start | bytes 3096584 | tf_op jit(solution)/shard_map/ppermute | solution.py:34
  614.5 28.9 %collective-permute-start.56 = (bf16[416,1152]{1,0:T(8,128)(2,1)S(1)}, bf16[416,1152]{1,0:T(8,128)(2,1)S(1)}, u32[]{:S(2)}, u32[]{:S(2)}) collective-permute-start(bf16[416,1152]{1,0:T(8,128)(2,1)S(1)} %get-tuple-element.141), channel_id=1, source_target_pairs={{0,4},{4,0},{1,5},{5,1},{2,6},{6,2},{3,7},{7,3},{8,12},{12,8},{9,1... | collective-permute-start | bytes 2875400 | tf_op jit(solution)/shard_map/ppermute | solution.py:38
  615.6 33.0 %collective-permute-start.52 = (f32[2,1152]{1,0:T(2,128)S(1)}, f32[2,1152]{1,0:T(2,128)S(1)}, u32[]{:S(2)}, u32[]{:S(2)}) collective-permute-start(f32[2,1152]{1,0:T(2,128)S(1)} %pad_maximum_fusion.3), channel_id=1, source_target_pairs={{0,2},{1,3},{2,0},{3,1},{4,6},{5,7},{6,4},{7,5},{8,10},{9,11},{10,... | collective-permute-start | bytes 27656 | tf_op jit(solution)/shard_map/ppermute | solution.py:34
  616.4 32.9 %collective-permute-start.53 = (f32[2,1152]{1,0:T(2,128)S(1)}, f32[2,1152]{1,0:T(2,128)S(1)}, u32[]{:S(2)}, u32[]{:S(2)}) collective-permute-start(f32[2,1152]{1,0:T(2,128)S(1)} %pad_maximum_fusion.3), channel_id=1, source_target_pairs={{0,4},{4,0},{1,5},{5,1},{2,6},{6,2},{3,7},{7,3},{8,12},{12,8},{9,1... | collective-permute-start | bytes 27656 | tf_op jit(solution)/shard_map/ppermute | solution.py:38
  619.5 30.8 %collective-permute-start.54 = (f32[2,1152]{1,0:T(2,128)S(1)}, f32[2,1152]{1,0:T(2,128)S(1)}, u32[]{:S(2)}, u32[]{:S(2)}) collective-permute-start(f32[2,1152]{1,0:T(2,128)S(1)} %pad_maximum_fusion.3), channel_id=1, source_target_pairs={{0,6},{1,7},{2,4},{3,5},{4,2},{5,3},{6,0},{7,1},{8,14},{9,15},{10,... | collective-permute-start | bytes 27656 | tf_op jit(solution)/shard_map/ppermute | solution.py:44
  643.4 11.7 %collective-permute-start.59 = (bf16[160,1152]{1,0:T(8,128)(2,1)}, bf16[160,1152]{1,0:T(8,128)(2,1)S(1)}, u32[]{:S(2)}, u32[]{:S(2)}) collective-permute-start(bf16[160,1152]{1,0:T(8,128)(2,1)} %get-tuple-element.149), channel_id=1, source_target_pairs={{0,2},{1,3},{2,0},{3,1},{4,6},{5,7},{6,4},{7,5},{8,10},{9,11},{10,... | collective-permute-start | bytes 1105928 | tf_op jit(solution)/shard_map/ppermute | solution.py:34
  644.7 9.9 %collective-permute-start.60 = (bf16[128,1152]{1,0:T(8,128)(2,1)S(1)}, bf16[128,1152]{1,0:T(8,128)(2,1)S(1)}, u32[]{:S(2)}, u32[]{:S(2)}) collective-permute-start(bf16[128,1152]{1,0:T(8,128)(2,1)S(1)} %get-tuple-element.150), channel_id=1, source_target_pairs={{0,4},{4,0},{1,5},{5,1},{2,6},{6,2},{3,7},{7,3},{8,12},{12,8},{9,1... | collective-permute-start | bytes 884744 | tf_op jit(solution)/shard_map/ppermute | solution.py:38
  648.6 25.4 %collective-permute-start.47 = (bf16[184,1152]{1,0:T(8,128)(2,1)S(1)}, bf16[184,1152]{1,0:T(8,128)(2,1)S(1)}, u32[]{:S(2)}, u32[]{:S(2)}) collective-permute-start(bf16[184,1152]{1,0:T(8,128)(2,1)S(1)} %slice.98), channel_id=1, source_target_pairs={{0,2},{1,3},{2,0},{3,1},{4,6},{5,7},{6,4},{7,5},{8,10},{9,11},{10,... | collective-permute-start | bytes 1271816 | tf_op jit(solution)/shard_map/ppermute | solution.py:34
  649.3 31.5 %collective-permute-start.57 = (bf16[224,1152]{1,0:T(8,128)(2,1)}, bf16[224,1152]{1,0:T(8,128)(2,1)}, u32[]{:S(2)}, u32[]{:S(2)}) collective-permute-start(bf16[224,1152]{1,0:T(8,128)(2,1)} %get-tuple-element.144), channel_id=1, source_target_pairs={{0,4},{4,0},{1,5},{5,1},{2,6},{6,2},{3,7},{7,3},{8,12},{12,8},{9,1... | collective-permute-start | bytes 1548296 | tf_op jit(solution)/shard_map/ppermute | solution.py:38
  650.3 30.4 %collective-permute-start.58 = (bf16[208,1152]{1,0:T(8,128)(2,1)}, bf16[208,1152]{1,0:T(8,128)(2,1)}, u32[]{:S(2)}, u32[]{:S(2)}) collective-permute-start(bf16[208,1152]{1,0:T(8,128)(2,1)} %get-tuple-element.145), channel_id=1, source_target_pairs={{0,2},{1,3},{2,0},{3,1},{4,6},{5,7},{6,4},{7,5},{8,10},{9,11},{10,... | collective-permute-start | bytes 1437704 | tf_op jit(solution)/shard_map/ppermute | solution.py:34
  656.9 22.7 %collective-permute-start.61 = (bf16[80,1152]{1,0:T(8,128)(2,1)S(1)}, bf16[80,1152]{1,0:T(8,128)(2,1)S(1)}, u32[]{:S(2)}, u32[]{:S(2)}) collective-permute-start(bf16[80,1152]{1,0:T(8,128)(2,1)S(1)} %get-tuple-element.153), channel_id=1, source_target_pairs={{0,4},{4,0},{1,5},{5,1},{2,6},{6,2},{3,7},{7,3},{8,12},{12,8},{9,1... | collective-permute-start | bytes 552968 | tf_op jit(solution)/shard_map/ppermute | solution.py:38
  658.0 21.7 %collective-permute-start.62 = (bf16[64,1152]{1,0:T(8,128)(2,1)S(1)}, bf16[64,1152]{1,0:T(8,128)(2,1)S(1)}, u32[]{:S(2)}, u32[]{:S(2)}) collective-permute-start(bf16[64,1152]{1,0:T(8,128)(2,1)S(1)} %get-tuple-element.154), channel_id=1, source_target_pairs={{0,2},{1,3},{2,0},{3,1},{4,6},{5,7},{6,4},{7,5},{8,10},{9,11},{10,... | collective-permute-start | bytes 442376 | tf_op jit(solution)/shard_map/ppermute | solution.py:34
  (125 other events, 2437.8 us)

commit v5 on v4

--- a/solution.py
+++ b/solution.py
@@ -687,7 +687,9 @@
     n = w_up.shape[0]
     half, block = halves_of(total)
 
-    def kernel(a_ref, b_ref, wu_ref, act_ref, slope_ref):
+    def kernel(a_ref, b_ref, wu_ref, act_ref, slope_ref, token):
+        token[...] = jnp.zeros_like(token)
+
         def rows(nb_ref):
             for at, k in spans(n, 512):
                 act, slope = gelu_both(dot_t(nb_ref[...], wu_ref[at : at + k, :]))
@@ -702,8 +704,8 @@
         past(kernel, 3, after),
         grid=(2 * half,),
         in_specs=[*halves_specs(half, block, width), VMEM, *[ANY] * len(after)],
-        out_specs=(by_rows, by_rows),
-        out_shape=(pltpu.HBM((2 * total, n), BF), pltpu.HBM((2 * total, n), BF)),
+        out_specs=(by_rows, by_rows, pl.BlockSpec((8, LANES), lambda i: (0, 0))),
+        out_shape=(pltpu.HBM((2 * total, n), BF), pltpu.HBM((2 * total, n), BF), shape((8, LANES), F32)),
         compiler_params=pltpu.CompilerParams(vmem_limit_bytes=18 * 2**20),
         cost_estimate=pl.CostEstimate(flops=int(5.6 * COST * total * width * n), bytes_accessed=int(12 * COST * total * width), transcendentals=0),
         name="unit_forward",
@@ -732,7 +734,8 @@
             wd_ref, refs = refs[0], refs[1:]
         saved_hbm, refs = refs[0], refs[1:]
         rows_hbm, refs = refs[: len(flat)], refs[len(flat) :]
-        out, held, sems = refs[0], refs[1 : 2 + kinds], refs[2 + kinds]
+        out, token, held, sems = refs[0], refs[1], refs[2 : 3 + kinds], refs[3 + kinds]
+        token[...] = jnp.zeros_like(token)
 
         def into(i):
             rows = slice(i % steps * block, (i % steps + 1) * block)
@@ -762,7 +765,8 @@
     args = [flags, *([w_down] if with_w else []), in_hbm(saved), *[in_hbm(a) for a in flat]]
     ins = [SMEM] + [VMEM] * with_w + [ANY] * (1 + len(flat))
     flops = (4 if with_w else 2) * total * len(sides) * width * n
-    return call(kernel, name, [shape((part, units), F32)], ins, scratch, args, flops, 40, after, 0.2)[0]
+    outs = [shape((part, units), F32), shape((8, LANES), F32)]
+    return call(kernel, name, outs, ins, scratch, args, flops, 40, after, 0.2)
 
 
 def join(name, pieces, after=()):
@@ -907,15 +911,15 @@
         return swap_x(low16(rows[padded_quarter:]))
 
     def both_images(rows, got, after=()):
-        def kernel(flag_ref, own_ref, got_ref, out):
+        def kernel(flag_ref, own_ref, got_ref, out, token):
+            token[...] = jnp.zeros_like(token)
             first = flag_ref[3] == 0
             own, other = own_ref[:quarter], up32(got_ref[...])[:quarter]
             out[:, 0, :] = jnp.where(first, own, other)
             out[:, 1, :] = jnp.where(first, other, own)
 
-        outs = [shape((quarter, 2, width), F32)]
-        pair = call(kernel, "both_images", outs, [SMEM, VMEM, VMEM], [], [flags, rows, got], 0, 16, after)[0]
-        return pair
+        outs = [shape((quarter, 2, width), F32), shape((8, LANES), F32)]
+        return call(kernel, "both_images", outs, [SMEM, VMEM, VMEM], [], [flags, rows, got], 0, 16, after)
 
     rows = 2 * padded_quarter
     valid = lax.dynamic_index_in_dim(valid_len, x_idx, 0, keepdims=False)
@@ -1015,7 +1019,7 @@
                 dy_x0, dy_y1 = swap_x(dy_low[:at]), swap_y(dy_low[at:])
         if tick:
             mode = "last" if last else "mid"
-            used, after = (sources, [act_all]) if last else (sources[-1:], [acts_got] if tick == 1 else [acts, nb_x1, nb_y0])
+            used, after = (sources, [unit_done]) if last else (sources[-1:], [acts_got] if tick == 1 else [acts_done, nb_x1, nb_y0])
             results = feed_back(mode, flags, used, slope, hidden, gains, weights[0], up_near + up_far, weights[2], after)
             hidden_grad, do = results[:2]
         if last:
@@ -1037,7 +1041,7 @@
             o_via = swap_x(o_parts[1]), swap_y(o_parts[2])
             dy_rest = tie(dy_low, dq)
             dy_x1, dy_y0 = swap_x(dy_rest[at:]), swap_y(dy_rest[:at])
-            after = [o_parts[0], dy_d0, dy_d1]
+            after = [o_parts[4], dy_d0, dy_d1]
         if plane and tick == 2:
             nb_four = join("join_normed", [normed_b, nb_x0, nb_x1, nb_y0, nb_y1, nb_d0, nb_d1], [dq])
             after = [nb_four]
@@ -1056,7 +1060,7 @@
             if plane:
                 nb_x1, nb_y0 = swap_x(normed_b[at:]), swap_y(normed_b[:at])
                 nb_d0, nb_d1 = swap_y(nb_x0), swap_x(nb_y1)
-            acts = both_images(out, acts_got)
+            acts, acts_done = both_images(out, acts_got)
             mix_keep, mix_give = core_halves(mix)
             na_far = swap_core(normed_a)
         elif tick == 2:
@@ -1065,8 +1069,8 @@
             else:
                 nb_all = lax.all_gather(normed_b, ("dp", "tensor"), axis=0, tiled=True)
                 nb_four, nb_far = jnp.split(nb_all, 2)
-            act_all, slope_all = unit_forward(nb_four, nb_far, up_near[0], [mix_keep, mix_give, na_far])
-            got, act_all = ties(got, act_all)
+            act_all, slope_all, unit_done = unit_forward(nb_four, nb_far, up_near[0], [mix_keep, mix_give, na_far])
+            got, unit_done = ties(got, unit_done)
         sources.append(got)
     dx, _, keep, give, gain_sum_a = back
 
@@ -1080,21 +1084,21 @@
         dy_four = join("join_dy", [dy_low, dy_x0, dy_x1, dy_y0, dy_y1, dy_d0, dy_d1], [qkv_parts[0]])
         dy_far = swap_core(dy_four)
         sides = [(nb_four, dy_four), (nb_far, dy_far)]
-        grad_up = unit_sums("up_grads", flags, sides, slope_all, down_near[0], units, part, [qkv_parts[0]])
-        over = scatter_middle("qkv_middle", *qkv_parts[3:], *via, [grad_up])
-        o_over = scatter_middle("output_middle", *o_parts[3:], *o_via, [grad_up])
-        grad_down = unit_sums("down_grads", flags, [(dy_four,), (dy_far,)], act_all, None, units, part, [grad_up, *gain_moves])
+        grad_up, up_done = unit_sums("up_grads", flags, sides, slope_all, down_near[0], units, part, [qkv_parts[0]])
+        over = scatter_middle("qkv_middle", *qkv_parts[3:], *via, [up_done])
+        o_over = scatter_middle("output_middle", *o_parts[3:], *o_via, [up_done])
+        grad_down, down_done = unit_sums("down_grads", flags, [(dy_four,), (dy_far,)], act_all, None, units, part, [up_done, *gain_moves])
         gain_sums = gain_sums + gain_moves[0] + gain_moves[1] + gain_moves[2]
         gain_sums = gain_sums + swap_core(gain_sums)
-        (grad_o,) = scatter_end("output_end", o_parts[0], *o_via, *o_over, 1, [grad_down])
-        grad_heads = scatter_end("qkv_end", qkv_parts[0], *via, *over, 3, [grad_down])
+        (grad_o,) = scatter_end("output_end", o_parts[0], *o_via, *o_over, 1, [down_done])
+        grad_heads = scatter_end("qkv_end", qkv_parts[0], *via, *over, 3, [down_done])
         gain_shard = lax.dynamic_slice_in_dim(gain_sums, (dp_idx * 4 + tensor_idx) * (width // 8), width // 8, 1)
-        grads_after = [grad_down]
+        grads_after = [down_done]
     else:
         dy_all = lax.all_gather(dy_low, ("dp", "tensor"), axis=0, tiled=True)
         dy_four, dy_far = jnp.split(dy_all, 2)
-        grad_up = unit_sums("up_grads", flags, [(nb_four, dy_four), (nb_far, dy_far)], slope_all, down_near[0], units, part)
-        grad_down = unit_sums("down_grads", flags, [(dy_four,), (dy_far,)], act_all, None, units, part)
+        grad_up, _ = unit_sums("up_grads", flags, [(nb_four, dy_four), (nb_far, dy_far)], slope_all, down_near[0], units, part)
+        grad_down, _ = unit_sums("down_grads", flags, [(dy_four,), (dy_far,)], act_all, None, units, part)
         grads_after = []
         both = lambda a, b: jnp.concatenate((a, b), axis=0)
         g = t_dot(both(keep, got), both(normed_a, na_far))
@@ -1105,7 +1109,7 @@
         g = g[:span] + up32(swap_x(low16(g[span:])))
         grad_o = up32(lax.psum_scatter(low16(g), "dp", scatter_dimension=1, tiled=True))
         gain_shard = lax.psum_scatter(gain_sums, ("dp", "tensor"), scatter_dimension=1, tiled=True)
-    grads = both_images(dx, grads_got, grads_after)
+    grads, _ = both_images(dx, grads_got, grads_after)
 
     return (
         jnp.transpose(acts, (1, 0, 2))[None],

time: 695 us -> 691 us (level)
    unnamed x220 -> x228, local copies, waits for them, and re-layouts: 35.2 us -> 32.3 us
  transfers between devices with their start and end apart: 64 -> 64, of which waited for: 25 -> 27; matrix products, arithmetic and copies ran while one was open for 2% -> 2% of each run, Pallas kernels for 30% -> 30%
where the time goes in v5:
time: 691 us; the launch traced here: 682 us
  Pallas kernels  366 us (53%)
  waiting for transfers between devices  202 us (29%)
  starting transfers between devices  62.6 us (9%)
  local copies, waits for them, and re-layouts  44 us (6%)
    pallas_call x40, Pallas kernels, call(): pl.pallas_call(past(kernel, len(args), after), out_shape=tuple(outs), in_...  337 us
    ppermute x15, waiting for transfers between devices, swap_y(): return lax.ppermute(a, 'dp', [(0, 1), (1, 0)])  85.3 us
    ppermute x6, waiting for transfers between devices, shift(): return lax.ppermute(a, 'section', pairs)  59.9 us
    ppermute x19, waiting for transfers between devices, swap_x(): return lax.ppermute(a, 'tensor', [(i, i ^ 2) for i in range(n)])  34.3 us
    unnamed x228, local copies, waits for them, and re-layouts  32.3 us
    ppermute x19, starting transfers between devices, swap_x(): return lax.ppermute(a, 'tensor', [(i, i ^ 2) for i in range(n)])  22.8 us
    ppermute x22, waiting for transfers between devices, swap_core(): return lax.ppermute(a, 'tensor', [(i, i ^ 1) for i in range(n)])  22.2 us
    pallas_call x1, Pallas kernels, unit_forward(): pl.pallas_call(past(kernel, 3, after), grid=(2 * half,), in_specs=[*halve...  17.7 us
  transfers between devices with their start and end apart: 64, of which 27 were waited for; matrix products, arithmetic and copies ran while one was open for 2% of the time, Pallas kernels for 30%

profile of v5, /device:TPU:0, one launch (start us, length us, event | category | flops | bytes accessed | tf_op | source)
XLA Modules:
  0.0 681.5 jit_solution(17436340826158371999)
XLA Ops:
  2.3 4.3 pack.1
  11.2 81.4 %collective-permute-done.4.refs_2_ = bf16[1664,1152]{1,0:T(8,128)(2,1)S(1)} collective-permute-done((bf16[1664,1152]{1,0:T(8,128)(2,1)S(1)}, bf16[1664,1152]{1,0:T(8,128)(2,1)S(1)}, u32[]{:S(2)}, u32[]{:S(2)}) %collective-permute-start.4) | collective-permute-done | bytes 3833888 | tf_op jit(solution)/shard_map/ppermute | solution.py:38
  96.0 4.4 heads_near.1.refs_3_.refs_5_.refs_0_
  106.5 3.3 slice.90.refs_6_
  112.0 4.3 heads_far.1.refs_6_.refs_1_
  123.0 7.2 %collective-permute-done = f32[2,144]{1,0:T(2,128)S(1)} collective-permute-done((f32[2,144]{1,0:T(2,128)S(1)}, f32[2,144]{1,0:T(2,128)S(1)}, u32[]{:S(2)}, u32[]{:S(2)}) %collective-permute-start) | collective-permute-done | bytes 1184 | tf_op jit(solution)/shard_map/ppermute | solution.py:34
  136.0 19.4 %layer_first.1 = (f32[368,1152]{1,0:T(8,128)S(1)}, bf16[368,1152]{1,0:T(8,128)(2,1)S(1)}) custom-call(s32[4]{0:T(128)S(1)} %pad_add_fusion.refs_0_.flag_ref, f32[8,736]{1,0:T(8,128)S(1)} %broadcast_in_dim.43.refs_1_.refs_0_.refs_2_.refs_6_, f32[2,1152]{1,0:T(2,128)S(1)} %maximum_select_fusion.refs_2_.refs_1_.refs_4_, ...), custom_call_target="tpu_custom_call" | custom-call | flops 10298064 | bytes 28049 | tf_op jit(solution)/shard_map/layer_first/pallas_call | solution.py:156
  155.5 5.2 collective-permute-done.11.refs_2_
  168.1 4.3 feed_up.2.refs_1_
  175.5 3.9 feed_up.3.refs_1_
  182.6 3.7 collective-permute-start.18
  186.3 11.3 %settle.1 = (bf16[4608,1152]{1,0:T(8,128)(2,1)S(1)}, bf16[4352,1152]{1,0:T(8,128)(2,1)S(1)}, bf16[4352,1152]{1,0:T(8,128)(2,1)S(1)}, f32[8,128]{1,0:T(8,128)}) custom-call(s32[4]{0:T(128)} %copy-done.84, bf16[4,288,1152]{2,1,0:T(8,128)(2,1)} %heads_near.1.refs_3_.refs_5_.refs_0_, bf16[4,288,1152]{2,1,0:T(8,128)(2,1)} %heads_far.1.refs_6_.refs_1_, ...), custom_call_target="tpu_custom_call" | custom-call | bytes 6291456 | tf_op jit(solution)/shard_map/settle/pallas_call | solution.py:368
  197.7 6.8 collective-permute-done.18.refs_5_
  208.3 25.5 %layer_mid.2 = bf16[368,1152]{1,0:T(8,128)(2,1)} custom-call(f32[8,736]{1,0:T(8,128)} %copy-done.55, f32[2,1152]{1,0:T(2,128)} %copy-done.57, bf16[4608,1152]{1,0:T(8,128)(2,1)S(1)} %get-tuple-element.95.refs_2_.refs_5_.refs_7_.refs_4_, bf16[4352,1152]{1,0:T(8,128)(2,1)S(1)} %get-tuple-element.98.refs_3_.refs_6_, ...), custom_call_target="tpu_custom_call" | custom-call | flops 1767794304 | bytes 6646169 | tf_op jit(solution)/shard_map/layer_mid/pallas_call | solution.py:156
  233.8 4.3 collective-permute-start.20
  238.1 18.3 %collective-permute-done.20.refs_5_.refs_7_ = bf16[368,1152]{1,0:T(8,128)(2,1)S(1)} collective-permute-done((bf16[368,1152]{1,0:T(8,128)(2,1)}, bf16[368,1152]{1,0:T(8,128)(2,1)S(1)}, u32[]{:S(2)}, u32[]{:S(2)}) %collective-permute-start.20) | collective-permute-done | bytes 847904 | tf_op jit(solution)/shard_map/ppermute | solution.py:50
  259.7 25.5 %layer_mid.3 = bf16[368,1152]{1,0:T(8,128)(2,1)} custom-call(f32[8,736]{1,0:T(8,128)} %copy-done.55, f32[2,1152]{1,0:T(2,128)} %copy-done.57, bf16[4608,1152]{1,0:T(8,128)(2,1)S(1)} %get-tuple-element.95.refs_2_.refs_5_.refs_7_.refs_4_, bf16[4352,1152]{1,0:T(8,128)(2,1)S(1)} %get-tuple-element.98.refs_3_.refs_6_, ...), custom_call_target="tpu_custom_call" | custom-call | flops 1767794304 | bytes 6646169 | tf_op jit(solution)/shard_map/layer_mid/pallas_call | solution.py:156
  285.1 4.3 collective-permute-start.22
  289.5 18.7 %collective-permute-done.22.refs_9_ = bf16[368,1152]{1,0:T(8,128)(2,1)S(1)} collective-permute-done((bf16[368,1152]{1,0:T(8,128)(2,1)}, bf16[368,1152]{1,0:T(8,128)(2,1)S(1)}, u32[]{:S(2)}, u32[]{:S(2)}) %collective-permute-start.22) | collective-permute-done | bytes 847904 | tf_op jit(solution)/shard_map/ppermute | solution.py:50
  312.4 4.0 copy-done.3
  316.4 8.9 %last_project.1 = (f32[368,1152]{1,0:T(8,128)S(1)}, bf16[368,1152]{1,0:T(8,128)(2,1)}, bf16[368,1152]{1,0:T(8,128)(2,1)S(1)}, bf16[736,2304]{1,0:T(8,128)(2,1)S(1)}) custom-call(s32[4]{0:T(128)S(1)} %copy-done.85, f32[2,1152]{1,0:T(2,128)S(1)} %copy-done.58, bf16[4608,1152]{1,0:T(8,128)(2,1)S(1)} %copy-done.3, f32[368,1152]{1,0:T(8,128)} %copy-done.34, ...), custom_call_target="tpu_custom_call" | custom-call | flops 488374272 | bytes 4667905 | tf_op jit(solution)/shard_map/last_project/pallas_call | solution.py:156
  325.3 10.8 %last_attention.1 = (bf16[368,1152]{1,0:T(8,128)(2,1)S(1)}, bf16[368,1152]{1,0:T(8,128)(2,1)S(1)}, f32[368,128]{1,0:T(8,128)S(1)}, f32[368,1152]{1,0:T(8,128)S(1)}, bf16[368,1152]{1,0:T(8,128)(2,1)S(1)}) custom-call(bf16[368,1152]{1,0:T(8,128)(2,1)S(1)} %get-tuple-element.101.refs_0_, bf16[736,2304]{1,0:T(8,128)(2,1)S(1)} %get-tuple-element.102.refs_1_, ...), custom_call_target="tpu_custom_call" | custom-call | flops 541432192 | bytes 3841228 | tf_op jit(solution)/shard_map/last_attention/pallas_call | solution.py:156
  337.4 4.5 copy-done.11
  341.9 22.9 %feed_turn.1 = (f32[368,1152]{1,0:T(8,128)}, bf16[368,4352]{1,0:T(8,128)(2,1)}, f32[368,1152]{1,0:T(8,128)}, bf16[368,1152]{1,0:T(8,128)(2,1)S(1)}, f32[368,1152]{1,0:T(8,128)}) custom-call(f32[368,1152]{1,0:T(8,128)} %copy-done.24, bf16[368,1152]{1,0:T(8,128)(2,1)S(1)} %get-tuple-element.105.refs_1_.refs_0_, f32[184,1152]{1,0:T(8,128)} %pad.8.refs_2_, ...), custom_call_target="tpu_custom_call" | custom-call | flops 1475975552 | bytes 7962726 | tf_op jit(solution)/shard_map/feed_turn/pallas_call | solution.py:156
  364.8 13.6 %attention_back.4 = (bf16[368,1152]{1,0:T(8,128)(2,1)S(1)}, bf16[368,2304]{1,0:T(8,128)(2,1)S(1)}, bf16[368,2304]{1,0:T(8,128)(2,1)S(1)}) custom-call(bf16[368,1152]{1,0:T(8,128)(2,1)S(1)} %get-tuple-element.101.refs_0_, bf16[736,2304]{1,0:T(8,128)(2,1)S(1)} %get-tuple-element.102.refs_1_, bf16[368,1152]{1,0:T(8,128)(2,1)S(1)} %get-tuple-element.110.refs_2_, ...), custom_call_target="tpu_custom_call" | custom-call | flops 1109393408 | bytes 2225664 | tf_op jit(solution)/shard_map/attention_back/pallas_call | solution.py:156
  378.7 3.4 collective-permute-done.26.refs_4_
  382.1 4.7 qkv_back.4
  392.8 9.7 %collective-permute-done.25.refs_2_.refs_11_ = bf16[184,1152]{1,0:T(8,128)(2,1)S(1)} collective-permute-done((bf16[184,1152]{1,0:T(8,128)(2,1)S(1)}, bf16[184,1152]{1,0:T(8,128)(2,1)S(1)}, u32[]{:S(2)}, u32[]{:S(2)}) %collective-permute-start.25) | collective-permute-done | bytes 423968 | tf_op jit(solution)/shard_map/ppermute | solution.py:34
  402.5 7.8 %collective-permute-done.27.refs_10_.refs_11_ = bf16[368,1152]{1,0:T(8,128)(2,1)S(1)} collective-permute-done((bf16[368,1152]{1,0:T(8,128)(2,1)S(1)}, bf16[368,1152]{1,0:T(8,128)(2,1)S(1)}, u32[]{:S(2)}, u32[]{:S(2)}) %collective-permute-start.27) | collective-permute-done | bytes 847904 | tf_op jit(solution)/shard_map/ppermute | solution.py:50
  410.4 14.2 %feed_back_mid.2 = (f32[368,1152]{1,0:T(8,128)S(1)}, bf16[368,1152]{1,0:T(8,128)(2,1)S(1)}) custom-call(s32[4]{0:T(128)S(1)} %copy-done.85, f32[2,1152]{1,0:T(2,128)S(1)} %copy-done.58, f32[368,1152]{1,0:T(8,128)S(1)} %copy-done.25, bf16[368,4352]{1,0:T(8,128)(2,1)S(1)} %copy-done.22, bf16[4608,1152]{1,0:T(8,128)(2,1)S(1)} %copy-done.4, ...), custom_call_target="tpu_custom_call" | custom-call | flops 835662656 | bytes 7454004 | tf_op jit(solution)/shard_map/feed_back_mid/pallas_call | solution.py:156
  425.9 13.7 %attention_back.5 = (bf16[368,1152]{1,0:T(8,128)(2,1)S(1)}, bf16[368,2304]{1,0:T(8,128)(2,1)S(1)}, bf16[368,2304]{1,0:T(8,128)(2,1)S(1)}) custom-call(bf16[368,1152]{1,0:T(8,128)(2,1)S(1)} %get-tuple-element.101.refs_0_, bf16[736,2304]{1,0:T(8,128)(2,1)S(1)} %copy-done.14, bf16[368,1152]{1,0:T(8,128)(2,1)S(1)} %get-tuple-element.118.refs_2_, ...), custom_call_target="tpu_custom_call" | custom-call | flops 1109393408 | bytes 2225664 | tf_op jit(solution)/shard_map/attention_back/pallas_call | solution.py:156
  439.7 3.6 collective-permute-done.30.refs_4_
  443.3 5.1 qkv_back.5
  456.0 6.7 collective-permute-done.32.refs_12_.refs_2_
  462.8 8.4 %collective-permute-done.31.refs_10_.refs_12_ = bf16[368,1152]{1,0:T(8,128)(2,1)S(1)} collective-permute-done((bf16[368,1152]{1,0:T(8,128)(2,1)S(1)}, bf16[368,1152]{1,0:T(8,128)(2,1)S(1)}, u32[]{:S(2)}, u32[]{:S(2)}) %collective-permute-start.31) | collective-permute-done | bytes 847904 | tf_op jit(solution)/shard_map/ppermute | solution.py:50
  471.2 14.2 %feed_back_mid.3 = (f32[368,1152]{1,0:T(8,128)S(1)}, bf16[368,1152]{1,0:T(8,128)(2,1)S(1)}) custom-call(s32[4]{0:T(128)S(1)} %copy-done.85, f32[2,1152]{1,0:T(2,128)S(1)} %copy-done.58, f32[368,1152]{1,0:T(8,128)S(1)} %copy-done.25, bf16[368,4352]{1,0:T(8,128)(2,1)S(1)} %copy-done.22, bf16[4608,1152]{1,0:T(8,128)(2,1)S(1)} %copy-done.4, ...), custom_call_target="tpu_custom_call" | custom-call | flops 835662656 | bytes 7454004 | tf_op jit(solution)/shard_map/feed_back_mid/pallas_call | solution.py:156
  490.5 13.7 %attention_back.6 = (bf16[368,1152]{1,0:T(8,128)(2,1)S(1)}, bf16[368,2304]{1,0:T(8,128)(2,1)S(1)}, bf16[368,2304]{1,0:T(8,128)(2,1)S(1)}) custom-call(bf16[368,1152]{1,0:T(8,128)(2,1)S(1)} %get-tuple-element.101.refs_0_, bf16[736,2304]{1,0:T(8,128)(2,1)S(1)} %copy-done.14, bf16[368,1152]{1,0:T(8,128)(2,1)S(1)} %copy-done.75, ...), custom_call_target="tpu_custom_call" | custom-call | flops 1109393408 | bytes 2225664 | tf_op jit(solution)/shard_map/attention_back/pallas_call | solution.py:156
  507.8 5.9 qkv_back.6
  523.0 17.7 %unit_forward.1 = (bf16[2944,1088]{1,0:T(8,128)(2,1)}, bf16[2944,1088]{1,0:T(8,128)(2,1)}, f32[8,128]{1,0:T(8,128)S(1)}) custom-call(bf16[1472,1152]{1,0:T(8,128)(2,1)} %join_normed.1.refs_8_.refs_0_.refs_3_, bf16[1472,1152]{1,0:T(8,128)(2,1)} %collective-permute-done.38.refs_1_.refs_5_, bf16[1088,1152]{1,0:T(8,128)(2,1)S(1)} %bitcast.66, ...), custom_call_target="tpu_custom_call" | custom-call | flops 1033182912 | bytes 2034892 | tf_op jit(solution)/shard_map/unit_forward/pallas_call | solution.py:703
  544.4 3.8 copy-done.6
  548.3 17.6 %feed_back_last.1 = (f32[368,1152]{1,0:T(8,128)S(1)}, bf16[368,1152]{1,0:T(8,128)(2,1)S(1)}, bf16[368,1152]{1,0:T(8,128)(2,1)S(1)}, f32[1,1152]{1,0:T(1,128)S(1)}) custom-call(s32[4]{0:T(128)S(1)} %copy-done.85, f32[2,1152]{1,0:T(2,128)S(1)} %copy-done.58, f32[368,1152]{1,0:T(8,128)S(1)} %copy-done.26, bf16[368,4352]{1,0:T(8,128)(2,1)S(1)} %copy-done.23, ...), custom_call_target="tpu_custom_call" | custom-call | flops 835662656 | bytes 8132763 | tf_op jit(solution)/shard_map/feed_back_last/pallas_call | solution.py:156
  566.0 13.6 %attention_back.7 = (bf16[368,1152]{1,0:T(8,128)(2,1)S(1)}, bf16[368,2304]{1,0:T(8,128)(2,1)S(1)}, bf16[368,2304]{1,0:T(8,128)(2,1)S(1)}) custom-call(bf16[368,1152]{1,0:T(8,128)(2,1)S(1)} %copy-done.31, bf16[736,2304]{1,0:T(8,128)(2,1)S(1)} %copy-done.15, bf16[368,1152]{1,0:T(8,128)(2,1)S(1)} %get-tuple-element.135.refs_2_, ...), custom_call_target="tpu_custom_call" | custom-call | flops 1109393408 | bytes 2225664 | tf_op jit(solution)/shard_map/attention_back/pallas_call | solution.py:156
  586.3 4.8 output_grads.1
  592.7 5.8 qkv_back.7
  601.7 7.1 %qkv_grads.1 = (f32[864,576]{1,0:T(8,128)S(1)}, bf16[448,1152]{1,0:T(8,128)(2,1)S(1)}, bf16[416,1152]{1,0:T(8,128)(2,1)S(1)}, bf16[208,1152]{1,0:T(8,128)(2,1)S(1)}, bf16[224,1152]{1,0:T(8,128)(2,1)S(1)}) custom-call(s32[4]{0:T(128)S(1)} %copy-done.85, bf16[368,1728]{1,0:T(8,128)(2,1)S(1)} %get-tuple-element.145.refs_1_, ...), custom_call_target="tpu_custom_call" | custom-call | flops 293024576 | bytes 1644136 | tf_op jit(solution)/shard_map/qkv_grads/pallas_call | solution.py:156
  621.6 22.1 %up_grads.1 = (f32[576,1076]{1,0:T(8,128)}, f32[8,128]{1,0:T(8,128)S(1)}) custom-call(s32[4]{0:T(128)S(1)} %copy-done.85, bf16[1088,1152]{1,0:T(8,128)(2,1)S(1)} %bitcast.77, bf16[2944,1088]{1,0:T(8,128)(2,1)} %get-tuple-element.148.refs_2_, bf16[1472,1152]{1,0:T(8,128)(2,1)} %join_normed.1.refs_8_.refs_0_.refs_3_, ...), custom_call_target="tpu_custom_call" | custom-call | flops 2951951104 | bytes 9488182 | tf_op jit(solution)/shard_map/up_grads/pallas_call | solution.py:156
  651.1 3.8 collective-permute-done.60.refs_3_.refs_2_
  658.5 14.0 %down_grads.1 = (f32[576,1076]{1,0:T(8,128)}, f32[8,128]{1,0:T(8,128)S(1)}) custom-call(s32[4]{0:T(128)S(1)} %copy-done.85, bf16[2944,1088]{1,0:T(8,128)(2,1)} %get-tuple-element.143.refs_1_, bf16[1472,1152]{1,0:T(8,128)(2,1)} %join_dy.1.refs_4_.refs_2_, bf16[1472,1152]{1,0:T(8,128)(2,1)} %copy-done.88, f32[8,128]{1,0:T(8,128)S(1)} %get-tuple-element.149.refs_4_, ...), custom_call_target="tpu_custom_call" | custom-call | flops 1475975552 | bytes 5772291 | tf_op jit(solution)/shard_map/down_grads/pallas_call | solution.py:156
  (391 shorter events, 137.2 us)
Async XLA Ops:
  6.6 85.9 %collective-permute-start.4 = (bf16[1664,1152]{1,0:T(8,128)(2,1)S(1)}, bf16[1664,1152]{1,0:T(8,128)(2,1)S(1)}, u32[]{:S(2)}, u32[]{:S(2)}) collective-permute-start(bf16[1664,1152]{1,0:T(8,128)(2,1)S(1)} %get-tuple-element.90.refs_1_), channel_id=1, source_target_pairs={{0,4},{4,0},{1,5},{5,1},{2,6},{6,2},{3,7},{7,3},{8,12},{12,8},{9,1... | collective-permute-start | bytes 11501576 | tf_op jit(solution)/shard_map/ppermute | solution.py:38
  9.7 84.7 %collective-permute-start.5 = (bf16[1664,1152]{1,0:T(8,128)(2,1)S(1)}, bf16[1664,1152]{1,0:T(8,128)(2,1)S(1)}, u32[]{:S(2)}, u32[]{:S(2)}) collective-permute-start(bf16[1664,1152]{1,0:T(8,128)(2,1)S(1)} %get-tuple-element.90.refs_1_), channel_id=1, source_target_pairs={{0,2},{1,3},{2,0},{3,1},{4,6},{5,7},{6,4},{7,5},{8,10},{9,11},{10,... | collective-permute-start | bytes 11501576 | tf_op jit(solution)/shard_map/ppermute | solution.py:34
  92.6 18.4 %collective-permute-start.6 = (bf16[288,1152]{1,0:T(8,128)(2,1)S(1)}, bf16[288,1152]{1,0:T(8,128)(2,1)S(1)}, u32[]{:S(2)}, u32[]{:S(2)}) collective-permute-start(bf16[288,1152]{1,0:T(8,128)(2,1)S(1)} %slice.88), channel_id=1, source_target_pairs={{0,2},{1,3},{2,0},{3,1},{4,6},{5,7},{6,4},{7,5},{8,10},{9,11},{10,... | collective-permute-start | bytes 1990664 | tf_op jit(solution)/shard_map/ppermute | solution.py:34
  94.4 16.6 %collective-permute-start.7 = (bf16[288,1152]{1,0:T(8,128)(2,1)S(1)}, bf16[288,1152]{1,0:T(8,128)(2,1)S(1)}, u32[]{:S(2)}, u32[]{:S(2)}) collective-permute-start(bf16[288,1152]{1,0:T(8,128)(2,1)S(1)} %slice.89), channel_id=1, source_target_pairs={{0,4},{4,0},{1,5},{5,1},{2,6},{6,2},{3,7},{7,3},{8,12},{12,8},{9,1... | collective-permute-start | bytes 1990664 | tf_op jit(solution)/shard_map/ppermute | solution.py:38
  100.4 34.9 %collective-permute-start.8 = (bf16[4,288,1152]{2,1,0:T(8,128)(2,1)}, bf16[4,288,1152]{2,1,0:T(8,128)(2,1)}, u32[]{:S(2)}, u32[]{:S(2)}) collective-permute-start(bf16[4,288,1152]{2,1,0:T(8,128)(2,1)} %heads_near.1.refs_3_.refs_5_.refs_0_), channel_id=1, source_target_pairs={{0,1},{1,0},{2,3},{3,2},{4,5},{5,4},{6,7},{7,6},{8,9},{9,8},{10,11... | collective-permute-start | bytes 7962632 | tf_op jit(solution)/shard_map/ppermute | solution.py:29
  116.4 19.4 %collective-permute-start.9 = (bf16[4,288,1152]{2,1,0:T(8,128)(2,1)}, bf16[4,288,1152]{2,1,0:T(8,128)(2,1)}, u32[]{:S(2)}, u32[]{:S(2)}) collective-permute-start(bf16[4,288,1152]{2,1,0:T(8,128)(2,1)} %heads_far.1.refs_6_.refs_1_), channel_id=1, source_target_pairs={{0,1},{1,0},{2,3},{3,2},{4,5},{5,4},{6,7},{7,6},{8,9},{9,8},{10,11... | collective-permute-start | bytes 7962632 | tf_op jit(solution)/shard_map/ppermute | solution.py:29
  118.9 11.4 %collective-permute-start.12 = (bf16[184,1152]{1,0:T(8,128)(2,1)S(1)}, bf16[184,1152]{1,0:T(8,128)(2,1)S(1)}, u32[]{:S(2)}, u32[]{:S(2)}) collective-permute-start(bf16[184,1152]{1,0:T(8,128)(2,1)S(1)} %get-tuple-element.92), channel_id=1, source_target_pairs={{0,2},{1,3},{2,0},{3,1},{4,6},{5,7},{6,4},{7,5},{8,10},{9,11},{10,... | collective-permute-start | bytes 1271816 | tf_op jit(solution)/shard_map/ppermute | solution.py:34
  122.3 7.8 %collective-permute-start = (f32[2,144]{1,0:T(2,128)S(1)}, f32[2,144]{1,0:T(2,128)S(1)}, u32[]{:S(2)}, u32[]{:S(2)}) collective-permute-start(f32[2,144]{1,0:T(2,128)S(1)} %bitcast.93), channel_id=1, source_target_pairs={{0,2},{1,3},{2,0},{3,1},{4,6},{5,7},{6,4},{7,5},{8,10},{9,11},{10,... | collective-permute-start | bytes 3464 | tf_op jit(solution)/shard_map/ppermute | solution.py:34
  130.4 30.3 %collective-permute-start.11 = (bf16[544,1152]{1,0:T(8,128)(2,1)}, bf16[544,1152]{1,0:T(8,128)(2,1)}, u32[]{:S(2)}, u32[]{:S(2)}) collective-permute-start(bf16[544,1152]{1,0:T(8,128)(2,1)} %slice.90.refs_6_), channel_id=1, source_target_pairs={{0,2},{1,3},{2,0},{3,1},{4,6},{5,7},{6,4},{7,5},{8,10},{9,11},{10,... | collective-permute-start | bytes 3760136 | tf_op jit(solution)/shard_map/ppermute | solution.py:34
  131.9 31.7 %collective-permute-start.16 = (bf16[544,1152]{1,0:T(8,128)(2,1)}, bf16[544,1152]{1,0:T(8,128)(2,1)S(1)}, u32[]{:S(2)}, u32[]{:S(2)}) collective-permute-start(bf16[544,1152]{1,0:T(8,128)(2,1)} %slice.91.refs_7_), channel_id=1, source_target_pairs={{0,4},{4,0},{1,5},{5,1},{2,6},{6,2},{3,7},{7,3},{8,12},{12,8},{9,1... | collective-permute-start | bytes 3760136 | tf_op jit(solution)/shard_map/ppermute | solution.py:38
  135.1 33.0 %collective-permute-start.10 = (bf16[1088,1152]{1,0:T(8,128)(2,1)S(1)}, bf16[1088,1152]{1,0:T(8,128)(2,1)S(1)}, u32[]{:S(2)}, u32[]{:S(2)}) collective-permute-start(bf16[1088,1152]{1,0:T(8,128)(2,1)S(1)} %bitcast.64), channel_id=1, source_target_pairs={{0,1},{1,0},{2,3},{3,2},{4,5},{5,4},{6,7},{7,6},{8,9},{9,8},{10,11... | collective-permute-start | bytes 7520264 | tf_op jit(solution)/shard_map/ppermute | solution.py:29
  135.2 37.1 %collective-permute-start.15 = (bf16[1088,1152]{1,0:T(8,128)(2,1)}, bf16[1088,1152]{1,0:T(8,128)(2,1)S(1)}, u32[]{:S(2)}, u32[]{:S(2)}) collective-permute-start(bf16[1088,1152]{1,0:T(8,128)(2,1)} %bitcast.74), channel_id=1, source_target_pairs={{0,1},{1,0},{2,3},{3,2},{4,5},{5,4},{6,7},{7,6},{8,9},{9,8},{10,11... | collective-permute-start | bytes 7520264 | tf_op jit(solution)/shard_map/ppermute | solution.py:29
  163.5 12.0 %collective-permute-start.14 = (bf16[1088,1152]{1,0:T(8,128)(2,1)S(1)}, bf16[1088,1152]{1,0:T(8,128)(2,1)S(1)}, u32[]{:S(2)}, u32[]{:S(2)}) collective-permute-start(bf16[1088,1152]{1,0:T(8,128)(2,1)S(1)} %bitcast.67), channel_id=1, source_target_pairs={{0,1},{1,0},{2,3},{3,2},{4,5},{5,4},{6,7},{7,6},{8,9},{9,8},{10,11... | collective-permute-start | bytes 7520264 | tf_op jit(solution)/shard_map/ppermute | solution.py:29
  167.6 11.8 %collective-permute-start.17 = (bf16[1088,1152]{1,0:T(8,128)(2,1)S(1)}, bf16[1088,1152]{1,0:T(8,128)(2,1)S(1)}, u32[]{:S(2)}, u32[]{:S(2)}) collective-permute-start(bf16[1088,1152]{1,0:T(8,128)(2,1)S(1)} %bitcast.78), channel_id=1, source_target_pairs={{0,1},{1,0},{2,3},{3,2},{4,5},{5,4},{6,7},{7,6},{8,9},{9,8},{10,11... | collective-permute-start | bytes 7520264 | tf_op jit(solution)/shard_map/ppermute | solution.py:29
  182.6 21.9 %collective-permute-start.18 = (bf16[368,1152]{1,0:T(8,128)(2,1)S(1)}, bf16[368,1152]{1,0:T(8,128)(2,1)S(1)}, u32[]{:S(2)}, u32[]{:S(2)}) collective-permute-start(bf16[368,1152]{1,0:T(8,128)(2,1)S(1)} %feed_down.3.refs_12_), channel_id=1, source_target_pairs={{0,8},{8,16},{16,24},{1,9},{9,17},{17,25},{2,10},{10,18},{18,26},{... | collective-permute-start | bytes 2543624 | tf_op jit(solution)/shard_map/ppermute | solution.py:50
  233.8 22.5 %collective-permute-start.20 = (bf16[368,1152]{1,0:T(8,128)(2,1)}, bf16[368,1152]{1,0:T(8,128)(2,1)S(1)}, u32[]{:S(2)}, u32[]{:S(2)}) collective-permute-start(bf16[368,1152]{1,0:T(8,128)(2,1)} %layer_mid.2), channel_id=1, source_target_pairs={{0,8},{8,16},{16,24},{1,9},{9,17},{17,25},{2,10},{10,18},{18,26},{... | collective-permute-start | bytes 2543624 | tf_op jit(solution)/shard_map/ppermute | solution.py:50
  285.1 23.0 %collective-permute-start.22 = (bf16[368,1152]{1,0:T(8,128)(2,1)}, bf16[368,1152]{1,0:T(8,128)(2,1)S(1)}, u32[]{:S(2)}, u32[]{:S(2)}) collective-permute-start(bf16[368,1152]{1,0:T(8,128)(2,1)} %layer_mid.3), channel_id=1, source_target_pairs={{0,8},{8,16},{16,24},{1,9},{9,17},{17,25},{2,10},{10,18},{18,26},{... | collective-permute-start | bytes 2543624 | tf_op jit(solution)/shard_map/ppermute | solution.py:50
  309.0 28.3 %collective-permute-start.24 = (bf16[184,1152]{1,0:T(8,128)(2,1)S(1)}, bf16[184,1152]{1,0:T(8,128)(2,1)S(1)}, u32[]{:S(2)}, u32[]{:S(2)}) collective-permute-start(bf16[184,1152]{1,0:T(8,128)(2,1)S(1)} %pad.9), channel_id=1, source_target_pairs={{0,2},{1,3},{2,0},{3,1},{4,6},{5,7},{6,4},{7,5},{8,10},{9,11},{10,... | collective-permute-start | bytes 1271816 | tf_op jit(solution)/shard_map/ppermute | solution.py:34
  386.8 23.5 %collective-permute-start.27 = (bf16[368,1152]{1,0:T(8,128)(2,1)S(1)}, bf16[368,1152]{1,0:T(8,128)(2,1)S(1)}, u32[]{:S(2)}, u32[]{:S(2)}) collective-permute-start(bf16[368,1152]{1,0:T(8,128)(2,1)S(1)} %qkv_back.4), channel_id=1, source_target_pairs={{8,0},{16,8},{24,16},{9,1},{17,9},{25,17},{10,2},{18,10},{26,18},{... | collective-permute-start | bytes 2543624 | tf_op jit(solution)/shard_map/ppermute | solution.py:50
  389.9 12.7 %collective-permute-start.25 = (bf16[184,1152]{1,0:T(8,128)(2,1)S(1)}, bf16[184,1152]{1,0:T(8,128)(2,1)S(1)}, u32[]{:S(2)}, u32[]{:S(2)}) collective-permute-start(bf16[184,1152]{1,0:T(8,128)(2,1)S(1)} %slice.99), channel_id=1, source_target_pairs={{0,2},{1,3},{2,0},{3,1},{4,6},{5,7},{6,4},{7,5},{8,10},{9,11},{10,... | collective-permute-start | bytes 1271816 | tf_op jit(solution)/shard_map/ppermute | solution.py:34
  390.5 35.4 %collective-permute-start.28 = (bf16[192,1152]{1,0:T(8,128)(2,1)S(1)}, bf16[192,1152]{1,0:T(8,128)(2,1)}, u32[]{:S(2)}, u32[]{:S(2)}) collective-permute-start(bf16[192,1152]{1,0:T(8,128)(2,1)S(1)} %slice.73), channel_id=1, source_target_pairs={{0,2},{1,3},{2,0},{3,1},{4,6},{5,7},{6,4},{7,5},{8,10},{9,11},{10,... | collective-permute-start | bytes 1327112 | tf_op jit(solution)/shard_map/ppermute | solution.py:34
  392.1 33.8 %collective-permute-start.29 = (bf16[176,1152]{1,0:T(8,128)(2,1)S(1)}, bf16[176,1152]{1,0:T(8,128)(2,1)S(1)}, u32[]{:S(2)}, u32[]{:S(2)}) collective-permute-start(bf16[176,1152]{1,0:T(8,128)(2,1)S(1)} %slice.74), channel_id=1, source_target_pairs={{0,4},{4,0},{1,5},{5,1},{2,6},{6,2},{3,7},{7,3},{8,12},{12,8},{9,1... | collective-permute-start | bytes 1216520 | tf_op jit(solution)/shard_map/ppermute | solution.py:38
  448.4 22.8 %collective-permute-start.31 = (bf16[368,1152]{1,0:T(8,128)(2,1)S(1)}, bf16[368,1152]{1,0:T(8,128)(2,1)S(1)}, u32[]{:S(2)}, u32[]{:S(2)}) collective-permute-start(bf16[368,1152]{1,0:T(8,128)(2,1)S(1)} %qkv_back.5), channel_id=1, source_target_pairs={{8,0},{16,8},{24,16},{9,1},{17,9},{25,17},{10,2},{18,10},{26,18},{... | collective-permute-start | bytes 2543624 | tf_op jit(solution)/shard_map/ppermute | solution.py:50
  449.7 13.1 %collective-permute-start.33 = (bf16[192,1152]{1,0:T(8,128)(2,1)S(1)}, bf16[192,1152]{1,0:T(8,128)(2,1)S(1)}, u32[]{:S(2)}, u32[]{:S(2)}) collective-permute-start(bf16[192,1152]{1,0:T(8,128)(2,1)S(1)} %copy-done.99), channel_id=1, source_target_pairs={{0,4},{4,0},{1,5},{5,1},{2,6},{6,2},{3,7},{7,3},{8,12},{12,8},{9,1... | collective-permute-start | bytes 1327112 | tf_op jit(solution)/shard_map/ppermute | solution.py:38
  450.4 12.3 %collective-permute-start.32 = (bf16[176,1152]{1,0:T(8,128)(2,1)S(1)}, bf16[176,1152]{1,0:T(8,128)(2,1)S(1)}, u32[]{:S(2)}, u32[]{:S(2)}) collective-permute-start(bf16[176,1152]{1,0:T(8,128)(2,1)S(1)} %copy-done.101), channel_id=1, source_target_pairs={{0,2},{1,3},{2,0},{3,1},{4,6},{5,7},{6,4},{7,5},{8,10},{9,11},{10,... | collective-permute-start | bytes 1216520 | tf_op jit(solution)/shard_map/ppermute | solution.py:34
  451.6 36.8 %collective-permute-start.34 = (bf16[192,1152]{1,0:T(8,128)(2,1)}, bf16[192,1152]{1,0:T(8,128)(2,1)S(1)}, u32[]{:S(2)}, u32[]{:S(2)}) collective-permute-start(bf16[192,1152]{1,0:T(8,128)(2,1)} %collective-permute-done.28.refs_7_.refs_1_), channel_id=1, source_target_pairs={{0,4},{4,0},{1,5},{5,1},{2,6},{6,2},{3,7},{7,3},{8,12},{12,8},{9,1... | collective-permute-start | bytes 1327112 | tf_op jit(solution)/shard_map/ppermute | solution.py:38
  452.4 35.2 %collective-permute-start.35 = (bf16[176,1152]{1,0:T(8,128)(2,1)S(1)}, bf16[176,1152]{1,0:T(8,128)(2,1)S(1)}, u32[]{:S(2)}, u32[]{:S(2)}) collective-permute-start(bf16[176,1152]{1,0:T(8,128)(2,1)S(1)} %copy-done.70), channel_id=1, source_target_pairs={{0,2},{1,3},{2,0},{3,1},{4,6},{5,7},{6,4},{7,5},{8,10},{9,11},{10,... | collective-permute-start | bytes 1216520 | tf_op jit(solution)/shard_map/ppermute | solution.py:34
  513.7 7.6 %collective-permute-start.38 = (bf16[1472,1152]{1,0:T(8,128)(2,1)}, bf16[1472,1152]{1,0:T(8,128)(2,1)}, u32[]{:S(2)}, u32[]{:S(2)}) collective-permute-start(bf16[1472,1152]{1,0:T(8,128)(2,1)} %join_normed.1.refs_8_.refs_0_.refs_3_), channel_id=1, source_target_pairs={{0,1},{1,0},{2,3},{3,2},{4,5},{5,4},{6,7},{7,6},{8,9},{9,8},{10,11... | collective-permute-start | bytes 10174472 | tf_op jit(solution)/shard_map/ppermute | solution.py:29
  514.2 26.5 %collective-permute-start.37 = (bf16[368,1152]{1,0:T(8,128)(2,1)}, bf16[368,1152]{1,0:T(8,128)(2,1)}, u32[]{:S(2)}, u32[]{:S(2)}) collective-permute-start(bf16[368,1152]{1,0:T(8,128)(2,1)} %qkv_back.6), channel_id=1, source_target_pairs={{8,0},{16,8},{24,16},{9,1},{17,9},{25,17},{10,2},{18,10},{26,18},{... | collective-permute-start | bytes 2543624 | tf_op jit(solution)/shard_map/ppermute | solution.py:50
  542.5 23.5 %collective-permute-start.40 = (bf16[192,1152]{1,0:T(8,128)(2,1)S(1)}, bf16[192,1152]{1,0:T(8,128)(2,1)S(1)}, u32[]{:S(2)}, u32[]{:S(2)}) collective-permute-start(bf16[192,1152]{1,0:T(8,128)(2,1)S(1)} %slice.93), channel_id=1, source_target_pairs={{0,2},{1,3},{2,0},{3,1},{4,6},{5,7},{6,4},{7,5},{8,10},{9,11},{10,... | collective-permute-start | bytes 1327112 | tf_op jit(solution)/shard_map/ppermute | solution.py:34
  543.1 22.8 %collective-permute-start.41 = (bf16[176,1152]{1,0:T(8,128)(2,1)S(1)}, bf16[176,1152]{1,0:T(8,128)(2,1)S(1)}, u32[]{:S(2)}, u32[]{:S(2)}) collective-permute-start(bf16[176,1152]{1,0:T(8,128)(2,1)S(1)} %slice.94), channel_id=1, source_target_pairs={{0,4},{4,0},{1,5},{5,1},{2,6},{6,2},{3,7},{7,3},{8,12},{12,8},{9,1... | collective-permute-start | bytes 1216520 | tf_op jit(solution)/shard_map/ppermute | solution.py:38
  579.6 13.2 %collective-permute-start.42 = (bf16[368,2304]{1,0:T(8,128)(2,1)S(1)}, bf16[368,2304]{1,0:T(8,128)(2,1)S(1)}, u32[]{:S(2)}, u32[]{:S(2)}) collective-permute-start(bf16[368,2304]{1,0:T(8,128)(2,1)S(1)} %get-tuple-element.138), channel_id=1, source_target_pairs={{0,1},{1,0},{2,3},{3,2},{4,5},{5,4},{6,7},{7,6},{8,9},{9,8},{10,11... | collective-permute-start | bytes 5087240 | tf_op jit(solution)/shard_map/ppermute | solution.py:29
  580.2 12.6 %collective-permute-start.45 = (bf16[192,1152]{1,0:T(8,128)(2,1)S(1)}, bf16[192,1152]{1,0:T(8,128)(2,1)S(1)}, u32[]{:S(2)}, u32[]{:S(2)}) collective-permute-start(bf16[192,1152]{1,0:T(8,128)(2,1)S(1)} %collective-permute-done.40.refs_7_.refs_1_), channel_id=1, source_target_pairs={{0,4},{4,0},{1,5},{5,1},{2,6},{6,2},{3,7},{7,3},{8,12},{12,8},{9,1... | collective-permute-start | bytes 1327112 | tf_op jit(solution)/shard_map/ppermute | solution.py:38
  580.9 11.8 %collective-permute-start.46 = (bf16[176,1152]{1,0:T(8,128)(2,1)S(1)}, bf16[176,1152]{1,0:T(8,128)(2,1)S(1)}, u32[]{:S(2)}, u32[]{:S(2)}) collective-permute-start(bf16[176,1152]{1,0:T(8,128)(2,1)S(1)} %collective-permute-done.41.refs_8_.refs_4_), channel_id=1, source_target_pairs={{0,2},{1,3},{2,0},{3,1},{4,6},{5,7},{6,4},{7,5},{8,10},{9,11},{10,... | collective-permute-start | bytes 1216520 | tf_op jit(solution)/shard_map/ppermute | solution.py:34
  598.7 12.9 %collective-permute-start.49 = (bf16[192,1152]{1,0:T(8,128)(2,1)S(1)}, bf16[192,1152]{1,0:T(8,128)(2,1)S(1)}, u32[]{:S(2)}, u32[]{:S(2)}) collective-permute-start(bf16[192,1152]{1,0:T(8,128)(2,1)S(1)} %slice.83), channel_id=1, source_target_pairs={{0,4},{4,0},{1,5},{5,1},{2,6},{6,2},{3,7},{7,3},{8,12},{12,8},{9,1... | collective-permute-start | bytes 1327112 | tf_op jit(solution)/shard_map/ppermute | solution.py:38
  600.0 11.6 %collective-permute-start.48 = (bf16[176,1152]{1,0:T(8,128)(2,1)S(1)}, bf16[176,1152]{1,0:T(8,128)(2,1)S(1)}, u32[]{:S(2)}, u32[]{:S(2)}) collective-permute-start(bf16[176,1152]{1,0:T(8,128)(2,1)S(1)} %slice.82), channel_id=1, source_target_pairs={{0,2},{1,3},{2,0},{3,1},{4,6},{5,7},{6,4},{7,5},{8,10},{9,11},{10,... | collective-permute-start | bytes 1216520 | tf_op jit(solution)/shard_map/ppermute | solution.py:34
  613.6 31.4 %collective-permute-start.55 = (bf16[448,1152]{1,0:T(8,128)(2,1)S(1)}, bf16[448,1152]{1,0:T(8,128)(2,1)S(1)}, u32[]{:S(2)}, u32[]{:S(2)}) collective-permute-start(bf16[448,1152]{1,0:T(8,128)(2,1)S(1)} %get-tuple-element.154), channel_id=1, source_target_pairs={{0,2},{1,3},{2,0},{3,1},{4,6},{5,7},{6,4},{7,5},{8,10},{9,11},{10,... | collective-permute-start | bytes 3096584 | tf_op jit(solution)/shard_map/ppermute | solution.py:34
  614.8 28.9 %collective-permute-start.56 = (bf16[416,1152]{1,0:T(8,128)(2,1)S(1)}, bf16[416,1152]{1,0:T(8,128)(2,1)S(1)}, u32[]{:S(2)}, u32[]{:S(2)}) collective-permute-start(bf16[416,1152]{1,0:T(8,128)(2,1)S(1)} %get-tuple-element.155), channel_id=1, source_target_pairs={{0,4},{4,0},{1,5},{5,1},{2,6},{6,2},{3,7},{7,3},{8,12},{12,8},{9,1... | collective-permute-start | bytes 2875400 | tf_op jit(solution)/shard_map/ppermute | solution.py:38
  615.9 32.2 %collective-permute-start.52 = (f32[2,1152]{1,0:T(2,128)S(1)}, f32[2,1152]{1,0:T(2,128)S(1)}, u32[]{:S(2)}, u32[]{:S(2)}) collective-permute-start(f32[2,1152]{1,0:T(2,128)S(1)} %pad_maximum_fusion.3), channel_id=1, source_target_pairs={{0,2},{1,3},{2,0},{3,1},{4,6},{5,7},{6,4},{7,5},{8,10},{9,11},{10,... | collective-permute-start | bytes 27656 | tf_op jit(solution)/shard_map/ppermute | solution.py:34
  616.6 32.1 %collective-permute-start.53 = (f32[2,1152]{1,0:T(2,128)S(1)}, f32[2,1152]{1,0:T(2,128)S(1)}, u32[]{:S(2)}, u32[]{:S(2)}) collective-permute-start(f32[2,1152]{1,0:T(2,128)S(1)} %pad_maximum_fusion.3), channel_id=1, source_target_pairs={{0,4},{4,0},{1,5},{5,1},{2,6},{6,2},{3,7},{7,3},{8,12},{12,8},{9,1... | collective-permute-start | bytes 27656 | tf_op jit(solution)/shard_map/ppermute | solution.py:38
  619.8 30.1 %collective-permute-start.54 = (f32[2,1152]{1,0:T(2,128)S(1)}, f32[2,1152]{1,0:T(2,128)S(1)}, u32[]{:S(2)}, u32[]{:S(2)}) collective-permute-start(f32[2,1152]{1,0:T(2,128)S(1)} %pad_maximum_fusion.3), channel_id=1, source_target_pairs={{0,6},{1,7},{2,4},{3,5},{4,2},{5,3},{6,0},{7,1},{8,14},{9,15},{10,... | collective-permute-start | bytes 27656 | tf_op jit(solution)/shard_map/ppermute | solution.py:44
  643.7 11.7 %collective-permute-start.59 = (bf16[160,1152]{1,0:T(8,128)(2,1)}, bf16[160,1152]{1,0:T(8,128)(2,1)S(1)}, u32[]{:S(2)}, u32[]{:S(2)}) collective-permute-start(bf16[160,1152]{1,0:T(8,128)(2,1)} %get-tuple-element.164), channel_id=1, source_target_pairs={{0,2},{1,3},{2,0},{3,1},{4,6},{5,7},{6,4},{7,5},{8,10},{9,11},{10,... | collective-permute-start | bytes 1105928 | tf_op jit(solution)/shard_map/ppermute | solution.py:34
  645.0 9.9 %collective-permute-start.60 = (bf16[128,1152]{1,0:T(8,128)(2,1)S(1)}, bf16[128,1152]{1,0:T(8,128)(2,1)S(1)}, u32[]{:S(2)}, u32[]{:S(2)}) collective-permute-start(bf16[128,1152]{1,0:T(8,128)(2,1)S(1)} %get-tuple-element.165), channel_id=1, source_target_pairs={{0,4},{4,0},{1,5},{5,1},{2,6},{6,2},{3,7},{7,3},{8,12},{12,8},{9,1... | collective-permute-start | bytes 884744 | tf_op jit(solution)/shard_map/ppermute | solution.py:38
  648.1 24.4 %collective-permute-start.47 = (bf16[184,1152]{1,0:T(8,128)(2,1)}, bf16[184,1152]{1,0:T(8,128)(2,1)S(1)}, u32[]{:S(2)}, u32[]{:S(2)}) collective-permute-start(bf16[184,1152]{1,0:T(8,128)(2,1)} %slice.98), channel_id=1, source_target_pairs={{0,2},{1,3},{2,0},{3,1},{4,6},{5,7},{6,4},{7,5},{8,10},{9,11},{10,... | collective-permute-start | bytes 1271816 | tf_op jit(solution)/shard_map/ppermute | solution.py:34
  648.8 29.5 %collective-permute-start.57 = (bf16[224,1152]{1,0:T(8,128)(2,1)}, bf16[224,1152]{1,0:T(8,128)(2,1)}, u32[]{:S(2)}, u32[]{:S(2)}) collective-permute-start(bf16[224,1152]{1,0:T(8,128)(2,1)} %get-tuple-element.158), channel_id=1, source_target_pairs={{0,4},{4,0},{1,5},{5,1},{2,6},{6,2},{3,7},{7,3},{8,12},{12,8},{9,1... | collective-permute-start | bytes 1548296 | tf_op jit(solution)/shard_map/ppermute | solution.py:38
  649.8 28.4 %collective-permute-start.58 = (bf16[208,1152]{1,0:T(8,128)(2,1)}, bf16[208,1152]{1,0:T(8,128)(2,1)}, u32[]{:S(2)}, u32[]{:S(2)}) collective-permute-start(bf16[208,1152]{1,0:T(8,128)(2,1)} %get-tuple-element.159), channel_id=1, source_target_pairs={{0,2},{1,3},{2,0},{3,1},{4,6},{5,7},{6,4},{7,5},{8,10},{9,11},{10,... | collective-permute-start | bytes 1437704 | tf_op jit(solution)/shard_map/ppermute | solution.py:34
  655.5 21.6 %collective-permute-start.61 = (bf16[80,1152]{1,0:T(8,128)(2,1)S(1)}, bf16[80,1152]{1,0:T(8,128)(2,1)S(1)}, u32[]{:S(2)}, u32[]{:S(2)}) collective-permute-start(bf16[80,1152]{1,0:T(8,128)(2,1)S(1)} %get-tuple-element.167), channel_id=1, source_target_pairs={{0,4},{4,0},{1,5},{5,1},{2,6},{6,2},{3,7},{7,3},{8,12},{12,8},{9,1... | collective-permute-start | bytes 552968 | tf_op jit(solution)/shard_map/ppermute | solution.py:38
  656.5 20.6 %collective-permute-start.62 = (bf16[64,1152]{1,0:T(8,128)(2,1)S(1)}, bf16[64,1152]{1,0:T(8,128)(2,1)S(1)}, u32[]{:S(2)}, u32[]{:S(2)}) collective-permute-start(bf16[64,1152]{1,0:T(8,128)(2,1)S(1)} %get-tuple-element.168), channel_id=1, source_target_pairs={{0,2},{1,3},{2,0},{3,1},{4,6},{5,7},{6,4},{7,5},{8,10},{9,11},{10,... | collective-permute-start | bytes 442376 | tf_op jit(solution)/shard_map/ppermute | solution.py:34
  (129 other events, 2443.5 us)

commit v6 on v5

--- a/solution.py
+++ b/solution.py
@@ -973,9 +973,9 @@
     down_near = [down_near, swap_core(down_near)]
     act_near = feed_up(normed_b, up_near)
     half_out = feed_down(hidden, act_near, down_near, F32)
-    up_far = put_together("up_far", far(at_up, h_units, over_up), flags, 1, h_units, [normed_b])[0]
+    up_far = put_together("up_far", far(at_up, h_units, over_up), flags, 1, h_units, [half_out])[0]
     up_far = [up_far, swap_core(up_far)]
-    down_far = put_together("down_far", far(at_down, h_units, over_down), flags, 1, h_units, [normed_b])[0]
+    down_far = put_together("down_far", far(at_down, h_units, over_down), flags, 1, h_units, [half_out])[0]
     down_far = [down_far, swap_core(down_far)]
     act_far = feed_up(normed_b, up_far)
     out = feed_down(half_out, act_far, down_far, BF)

time: 691 us -> 699 us (1.012)
    unnamed x228 -> x200, local copies, waits for them, and re-layouts: 32.3 us -> 32.6 us
  transfers between devices with their start and end apart: 64 -> 64, of which waited for: 27 -> 33; matrix products, arithmetic and copies ran while one was open for 2% -> 2% of each run, Pallas kernels for 30% -> 30%
where the time goes in v6:
time: 699 us; the launch traced here: 689 us
  Pallas kernels  371 us (53%)
  waiting for transfers between devices  208 us (30%)
  starting transfers between devices  59.2 us (8%)
  local copies, waits for them, and re-layouts  41 us (6%)
  other arithmetic  7.36 us (1%)
    pallas_call x40, Pallas kernels, call(): pl.pallas_call(past(kernel, len(args), after), out_shape=tuple(outs), in_...  342 us
    ppermute x15, waiting for transfers between devices, swap_y(): return lax.ppermute(a, 'dp', [(0, 1), (1, 0)])  87 us
    ppermute x6, waiting for transfers between devices, shift(): return lax.ppermute(a, 'section', pairs)  60 us
    unnamed x200, local copies, waits for them, and re-layouts  32.6 us
    ppermute x19, waiting for transfers between devices, swap_x(): return lax.ppermute(a, 'tensor', [(i, i ^ 2) for i in range(n)])  30.6 us
    ppermute x22, waiting for transfers between devices, swap_core(): return lax.ppermute(a, 'tensor', [(i, i ^ 1) for i in range(n)])  28.2 us
    ppermute x19, starting transfers between devices, swap_x(): return lax.ppermute(a, 'tensor', [(i, i ^ 2) for i in range(n)])  19.5 us
    pallas_call x1, Pallas kernels, unit_forward(): pl.pallas_call(past(kernel, 3, after), grid=(2 * half,), in_specs=[*halve...  18.5 us
  transfers between devices with their start and end apart: 64, of which 33 were waited for; matrix products, arithmetic and copies ran while one was open for 2% of the time, Pallas kernels for 30%

profile of v6, /device:TPU:0, one launch (start us, length us, event | category | flops | bytes accessed | tf_op | source)
XLA Modules:
  0.0 689.1 jit_solution(4593836601335604641)
XLA Ops:
  2.3 4.3 pack.1
  11.2 81.4 %collective-permute-done.4.refs_2_ = bf16[1664,1152]{1,0:T(8,128)(2,1)S(1)} collective-permute-done((bf16[1664,1152]{1,0:T(8,128)(2,1)S(1)}, bf16[1664,1152]{1,0:T(8,128)(2,1)S(1)}, u32[]{:S(2)}, u32[]{:S(2)}) %collective-permute-start.4) | collective-permute-done | bytes 3833888 | tf_op jit(solution)/shard_map/ppermute | solution.py:38
  94.5 4.4 heads_near.1.refs_3_.refs_5_.refs_0_
  104.0 4.3 up_near.1
  108.3 4.2 down_near.1
  114.1 3.8 collective-permute-done.6.refs_2_
  119.8 4.3 heads_far.1.refs_6_.refs_1_
  144.4 20.3 %layer_first.1 = (f32[368,1152]{1,0:T(8,128)S(1)}, bf16[368,1152]{1,0:T(8,128)(2,1)S(1)}) custom-call(s32[4]{0:T(128)S(1)} %pad_add_fusion.refs_0_.flag_ref, f32[8,736]{1,0:T(8,128)S(1)} %broadcast_in_dim.43.refs_1_.refs_0_.refs_2_.refs_6_, f32[2,1152]{1,0:T(2,128)S(1)} %maximum_select_fusion.refs_2_.refs_1_.refs_4_, ...), custom_call_target="tpu_custom_call" | custom-call | flops 10298064 | bytes 28049 | tf_op jit(solution)/shard_map/layer_first/pallas_call | solution.py:156
  164.8 4.9 feed_up.2.refs_1_
  169.6 5.3 feed_down.2.refs_3_.refs_0_
  182.6 3.8 feed_up.3.refs_1_
  189.7 3.7 collective-permute-start.18
  193.4 11.3 %settle.1 = (bf16[4608,1152]{1,0:T(8,128)(2,1)S(1)}, bf16[4352,1152]{1,0:T(8,128)(2,1)S(1)}, bf16[4352,1152]{1,0:T(8,128)(2,1)S(1)}, f32[8,128]{1,0:T(8,128)}) custom-call(s32[4]{0:T(128)} %copy-done.73, bf16[4,288,1152]{2,1,0:T(8,128)(2,1)} %heads_near.1.refs_3_.refs_5_.refs_0_, bf16[4,288,1152]{2,1,0:T(8,128)(2,1)} %heads_far.1.refs_6_.refs_1_, ...), custom_call_target="tpu_custom_call" | custom-call | bytes 6291456 | tf_op jit(solution)/shard_map/settle/pallas_call | solution.py:368
  204.8 6.8 collective-permute-done.18.refs_5_
  215.4 25.5 %layer_mid.2 = bf16[368,1152]{1,0:T(8,128)(2,1)} custom-call(f32[8,736]{1,0:T(8,128)} %copy-done.44, f32[2,1152]{1,0:T(2,128)} %copy-done.46, bf16[4608,1152]{1,0:T(8,128)(2,1)S(1)} %get-tuple-element.95.refs_2_.refs_5_.refs_7_.refs_4_, bf16[4352,1152]{1,0:T(8,128)(2,1)S(1)} %get-tuple-element.98.refs_3_.refs_6_, ...), custom_call_target="tpu_custom_call" | custom-call | flops 1767794304 | bytes 6646169 | tf_op jit(solution)/shard_map/layer_mid/pallas_call | solution.py:156
  240.9 4.2 collective-permute-start.20
  245.1 18.3 %collective-permute-done.20.refs_5_.refs_7_ = bf16[368,1152]{1,0:T(8,128)(2,1)S(1)} collective-permute-done((bf16[368,1152]{1,0:T(8,128)(2,1)}, bf16[368,1152]{1,0:T(8,128)(2,1)S(1)}, u32[]{:S(2)}, u32[]{:S(2)}) %collective-permute-start.20) | collective-permute-done | bytes 847904 | tf_op jit(solution)/shard_map/ppermute | solution.py:50
  266.7 25.5 %layer_mid.3 = bf16[368,1152]{1,0:T(8,128)(2,1)} custom-call(f32[8,736]{1,0:T(8,128)} %copy-done.44, f32[2,1152]{1,0:T(2,128)} %copy-done.46, bf16[4608,1152]{1,0:T(8,128)(2,1)S(1)} %get-tuple-element.95.refs_2_.refs_5_.refs_7_.refs_4_, bf16[4352,1152]{1,0:T(8,128)(2,1)S(1)} %get-tuple-element.98.refs_3_.refs_6_, ...), custom_call_target="tpu_custom_call" | custom-call | flops 1767794304 | bytes 6646169 | tf_op jit(solution)/shard_map/layer_mid/pallas_call | solution.py:156
  292.2 4.3 collective-permute-start.22
  296.5 18.7 %collective-permute-done.22.refs_9_ = bf16[368,1152]{1,0:T(8,128)(2,1)S(1)} collective-permute-done((bf16[368,1152]{1,0:T(8,128)(2,1)}, bf16[368,1152]{1,0:T(8,128)(2,1)S(1)}, u32[]{:S(2)}, u32[]{:S(2)}) %collective-permute-start.22) | collective-permute-done | bytes 847904 | tf_op jit(solution)/shard_map/ppermute | solution.py:50
  319.6 4.0 copy-done.3
  323.7 8.8 %last_project.1 = (f32[368,1152]{1,0:T(8,128)S(1)}, bf16[368,1152]{1,0:T(8,128)(2,1)}, bf16[368,1152]{1,0:T(8,128)(2,1)S(1)}, bf16[736,2304]{1,0:T(8,128)(2,1)S(1)}) custom-call(s32[4]{0:T(128)S(1)} %copy-done.74, f32[2,1152]{1,0:T(2,128)S(1)} %copy-done.47, bf16[4608,1152]{1,0:T(8,128)(2,1)S(1)} %copy-done.3, f32[368,1152]{1,0:T(8,128)} %copy-done.26, ...), custom_call_target="tpu_custom_call" | custom-call | flops 488374272 | bytes 4667905 | tf_op jit(solution)/shard_map/last_project/pallas_call | solution.py:156
  332.5 10.3 %last_attention.1 = (bf16[368,1152]{1,0:T(8,128)(2,1)S(1)}, bf16[368,1152]{1,0:T(8,128)(2,1)S(1)}, f32[368,128]{1,0:T(8,128)S(1)}, f32[368,1152]{1,0:T(8,128)S(1)}, bf16[368,1152]{1,0:T(8,128)(2,1)S(1)}) custom-call(bf16[368,1152]{1,0:T(8,128)(2,1)S(1)} %get-tuple-element.101.refs_0_, bf16[736,2304]{1,0:T(8,128)(2,1)S(1)} %get-tuple-element.102.refs_1_, ...), custom_call_target="tpu_custom_call" | custom-call | flops 541432192 | bytes 3841228 | tf_op jit(solution)/shard_map/last_attention/pallas_call | solution.py:156
  344.1 4.2 copy-done.8
  348.3 22.4 %feed_turn.1 = (f32[368,1152]{1,0:T(8,128)}, bf16[368,4352]{1,0:T(8,128)(2,1)}, f32[368,1152]{1,0:T(8,128)}, bf16[368,1152]{1,0:T(8,128)(2,1)S(1)}, f32[368,1152]{1,0:T(8,128)}) custom-call(f32[368,1152]{1,0:T(8,128)} %copy-done.20, bf16[368,1152]{1,0:T(8,128)(2,1)S(1)} %get-tuple-element.105.refs_1_.refs_0_, f32[184,1152]{1,0:T(8,128)} %pad.8.refs_2_, ...), custom_call_target="tpu_custom_call" | custom-call | flops 1475975552 | bytes 7962726 | tf_op jit(solution)/shard_map/feed_turn/pallas_call | solution.py:156
  370.7 13.4 %attention_back.4 = (bf16[368,1152]{1,0:T(8,128)(2,1)S(1)}, bf16[368,2304]{1,0:T(8,128)(2,1)S(1)}, bf16[368,2304]{1,0:T(8,128)(2,1)S(1)}) custom-call(bf16[368,1152]{1,0:T(8,128)(2,1)S(1)} %get-tuple-element.101.refs_0_, bf16[736,2304]{1,0:T(8,128)(2,1)S(1)} %get-tuple-element.102.refs_1_, bf16[368,1152]{1,0:T(8,128)(2,1)S(1)} %get-tuple-element.110.refs_2_, ...), custom_call_target="tpu_custom_call" | custom-call | flops 1109393408 | bytes 2225664 | tf_op jit(solution)/shard_map/attention_back/pallas_call | solution.py:156
  387.8 4.8 qkv_back.4
  398.5 9.8 %collective-permute-done.25.refs_2_.refs_11_ = bf16[184,1152]{1,0:T(8,128)(2,1)S(1)} collective-permute-done((bf16[184,1152]{1,0:T(8,128)(2,1)S(1)}, bf16[184,1152]{1,0:T(8,128)(2,1)S(1)}, u32[]{:S(2)}, u32[]{:S(2)}) %collective-permute-start.25) | collective-permute-done | bytes 423968 | tf_op jit(solution)/shard_map/ppermute | solution.py:34
  408.3 7.8 %collective-permute-done.27.refs_10_.refs_11_ = bf16[368,1152]{1,0:T(8,128)(2,1)S(1)} collective-permute-done((bf16[368,1152]{1,0:T(8,128)(2,1)S(1)}, bf16[368,1152]{1,0:T(8,128)(2,1)S(1)}, u32[]{:S(2)}, u32[]{:S(2)}) %collective-permute-start.27) | collective-permute-done | bytes 847904 | tf_op jit(solution)/shard_map/ppermute | solution.py:50
  416.2 14.1 %feed_back_mid.2 = (f32[368,1152]{1,0:T(8,128)S(1)}, bf16[368,1152]{1,0:T(8,128)(2,1)S(1)}) custom-call(s32[4]{0:T(128)S(1)} %copy-done.74, f32[2,1152]{1,0:T(2,128)S(1)} %copy-done.47, f32[368,1152]{1,0:T(8,128)S(1)} %copy-done.21, bf16[368,4352]{1,0:T(8,128)(2,1)S(1)} %copy-done.18, bf16[4608,1152]{1,0:T(8,128)(2,1)S(1)} %copy-done.4, ...), custom_call_target="tpu_custom_call" | custom-call | flops 835662656 | bytes 7454004 | tf_op jit(solution)/shard_map/feed_back_mid/pallas_call | solution.py:156
  431.7 13.5 %attention_back.5 = (bf16[368,1152]{1,0:T(8,128)(2,1)S(1)}, bf16[368,2304]{1,0:T(8,128)(2,1)S(1)}, bf16[368,2304]{1,0:T(8,128)(2,1)S(1)}) custom-call(bf16[368,1152]{1,0:T(8,128)(2,1)S(1)} %get-tuple-element.101.refs_0_, bf16[736,2304]{1,0:T(8,128)(2,1)S(1)} %copy-done.11, bf16[368,1152]{1,0:T(8,128)(2,1)S(1)} %get-tuple-element.118.refs_2_, ...), custom_call_target="tpu_custom_call" | custom-call | flops 1109393408 | bytes 2225664 | tf_op jit(solution)/shard_map/attention_back/pallas_call | solution.py:156
  448.9 5.2 qkv_back.5
  461.7 6.6 collective-permute-done.32.refs_12_.refs_2_
  468.5 8.4 %collective-permute-done.31.refs_10_.refs_12_ = bf16[368,1152]{1,0:T(8,128)(2,1)S(1)} collective-permute-done((bf16[368,1152]{1,0:T(8,128)(2,1)S(1)}, bf16[368,1152]{1,0:T(8,128)(2,1)S(1)}, u32[]{:S(2)}, u32[]{:S(2)}) %collective-permute-start.31) | collective-permute-done | bytes 847904 | tf_op jit(solution)/shard_map/ppermute | solution.py:50
  476.9 14.1 %feed_back_mid.3 = (f32[368,1152]{1,0:T(8,128)S(1)}, bf16[368,1152]{1,0:T(8,128)(2,1)S(1)}) custom-call(s32[4]{0:T(128)S(1)} %copy-done.74, f32[2,1152]{1,0:T(2,128)S(1)} %copy-done.47, f32[368,1152]{1,0:T(8,128)S(1)} %copy-done.21, bf16[368,4352]{1,0:T(8,128)(2,1)S(1)} %copy-done.18, bf16[4608,1152]{1,0:T(8,128)(2,1)S(1)} %copy-done.4, ...), custom_call_target="tpu_custom_call" | custom-call | flops 835662656 | bytes 7454004 | tf_op jit(solution)/shard_map/feed_back_mid/pallas_call | solution.py:156
  497.9 13.6 %attention_back.6 = (bf16[368,1152]{1,0:T(8,128)(2,1)S(1)}, bf16[368,2304]{1,0:T(8,128)(2,1)S(1)}, bf16[368,2304]{1,0:T(8,128)(2,1)S(1)}) custom-call(bf16[368,1152]{1,0:T(8,128)(2,1)S(1)} %get-tuple-element.101.refs_0_, bf16[736,2304]{1,0:T(8,128)(2,1)S(1)} %copy-done.11, bf16[368,1152]{1,0:T(8,128)(2,1)S(1)} %copy-done.66, ...), custom_call_target="tpu_custom_call" | custom-call | flops 1109393408 | bytes 2225664 | tf_op jit(solution)/shard_map/attention_back/pallas_call | solution.py:156
  515.1 6.0 qkv_back.6
  523.6 4.6 collective-permute-done.39.refs_5_.refs_4_
  528.6 18.5 %unit_forward.1 = (bf16[2944,1088]{1,0:T(8,128)(2,1)}, bf16[2944,1088]{1,0:T(8,128)(2,1)}, f32[8,128]{1,0:T(8,128)S(1)}) custom-call(bf16[1472,1152]{1,0:T(8,128)(2,1)} %join_normed.1.refs_8_.refs_0_.refs_3_, bf16[1472,1152]{1,0:T(8,128)(2,1)} %collective-permute-done.38.refs_1_.refs_5_, bf16[1088,1152]{1,0:T(8,128)(2,1)} %bitcast.16.refs_4_.refs_1_.refs_6_.refs_2_, ...), custom_call_target="tpu_custom_call" | custom-call | flops 1033182912 | bytes 2034892 | tf_op jit(solution)/shard_map/unit_forward/pallas_call | solution.py:703
  550.8 3.8 copy-done.6
  554.7 17.5 %feed_back_last.1 = (f32[368,1152]{1,0:T(8,128)S(1)}, bf16[368,1152]{1,0:T(8,128)(2,1)S(1)}, bf16[368,1152]{1,0:T(8,128)(2,1)S(1)}, f32[1,1152]{1,0:T(1,128)S(1)}) custom-call(s32[4]{0:T(128)S(1)} %copy-done.74, f32[2,1152]{1,0:T(2,128)S(1)} %copy-done.47, f32[368,1152]{1,0:T(8,128)S(1)} %copy-done.22, bf16[368,4352]{1,0:T(8,128)(2,1)S(1)} %copy-done.19, ...), custom_call_target="tpu_custom_call" | custom-call | flops 835662656 | bytes 8132763 | tf_op jit(solution)/shard_map/feed_back_last/pallas_call | solution.py:156
  572.3 13.5 %attention_back.7 = (bf16[368,1152]{1,0:T(8,128)(2,1)S(1)}, bf16[368,2304]{1,0:T(8,128)(2,1)S(1)}, bf16[368,2304]{1,0:T(8,128)(2,1)S(1)}) custom-call(bf16[368,1152]{1,0:T(8,128)(2,1)S(1)} %get-tuple-element.101.refs_0_, bf16[736,2304]{1,0:T(8,128)(2,1)S(1)} %copy-done.12, bf16[368,1152]{1,0:T(8,128)(2,1)S(1)} %get-tuple-element.135.refs_2_, ...), custom_call_target="tpu_custom_call" | custom-call | flops 1109393408 | bytes 2225664 | tf_op jit(solution)/shard_map/attention_back/pallas_call | solution.py:156
  591.3 4.8 output_grads.1
  599.6 5.9 qkv_back.7
  608.6 7.1 %qkv_grads.1 = (f32[864,576]{1,0:T(8,128)S(1)}, bf16[448,1152]{1,0:T(8,128)(2,1)S(1)}, bf16[416,1152]{1,0:T(8,128)(2,1)S(1)}, bf16[208,1152]{1,0:T(8,128)(2,1)S(1)}, bf16[224,1152]{1,0:T(8,128)(2,1)S(1)}) custom-call(s32[4]{0:T(128)S(1)} %copy-done.74, bf16[368,1728]{1,0:T(8,128)(2,1)S(1)} %get-tuple-element.145.refs_1_, ...), custom_call_target="tpu_custom_call" | custom-call | flops 293024576 | bytes 1644136 | tf_op jit(solution)/shard_map/qkv_grads/pallas_call | solution.py:156
  628.2 23.1 %up_grads.1 = (f32[576,1076]{1,0:T(8,128)}, f32[8,128]{1,0:T(8,128)S(1)}) custom-call(s32[4]{0:T(128)S(1)} %copy-done.74, bf16[1088,1152]{1,0:T(8,128)(2,1)} %bitcast.17.refs_5_.refs_2_.refs_8_.refs_1_, bf16[2944,1088]{1,0:T(8,128)(2,1)} %get-tuple-element.148.refs_2_, bf16[1472,1152]{1,0:T(8,128)(2,1)} %join_normed.1.refs_8_.refs_0_.refs_3_, ...), custom_call_target="tpu_custom_call" | custom-call | flops 2951951104 | bytes 9488182 | tf_op jit(solution)/shard_map/up_grads/pallas_call | solution.py:156
  658.3 3.8 collective-permute-done.60.refs_3_.refs_2_
  665.7 13.9 %down_grads.1 = (f32[576,1076]{1,0:T(8,128)}, f32[8,128]{1,0:T(8,128)S(1)}) custom-call(s32[4]{0:T(128)S(1)} %copy-done.74, bf16[2944,1088]{1,0:T(8,128)(2,1)} %get-tuple-element.143.refs_1_, bf16[1472,1152]{1,0:T(8,128)(2,1)} %join_dy.1.refs_4_.refs_2_, bf16[1472,1152]{1,0:T(8,128)(2,1)} %copy-done.77, f32[8,128]{1,0:T(8,128)S(1)} %get-tuple-element.149.refs_4_, ...), custom_call_target="tpu_custom_call" | custom-call | flops 1475975552 | bytes 5772291 | tf_op jit(solution)/shard_map/down_grads/pallas_call | solution.py:156
  (363 shorter events, 144.1 us)
Async XLA Ops:
  6.6 85.9 %collective-permute-start.4 = (bf16[1664,1152]{1,0:T(8,128)(2,1)S(1)}, bf16[1664,1152]{1,0:T(8,128)(2,1)S(1)}, u32[]{:S(2)}, u32[]{:S(2)}) collective-permute-start(bf16[1664,1152]{1,0:T(8,128)(2,1)S(1)} %get-tuple-element.90.refs_1_), channel_id=1, source_target_pairs={{0,4},{4,0},{1,5},{5,1},{2,6},{6,2},{3,7},{7,3},{8,12},{12,8},{9,1... | collective-permute-start | bytes 11501576 | tf_op jit(solution)/shard_map/ppermute | solution.py:38
  9.7 92.2 %collective-permute-start.5 = (bf16[1664,1152]{1,0:T(8,128)(2,1)S(1)}, bf16[1664,1152]{1,0:T(8,128)(2,1)S(1)}, u32[]{:S(2)}, u32[]{:S(2)}) collective-permute-start(bf16[1664,1152]{1,0:T(8,128)(2,1)S(1)} %get-tuple-element.90.refs_1_), channel_id=1, source_target_pairs={{0,2},{1,3},{2,0},{3,1},{4,6},{5,7},{6,4},{7,5},{8,10},{9,11},{10,... | collective-permute-start | bytes 11501576 | tf_op jit(solution)/shard_map/ppermute | solution.py:34
  98.8 42.0 %collective-permute-start.8 = (bf16[4,288,1152]{2,1,0:T(8,128)(2,1)}, bf16[4,288,1152]{2,1,0:T(8,128)(2,1)}, u32[]{:S(2)}, u32[]{:S(2)}) collective-permute-start(bf16[4,288,1152]{2,1,0:T(8,128)(2,1)} %heads_near.1.refs_3_.refs_5_.refs_0_), channel_id=1, source_target_pairs={{0,1},{1,0},{2,3},{3,2},{4,5},{5,4},{6,7},{7,6},{8,9},{9,8},{10,11... | collective-permute-start | bytes 7962632 | tf_op jit(solution)/shard_map/ppermute | solution.py:29
  100.1 17.8 %collective-permute-start.6 = (bf16[288,1152]{1,0:T(8,128)(2,1)S(1)}, bf16[288,1152]{1,0:T(8,128)(2,1)S(1)}, u32[]{:S(2)}, u32[]{:S(2)}) collective-permute-start(bf16[288,1152]{1,0:T(8,128)(2,1)S(1)} %slice.88), channel_id=1, source_target_pairs={{0,2},{1,3},{2,0},{3,1},{4,6},{5,7},{6,4},{7,5},{8,10},{9,11},{10,... | collective-permute-start | bytes 1990664 | tf_op jit(solution)/shard_map/ppermute | solution.py:34
  101.9 17.1 %collective-permute-start.7 = (bf16[288,1152]{1,0:T(8,128)(2,1)S(1)}, bf16[288,1152]{1,0:T(8,128)(2,1)S(1)}, u32[]{:S(2)}, u32[]{:S(2)}) collective-permute-start(bf16[288,1152]{1,0:T(8,128)(2,1)S(1)} %slice.89), channel_id=1, source_target_pairs={{0,4},{4,0},{1,5},{5,1},{2,6},{6,2},{3,7},{7,3},{8,12},{12,8},{9,1... | collective-permute-start | bytes 1990664 | tf_op jit(solution)/shard_map/ppermute | solution.py:38
  103.5 29.0 %collective-permute-start.12 = (bf16[184,1152]{1,0:T(8,128)(2,1)S(1)}, bf16[184,1152]{1,0:T(8,128)(2,1)S(1)}, u32[]{:S(2)}, u32[]{:S(2)}) collective-permute-start(bf16[184,1152]{1,0:T(8,128)(2,1)S(1)} %get-tuple-element.92), channel_id=1, source_target_pairs={{0,2},{1,3},{2,0},{3,1},{4,6},{5,7},{6,4},{7,5},{8,10},{9,11},{10,... | collective-permute-start | bytes 1271816 | tf_op jit(solution)/shard_map/ppermute | solution.py:34
  124.2 20.2 %collective-permute-start.9 = (bf16[4,288,1152]{2,1,0:T(8,128)(2,1)}, bf16[4,288,1152]{2,1,0:T(8,128)(2,1)}, u32[]{:S(2)}, u32[]{:S(2)}) collective-permute-start(bf16[4,288,1152]{2,1,0:T(8,128)(2,1)} %heads_far.1.refs_6_.refs_1_), channel_id=1, source_target_pairs={{0,1},{1,0},{2,3},{3,2},{4,5},{5,4},{6,7},{7,6},{8,9},{9,8},{10,11... | collective-permute-start | bytes 7962632 | tf_op jit(solution)/shard_map/ppermute | solution.py:29
  129.6 35.1 %collective-permute-start.10 = (bf16[1088,1152]{1,0:T(8,128)(2,1)}, bf16[1088,1152]{1,0:T(8,128)(2,1)}, u32[]{:S(2)}, u32[]{:S(2)}) collective-permute-start(bf16[1088,1152]{1,0:T(8,128)(2,1)} %bitcast.16.refs_4_.refs_1_.refs_6_.refs_2_), channel_id=1, source_target_pairs={{0,1},{1,0},{2,3},{3,2},{4,5},{5,4},{6,7},{7,6},{8,9},{9,8},{10,11... | collective-permute-start | bytes 7520264 | tf_op jit(solution)/shard_map/ppermute | solution.py:29
  132.4 37.2 %collective-permute-start.14 = (bf16[1088,1152]{1,0:T(8,128)(2,1)}, bf16[1088,1152]{1,0:T(8,128)(2,1)}, u32[]{:S(2)}, u32[]{:S(2)}) collective-permute-start(bf16[1088,1152]{1,0:T(8,128)(2,1)} %bitcast.17.refs_5_.refs_2_.refs_8_.refs_1_), channel_id=1, source_target_pairs={{0,1},{1,0},{2,3},{3,2},{4,5},{5,4},{6,7},{7,6},{8,9},{9,8},{10,11... | collective-permute-start | bytes 7520264 | tf_op jit(solution)/shard_map/ppermute | solution.py:29
  139.5 35.4 %collective-permute-start.11 = (bf16[544,1152]{1,0:T(8,128)(2,1)}, bf16[544,1152]{1,0:T(8,128)(2,1)}, u32[]{:S(2)}, u32[]{:S(2)}) collective-permute-start(bf16[544,1152]{1,0:T(8,128)(2,1)} %copy-done.34), channel_id=1, source_target_pairs={{0,2},{1,3},{2,0},{3,1},{4,6},{5,7},{6,4},{7,5},{8,10},{9,11},{10,... | collective-permute-start | bytes 3760136 | tf_op jit(solution)/shard_map/ppermute | solution.py:34
  140.8 37.1 %collective-permute-start.16 = (bf16[544,1152]{1,0:T(8,128)(2,1)S(1)}, bf16[544,1152]{1,0:T(8,128)(2,1)}, u32[]{:S(2)}, u32[]{:S(2)}) collective-permute-start(bf16[544,1152]{1,0:T(8,128)(2,1)S(1)} %slice.91.refs_7_), channel_id=1, source_target_pairs={{0,4},{4,0},{1,5},{5,1},{2,6},{6,2},{3,7},{7,3},{8,12},{12,8},{9,1... | collective-permute-start | bytes 3760136 | tf_op jit(solution)/shard_map/ppermute | solution.py:38
  181.0 5.5 collective-permute-start.17
  189.7 21.9 %collective-permute-start.18 = (bf16[368,1152]{1,0:T(8,128)(2,1)S(1)}, bf16[368,1152]{1,0:T(8,128)(2,1)S(1)}, u32[]{:S(2)}, u32[]{:S(2)}) collective-permute-start(bf16[368,1152]{1,0:T(8,128)(2,1)S(1)} %feed_down.3.refs_12_), channel_id=1, source_target_pairs={{0,8},{8,16},{16,24},{1,9},{9,17},{17,25},{2,10},{10,18},{18,26},{... | collective-permute-start | bytes 2543624 | tf_op jit(solution)/shard_map/ppermute | solution.py:50
  240.9 22.5 %collective-permute-start.20 = (bf16[368,1152]{1,0:T(8,128)(2,1)}, bf16[368,1152]{1,0:T(8,128)(2,1)S(1)}, u32[]{:S(2)}, u32[]{:S(2)}) collective-permute-start(bf16[368,1152]{1,0:T(8,128)(2,1)} %layer_mid.2), channel_id=1, source_target_pairs={{0,8},{8,16},{16,24},{1,9},{9,17},{17,25},{2,10},{10,18},{18,26},{... | collective-permute-start | bytes 2543624 | tf_op jit(solution)/shard_map/ppermute | solution.py:50
  292.2 23.0 %collective-permute-start.22 = (bf16[368,1152]{1,0:T(8,128)(2,1)}, bf16[368,1152]{1,0:T(8,128)(2,1)S(1)}, u32[]{:S(2)}, u32[]{:S(2)}) collective-permute-start(bf16[368,1152]{1,0:T(8,128)(2,1)} %layer_mid.3), channel_id=1, source_target_pairs={{0,8},{8,16},{16,24},{1,9},{9,17},{17,25},{2,10},{10,18},{18,26},{... | collective-permute-start | bytes 2543624 | tf_op jit(solution)/shard_map/ppermute | solution.py:50
  316.1 28.0 %collective-permute-start.24 = (bf16[184,1152]{1,0:T(8,128)(2,1)S(1)}, bf16[184,1152]{1,0:T(8,128)(2,1)S(1)}, u32[]{:S(2)}, u32[]{:S(2)}) collective-permute-start(bf16[184,1152]{1,0:T(8,128)(2,1)S(1)} %pad.9), channel_id=1, source_target_pairs={{0,2},{1,3},{2,0},{3,1},{4,6},{5,7},{6,4},{7,5},{8,10},{9,11},{10,... | collective-permute-start | bytes 1271816 | tf_op jit(solution)/shard_map/ppermute | solution.py:34
  392.6 23.6 %collective-permute-start.27 = (bf16[368,1152]{1,0:T(8,128)(2,1)S(1)}, bf16[368,1152]{1,0:T(8,128)(2,1)S(1)}, u32[]{:S(2)}, u32[]{:S(2)}) collective-permute-start(bf16[368,1152]{1,0:T(8,128)(2,1)S(1)} %qkv_back.4), channel_id=1, source_target_pairs={{8,0},{16,8},{24,16},{9,1},{17,9},{25,17},{10,2},{18,10},{26,18},{... | collective-permute-start | bytes 2543624 | tf_op jit(solution)/shard_map/ppermute | solution.py:50
  395.6 12.7 %collective-permute-start.25 = (bf16[184,1152]{1,0:T(8,128)(2,1)S(1)}, bf16[184,1152]{1,0:T(8,128)(2,1)S(1)}, u32[]{:S(2)}, u32[]{:S(2)}) collective-permute-start(bf16[184,1152]{1,0:T(8,128)(2,1)S(1)} %slice.99), channel_id=1, source_target_pairs={{0,2},{1,3},{2,0},{3,1},{4,6},{5,7},{6,4},{7,5},{8,10},{9,11},{10,... | collective-permute-start | bytes 1271816 | tf_op jit(solution)/shard_map/ppermute | solution.py:34
  397.0 34.6 %collective-permute-start.28 = (bf16[192,1152]{1,0:T(8,128)(2,1)S(1)}, bf16[192,1152]{1,0:T(8,128)(2,1)S(1)}, u32[]{:S(2)}, u32[]{:S(2)}) collective-permute-start(bf16[192,1152]{1,0:T(8,128)(2,1)S(1)} %slice.73), channel_id=1, source_target_pairs={{0,2},{1,3},{2,0},{3,1},{4,6},{5,7},{6,4},{7,5},{8,10},{9,11},{10,... | collective-permute-start | bytes 1327112 | tf_op jit(solution)/shard_map/ppermute | solution.py:34
  397.9 33.8 %collective-permute-start.29 = (bf16[176,1152]{1,0:T(8,128)(2,1)S(1)}, bf16[176,1152]{1,0:T(8,128)(2,1)S(1)}, u32[]{:S(2)}, u32[]{:S(2)}) collective-permute-start(bf16[176,1152]{1,0:T(8,128)(2,1)S(1)} %slice.74), channel_id=1, source_target_pairs={{0,4},{4,0},{1,5},{5,1},{2,6},{6,2},{3,7},{7,3},{8,12},{12,8},{9,1... | collective-permute-start | bytes 1216520 | tf_op jit(solution)/shard_map/ppermute | solution.py:38
  454.1 22.8 %collective-permute-start.31 = (bf16[368,1152]{1,0:T(8,128)(2,1)S(1)}, bf16[368,1152]{1,0:T(8,128)(2,1)S(1)}, u32[]{:S(2)}, u32[]{:S(2)}) collective-permute-start(bf16[368,1152]{1,0:T(8,128)(2,1)S(1)} %qkv_back.5), channel_id=1, source_target_pairs={{8,0},{16,8},{24,16},{9,1},{17,9},{25,17},{10,2},{18,10},{26,18},{... | collective-permute-start | bytes 2543624 | tf_op jit(solution)/shard_map/ppermute | solution.py:50
  455.4 13.1 %collective-permute-start.33 = (bf16[192,1152]{1,0:T(8,128)(2,1)S(1)}, bf16[192,1152]{1,0:T(8,128)(2,1)S(1)}, u32[]{:S(2)}, u32[]{:S(2)}) collective-permute-start(bf16[192,1152]{1,0:T(8,128)(2,1)S(1)} %slice.73), channel_id=1, source_target_pairs={{0,4},{4,0},{1,5},{5,1},{2,6},{6,2},{3,7},{7,3},{8,12},{12,8},{9,1... | collective-permute-start | bytes 1327112 | tf_op jit(solution)/shard_map/ppermute | solution.py:38
  456.0 12.3 %collective-permute-start.32 = (bf16[176,1152]{1,0:T(8,128)(2,1)S(1)}, bf16[176,1152]{1,0:T(8,128)(2,1)S(1)}, u32[]{:S(2)}, u32[]{:S(2)}) collective-permute-start(bf16[176,1152]{1,0:T(8,128)(2,1)S(1)} %slice.74), channel_id=1, source_target_pairs={{0,2},{1,3},{2,0},{3,1},{4,6},{5,7},{6,4},{7,5},{8,10},{9,11},{10,... | collective-permute-start | bytes 1216520 | tf_op jit(solution)/shard_map/ppermute | solution.py:34
  457.3 36.6 %collective-permute-start.34 = (bf16[192,1152]{1,0:T(8,128)(2,1)S(1)}, bf16[192,1152]{1,0:T(8,128)(2,1)S(1)}, u32[]{:S(2)}, u32[]{:S(2)}) collective-permute-start(bf16[192,1152]{1,0:T(8,128)(2,1)S(1)} %collective-permute-done.28.refs_7_.refs_1_), channel_id=1, source_target_pairs={{0,4},{4,0},{1,5},{5,1},{2,6},{6,2},{3,7},{7,3},{8,12},{12,8},{9,1... | collective-permute-start | bytes 1327112 | tf_op jit(solution)/shard_map/ppermute | solution.py:38
  458.8 34.4 %collective-permute-start.35 = (bf16[176,1152]{1,0:T(8,128)(2,1)S(1)}, bf16[176,1152]{1,0:T(8,128)(2,1)S(1)}, u32[]{:S(2)}, u32[]{:S(2)}) collective-permute-start(bf16[176,1152]{1,0:T(8,128)(2,1)S(1)} %copy-done.61), channel_id=1, source_target_pairs={{0,2},{1,3},{2,0},{3,1},{4,6},{5,7},{6,4},{7,5},{8,10},{9,11},{10,... | collective-permute-start | bytes 1216520 | tf_op jit(solution)/shard_map/ppermute | solution.py:34
  521.0 7.6 %collective-permute-start.38 = (bf16[1472,1152]{1,0:T(8,128)(2,1)}, bf16[1472,1152]{1,0:T(8,128)(2,1)}, u32[]{:S(2)}, u32[]{:S(2)}) collective-permute-start(bf16[1472,1152]{1,0:T(8,128)(2,1)} %join_normed.1.refs_8_.refs_0_.refs_3_), channel_id=1, source_target_pairs={{0,1},{1,0},{2,3},{3,2},{4,5},{5,4},{6,7},{7,6},{8,9},{9,8},{10,11... | collective-permute-start | bytes 10174472 | tf_op jit(solution)/shard_map/ppermute | solution.py:29
  521.2 7.1 %collective-permute-start.39 = (bf16[368,1152]{1,0:T(8,128)(2,1)}, bf16[368,1152]{1,0:T(8,128)(2,1)S(1)}, u32[]{:S(2)}, u32[]{:S(2)}) collective-permute-start(bf16[368,1152]{1,0:T(8,128)(2,1)} %get-tuple-element.131.refs_3_), channel_id=1, source_target_pairs={{0,1},{1,0},{2,3},{3,2},{4,5},{5,4},{6,7},{7,6},{8,9},{9,8},{10,11... | collective-permute-start | bytes 2543624 | tf_op jit(solution)/shard_map/ppermute | solution.py:29
  521.5 25.6 %collective-permute-start.37 = (bf16[368,1152]{1,0:T(8,128)(2,1)}, bf16[368,1152]{1,0:T(8,128)(2,1)}, u32[]{:S(2)}, u32[]{:S(2)}) collective-permute-start(bf16[368,1152]{1,0:T(8,128)(2,1)} %qkv_back.6), channel_id=1, source_target_pairs={{8,0},{16,8},{24,16},{9,1},{17,9},{25,17},{10,2},{18,10},{26,18},{... | collective-permute-start | bytes 2543624 | tf_op jit(solution)/shard_map/ppermute | solution.py:50
  548.8 23.4 %collective-permute-start.40 = (bf16[192,1152]{1,0:T(8,128)(2,1)S(1)}, bf16[192,1152]{1,0:T(8,128)(2,1)S(1)}, u32[]{:S(2)}, u32[]{:S(2)}) collective-permute-start(bf16[192,1152]{1,0:T(8,128)(2,1)S(1)} %slice.93), channel_id=1, source_target_pairs={{0,2},{1,3},{2,0},{3,1},{4,6},{5,7},{6,4},{7,5},{8,10},{9,11},{10,... | collective-permute-start | bytes 1327112 | tf_op jit(solution)/shard_map/ppermute | solution.py:34
  550.2 22.0 %collective-permute-start.41 = (bf16[176,1152]{1,0:T(8,128)(2,1)S(1)}, bf16[176,1152]{1,0:T(8,128)(2,1)S(1)}, u32[]{:S(2)}, u32[]{:S(2)}) collective-permute-start(bf16[176,1152]{1,0:T(8,128)(2,1)S(1)} %slice.94), channel_id=1, source_target_pairs={{0,4},{4,0},{1,5},{5,1},{2,6},{6,2},{3,7},{7,3},{8,12},{12,8},{9,1... | collective-permute-start | bytes 1216520 | tf_op jit(solution)/shard_map/ppermute | solution.py:38
  585.8 13.8 %collective-permute-start.42 = (bf16[368,2304]{1,0:T(8,128)(2,1)S(1)}, bf16[368,2304]{1,0:T(8,128)(2,1)S(1)}, u32[]{:S(2)}, u32[]{:S(2)}) collective-permute-start(bf16[368,2304]{1,0:T(8,128)(2,1)S(1)} %get-tuple-element.138), channel_id=1, source_target_pairs={{0,1},{1,0},{2,3},{3,2},{4,5},{5,4},{6,7},{7,6},{8,9},{9,8},{10,11... | collective-permute-start | bytes 5087240 | tf_op jit(solution)/shard_map/ppermute | solution.py:29
  586.4 13.3 %collective-permute-start.45 = (bf16[192,1152]{1,0:T(8,128)(2,1)S(1)}, bf16[192,1152]{1,0:T(8,128)(2,1)S(1)}, u32[]{:S(2)}, u32[]{:S(2)}) collective-permute-start(bf16[192,1152]{1,0:T(8,128)(2,1)S(1)} %collective-permute-done.40.refs_7_.refs_1_), channel_id=1, source_target_pairs={{0,4},{4,0},{1,5},{5,1},{2,6},{6,2},{3,7},{7,3},{8,12},{12,8},{9,1... | collective-permute-start | bytes 1327112 | tf_op jit(solution)/shard_map/ppermute | solution.py:38
  587.8 11.8 %collective-permute-start.46 = (bf16[176,1152]{1,0:T(8,128)(2,1)S(1)}, bf16[176,1152]{1,0:T(8,128)(2,1)S(1)}, u32[]{:S(2)}, u32[]{:S(2)}) collective-permute-start(bf16[176,1152]{1,0:T(8,128)(2,1)S(1)} %collective-permute-done.41.refs_8_.refs_4_), channel_id=1, source_target_pairs={{0,2},{1,3},{2,0},{3,1},{4,6},{5,7},{6,4},{7,5},{8,10},{9,11},{10,... | collective-permute-start | bytes 1216520 | tf_op jit(solution)/shard_map/ppermute | solution.py:34
  605.6 12.6 %collective-permute-start.49 = (bf16[192,1152]{1,0:T(8,128)(2,1)S(1)}, bf16[192,1152]{1,0:T(8,128)(2,1)S(1)}, u32[]{:S(2)}, u32[]{:S(2)}) collective-permute-start(bf16[192,1152]{1,0:T(8,128)(2,1)S(1)} %slice.83), channel_id=1, source_target_pairs={{0,4},{4,0},{1,5},{5,1},{2,6},{6,2},{3,7},{7,3},{8,12},{12,8},{9,1... | collective-permute-start | bytes 1327112 | tf_op jit(solution)/shard_map/ppermute | solution.py:38
  606.3 11.6 %collective-permute-start.48 = (bf16[176,1152]{1,0:T(8,128)(2,1)S(1)}, bf16[176,1152]{1,0:T(8,128)(2,1)S(1)}, u32[]{:S(2)}, u32[]{:S(2)}) collective-permute-start(bf16[176,1152]{1,0:T(8,128)(2,1)S(1)} %slice.82), channel_id=1, source_target_pairs={{0,2},{1,3},{2,0},{3,1},{4,6},{5,7},{6,4},{7,5},{8,10},{9,11},{10,... | collective-permute-start | bytes 1216520 | tf_op jit(solution)/shard_map/ppermute | solution.py:34
  620.2 6.2 collective-permute-start.51
  620.2 32.0 %collective-permute-start.55 = (bf16[448,1152]{1,0:T(8,128)(2,1)S(1)}, bf16[448,1152]{1,0:T(8,128)(2,1)S(1)}, u32[]{:S(2)}, u32[]{:S(2)}) collective-permute-start(bf16[448,1152]{1,0:T(8,128)(2,1)S(1)} %get-tuple-element.154), channel_id=1, source_target_pairs={{0,2},{1,3},{2,0},{3,1},{4,6},{5,7},{6,4},{7,5},{8,10},{9,11},{10,... | collective-permute-start | bytes 3096584 | tf_op jit(solution)/shard_map/ppermute | solution.py:34
  621.0 30.3 %collective-permute-start.56 = (bf16[416,1152]{1,0:T(8,128)(2,1)S(1)}, bf16[416,1152]{1,0:T(8,128)(2,1)S(1)}, u32[]{:S(2)}, u32[]{:S(2)}) collective-permute-start(bf16[416,1152]{1,0:T(8,128)(2,1)S(1)} %get-tuple-element.155), channel_id=1, source_target_pairs={{0,4},{4,0},{1,5},{5,1},{2,6},{6,2},{3,7},{7,3},{8,12},{12,8},{9,1... | collective-permute-start | bytes 2875400 | tf_op jit(solution)/shard_map/ppermute | solution.py:38
  622.1 33.2 %collective-permute-start.52 = (f32[2,1152]{1,0:T(2,128)S(1)}, f32[2,1152]{1,0:T(2,128)S(1)}, u32[]{:S(2)}, u32[]{:S(2)}) collective-permute-start(f32[2,1152]{1,0:T(2,128)S(1)} %pad_maximum_fusion.3), channel_id=1, source_target_pairs={{0,2},{1,3},{2,0},{3,1},{4,6},{5,7},{6,4},{7,5},{8,10},{9,11},{10,... | collective-permute-start | bytes 27656 | tf_op jit(solution)/shard_map/ppermute | solution.py:34
  623.4 33.1 %collective-permute-start.53 = (f32[2,1152]{1,0:T(2,128)S(1)}, f32[2,1152]{1,0:T(2,128)S(1)}, u32[]{:S(2)}, u32[]{:S(2)}) collective-permute-start(f32[2,1152]{1,0:T(2,128)S(1)} %pad_maximum_fusion.3), channel_id=1, source_target_pairs={{0,4},{4,0},{1,5},{5,1},{2,6},{6,2},{3,7},{7,3},{8,12},{12,8},{9,1... | collective-permute-start | bytes 27656 | tf_op jit(solution)/shard_map/ppermute | solution.py:38
  626.4 31.1 %collective-permute-start.54 = (f32[2,1152]{1,0:T(2,128)S(1)}, f32[2,1152]{1,0:T(2,128)S(1)}, u32[]{:S(2)}, u32[]{:S(2)}) collective-permute-start(f32[2,1152]{1,0:T(2,128)S(1)} %pad_maximum_fusion.3), channel_id=1, source_target_pairs={{0,6},{1,7},{2,4},{3,5},{4,2},{5,3},{6,0},{7,1},{8,14},{9,15},{10,... | collective-permute-start | bytes 27656 | tf_op jit(solution)/shard_map/ppermute | solution.py:44
  651.3 11.7 %collective-permute-start.59 = (bf16[160,1152]{1,0:T(8,128)(2,1)}, bf16[160,1152]{1,0:T(8,128)(2,1)S(1)}, u32[]{:S(2)}, u32[]{:S(2)}) collective-permute-start(bf16[160,1152]{1,0:T(8,128)(2,1)} %get-tuple-element.164), channel_id=1, source_target_pairs={{0,2},{1,3},{2,0},{3,1},{4,6},{5,7},{6,4},{7,5},{8,10},{9,11},{10,... | collective-permute-start | bytes 1105928 | tf_op jit(solution)/shard_map/ppermute | solution.py:34
  652.2 9.9 %collective-permute-start.60 = (bf16[128,1152]{1,0:T(8,128)(2,1)S(1)}, bf16[128,1152]{1,0:T(8,128)(2,1)S(1)}, u32[]{:S(2)}, u32[]{:S(2)}) collective-permute-start(bf16[128,1152]{1,0:T(8,128)(2,1)S(1)} %get-tuple-element.165), channel_id=1, source_target_pairs={{0,4},{4,0},{1,5},{5,1},{2,6},{6,2},{3,7},{7,3},{8,12},{12,8},{9,1... | collective-permute-start | bytes 884744 | tf_op jit(solution)/shard_map/ppermute | solution.py:38
  655.3 24.4 %collective-permute-start.47 = (bf16[184,1152]{1,0:T(8,128)(2,1)}, bf16[184,1152]{1,0:T(8,128)(2,1)S(1)}, u32[]{:S(2)}, u32[]{:S(2)}) collective-permute-start(bf16[184,1152]{1,0:T(8,128)(2,1)} %slice.98), channel_id=1, source_target_pairs={{0,2},{1,3},{2,0},{3,1},{4,6},{5,7},{6,4},{7,5},{8,10},{9,11},{10,... | collective-permute-start | bytes 1271816 | tf_op jit(solution)/shard_map/ppermute | solution.py:34
  656.5 29.4 %collective-permute-start.57 = (bf16[224,1152]{1,0:T(8,128)(2,1)}, bf16[224,1152]{1,0:T(8,128)(2,1)}, u32[]{:S(2)}, u32[]{:S(2)}) collective-permute-start(bf16[224,1152]{1,0:T(8,128)(2,1)} %get-tuple-element.158), channel_id=1, source_target_pairs={{0,4},{4,0},{1,5},{5,1},{2,6},{6,2},{3,7},{7,3},{8,12},{12,8},{9,1... | collective-permute-start | bytes 1548296 | tf_op jit(solution)/shard_map/ppermute | solution.py:38
  657.5 28.4 %collective-permute-start.58 = (bf16[208,1152]{1,0:T(8,128)(2,1)}, bf16[208,1152]{1,0:T(8,128)(2,1)}, u32[]{:S(2)}, u32[]{:S(2)}) collective-permute-start(bf16[208,1152]{1,0:T(8,128)(2,1)} %get-tuple-element.159), channel_id=1, source_target_pairs={{0,2},{1,3},{2,0},{3,1},{4,6},{5,7},{6,4},{7,5},{8,10},{9,11},{10,... | collective-permute-start | bytes 1437704 | tf_op jit(solution)/shard_map/ppermute | solution.py:34
  663.1 21.6 %collective-permute-start.61 = (bf16[80,1152]{1,0:T(8,128)(2,1)S(1)}, bf16[80,1152]{1,0:T(8,128)(2,1)S(1)}, u32[]{:S(2)}, u32[]{:S(2)}) collective-permute-start(bf16[80,1152]{1,0:T(8,128)(2,1)S(1)} %get-tuple-element.167), channel_id=1, source_target_pairs={{0,4},{4,0},{1,5},{5,1},{2,6},{6,2},{3,7},{7,3},{8,12},{12,8},{9,1... | collective-permute-start | bytes 552968 | tf_op jit(solution)/shard_map/ppermute | solution.py:38
  664.3 20.5 %collective-permute-start.62 = (bf16[64,1152]{1,0:T(8,128)(2,1)S(1)}, bf16[64,1152]{1,0:T(8,128)(2,1)S(1)}, u32[]{:S(2)}, u32[]{:S(2)}) collective-permute-start(bf16[64,1152]{1,0:T(8,128)(2,1)S(1)} %get-tuple-element.168), channel_id=1, source_target_pairs={{0,2},{1,3},{2,0},{3,1},{4,6},{5,7},{6,4},{7,5},{8,10},{9,11},{10,... | collective-permute-start | bytes 442376 | tf_op jit(solution)/shard_map/ppermute | solution.py:34
  (115 other events, 2149.0 us)
